TPU v7x, 32 devices: a whole 2x2x4 slice. The times are simulated.
32 devices in a mesh: seq: 8 (over y, x, core), batch: 4 (over z).
Axes of the slice: x: 2, y: 2, z: 4, core: 2. Of those that a mesh axis runs over, the one named last changes fastest.
Arguments:
- inputs: bfloat16 [4, 2048, 2048], P('batch', 'seq'), may hold values from -106.50967 to 106.50967
- output_grad: bfloat16 [4, 2048, 2048], P('batch', 'seq'), may hold values from -6 to 6
- norm_gain: float32 [2048], replicated, may hold values from 0.1 to 1.9
- gate_bias: float32 [2048], P('seq'), as said below
- state_in: float32 [4, 2048], P('batch', 'seq'), may hold values from -6 to 6
- w_gate: bfloat16 [2048, 2048], P('seq'), may hold values from -0.44194174 to 0.44194174
- w_cand: bfloat16 [2048, 2048], P('seq'), may hold values from -0.125 to 0.125
- w_out: bfloat16 [2048, 2048], P('seq'), may hold values from -0.125 to 0.125
Outputs:
- layer_out: bfloat16 [4, 2048, 2048], P('batch', 'seq')
- input_grad: bfloat16 [4, 2048, 2048], P('batch', 'seq')
- state_grad: float32 [4, 2048], P('batch', 'seq')
- bias_grad: float32 [2048], P('seq')
Inputs may be any that keep to these rules, and one draw needn't show every extreme that they name: `gate_bias`: every value is at least -ln(2048) - 1.5.
All inputs are finite; a program needn't handle non-finite values.
Results may differ from a plain program's by a relative error of at most 0.013.
Values may be sent and summed in bfloat16 or wider, within the bound.
No kernel may reach another device: no remote copies, remote signals or barrier semaphores. Data moves between devices by JAX's collectives and lax.ppermute only.
A program may use at most 128 MiB of HBM per device.

v0:
```python
import functools

import jax
import jax.numpy as jnp
from jax import lax
from jax.experimental import pallas as pl
from jax.experimental.pallas import tpu as pltpu
from jax.sharding import PartitionSpec as P

EPSILON = 1e-06
SEGMENTS = 8
F32 = jnp.float32
BF16 = jnp.bfloat16


def params(mebibytes):
    return pltpu.CompilerParams(vmem_limit_bytes=mebibytes * 1024 * 1024)


def cost(flops, moved):
    return pl.CostEstimate(flops=int(flops), bytes_accessed=int(moved), transcendentals=0)


def hop(value, offset, count):
    return lax.ppermute(value, "seq", [(i, i ^ offset) for i in range(count)])


def swap_batch(value, offset, count):
    return lax.ppermute(value, "batch", [(i, i ^ offset) for i in range(count)])


def after(values, *earlier):
    return lax.optimization_barrier(tuple(values) + tuple(earlier))[: len(values)]


def place(rows):
    steps = rows // SEGMENTS
    out = lax.broadcasted_iota(jnp.int32, (rows, rows), 0)
    inn = lax.broadcasted_iota(jnp.int32, (rows, rows), 1)
    source = lax.rem(out, SEGMENTS) * steps + lax.div(out, SEGMENTS)
    return (source == inn).astype(F32).astype(BF16)


def place_back(rows):
    steps = rows // SEGMENTS
    out = lax.broadcasted_iota(jnp.int32, (rows, rows), 0)
    inn = lax.broadcasted_iota(jnp.int32, (rows, rows), 1)
    source = lax.rem(out, steps) * SEGMENTS + lax.div(out, steps)
    return (source == inn).astype(F32).astype(BF16)


def dot(a, b):
    return lax.dot_general(a, b, (((1,), (0,)), ((), ())), preferred_element_type=F32)


def tiles(count, tile, body):
    @pl.loop(0, count // tile)
    def _(index):
        body(pl.ds(pl.multiple_of(index * tile, tile), tile))


class Shards:
    def __init__(self, groups):
        self.groups = groups
        self.pieces = [piece for group in groups for piece in group]
        self.depth = sum(piece.shape[0] for piece in groups[0])
        self.width = groups[0][0].shape[1]

    def copies(self, refs, buffer, sems, slot_of):
        out, position = [], 0
        for index, group in enumerate(self.groups):
            start, made = slot_of(index) * self.depth, []
            for piece in group:
                rows = piece.shape[0]
                made.append(
                    pltpu.make_async_copy(refs[position], buffer.at[pl.ds(start, rows), :], sems.at[position])
                )
                start, position = start + rows, position + 1
            out.append(made)
        return out


VMEM_SPEC = pl.BlockSpec(memory_space=pltpu.VMEM)
SMEM_SPEC = pl.BlockSpec(memory_space=pltpu.SMEM)
ANY_SPEC = pl.BlockSpec(memory_space=pl.ANY)


def norm_call(where, x, g, gain, depth):
    rows, width = x.shape

    def kernel(where_ref, x_ref, g_ref, gain_ref, normed_ref, grads_ref, hold):
        def rows_body(span):
            x = x_ref[span, :].astype(F32)
            scale = lax.rsqrt(jnp.mean(x * x, axis=-1, keepdims=True) + EPSILON)
            hold[span, :] = (x * scale * gain_ref[...]).astype(BF16)

        tiles(rows, min(32, rows), rows_body)
        order = place(rows)
        for index in range(width // depth):
            source = pl.ds(pl.multiple_of((where_ref[0] ^ index) * depth, depth), depth)
            normed_ref[:, index * depth : (index + 1) * depth] = dot(order, hold[:, source]).astype(BF16)

        def grads_body(span):
            grads_ref[span, :] = dot(order, g_ref[:, span]).T.astype(BF16)

        tiles(width, min(512, width), grads_body)

    return pl.pallas_call(
        kernel,
        out_shape=[jax.ShapeDtypeStruct((rows, width), BF16), jax.ShapeDtypeStruct((width, rows), BF16)],
        in_specs=[SMEM_SPEC] + [VMEM_SPEC] * 3,
        out_specs=[VMEM_SPEC] * 2,
        scratch_shapes=[pltpu.VMEM(x.shape, BF16)],
        compiler_params=params(12),
        cost_estimate=cost(4 * rows * x.size, 8 * x.size),
        name="norm_rows",
    )(where, x, g, gain)


def project_call(x, shards, tile, dtype, skip=0):
    rows, width = x.shape[0], shards.width
    count, depth = len(shards.groups), shards.depth
    span_in = slice(skip, skip + count * depth)

    def kernel(x_ref, *refs):
        refs, (out_ref, held, sems) = refs[:-3], refs[-3:]
        copies = [c for made in shards.copies(refs, held, sems, lambda i: i) for c in made]
        for c in copies:
            c.start()
        for c in copies:
            c.wait()

        def body(span):
            out_ref[:, span] = dot(x_ref[:, span_in], held[:, span]).astype(dtype)

        tiles(width, tile, body)

    return pl.pallas_call(
        kernel,
        out_shape=jax.ShapeDtypeStruct((rows, width), dtype),
        in_specs=[VMEM_SPEC] + [ANY_SPEC] * len(shards.pieces),
        out_specs=VMEM_SPEC,
        scratch_shapes=[
            pltpu.VMEM((count * depth, width), BF16),
            pltpu.SemaphoreType.DMA((len(shards.pieces),)),
        ],
        compiler_params=params(16),
        cost_estimate=cost(2 * rows * count * depth * width, 2 * count * depth * width),
        name="project",
    )(x, *shards.pieces)


def back_call(where, grads, shards):
    width, rows = grads.shape
    count, depth = len(shards.groups), shards.depth

    def kernel(where_ref, g_ref, *refs):
        refs, (out_ref, held, sems) = refs[:-3], refs[-3:]
        copies = shards.copies(refs, held, sems, lambda i: i)
        for made in copies:
            for c in made:
                c.start()
        for index, made in enumerate(copies):
            for c in made:
                c.wait()
            target = pl.multiple_of((where_ref[0] ^ index) * depth, depth)
            for part in range(0, depth, min(depth, 256)):
                size = min(depth, 256)
                block = held[index * depth + part : index * depth + part + size, :]
                out_ref[:, pl.ds(pl.multiple_of(target + part, size), size)] = dot(block, g_ref[...]).T.astype(BF16)

    return pl.pallas_call(
        kernel,
        out_shape=jax.ShapeDtypeStruct((rows, count * depth), BF16),
        in_specs=[SMEM_SPEC, VMEM_SPEC] + [ANY_SPEC] * len(shards.pieces),
        out_specs=VMEM_SPEC,
        scratch_shapes=[
            pltpu.VMEM((count * depth, width), BF16),
            pltpu.SemaphoreType.DMA((len(shards.pieces),)),
        ],
        compiler_params=params(16),
        cost_estimate=cost(2 * rows * count * depth * width, 2 * count * depth * width),
        name="back_rows",
    )(where, grads, *shards.pieces)


def gates(x):
    small = jnp.exp(-jnp.abs(x))
    large = 1.0 / (1.0 + small)
    small = small * large
    up = x >= 0
    return jnp.where(up, large, small), jnp.where(up, small, large)


def slab_pair(ref, pair, span):
    both = ref[pair * 2 * SEGMENTS : (pair + 1) * 2 * SEGMENTS, span].astype(F32)
    return both[:SEGMENTS], both[SEGMENTS:]


def choose(where_ref, one, other):
    straight = where_ref[1] == 0
    return jnp.where(straight, one, other), jnp.where(straight, other, one)


def totals_call(where, x, partial, shards, skip, first_pre, back, bias, tile):
    rows, width = first_pre.shape
    pairs = rows // (2 * SEGMENTS)
    count, depth = len(shards.groups), shards.depth
    extra = [] if partial is None else [partial]

    def kernel(where_ref, x_ref, first_ref, back_ref, bias_ref, *refs):
        partial_refs, refs = refs[: len(extra)], refs[len(extra) :]
        refs, (second_ref, parts_ref, whole_ref, held, sems) = refs[:-5], refs[-5:]
        copies = [c for made in shards.copies(refs, held, sems, lambda i: i) for c in made]
        for c in copies:
            c.start()
        for c in copies:
            c.wait()

        def body(span):
            total = dot(x_ref[:, skip : skip + count * depth], held[:, span])
            for ref in partial_refs:
                total = total + ref[:, span]
            second_ref[:, span] = total.astype(BF16)
            bias = bias_ref[:, span]
            keep = jnp.ones((SEGMENTS, tile), F32)
            state = leaving = jnp.zeros((SEGMENTS, tile), F32)
            for pair in range(pairs):
                slabs = [slab_pair(ref, pair, span) for ref in (first_ref, second_ref, back_ref)]
                for a, b, g in zip(*slabs):
                    gate, cand = choose(where_ref, a, b)
                    update, retain = gates(gate + bias)
                    keep = keep * retain
                    state = retain * state + update * cand
                    leaving = leaving + keep * g
            parts_ref[0, :, span], parts_ref[1, :, span], parts_ref[2, :, span] = keep, state, leaving
            whole_keep, whole_state = keep[0:1], state[0:1]
            for s in range(1, SEGMENTS):
                whole_state = keep[s : s + 1] * whole_state + state[s : s + 1]
                whole_keep = whole_keep * keep[s : s + 1]
            whole_leaving = leaving[SEGMENTS - 1 :]
            for s in range(SEGMENTS - 2, -1, -1):
                whole_leaving = keep[s : s + 1] * whole_leaving + leaving[s : s + 1]
            whole_ref[0:1, span], whole_ref[1:2, span], whole_ref[2:3, span] = whole_keep, whole_state, whole_leaving

        tiles(width, tile, body)

    return pl.pallas_call(
        kernel,
        out_shape=[
            jax.ShapeDtypeStruct((rows, width), BF16),
            jax.ShapeDtypeStruct((3, SEGMENTS, width), F32),
            jax.ShapeDtypeStruct((3, width), F32),
        ],
        in_specs=[SMEM_SPEC] + [VMEM_SPEC] * (4 + len(extra)) + [ANY_SPEC] * len(shards.pieces),
        out_specs=[VMEM_SPEC] * 3,
        scratch_shapes=[
            pltpu.VMEM((count * depth, width), BF16),
            pltpu.SemaphoreType.DMA((len(shards.pieces),)),
        ],
        compiler_params=params(20),
        cost_estimate=cost(2 * rows * count * depth * width, 2 * count * depth * width),
        name="project_totals",
    )(where, x, first_pre, back, bias, *extra, *shards.pieces)


def scan_call(where, first_pre, second_pre, back, bias, initial, parts, wholes, ranks, tile):
    rows, width = first_pre.shape
    pairs = rows // (2 * SEGMENTS)

    def kernel(where_ref, first_ref, second_ref, back_ref, bias_ref, initial_ref, parts_ref, wholes_ref, *refs):
        (state_ref, one_ref, other_ref, bias_grad_ref, state_grad_ref) = refs[:5]
        kept, updates, slopes, one_hold, other_hold, state_hold = refs[5:]
        me = where_ref[2]
        order = place_back(rows)

        def body(span):
            entering = initial_ref[:, span]
            blocks = [wholes_ref[rank, :, span] for rank in range(ranks)]
            for rank in range(ranks):
                block = blocks[rank]
                entering = jnp.where(rank < me, block[0:1] * entering + block[1:2], entering)
            arriving = state_grad = blocks[0][2:3] * 0.0
            for rank in range(ranks - 1, -1, -1):
                block = blocks[rank]
                arriving = jnp.where(rank == me, state_grad, arriving)
                state_grad = block[0:1] * state_grad + block[2:3]
            state_grad_ref[:, span] = state_grad
            keep, ends, leaves = parts_ref[0, :, span], parts_ref[1, :, span], parts_ref[2, :, span]
            starts = [entering]
            for s in range(SEGMENTS - 1):
                starts.append(keep[s : s + 1] * starts[-1] + ends[s : s + 1])
            tails = [arriving]
            for s in range(SEGMENTS - 1, 0, -1):
                tails.append(keep[s : s + 1] * tails[-1] + leaves[s : s + 1])
            state = jnp.concatenate(starts, axis=0)
            leaving = jnp.concatenate(tails[::-1], axis=0)
            bias = bias_ref[:, span]

            for pair in range(pairs):
                states, retains, ups, slope = [], [], [], []
                for a, b in zip(slab_pair(first_ref, pair, span), slab_pair(second_ref, pair, span)):
                    gate, cand = choose(where_ref, a, b)
                    update, retain = gates(gate + bias)
                    retains.append(retain)
                    ups.append(update)
                    slope.append((cand - state) * update * retain)
                    state = retain * state + update * cand
                    states.append(state)
                here = slice(pair * 2 * SEGMENTS, (pair + 1) * 2 * SEGMENTS)
                state_hold[here, :] = jnp.concatenate(states, axis=0).astype(BF16)
                kept[here, :] = jnp.concatenate(retains, axis=0)
                updates[here, :] = jnp.concatenate(ups, axis=0)
                slopes[here, :] = jnp.concatenate(slope, axis=0)

            total = jnp.zeros((SEGMENTS, tile), F32)
            for pair in range(pairs - 1, -1, -1):
                here = slice(pair * 2 * SEGMENTS, (pair + 1) * 2 * SEGMENTS)
                grads = slab_pair(back_ref, pair, span)
                retain, update, slope = kept[here, :], updates[here, :], slopes[here, :]
                late = grads[1] + leaving
                early = grads[0] + retain[SEGMENTS:] * late
                leaving = retain[:SEGMENTS] * early
                carried = jnp.concatenate([early, late], axis=0)
                gate_grad = carried * slope
                cand_grad = carried * update
                total = total + gate_grad[:SEGMENTS] + gate_grad[SEGMENTS:]
                one, other = choose(where_ref, gate_grad, cand_grad)
                one_hold[here, :] = one.astype(BF16)
                other_hold[here, :] = other.astype(BF16)
            bias_grad_ref[:, span] = jnp.sum(total, axis=0, keepdims=True)
            state_ref[:, span] = dot(order, state_hold[...]).astype(BF16)
            one_ref[span, :] = dot(order, one_hold[...]).T.astype(BF16)
            other_ref[span, :] = dot(order, other_hold[...]).T.astype(BF16)

        tiles(width, tile, body)

    wide = jax.ShapeDtypeStruct((rows, width), BF16)
    tall = jax.ShapeDtypeStruct((width, rows), BF16)
    flat = jax.ShapeDtypeStruct((1, width), F32)
    return pl.pallas_call(
        kernel,
        out_shape=[wide, tall, tall, flat, flat],
        in_specs=[SMEM_SPEC] + [VMEM_SPEC] * 7,
        out_specs=[VMEM_SPEC] * 5,
        scratch_shapes=[pltpu.VMEM((rows, tile), F32)] * 3 + [pltpu.VMEM((rows, tile), BF16)] * 3,
        compiler_params=params(16),
        cost_estimate=cost(6 * rows * rows * width, 12 * rows * width),
        name="scan_rows",
    )(where, first_pre, second_pre, back, bias, initial, parts, wholes)


def layer_call(where, state_rows, residual, shards, tile):
    rows, width = residual.shape
    count, depth = len(shards.groups), shards.depth

    def kernel(where_ref, x_ref, residual_ref, *refs):
        refs, (out_ref, held, ordered, sems) = refs[:-4], refs[-4:]
        copies = [c for made in shards.copies(refs, held, sems, lambda i: i) for c in made]
        for c in copies:
            c.start()
        for index in range(count):
            source = pl.ds(pl.multiple_of((where_ref[0] ^ index) * depth, depth), depth)
            ordered[:, index * depth : (index + 1) * depth] = x_ref[:, source]
        for c in copies:
            c.wait()

        def body(span):
            out_ref[:, span] = (residual_ref[:, span].astype(F32) + dot(ordered[...], held[:, span])).astype(BF16)

        tiles(width, tile, body)

    return pl.pallas_call(
        kernel,
        out_shape=jax.ShapeDtypeStruct((rows, width), BF16),
        in_specs=[SMEM_SPEC] + [VMEM_SPEC] * 2 + [ANY_SPEC] * len(shards.pieces),
        out_specs=VMEM_SPEC,
        scratch_shapes=[
            pltpu.VMEM((count * depth, width), BF16),
            pltpu.VMEM((rows, count * depth), BF16),
            pltpu.SemaphoreType.DMA((len(shards.pieces),)),
        ],
        compiler_params=params(18),
        cost_estimate=cost(2 * rows * count * depth * width, 2 * count * depth * width),
        name="layer_rows",
    )(where, state_rows, residual, *shards.pieces)


def input_grad_call(where, one, other, first, second, x, grads, gain):
    rows, width = x.shape
    hidden = one.shape[0]
    count, depth = len(first.groups), first.depth
    slots = min(count, 4)

    def kernel(where_ref, one_ref, other_ref, x_ref, grads_ref, gain_ref, *refs):
        first_refs = refs[: len(first.pieces)]
        second_refs = refs[len(first.pieces) : len(first.pieces) + len(second.pieces)]
        out_ref, first_held, second_held, total, first_sems, second_sems = refs[-6:]
        copies = [
            a + b
            for a, b in zip(
                first.copies(first_refs, first_held, first_sems, lambda i: i % slots),
                second.copies(second_refs, second_held, second_sems, lambda i: i % slots),
            )
        ]
        for made in copies[:slots]:
            for c in made:
                c.start()
        size = min(depth, 256)
        for index, made in enumerate(copies):
            for c in made:
                c.wait()
            target = pl.multiple_of((where_ref[0] ^ index) * depth, depth)
            for part in range(0, depth, size):
                here = slice(index % slots * depth + part, index % slots * depth + part + size)
                term = dot(first_held[here, :], one_ref[...]) + dot(second_held[here, :], other_ref[...])
                total[:, pl.ds(pl.multiple_of(target + part, size), size)] = term.T
            if index + slots < count:
                for c in copies[index + slots]:
                    c.start()

        def body(span):
            x = x_ref[span, :].astype(F32)
            scale = lax.rsqrt(jnp.mean(x * x, axis=-1, keepdims=True) + EPSILON)
            unit = x * scale
            unit_grad = total[span, :] * gain_ref[...]
            along = jnp.mean(unit_grad * unit, axis=-1, keepdims=True)
            out = grads_ref[span, :].astype(F32) + scale * (unit_grad - unit * along)
            out_ref[span, :] = out.astype(BF16)

        tiles(rows, min(32, rows), body)

    return pl.pallas_call(
        kernel,
        out_shape=jax.ShapeDtypeStruct((rows, width), BF16),
        in_specs=[SMEM_SPEC] + [VMEM_SPEC] * 5 + [ANY_SPEC] * (len(first.pieces) + len(second.pieces)),
        out_specs=VMEM_SPEC,
        scratch_shapes=[
            pltpu.VMEM((slots * depth, hidden), BF16),
            pltpu.VMEM((slots * depth, hidden), BF16),
            pltpu.VMEM((rows, width), F32),
            pltpu.SemaphoreType.DMA((len(first.pieces),)),
            pltpu.SemaphoreType.DMA((len(second.pieces),)),
        ],
        compiler_params=params(24),
        cost_estimate=cost(4 * one.size * width, 4 * hidden * width),
        name="input_grad_rows",
    )(where, one, other, x, grads, gain, *first.pieces, *second.pieces)


def gathered_rows(gate_bias, state_in):
    both = lax.all_gather(jnp.stack([gate_bias, state_in[0]]), "seq", axis=1, tiled=True)
    return both[0:1], both[1:2]


def front_on_cube(ranks, batches, where, turned, tile, rows_in, grad_rows, gain, gate_bias, state_in, w_gate, w_cand, w_out):
    half = w_gate.shape[0] // 2
    depth = w_gate.shape[0]
    halves = lambda w: (w[:half], w[half:])
    straight = turned == 0
    own_f = [jnp.where(straight, a, b) for a, b in zip(halves(w_gate), halves(w_cand))]
    send = lambda value, offset: hop(value, offset, ranks)
    core = lambda value: hop(value, 1, ranks)
    over = lambda value: swap_batch(value, 1, batches)

    f2a, f4a = send(own_f[0], 2), send(own_f[0], 4)
    f2b, f4b = send(own_f[1], 2), send(own_f[1], 4)
    own_s = jnp.where(straight, w_cand, w_gate)
    own_t = halves(w_out)
    f1 = [core(v) for v in own_f]
    s1, t1 = core(own_s), core(w_out)
    bias, initial = gathered_rows(gate_bias, state_in)
    normed, grads = norm_call(where, rows_in, grad_rows, gain, depth)

    f2a, f4a, t2a_in, normed, grads, bias, initial = after((f2a, f4a, own_t[0], normed, grads, bias, initial))
    t2a, f6a, s2a = send(t2a_in, 2), send(f2a, 4), over(f2a)
    f3a, f5a = core(f2a), core(f4a)
    f2b, f4b, t4a_in, s4a_in = after((f2b, f4b, own_t[0], f4a))
    f6b, t4a, s4a = send(f4b, 2), send(t4a_in, 4), over(s4a_in)
    f3b, f5b = core(f2b), core(f4b)
    t2a, f6a, t2b_in, t4b_in, s2b_in = after((t2a, f6a, own_t[1], own_t[1], f2b), f6a)
    t2b, t4b, s2b = send(t2b_in, 2), send(t4b_in, 4), over(s2b_in)
    f7a, t3a = core(f6a), core(t2a)
    f6b, t4a, s2a, t2a_in, s4b_in = after((f6b, t4a, s2a, t2a, f4b))
    t6a, s4b = send(t2a_in, 4), over(s4b_in)
    f7b, t5a, s3a = core(f6b), core(t4a), core(s2a)
    first = Shards([own_f, f1, [f2a, f2b], [f3a, f3b], [f4a, f4b], [f5a, f5b], [f6a, f6b], [f7a, f7b]])
    first_pre = project_call(normed, first, tile, BF16)
    t2b, t4b, s4a, s6a_in, first_pre = after((t2b, t4b, s4a, f6a, first_pre))
    t6b, s6a = send(t4b, 2), over(s6a_in)
    t3b, t5b, s5a = core(t2b), core(t4b), core(s4a)
    t6a, t6b, s2b, s4b, s6b_in = after((t6a, t6b, s2b, s4b, f6b))
    s6b = over(s6b_in)
    t7a, t7b, s3b, s5b = core(t6a), core(t6b), core(s2b), core(s4b)
    third = Shards([[w_out], [t1], [t2a, t2b], [t3a, t3b], [t4a, t4b], [t5a, t5b], [t6a, t6b], [t7a, t7b]])
    (s6a,) = after((s6a,), t7b)
    s7a = core(s6a)
    most = [[own_s], [s1], [s2a, s2b], [s3a, s3b], [s4a, s4b], [s5a, s5b]]
    back = back_call(where, grads, third)
    partial = project_call(normed, Shards(most), tile, F32)
    s6b, back, partial = after((s6b, back, partial))
    s7b = core(s6b)
    last = [[s6a, s6b], [s7a, s7b]]
    second = Shards(most + last)
    second_pre, parts, whole = totals_call(
        where, normed, partial, Shards(last), len(most) * depth, first_pre, back, bias, tile
    )
    return first, second, third, first_pre, second_pre, back, bias, initial, parts, whole


def front(where, tile, rows_in, grad_rows, gain, gate_bias, state_in, w_gate, w_cand, w_out):
    first, second, third = (
        Shards([[lax.all_gather(w, "seq", tiled=True)]]) for w in (w_gate, w_cand, w_out)
    )
    bias, initial = gathered_rows(gate_bias, state_in)
    normed, grads = norm_call(where, rows_in, grad_rows, gain, first.depth)
    first_pre = project_call(normed, first, tile, BF16)
    back = back_call(where, grads, third)
    second_pre, parts, whole = totals_call(where, normed, None, second, 0, first_pre, back, bias, tile)
    return first, second, third, first_pre, second_pre, back, bias, initial, parts, whole


def on_device(ranks, batches, inputs, output_grad, norm_gain, gate_bias, state_in, w_gate, w_cand, w_out):
    rows_in, grad_rows = inputs[0], output_grad[0]
    gain = norm_gain[None, :]
    hidden = w_gate.shape[1]
    tile = min(512, hidden)
    me = lax.axis_index("seq")
    given = (rows_in, grad_rows, gain, gate_bias, state_in, w_gate, w_cand, w_out)
    if ranks == 8 and batches % 2 == 0:
        turned = lax.axis_index("batch") % 2
        where = jnp.stack([me, turned, me]).astype(jnp.int32)
        found = front_on_cube(ranks, batches, where, turned, tile, *given)
    else:
        nought = jnp.zeros_like(me)
        where = jnp.stack([nought, nought, me]).astype(jnp.int32)
        found = front(where, tile, *given)
    first, second, third, first_pre, second_pre, back, bias, initial, parts, whole = found
    wholes = lax.all_gather(whole, "seq")
    state_rows, one, other, bias_part, state_grad = scan_call(
        where, first_pre, second_pre, back, bias, initial, parts, wholes, ranks, tile
    )
    width = hidden // ranks
    everyone = lax.all_gather(bias_part[0], ("seq", "batch"))
    bias_grad = lax.dynamic_slice_in_dim(jnp.sum(everyone, axis=0), me * width, width, 0)
    layer_out = layer_call(where, state_rows, rows_in, third, tile)
    input_grad = input_grad_call(where, one, other, first, second, rows_in, grad_rows, gain)
    state_out = lax.dynamic_slice_in_dim(state_grad, me * width, width, 1)
    return (layer_out[None], input_grad[None], state_out, bias_grad)


def solution(mesh):
    body = functools.partial(on_device, mesh.shape["seq"], mesh.shape["batch"])
    rows = P("batch", "seq", None)
    return jax.shard_map(
        body,
        mesh=mesh,
        in_specs=(rows, rows, P(), P("seq"), P("batch", "seq"), P("seq", None), P("seq", None), P("seq", None)),
        out_specs=(rows, rows, P("batch", "seq"), P("seq")),
        check_vma=False,
    )
```

profile of v0, /device:TPU:0, one launch (start us, length us, event | category | flops | bytes accessed | tf_op | source)
XLA Modules:
  0.0 293.1 jit_solution(5661995200683483041)
XLA Ops:
  0.7 2.8 slice_select_fusion
  3.9 2.5 collective-permute-start.5
  6.4 1.5 collective-permute-start.4
  8.4 26.3 %all_gather.12 = f32[2,2048]{1,0:T(2,128)S(1)} all-gather(f32[2,256]{1,0:T(2,128)S(1)} %pad_maximum_fusion), channel_id=1, replica_groups=mesh['seq'=8,'batch'=4] {'seq'}, dimensions={1}, use_global_device_ids=true | all-gather | bytes 18432 | tf_op jit(solution)/shard_map/all_gather | solution.py:452
  34.8 1.6 collective-permute-start
  37.6 3.3 %norm_rows.1 = (bf16[256,2048]{1,0:T(8,128)(2,1)S(1)}, bf16[2048,256]{1,0:T(8,128)(2,1)S(1)}) custom-call(s32[3]{0:T(128)S(1)} %pad_add_fusion.where_ref, bf16[256,2048]{1,0:T(8,128)(2,1)S(1)} %bitcast.10, bf16[256,2048]{1,0:T(8,128)(2,1)S(1)} %bitcast.13, f32[1,2048]{1,0:T(1,128)S(1)} %bitcast.15), custom_call_target="tpu_custom_call" | custom-call | flops 536870912 | bytes 4194304 | tf_op jit(solution)/shard_map/norm_rows/pallas_call | solution.py:108
  41.0 8.2 %collective-permute-done.refs_4_ = bf16[128,2048]{1,0:T(8,128)(2,1)S(1)} collective-permute-done((bf16[128,2048]{1,0:T(8,128)(2,1)}, bf16[128,2048]{1,0:T(8,128)(2,1)S(1)}, u32[]{:S(2)}, u32[]{:S(2)}) %collective-permute-start) | collective-permute-done | bytes 524320 | tf_op jit(solution)/shard_map/ppermute | solution.py:25
  49.3 1.6 collective-permute-start.16
  51.4 1.5 collective-permute-start.2
  52.9 1.6 collective-permute-start.17
  55.0 9.2 %collective-permute-done.16.refs_6_ = bf16[128,2048]{1,0:T(8,128)(2,1)S(1)} collective-permute-done((bf16[128,2048]{1,0:T(8,128)(2,1)S(1)}, bf16[128,2048]{1,0:T(8,128)(2,1)S(1)}, u32[]{:S(2)}, u32[]{:S(2)}) %collective-permute-start.16) | collective-permute-done | bytes 524320 | tf_op jit(solution)/shard_map/ppermute | solution.py:25
  64.2 1.6 collective-permute-start.8
  65.9 9.4 %collective-permute-done.2.refs_2_ = bf16[128,2048]{1,0:T(8,128)(2,1)S(1)} collective-permute-done((bf16[128,2048]{1,0:T(8,128)(2,1)S(1)}, bf16[128,2048]{1,0:T(8,128)(2,1)S(1)}, u32[]{:S(2)}, u32[]{:S(2)}) %collective-permute-start.2) | collective-permute-done | bytes 524320 | tf_op jit(solution)/shard_map/ppermute | solution.py:25
  80.2 11.3 %collective-permute-done.6.refs_3_ = bf16[128,2048]{1,0:T(8,128)(2,1)S(1)} collective-permute-done((bf16[128,2048]{1,0:T(8,128)(2,1)S(1)}, bf16[128,2048]{1,0:T(8,128)(2,1)S(1)}, u32[]{:S(2)}, u32[]{:S(2)}) %collective-permute-start.6) | collective-permute-done | bytes 524320 | tf_op jit(solution)/shard_map/ppermute | solution.py:25
  91.5 9.9 %collective-permute-done.7.refs_7_ = bf16[128,2048]{1,0:T(8,128)(2,1)S(1)} collective-permute-done((bf16[128,2048]{1,0:T(8,128)(2,1)S(1)}, bf16[128,2048]{1,0:T(8,128)(2,1)S(1)}, u32[]{:S(2)}, u32[]{:S(2)}) %collective-permute-start.7) | collective-permute-done | bytes 524320 | tf_op jit(solution)/shard_map/ppermute | solution.py:25
  101.5 1.6 collective-permute-start.23
  103.5 4.9 %project.2.first_ref = bf16[256,2048]{1,0:T(8,128)(2,1)S(1)} custom-call(bf16[256,2048]{1,0:T(8,128)(2,1)S(1)} %get-tuple-element.59.x_ref, bf16[128,2048]{1,0:T(8,128)(2,1)} %get-tuple-element.95.refs_0_, bf16[128,2048]{1,0:T(8,128)(2,1)} %get-tuple-element.94.refs_1_, bf16[128,2048]{1,0:T(8,128)(2,1)} %collective-permute-done.9.refs_2_, ...), custom_call_target="tpu_custom_call" | custom-call | flops 2147483648 | bytes 8388608 | tf_op jit(solution)/shard_map/project/pallas_call | solution.py:138
  109.1 7.5 %collective-permute-done.23.refs_7_.refs_23_ = bf16[128,2048]{1,0:T(8,128)(2,1)S(1)} collective-permute-done((bf16[128,2048]{1,0:T(8,128)(2,1)}, bf16[128,2048]{1,0:T(8,128)(2,1)S(1)}, u32[]{:S(2)}, u32[]{:S(2)}) %collective-permute-start.23) | collective-permute-done | bytes 524320 | tf_op jit(solution)/shard_map/ppermute | solution.py:29
  116.5 9.1 %collective-permute-done.22.refs_3_.refs_19_ = bf16[128,2048]{1,0:T(8,128)(2,1)S(1)} collective-permute-done((bf16[128,2048]{1,0:T(8,128)(2,1)}, bf16[128,2048]{1,0:T(8,128)(2,1)S(1)}, u32[]{:S(2)}, u32[]{:S(2)}) %collective-permute-start.22) | collective-permute-done | bytes 524320 | tf_op jit(solution)/shard_map/ppermute | solution.py:29
  125.7 1.6 collective-permute-start.37
  128.3 11.8 %collective-permute-done.37.refs_1_.refs_26_ = bf16[128,2048]{1,0:T(8,128)(2,1)} collective-permute-done((bf16[128,2048]{1,0:T(8,128)(2,1)S(1)}, bf16[128,2048]{1,0:T(8,128)(2,1)}, u32[]{:S(2)}, u32[]{:S(2)}) %collective-permute-start.37) | collective-permute-done | bytes 524320 | tf_op jit(solution)/shard_map/ppermute | solution.py:29
  141.2 1.6 collective-permute-start.24
  142.8 2.8 project.3.refs_0_
  147.2 7.4 %back_rows.1.back_ref = bf16[256,2048]{1,0:T(8,128)(2,1)S(1)} custom-call(s32[3]{0:T(128)S(1)} %pad_add_fusion.where_ref, bf16[2048,256]{1,0:T(8,128)(2,1)S(1)} %get-tuple-element.70.g_ref, bf16[256,2048]{1,0:T(8,128)(2,1)S(1)} %copy-done.5, bf16[256,2048]{1,0:T(8,128)(2,1)S(1)} %collective-permute-done.25.refs_1_, ...), custom_call_target="tpu_custom_call" | custom-call | flops 2147483648 | bytes 8388608 | tf_op jit(solution)/shard_map/back_rows/pallas_call | solution.py:172
  156.1 1.9 collective-permute-done.39.refs_4_.refs_29_
  160.4 1.6 copy-done.11
  162.0 5.1 %project_totals.1 = (bf16[256,2048]{1,0:T(8,128)(2,1)S(1)}, f32[3,8,2048]{2,1,0:T(8,128)S(1)}, f32[3,2048]{1,0:T(4,128)S(1)}) custom-call(s32[3]{0:T(128)S(1)} %pad_add_fusion.where_ref, bf16[256,2048]{1,0:T(8,128)(2,1)S(1)} %get-tuple-element.59.x_ref, bf16[256,2048]{1,0:T(8,128)(2,1)S(1)} %copy-done.2, bf16[256,2048]{1,0:T(8,128)(2,1)S(1)} %copy-done.8, ...), custom_call_target="tpu_custom_call" | custom-call | flops 536870912 | bytes 2097152 | tf_op jit(solution)/shard_map/project_totals/pallas_call | solution.py:248
  167.1 8.5 %all-gather.1.wholes_ref = f32[8,3,2048]{2,1,0:T(4,128)S(1)} all-gather(f32[1,3,2048]{2,1,0:T(4,128)S(1)} %bitcast.17), channel_id=2, replica_groups=mesh['seq'=8,'batch'=4] {'seq'}, dimensions={0}, use_global_device_ids=true | all-gather | bytes 221184 | tf_op jit(solution)/shard_map/all_gather | solution.py:539
  175.7 4.7 %scan_rows.1 = (bf16[256,2048]{1,0:T(8,128)(2,1)S(1)}, bf16[2048,256]{1,0:T(8,128)(2,1)S(1)}, bf16[2048,256]{1,0:T(8,128)(2,1)S(1)}, f32[1,2048]{1,0:T(1,128)S(1)}, f32[1,2048]{1,0:T(1,128)S(1)}) custom-call(s32[3]{0:T(128)S(1)} %pad_add_fusion.where_ref, bf16[256,2048]{1,0:T(8,128)(2,1)S(1)} %copy-done.3, ...), custom_call_target="tpu_custom_call" | custom-call | flops 805306368 | bytes 6291456 | tf_op jit(solution)/shard_map/scan_rows/pallas_call | solution.py:341
  183.3 69.4 %all-gather.2 = f32[32,1,2048]{2,1,0:T(1,128)S(1)} all-gather(f32[1,1,2048]{2,1,0:T(1,128)S(1)} %bitcast.18), channel_id=1, replica_groups=mesh['seq'=8,'batch'=4] {'seq','batch'}, dimensions={0}, use_global_device_ids=true | all-gather | bytes 270336 | tf_op jit(solution)/shard_map/all_gather | solution.py:544
  269.2 5.3 %layer_rows.1 = bf16[256,2048]{1,0:T(8,128)(2,1)} custom-call(s32[3]{0:T(128)S(1)} %pad_add_fusion.where_ref, bf16[256,2048]{1,0:T(8,128)(2,1)S(1)} %copy-done.84, bf16[256,2048]{1,0:T(8,128)(2,1)S(1)} %bitcast.11, bf16[256,2048]{1,0:T(8,128)(2,1)S(1)} %copy-done.6, bf16[256,2048]{1,0:T(8,128)(2,1)S(1)} %copy-done.17, bf16[128,2048]{1,0:T(8,128)(2,1)S(1)} %copy-done.58, ...), custom_call_target="tpu_custom_call" | custom-call | flops 2147483648 | bytes 8388608 | tf_op jit(solution)/shard_map/layer_rows/pallas_call | solution.py:373
  277.1 15.8 %input_grad_rows.1 = bf16[256,2048]{1,0:T(8,128)(2,1)} custom-call(s32[3]{0:T(128)S(1)} %pad_add_fusion.where_ref, bf16[2048,256]{1,0:T(8,128)(2,1)S(1)} %copy-done.80, bf16[2048,256]{1,0:T(8,128)(2,1)S(1)} %copy-done.82, bf16[256,2048]{1,0:T(8,128)(2,1)S(1)} %bitcast.12, bf16[256,2048]{1,0:T(8,128)(2,1)S(1)} %bitcast.14, f32[1,2048]{1,0:T(1,128)S(1)} %bitcast.16, ...), custom_call_target="tpu_custom_call" | custom-call | flops 4294967296 | bytes 16777216 | tf_op jit(solution)/shard_map/input_grad_rows/pallas_call | solution.py:433
  (248 shorter events, 38.6 us)
Async XLA Ops:
  3.5 49.4 %collective-permute-start.10 = (bf16[128,2048]{1,0:T(8,128)(2,1)}, bf16[128,2048]{1,0:T(8,128)(2,1)}, u32[]{:S(2)}, u32[]{:S(2)}) collective-permute-start(bf16[128,2048]{1,0:T(8,128)(2,1)} %get-tuple-element.94.refs_1_), channel_id=1, source_target_pairs={{0,4},{4,0},{8,12},{12,8},{16,20},{20,16},{24,28},{28,24},{1,5},{5... | collective-permute-start | bytes 1572872 | tf_op jit(solution)/shard_map/ppermute | solution.py:25
  3.9 45.4 %collective-permute-start.5 = (bf16[128,2048]{1,0:T(8,128)(2,1)}, bf16[128,2048]{1,0:T(8,128)(2,1)}, u32[]{:S(2)}, u32[]{:S(2)}) collective-permute-start(bf16[128,2048]{1,0:T(8,128)(2,1)} %get-tuple-element.94.refs_1_), channel_id=1, source_target_pairs={{0,16},{4,20},{8,24},{12,28},{16,0},{20,4},{24,8},{28,12},{1,17},{... | collective-permute-start | bytes 1572872 | tf_op jit(solution)/shard_map/ppermute | solution.py:25
  6.4 42.9 %collective-permute-start.4 = (bf16[128,2048]{1,0:T(8,128)(2,1)}, bf16[128,2048]{1,0:T(8,128)(2,1)}, u32[]{:S(2)}, u32[]{:S(2)}) collective-permute-start(bf16[128,2048]{1,0:T(8,128)(2,1)} %get-tuple-element.94.refs_1_), channel_id=1, source_target_pairs={{0,8},{4,12},{8,0},{12,4},{16,24},{20,28},{24,16},{28,20},{1,9},{5... | collective-permute-start | bytes 1572872 | tf_op jit(solution)/shard_map/ppermute | solution.py:25
  7.9 46.5 %collective-permute-start.9 = (bf16[128,2048]{1,0:T(8,128)(2,1)}, bf16[128,2048]{1,0:T(8,128)(2,1)}, u32[]{:S(2)}, u32[]{:S(2)}) collective-permute-start(bf16[128,2048]{1,0:T(8,128)(2,1)} %get-tuple-element.95.refs_0_), channel_id=1, source_target_pairs={{0,4},{4,0},{8,12},{12,8},{16,20},{20,16},{24,28},{28,24},{1,5},{5... | collective-permute-start | bytes 1572872 | tf_op jit(solution)/shard_map/ppermute | solution.py:25
  7.9 26.9 %collective-permute-start.1 = (bf16[128,2048]{1,0:T(8,128)(2,1)}, bf16[128,2048]{1,0:T(8,128)(2,1)S(1)}, u32[]{:S(2)}, u32[]{:S(2)}) collective-permute-start(bf16[128,2048]{1,0:T(8,128)(2,1)} %get-tuple-element.95.refs_0_), channel_id=1, source_target_pairs={{0,16},{4,20},{8,24},{12,28},{16,0},{20,4},{24,8},{28,12},{1,17},{... | collective-permute-start | bytes 1572872 | tf_op jit(solution)/shard_map/ppermute | solution.py:25
  34.8 14.4 %collective-permute-start = (bf16[128,2048]{1,0:T(8,128)(2,1)}, bf16[128,2048]{1,0:T(8,128)(2,1)S(1)}, u32[]{:S(2)}, u32[]{:S(2)}) collective-permute-start(bf16[128,2048]{1,0:T(8,128)(2,1)} %get-tuple-element.95.refs_0_), channel_id=1, source_target_pairs={{0,8},{4,12},{8,0},{12,4},{16,24},{20,28},{24,16},{28,20},{1,9},{5... | collective-permute-start | bytes 1572872 | tf_op jit(solution)/shard_map/ppermute | solution.py:25
  49.3 14.9 %collective-permute-start.16 = (bf16[128,2048]{1,0:T(8,128)(2,1)S(1)}, bf16[128,2048]{1,0:T(8,128)(2,1)S(1)}, u32[]{:S(2)}, u32[]{:S(2)}) collective-permute-start(bf16[128,2048]{1,0:T(8,128)(2,1)S(1)} %get-tuple-element.61), channel_id=1, source_target_pairs={{0,16},{4,20},{8,24},{12,28},{16,0},{20,4},{24,8},{28,12},{1,17},{... | collective-permute-start | bytes 1572872 | tf_op jit(solution)/shard_map/ppermute | solution.py:25
  50.8 15.1 %collective-permute-start.15 = (bf16[128,2048]{1,0:T(8,128)(2,1)}, bf16[128,2048]{1,0:T(8,128)(2,1)S(1)}, u32[]{:S(2)}, u32[]{:S(2)}) collective-permute-start(bf16[128,2048]{1,0:T(8,128)(2,1)} %collective-permute-done.5.refs_9_), channel_id=1, source_target_pairs={{0,8},{4,12},{8,0},{12,4},{16,24},{20,28},{24,16},{28,20},{1,9},{5... | collective-permute-start | bytes 1572872 | tf_op jit(solution)/shard_map/ppermute | solution.py:25
  51.4 24.0 %collective-permute-start.2 = (bf16[128,2048]{1,0:T(8,128)(2,1)S(1)}, bf16[128,2048]{1,0:T(8,128)(2,1)S(1)}, u32[]{:S(2)}, u32[]{:S(2)}) collective-permute-start(bf16[128,2048]{1,0:T(8,128)(2,1)S(1)} %get-tuple-element.61), channel_id=1, source_target_pairs={{0,8},{4,12},{8,0},{12,4},{16,24},{20,28},{24,16},{28,20},{1,9},{5... | collective-permute-start | bytes 1572872 | tf_op jit(solution)/shard_map/ppermute | solution.py:25
  52.9 22.5 %collective-permute-start.17 = (bf16[128,2048]{1,0:T(8,128)(2,1)S(1)}, bf16[128,2048]{1,0:T(8,128)(2,1)S(1)}, u32[]{:S(2)}, u32[]{:S(2)}) collective-permute-start(bf16[128,2048]{1,0:T(8,128)(2,1)S(1)} %collective-permute-done.refs_4_), channel_id=1, source_target_pairs={{0,1},{1,0},{2,3},{3,2},{4,5},{5,4},{6,7},{7,6},{8,9},{9,8},{10,11... | collective-permute-start | bytes 1572872 | tf_op jit(solution)/shard_map/ppermute | solution.py:29
  54.4 21.4 %collective-permute-start.3 = (bf16[128,2048]{1,0:T(8,128)(2,1)S(1)}, bf16[128,2048]{1,0:T(8,128)(2,1)S(1)}, u32[]{:S(2)}, u32[]{:S(2)}) collective-permute-start(bf16[128,2048]{1,0:T(8,128)(2,1)S(1)} %collective-permute-done.refs_4_), channel_id=1, source_target_pairs={{0,16},{4,20},{8,24},{12,28},{16,0},{20,4},{24,8},{28,12},{1,17},{... | collective-permute-start | bytes 1572872 | tf_op jit(solution)/shard_map/ppermute | solution.py:25
  64.2 12.4 %collective-permute-start.8 = (bf16[128,2048]{1,0:T(8,128)(2,1)S(1)}, bf16[128,2048]{1,0:T(8,128)(2,1)S(1)}, u32[]{:S(2)}, u32[]{:S(2)}) collective-permute-start(bf16[128,2048]{1,0:T(8,128)(2,1)S(1)} %copy-done.19), channel_id=1, source_target_pairs={{0,1},{1,0},{2,3},{3,2},{4,5},{5,4},{6,7},{7,6},{8,9},{9,8},{10,11... | collective-permute-start | bytes 1572872 | tf_op jit(solution)/shard_map/ppermute | solution.py:29
  65.9 11.2 %collective-permute-start.12 = (bf16[128,2048]{1,0:T(8,128)(2,1)}, bf16[128,2048]{1,0:T(8,128)(2,1)S(1)}, u32[]{:S(2)}, u32[]{:S(2)}) collective-permute-start(bf16[128,2048]{1,0:T(8,128)(2,1)} %collective-permute-done.4.refs_5_), channel_id=1, source_target_pairs={{0,4},{4,0},{8,12},{12,8},{16,20},{20,16},{24,28},{28,24},{1,5},{5... | collective-permute-start | bytes 1572872 | tf_op jit(solution)/shard_map/ppermute | solution.py:25
  76.6 31.8 %collective-permute-start.20 = (bf16[128,2048]{1,0:T(8,128)(2,1)S(1)}, bf16[128,2048]{1,0:T(8,128)(2,1)S(1)}, u32[]{:S(2)}, u32[]{:S(2)}) collective-permute-start(bf16[128,2048]{1,0:T(8,128)(2,1)S(1)} %collective-permute-done.2.refs_2_), channel_id=1, source_target_pairs={{0,16},{4,20},{8,24},{12,28},{16,0},{20,4},{24,8},{28,12},{1,17},{... | collective-permute-start | bytes 1572872 | tf_op jit(solution)/shard_map/ppermute | solution.py:25
  77.5 14.0 %collective-permute-start.6 = (bf16[128,2048]{1,0:T(8,128)(2,1)S(1)}, bf16[128,2048]{1,0:T(8,128)(2,1)S(1)}, u32[]{:S(2)}, u32[]{:S(2)}) collective-permute-start(bf16[128,2048]{1,0:T(8,128)(2,1)S(1)} %get-tuple-element.56), channel_id=1, source_target_pairs={{0,8},{4,12},{8,0},{12,4},{16,24},{20,28},{24,16},{28,20},{1,9},{5... | collective-permute-start | bytes 1572872 | tf_op jit(solution)/shard_map/ppermute | solution.py:25
  78.7 22.7 %collective-permute-start.7 = (bf16[128,2048]{1,0:T(8,128)(2,1)S(1)}, bf16[128,2048]{1,0:T(8,128)(2,1)S(1)}, u32[]{:S(2)}, u32[]{:S(2)}) collective-permute-start(bf16[128,2048]{1,0:T(8,128)(2,1)S(1)} %get-tuple-element.56), channel_id=1, source_target_pairs={{0,16},{4,20},{8,24},{12,28},{16,0},{20,4},{24,8},{28,12},{1,17},{... | collective-permute-start | bytes 1572872 | tf_op jit(solution)/shard_map/ppermute | solution.py:25
  79.5 23.5 %collective-permute-start.18 = (bf16[128,2048]{1,0:T(8,128)(2,1)S(1)}, bf16[128,2048]{1,0:T(8,128)(2,1)S(1)}, u32[]{:S(2)}, u32[]{:S(2)}) collective-permute-start(bf16[128,2048]{1,0:T(8,128)(2,1)S(1)} %collective-permute-done.3.refs_12_), channel_id=1, source_target_pairs={{0,4},{4,0},{8,12},{12,8},{16,20},{20,16},{24,28},{28,24},{1,5},{5... | collective-permute-start | bytes 1572872 | tf_op jit(solution)/shard_map/ppermute | solution.py:25
  79.7 47.6 %collective-permute-start.32 = (bf16[256,2048]{1,0:T(8,128)(2,1)S(1)}, bf16[256,2048]{1,0:T(8,128)(2,1)S(1)}, u32[]{:S(2)}, u32[]{:S(2)}) collective-permute-start(bf16[256,2048]{1,0:T(8,128)(2,1)S(1)} %broadcast_select_fusion.refs_0_.refs_16_), channel_id=1, source_target_pairs={{0,4},{4,0},{8,12},{12,8},{16,20},{20,16},{24,28},{28,24},{1,5},{5... | collective-permute-start | bytes 3145736 | tf_op jit(solution)/shard_map/ppermute | solution.py:25
  91.5 36.0 %collective-permute-start.25 = (bf16[256,2048]{1,0:T(8,128)(2,1)S(1)}, bf16[256,2048]{1,0:T(8,128)(2,1)S(1)}, u32[]{:S(2)}, u32[]{:S(2)}) collective-permute-start(bf16[256,2048]{1,0:T(8,128)(2,1)S(1)} %copy-done.5), channel_id=1, source_target_pairs={{0,4},{4,0},{8,12},{12,8},{16,20},{20,16},{24,28},{28,24},{1,5},{5... | collective-permute-start | bytes 3145736 | tf_op jit(solution)/shard_map/ppermute | solution.py:25
  101.5 15.1 %collective-permute-start.23 = (bf16[128,2048]{1,0:T(8,128)(2,1)}, bf16[128,2048]{1,0:T(8,128)(2,1)S(1)}, u32[]{:S(2)}, u32[]{:S(2)}) collective-permute-start(bf16[128,2048]{1,0:T(8,128)(2,1)} %collective-permute-done.5.refs_9_), channel_id=1, source_target_pairs={{0,1},{1,0},{2,3},{3,2},{4,5},{5,4},{6,7},{7,6},{8,9},{9,8},{10,11... | collective-permute-start | bytes 1572872 | tf_op jit(solution)/shard_map/ppermute | solution.py:29
  103.0 22.6 %collective-permute-start.22 = (bf16[128,2048]{1,0:T(8,128)(2,1)}, bf16[128,2048]{1,0:T(8,128)(2,1)S(1)}, u32[]{:S(2)}, u32[]{:S(2)}) collective-permute-start(bf16[128,2048]{1,0:T(8,128)(2,1)} %collective-permute-done.4.refs_5_), channel_id=1, source_target_pairs={{0,1},{1,0},{2,3},{3,2},{4,5},{5,4},{6,7},{7,6},{8,9},{9,8},{10,11... | collective-permute-start | bytes 1572872 | tf_op jit(solution)/shard_map/ppermute | solution.py:29
  108.5 17.2 %collective-permute-start.21 = (bf16[128,2048]{1,0:T(8,128)(2,1)S(1)}, bf16[128,2048]{1,0:T(8,128)(2,1)S(1)}, u32[]{:S(2)}, u32[]{:S(2)}) collective-permute-start(bf16[128,2048]{1,0:T(8,128)(2,1)S(1)} %collective-permute-done.7.refs_7_), channel_id=1, source_target_pairs={{0,8},{4,12},{8,0},{12,4},{16,24},{20,28},{24,16},{28,20},{1,9},{5... | collective-permute-start | bytes 1572872 | tf_op jit(solution)/shard_map/ppermute | solution.py:25
  116.5 11.3 %collective-permute-start.28 = (bf16[128,2048]{1,0:T(8,128)(2,1)S(1)}, bf16[128,2048]{1,0:T(8,128)(2,1)S(1)}, u32[]{:S(2)}, u32[]{:S(2)}) collective-permute-start(bf16[128,2048]{1,0:T(8,128)(2,1)S(1)} %collective-permute-done.16.refs_6_), channel_id=1, source_target_pairs={{0,4},{4,0},{8,12},{12,8},{16,20},{20,16},{24,28},{28,24},{1,5},{5... | collective-permute-start | bytes 1572872 | tf_op jit(solution)/shard_map/ppermute | solution.py:25
  125.7 14.5 %collective-permute-start.37 = (bf16[128,2048]{1,0:T(8,128)(2,1)S(1)}, bf16[128,2048]{1,0:T(8,128)(2,1)}, u32[]{:S(2)}, u32[]{:S(2)}) collective-permute-start(bf16[128,2048]{1,0:T(8,128)(2,1)S(1)} %collective-permute-done.3.refs_12_), channel_id=1, source_target_pairs={{0,1},{1,0},{2,3},{3,2},{4,5},{5,4},{6,7},{7,6},{8,9},{9,8},{10,11... | collective-permute-start | bytes 1572872 | tf_op jit(solution)/shard_map/ppermute | solution.py:29
  127.3 12.8 %collective-permute-start.35 = (bf16[128,2048]{1,0:T(8,128)(2,1)S(1)}, bf16[128,2048]{1,0:T(8,128)(2,1)S(1)}, u32[]{:S(2)}, u32[]{:S(2)}) collective-permute-start(bf16[128,2048]{1,0:T(8,128)(2,1)S(1)} %collective-permute-done.8.refs_6_.refs_22_), channel_id=1, source_target_pairs={{0,4},{4,0},{8,12},{12,8},{16,20},{20,16},{24,28},{28,24},{1,5},{5... | collective-permute-start | bytes 1572872 | tf_op jit(solution)/shard_map/ppermute | solution.py:25
  127.5 13.1 %collective-permute-start.31 = (bf16[128,2048]{1,0:T(8,128)(2,1)S(1)}, bf16[128,2048]{1,0:T(8,128)(2,1)S(1)}, u32[]{:S(2)}, u32[]{:S(2)}) collective-permute-start(bf16[128,2048]{1,0:T(8,128)(2,1)S(1)} %collective-permute-done.21.refs_11_), channel_id=1, source_target_pairs={{0,4},{4,0},{8,12},{12,8},{16,20},{20,16},{24,28},{28,24},{1,5},{5... | collective-permute-start | bytes 1572872 | tf_op jit(solution)/shard_map/ppermute | solution.py:25
  127.8 12.9 %collective-permute-start.34 = (bf16[128,2048]{1,0:T(8,128)(2,1)S(1)}, bf16[128,2048]{1,0:T(8,128)(2,1)S(1)}, u32[]{:S(2)}, u32[]{:S(2)}) collective-permute-start(bf16[128,2048]{1,0:T(8,128)(2,1)S(1)} %collective-permute-done.22.refs_3_.refs_19_), channel_id=1, source_target_pairs={{0,4},{4,0},{8,12},{12,8},{16,20},{20,16},{24,28},{28,24},{1,5},{5... | collective-permute-start | bytes 1572872 | tf_op jit(solution)/shard_map/ppermute | solution.py:25
  128.0 13.1 %collective-permute-start.36 = (bf16[128,2048]{1,0:T(8,128)(2,1)S(1)}, bf16[128,2048]{1,0:T(8,128)(2,1)S(1)}, u32[]{:S(2)}, u32[]{:S(2)}) collective-permute-start(bf16[128,2048]{1,0:T(8,128)(2,1)S(1)} %collective-permute-done.23.refs_7_.refs_23_), channel_id=1, source_target_pairs={{0,4},{4,0},{8,12},{12,8},{16,20},{20,16},{24,28},{28,24},{1,5},{5... | collective-permute-start | bytes 1572872 | tf_op jit(solution)/shard_map/ppermute | solution.py:25
  140.1 6.9 %collective-permute-start.26 = (bf16[128,2048]{1,0:T(8,128)(2,1)S(1)}, bf16[128,2048]{1,0:T(8,128)(2,1)S(1)}, u32[]{:S(2)}, u32[]{:S(2)}) collective-permute-start(bf16[128,2048]{1,0:T(8,128)(2,1)S(1)} %collective-permute-done.2.refs_2_), channel_id=1, source_target_pairs={{0,4},{4,0},{8,12},{12,8},{16,20},{20,16},{24,28},{28,24},{1,5},{5... | collective-permute-start | bytes 1572872 | tf_op jit(solution)/shard_map/ppermute | solution.py:25
  140.2 6.9 %collective-permute-start.29 = (bf16[128,2048]{1,0:T(8,128)(2,1)S(1)}, bf16[128,2048]{1,0:T(8,128)(2,1)S(1)}, u32[]{:S(2)}, u32[]{:S(2)}) collective-permute-start(bf16[128,2048]{1,0:T(8,128)(2,1)S(1)} %collective-permute-done.7.refs_7_), channel_id=1, source_target_pairs={{0,4},{4,0},{8,12},{12,8},{16,20},{20,16},{24,28},{28,24},{1,5},{5... | collective-permute-start | bytes 1572872 | tf_op jit(solution)/shard_map/ppermute | solution.py:25
  141.2 14.4 %collective-permute-start.24 = (bf16[128,2048]{1,0:T(8,128)(2,1)S(1)}, bf16[128,2048]{1,0:T(8,128)(2,1)}, u32[]{:S(2)}, u32[]{:S(2)}) collective-permute-start(bf16[128,2048]{1,0:T(8,128)(2,1)S(1)} %collective-permute-done.15.refs_13_), channel_id=1, source_target_pairs={{0,1},{1,0},{2,3},{3,2},{4,5},{5,4},{6,7},{7,6},{8,9},{9,8},{10,11... | collective-permute-start | bytes 1572872 | tf_op jit(solution)/shard_map/ppermute | solution.py:29
  147.1 9.0 %collective-permute-start.38 = (bf16[128,2048]{1,0:T(8,128)(2,1)}, bf16[128,2048]{1,0:T(8,128)(2,1)}, u32[]{:S(2)}, u32[]{:S(2)}) collective-permute-start(bf16[128,2048]{1,0:T(8,128)(2,1)} %collective-permute-done.37.refs_1_.refs_26_), channel_id=1, source_target_pairs={{0,4},{4,0},{8,12},{12,8},{16,20},{20,16},{24,28},{28,24},{1,5},{5... | collective-permute-start | bytes 1572872 | tf_op jit(solution)/shard_map/ppermute | solution.py:25
  (98 other events, 1564.0 us)
where the time goes:
time: 294 us; the launch traced here: 293 us
  blocking collectives  104 us (35%)
  waiting for transfers between devices  79.5 us (27%)
  Pallas kernels  49.2 us (17%)
  local copies, waits for them, and re-layouts  29.4 us (10%)
  starting transfers between devices  25.9 us (9%)
  other arithmetic  3.12 us (1%)
    all_gather x1, blocking collectives, on_device(): everyone = lax.all_gather(bias_part[0], ('seq', 'batch'))  69.4 us
    ppermute x34, waiting for transfers between devices, hop(): return lax.ppermute(value, 'seq', [(i, i ^ offset) for i in range(count)])  50.5 us
    ppermute x6, waiting for transfers between devices, swap_batch(): return lax.ppermute(value, 'batch', [(i, i ^ offset) for i in range(count)])  29 us
    unnamed x180, local copies, waits for them, and re-layouts  28.1 us
    all_gather x1, blocking collectives, gathered_rows(): lax.all_gather(jnp.stack([gate_bias, state_in[0]]), 'seq', axis=1, tiled=...  26.3 us
    ppermute x34, starting transfers between devices, hop(): return lax.ppermute(value, 'seq', [(i, i ^ offset) for i in range(count)])  17.5 us
    pallas_call x1, Pallas kernels, input_grad_call(): pl.pallas_call(kernel, out_shape=jax.ShapeDtypeStruct((rows, width), BF16...  15.8 us
    all_gather x1, blocking collectives, on_device(): wholes = lax.all_gather(whole, 'seq')  8.53 us
  transfers between devices with their start and end apart: 40, of which 12 were waited for; matrix products, arithmetic and copies ran while one was open for 0% of the time, Pallas kernels for 6%

commit v1 on v0

--- a/solution.py
+++ b/solution.py
@@ -66,23 +66,27 @@
         self.depth = sum(piece.shape[0] for piece in groups[0])
         self.width = groups[0][0].shape[1]
 
-    def copies(self, refs, buffer, sems, slot_of):
-        out, position = [], 0
-        for index, group in enumerate(self.groups):
-            start, made = slot_of(index) * self.depth, []
-            for piece in group:
-                rows = piece.shape[0]
-                made.append(
-                    pltpu.make_async_copy(refs[position], buffer.at[pl.ds(start, rows), :], sems.at[position])
-                )
-                start, position = start + rows, position + 1
-            out.append(made)
-        return out
+    def operands(self):
+        return [pltpu.with_memory_space_constraint(piece, pltpu.VMEM) for piece in self.pieces]
+
+    def block(self, refs, index, part, size):
+        position = sum(len(group) for group in self.groups[:index])
+        found, start = [], 0
+        for offset, piece in enumerate(self.groups[index]):
+            rows = piece.shape[0]
+            low, high = max(part, start), min(part + size, start + rows)
+            if low < high:
+                found.append(refs[position + offset][low - start : high - start, :])
+            start += rows
+        return found[0] if len(found) == 1 else jnp.concatenate(found, axis=0)
+
+    def columns(self, refs, span):
+        found = [ref[:, span] for ref in refs]
+        return found[0] if len(found) == 1 else jnp.concatenate(found, axis=0)
 
 
 VMEM_SPEC = pl.BlockSpec(memory_space=pltpu.VMEM)
 SMEM_SPEC = pl.BlockSpec(memory_space=pltpu.SMEM)
-ANY_SPEC = pl.BlockSpec(memory_space=pl.ANY)
 
 
 def norm_call(where, x, g, gain, depth):
@@ -111,7 +115,7 @@
         in_specs=[SMEM_SPEC] + [VMEM_SPEC] * 3,
         out_specs=[VMEM_SPEC] * 2,
         scratch_shapes=[pltpu.VMEM(x.shape, BF16)],
-        compiler_params=params(12),
+        compiler_params=params(14),
         cost_estimate=cost(4 * rows * x.size, 8 * x.size),
         name="norm_rows",
     )(where, x, g, gain)
@@ -123,31 +127,22 @@
     span_in = slice(skip, skip + count * depth)
 
     def kernel(x_ref, *refs):
-        refs, (out_ref, held, sems) = refs[:-3], refs[-3:]
-        copies = [c for made in shards.copies(refs, held, sems, lambda i: i) for c in made]
-        for c in copies:
-            c.start()
-        for c in copies:
-            c.wait()
+        refs, out_ref = refs[:-1], refs[-1]
 
         def body(span):
-            out_ref[:, span] = dot(x_ref[:, span_in], held[:, span]).astype(dtype)
+            out_ref[:, span] = dot(x_ref[:, span_in], shards.columns(refs, span)).astype(dtype)
 
         tiles(width, tile, body)
 
     return pl.pallas_call(
         kernel,
         out_shape=jax.ShapeDtypeStruct((rows, width), dtype),
-        in_specs=[VMEM_SPEC] + [ANY_SPEC] * len(shards.pieces),
+        in_specs=[VMEM_SPEC] + [VMEM_SPEC] * len(shards.pieces),
         out_specs=VMEM_SPEC,
-        scratch_shapes=[
-            pltpu.VMEM((count * depth, width), BF16),
-            pltpu.SemaphoreType.DMA((len(shards.pieces),)),
-        ],
-        compiler_params=params(16),
+        compiler_params=params(14),
         cost_estimate=cost(2 * rows * count * depth * width, 2 * count * depth * width),
         name="project",
-    )(x, *shards.pieces)
+    )(x, *shards.operands())
 
 
 def back_call(where, grads, shards):
@@ -155,33 +150,23 @@
     count, depth = len(shards.groups), shards.depth
 
     def kernel(where_ref, g_ref, *refs):
-        refs, (out_ref, held, sems) = refs[:-3], refs[-3:]
-        copies = shards.copies(refs, held, sems, lambda i: i)
-        for made in copies:
-            for c in made:
-                c.start()
-        for index, made in enumerate(copies):
-            for c in made:
-                c.wait()
-            target = pl.multiple_of((where_ref[0] ^ index) * depth, depth)
-            for part in range(0, depth, min(depth, 256)):
-                size = min(depth, 256)
-                block = held[index * depth + part : index * depth + part + size, :]
-                out_ref[:, pl.ds(pl.multiple_of(target + part, size), size)] = dot(block, g_ref[...]).T.astype(BF16)
+        refs, out_ref = refs[:-1], refs[-1]
+        size = min(depth, 256)
+        for index in range(count):
+            for part in range(0, depth, size):
+                target = pl.multiple_of((where_ref[0] ^ index) * depth + part, size)
+                term = dot(shards.block(refs, index, part, size), g_ref[...])
+                out_ref[:, pl.ds(target, size)] = term.T.astype(BF16)
 
     return pl.pallas_call(
         kernel,
         out_shape=jax.ShapeDtypeStruct((rows, count * depth), BF16),
-        in_specs=[SMEM_SPEC, VMEM_SPEC] + [ANY_SPEC] * len(shards.pieces),
+        in_specs=[SMEM_SPEC, VMEM_SPEC] + [VMEM_SPEC] * len(shards.pieces),
         out_specs=VMEM_SPEC,
-        scratch_shapes=[
-            pltpu.VMEM((count * depth, width), BF16),
-            pltpu.SemaphoreType.DMA((len(shards.pieces),)),
-        ],
-        compiler_params=params(16),
+        compiler_params=params(14),
         cost_estimate=cost(2 * rows * count * depth * width, 2 * count * depth * width),
         name="back_rows",
-    )(where, grads, *shards.pieces)
+    )(where, grads, *shards.operands())
 
 
 def gates(x):
@@ -210,15 +195,10 @@
 
     def kernel(where_ref, x_ref, first_ref, back_ref, bias_ref, *refs):
         partial_refs, refs = refs[: len(extra)], refs[len(extra) :]
-        refs, (second_ref, parts_ref, whole_ref, held, sems) = refs[:-5], refs[-5:]
-        copies = [c for made in shards.copies(refs, held, sems, lambda i: i) for c in made]
-        for c in copies:
-            c.start()
-        for c in copies:
-            c.wait()
+        refs, (second_ref, parts_ref, whole_ref) = refs[:-3], refs[-3:]
 
         def body(span):
-            total = dot(x_ref[:, skip : skip + count * depth], held[:, span])
+            total = dot(x_ref[:, skip : skip + count * depth], shards.columns(refs, span))
             for ref in partial_refs:
                 total = total + ref[:, span]
             second_ref[:, span] = total.astype(BF16)
@@ -252,16 +232,12 @@
             jax.ShapeDtypeStruct((3, SEGMENTS, width), F32),
             jax.ShapeDtypeStruct((3, width), F32),
         ],
-        in_specs=[SMEM_SPEC] + [VMEM_SPEC] * (4 + len(extra)) + [ANY_SPEC] * len(shards.pieces),
+        in_specs=[SMEM_SPEC] + [VMEM_SPEC] * (4 + len(extra)) + [VMEM_SPEC] * len(shards.pieces),
         out_specs=[VMEM_SPEC] * 3,
-        scratch_shapes=[
-            pltpu.VMEM((count * depth, width), BF16),
-            pltpu.SemaphoreType.DMA((len(shards.pieces),)),
-        ],
-        compiler_params=params(20),
+        compiler_params=params(14),
         cost_estimate=cost(2 * rows * count * depth * width, 2 * count * depth * width),
         name="project_totals",
-    )(where, x, first_pre, back, bias, *extra, *shards.pieces)
+    )(where, x, first_pre, back, bias, *extra, *shards.operands())
 
 
 def scan_call(where, first_pre, second_pre, back, bias, initial, parts, wholes, ranks, tile):
@@ -344,7 +320,7 @@
         in_specs=[SMEM_SPEC] + [VMEM_SPEC] * 7,
         out_specs=[VMEM_SPEC] * 5,
         scratch_shapes=[pltpu.VMEM((rows, tile), F32)] * 3 + [pltpu.VMEM((rows, tile), BF16)] * 3,
-        compiler_params=params(16),
+        compiler_params=params(14),
         cost_estimate=cost(6 * rows * rows * width, 12 * rows * width),
         name="scan_rows",
     )(where, first_pre, second_pre, back, bias, initial, parts, wholes)
@@ -355,69 +331,45 @@
     count, depth = len(shards.groups), shards.depth
 
     def kernel(where_ref, x_ref, residual_ref, *refs):
-        refs, (out_ref, held, ordered, sems) = refs[:-4], refs[-4:]
-        copies = [c for made in shards.copies(refs, held, sems, lambda i: i) for c in made]
-        for c in copies:
-            c.start()
+        refs, (out_ref, ordered) = refs[:-2], refs[-2:]
         for index in range(count):
             source = pl.ds(pl.multiple_of((where_ref[0] ^ index) * depth, depth), depth)
             ordered[:, index * depth : (index + 1) * depth] = x_ref[:, source]
-        for c in copies:
-            c.wait()
 
         def body(span):
-            out_ref[:, span] = (residual_ref[:, span].astype(F32) + dot(ordered[...], held[:, span])).astype(BF16)
+            total = dot(ordered[...], shards.columns(refs, span))
+            out_ref[:, span] = (residual_ref[:, span].astype(F32) + total).astype(BF16)
 
         tiles(width, tile, body)
 
     return pl.pallas_call(
         kernel,
         out_shape=jax.ShapeDtypeStruct((rows, width), BF16),
-        in_specs=[SMEM_SPEC] + [VMEM_SPEC] * 2 + [ANY_SPEC] * len(shards.pieces),
+        in_specs=[SMEM_SPEC] + [VMEM_SPEC] * 2 + [VMEM_SPEC] * len(shards.pieces),
         out_specs=VMEM_SPEC,
-        scratch_shapes=[
-            pltpu.VMEM((count * depth, width), BF16),
-            pltpu.VMEM((rows, count * depth), BF16),
-            pltpu.SemaphoreType.DMA((len(shards.pieces),)),
-        ],
-        compiler_params=params(18),
+        scratch_shapes=[pltpu.VMEM((rows, count * depth), BF16)],
+        compiler_params=params(14),
         cost_estimate=cost(2 * rows * count * depth * width, 2 * count * depth * width),
         name="layer_rows",
-    )(where, state_rows, residual, *shards.pieces)
+    )(where, state_rows, residual, *shards.operands())
 
 
 def input_grad_call(where, one, other, first, second, x, grads, gain):
     rows, width = x.shape
     hidden = one.shape[0]
     count, depth = len(first.groups), first.depth
-    slots = min(count, 4)
 
     def kernel(where_ref, one_ref, other_ref, x_ref, grads_ref, gain_ref, *refs):
         first_refs = refs[: len(first.pieces)]
         second_refs = refs[len(first.pieces) : len(first.pieces) + len(second.pieces)]
-        out_ref, first_held, second_held, total, first_sems, second_sems = refs[-6:]
-        copies = [
-            a + b
-            for a, b in zip(
-                first.copies(first_refs, first_held, first_sems, lambda i: i % slots),
-                second.copies(second_refs, second_held, second_sems, lambda i: i % slots),
-            )
-        ]
-        for made in copies[:slots]:
-            for c in made:
-                c.start()
+        out_ref, total = refs[-2:]
         size = min(depth, 256)
-        for index, made in enumerate(copies):
-            for c in made:
-                c.wait()
-            target = pl.multiple_of((where_ref[0] ^ index) * depth, depth)
+        for index in range(count):
             for part in range(0, depth, size):
-                here = slice(index % slots * depth + part, index % slots * depth + part + size)
-                term = dot(first_held[here, :], one_ref[...]) + dot(second_held[here, :], other_ref[...])
-                total[:, pl.ds(pl.multiple_of(target + part, size), size)] = term.T
-            if index + slots < count:
-                for c in copies[index + slots]:
-                    c.start()
+                target = pl.multiple_of((where_ref[0] ^ index) * depth + part, size)
+                term = dot(first.block(first_refs, index, part, size), one_ref[...])
+                term = term + dot(second.block(second_refs, index, part, size), other_ref[...])
+                total[:, pl.ds(target, size)] = term.T
 
         def body(span):
             x = x_ref[span, :].astype(F32)
@@ -433,19 +385,13 @@
     return pl.pallas_call(
         kernel,
         out_shape=jax.ShapeDtypeStruct((rows, width), BF16),
-        in_specs=[SMEM_SPEC] + [VMEM_SPEC] * 5 + [ANY_SPEC] * (len(first.pieces) + len(second.pieces)),
+        in_specs=[SMEM_SPEC] + [VMEM_SPEC] * 5 + [VMEM_SPEC] * (len(first.pieces) + len(second.pieces)),
         out_specs=VMEM_SPEC,
-        scratch_shapes=[
-            pltpu.VMEM((slots * depth, hidden), BF16),
-            pltpu.VMEM((slots * depth, hidden), BF16),
-            pltpu.VMEM((rows, width), F32),
-            pltpu.SemaphoreType.DMA((len(first.pieces),)),
-            pltpu.SemaphoreType.DMA((len(second.pieces),)),
-        ],
-        compiler_params=params(24),
+        scratch_shapes=[pltpu.VMEM((rows, width), F32)],
+        compiler_params=params(14),
         cost_estimate=cost(4 * one.size * width, 4 * hidden * width),
         name="input_grad_rows",
-    )(where, one, other, x, grads, gain, *first.pieces, *second.pieces)
+    )(where, one, other, x, grads, gain, *first.operands(), *second.operands())
 
 
 def gathered_rows(gate_bias, state_in):
@@ -458,47 +404,60 @@
     depth = w_gate.shape[0]
     halves = lambda w: (w[:half], w[half:])
     straight = turned == 0
-    own_f = [jnp.where(straight, a, b) for a, b in zip(halves(w_gate), halves(w_cand))]
     send = lambda value, offset: hop(value, offset, ranks)
     core = lambda value: hop(value, 1, ranks)
     over = lambda value: swap_batch(value, 1, batches)
-
+    me = lax.axis_index("seq")
+
+    def in_order(value, came, offset):
+        low = (me // offset) % 2 == 0
+        return jnp.where(low, jnp.concatenate([value, came], axis=1), jnp.concatenate([came, value], axis=1))
+
+    own_f = [jnp.where(straight, a, b) for a, b in zip(halves(w_gate), halves(w_cand))]
     f2a, f4a = send(own_f[0], 2), send(own_f[0], 4)
-    f2b, f4b = send(own_f[1], 2), send(own_f[1], 4)
-    own_s = jnp.where(straight, w_cand, w_gate)
-    own_t = halves(w_out)
     f1 = [core(v) for v in own_f]
-    s1, t1 = core(own_s), core(w_out)
-    bias, initial = gathered_rows(gate_bias, state_in)
+    both = jnp.stack([gate_bias, state_in[0]])
+    came = core(both)
     normed, grads = norm_call(where, rows_in, grad_rows, gain, depth)
-
-    f2a, f4a, t2a_in, normed, grads, bias, initial = after((f2a, f4a, own_t[0], normed, grads, bias, initial))
-    t2a, f6a, s2a = send(t2a_in, 2), send(f2a, 4), over(f2a)
+    f2a, f4a, f1a, f1b, came, normed, grads, f_b, own_t, own_s0, own_s1 = after(
+        (f2a, f4a, f1[0], f1[1], came, normed, grads, own_f[1], w_out, w_gate, w_cand)
+    )
+    f1 = [f1a, f1b]
+    both = in_order(both, came, 1)
+    t_a, t_b = halves(own_t)
+    came = send(both, 2)
+    f2b, f4b = send(f_b, 2), send(f_b, 4)
+    s2a, s4a = over(f2a), over(f4a)
+    t2a, t4a = send(t_a, 2), send(t_a, 4)
     f3a, f5a = core(f2a), core(f4a)
-    f2b, f4b, t4a_in, s4a_in = after((f2b, f4b, own_t[0], f4a))
-    f6b, t4a, s4a = send(f4b, 2), send(t4a_in, 4), over(s4a_in)
-    f3b, f5b = core(f2b), core(f4b)
-    t2a, f6a, t2b_in, t4b_in, s2b_in = after((t2a, f6a, own_t[1], own_t[1], f2b), f6a)
-    t2b, t4b, s2b = send(t2b_in, 2), send(t4b_in, 4), over(s2b_in)
-    f7a, t3a = core(f6a), core(t2a)
-    f6b, t4a, s2a, t2a_in, s4b_in = after((f6b, t4a, s2a, t2a, f4b))
-    t6a, s4b = send(t2a_in, 4), over(s4b_in)
-    f7b, t5a, s3a = core(f6b), core(t4a), core(s2a)
+    own_s = jnp.where(straight, own_s1, own_s0)
+    s1, t1 = core(own_s), core(own_t)
+    came, f2b, f4b, s2a, s4a, t2a, t4a, f3a, f5a, s1, t1, own_s, t_b, f2a, both = after(
+        (came, f2b, f4b, s2a, s4a, t2a, t4a, f3a, f5a, s1, t1, own_s, t_b, f2a, both)
+    )
+    both = in_order(both, came, 2)
+    came = send(both, 4)
+    f6a, f6b = send(f2a, 4), send(f4b, 2)
+    s2b, s4b = over(f2b), over(f4b)
+    t2b, t4b = send(t_b, 2), send(t_b, 4)
+    f3b, f5b, s3a, s5a, t3a, t5a = core(f2b), core(f4b), core(s2a), core(s4a), core(t2a), core(t4a)
+    came, f6a, f6b, s2b, s4b, t2b, t4b, f3b, f5b, s3a, s5a, t3a, t5a, both, t2a = after(
+        (came, f6a, f6b, s2b, s4b, t2b, t4b, f3b, f5b, s3a, s5a, t3a, t5a, both, t2a)
+    )
+    both = in_order(both, came, 4)
+    bias, initial = both[0:1], both[1:2]
+    s6a, s6b = over(f6a), over(f6b)
+    t6a, t6b = send(t2a, 4), send(t4b, 2)
+    f7a, f7b, s3b, s5b, t3b, t5b = core(f6a), core(f6b), core(s2b), core(s4b), core(t2b), core(t4b)
     first = Shards([own_f, f1, [f2a, f2b], [f3a, f3b], [f4a, f4b], [f5a, f5b], [f6a, f6b], [f7a, f7b]])
+    most = [[own_s], [s1], [s2a, s2b], [s3a, s3b], [s4a, s4b], [s5a, s5b]]
     first_pre = project_call(normed, first, tile, BF16)
-    t2b, t4b, s4a, s6a_in, first_pre = after((t2b, t4b, s4a, f6a, first_pre))
-    t6b, s6a = send(t4b, 2), over(s6a_in)
-    t3b, t5b, s5a = core(t2b), core(t4b), core(s4a)
-    t6a, t6b, s2b, s4b, s6b_in = after((t6a, t6b, s2b, s4b, f6b))
-    s6b = over(s6b_in)
-    t7a, t7b, s3b, s5b = core(t6a), core(t6b), core(s2b), core(s4b)
-    third = Shards([[w_out], [t1], [t2a, t2b], [t3a, t3b], [t4a, t4b], [t5a, t5b], [t6a, t6b], [t7a, t7b]])
-    (s6a,) = after((s6a,), t7b)
-    s7a = core(s6a)
-    most = [[own_s], [s1], [s2a, s2b], [s3a, s3b], [s4a, s4b], [s5a, s5b]]
+    t6a, t6b, s6a, first_pre, normed, grads = after((t6a, t6b, s6a, first_pre, normed, grads))
+    t7a, t7b, s7a = core(t6a), core(t6b), core(s6a)
+    third = Shards([[own_t], [t1], [t2a, t2b], [t3a, t3b], [t4a, t4b], [t5a, t5b], [t6a, t6b], [t7a, t7b]])
+    partial = project_call(normed, Shards(most), tile, F32)
     back = back_call(where, grads, third)
-    partial = project_call(normed, Shards(most), tile, F32)
-    s6b, back, partial = after((s6b, back, partial))
+    s6b, s7a, back, partial = after((s6b, s7a, back, partial))
     s7b = core(s6b)
     last = [[s6a, s6b], [s7a, s7b]]
     second = Shards(most + last)
@@ -527,7 +486,8 @@
     tile = min(512, hidden)
     me = lax.axis_index("seq")
     given = (rows_in, grad_rows, gain, gate_bias, state_in, w_gate, w_cand, w_out)
-    if ranks == 8 and batches % 2 == 0:
+    cube = ranks == 8 and batches in (2, 4, 8)
+    if cube:
         turned = lax.axis_index("batch") % 2
         where = jnp.stack([me, turned, me]).astype(jnp.int32)
         found = front_on_cube(ranks, batches, where, turned, tile, *given)
@@ -541,9 +501,20 @@
         where, first_pre, second_pre, back, bias, initial, parts, wholes, ranks, tile
     )
     width = hidden // ranks
-    everyone = lax.all_gather(bias_part[0], ("seq", "batch"))
-    bias_grad = lax.dynamic_slice_in_dim(jnp.sum(everyone, axis=0), me * width, width, 0)
-    layer_out = layer_call(where, state_rows, rows_in, third, tile)
+    own_width = lambda row: lax.dynamic_slice_in_dim(row, me * width, width, 0)
+    if cube:
+        pair = bias_part + hop(bias_part, 1, ranks)
+        near = [hop(pair, offset, ranks) for offset in (2, 4, 6)]
+        layer_out = layer_call(where, state_rows, rows_in, third, tile)
+        layer_out, *near = after((layer_out,) + tuple(near))
+        plane = own_width((pair + near[0] + near[1] + near[2])[0])
+        far = [swap_batch(plane, offset, batches) for offset in range(1, batches)]
+        bias_grad = plane + sum(far[1:], far[0])
+        one, other, plane = after((one, other, plane), layer_out)
+    else:
+        over_seq = lax.psum_scatter(bias_part[0], "seq", scatter_dimension=0, tiled=True)
+        bias_grad = lax.psum(over_seq, "batch")
+        layer_out = layer_call(where, state_rows, rows_in, third, tile)
     input_grad = input_grad_call(where, one, other, first, second, rows_in, grad_rows, gain)
     state_out = lax.dynamic_slice_in_dim(state_grad, me * width, width, 1)
     return (layer_out[None], input_grad[None], state_out, bias_grad)

time: 294 us -> 197 us (0.67)
  blocking collectives: 104 us -> 9.48 us
  starting transfers between devices: 25.9 us -> 36.9 us
  Pallas kernels: 49.2 us -> 40.3 us
  waiting for transfers between devices: 79.5 us -> 74.8 us
    all_gather x2 -> x0, blocking collectives: 95.7 us -> none  [the longest x1 69.4 us: on_device(): everyone = lax.all_gather(bias_part[0], ('seq', 'batch'))]
    ppermute x34 -> x41, starting transfers between devices: 17.5 us -> 26.4 us  [hop(): return lax.ppermute(value, 'seq', [(i, i ^ offset) for i in range(count)])]
    pallas_call x1, Pallas kernels: 15.8 us -> 10.2 us  [input_grad_call(): pl.pallas_call(kernel, out_shape=jax.ShapeDtypeStruct((rows, width), BF16...]
    unnamed x180 -> x144, local copies, waits for them, and re-layouts: 28.1 us -> 25.4 us
    ppermute x6 -> x9, waiting for transfers between devices: 29 us -> 26.3 us  [swap_batch(): return lax.ppermute(value, 'batch', [(i, i ^ offset) for i in range(count)])]
    ppermute x34 -> x41, waiting for transfers between devices: 50.5 us -> 48.4 us  [hop(): return lax.ppermute(value, 'seq', [(i, i ^ offset) for i in range(count)])]
    ppermute x6 -> x9, starting transfers between devices: 8.46 us -> 10.5 us  [swap_batch(): return lax.ppermute(value, 'batch', [(i, i ^ offset) for i in range(count)])]
  transfers between devices with their start and end apart: 40 -> 50, of which waited for: 12 -> 15; matrix products, arithmetic and copies ran while one was open for 0% -> 2% of each run, Pallas kernels for 6% -> 16%
where the time goes in v1:
time: 197 us; the launch traced here: 196 us
  waiting for transfers between devices  74.8 us (38%)
  Pallas kernels  40.3 us (20%)
  starting transfers between devices  36.9 us (19%)
  local copies, waits for them, and re-layouts  28.2 us (14%)
  blocking collectives  9.48 us (5%)
  other arithmetic  4.77 us (2%)
    ppermute x41, waiting for transfers between devices, hop(): return lax.ppermute(value, 'seq', [(i, i ^ offset) for i in range(count)])  48.4 us
    ppermute x41, starting transfers between devices, hop(): return lax.ppermute(value, 'seq', [(i, i ^ offset) for i in range(count)])  26.4 us
    ppermute x9, waiting for transfers between devices, swap_batch(): return lax.ppermute(value, 'batch', [(i, i ^ offset) for i in range(count)])  26.3 us
    unnamed x144, local copies, waits for them, and re-layouts  25.4 us
    ppermute x9, starting transfers between devices, swap_batch(): return lax.ppermute(value, 'batch', [(i, i ^ offset) for i in range(count)])  10.5 us
    pallas_call x1, Pallas kernels, input_grad_call(): pl.pallas_call(kernel, out_shape=jax.ShapeDtypeStruct((rows, width), BF16...  10.2 us
    all_gather x1, blocking collectives, on_device(): wholes = lax.all_gather(whole, 'seq')  9.48 us
    pallas_call x2, Pallas kernels, project_call(): pl.pallas_call(kernel, out_shape=jax.ShapeDtypeStruct((rows, width), dtyp...  7.15 us
  transfers between devices with their start and end apart: 50, of which 15 were waited for; matrix products, arithmetic and copies ran while one was open for 2% of the time, Pallas kernels for 16%

profile of v1, /device:TPU:0, one launch (start us, length us, event | category | flops | bytes accessed | tf_op | source)
XLA Modules:
  0.0 195.7 jit_solution(7188084264792412630)
XLA Ops:
  0.7 2.7 %slice_select_fusion = (bf16[128,2048]{1,0:T(8,128)(2,1)}, bf16[128,2048]{1,0:T(8,128)(2,1)}) fusion(bf16[256,2048]{1,0:T(8,128)(2,1)} %param.14, bf16[256,2048]{1,0:T(8,128)(2,1)} %param.13, pred[]{:T(512)S(6)} %eq.19), kind=kLoop, calls=%fused_computation.1 | loop fusion | flops 524288 | bytes 3145729 | tf_op jit(solution)/shard_map/jit(_where)/select_n | solution.py:416
  4.0 3.0 %collective-permute-start.1 = (bf16[128,2048]{1,0:T(8,128)(2,1)}, bf16[128,2048]{1,0:T(8,128)(2,1)}, u32[]{:S(2)}, u32[]{:S(2)}) collective-permute-start(bf16[128,2048]{1,0:T(8,128)(2,1)} %get-tuple-element.139.refs_0_), channel_id=1, source_target_pairs={{0,16},{4,20},{8,24},{12,28},{16,0},{20,4},{24,8},{28,12},{1,17},{... | collective-permute-start | bytes 1572872 | tf_op jit(solution)/shard_map/ppermute | solution.py:25
  6.9 1.5 collective-permute-start
  8.6 3.3 %norm_rows.1 = (bf16[256,2048]{1,0:T(8,128)(2,1)S(1)}, bf16[2048,256]{1,0:T(8,128)(2,1)S(1)}) custom-call(s32[3]{0:T(128)S(1)} %pad_add_fusion.where_ref, bf16[256,2048]{1,0:T(8,128)(2,1)S(1)} %bitcast.10, bf16[256,2048]{1,0:T(8,128)(2,1)S(1)} %bitcast.13, f32[1,2048]{1,0:T(1,128)S(1)} %bitcast.15), custom_call_target="tpu_custom_call" | custom-call | flops 536870912 | bytes 4194304 | tf_op jit(solution)/shard_map/norm_rows/pallas_call | solution.py:112
  12.9 6.4 %collective-permute-done.1.refs_8_ = bf16[128,2048]{1,0:T(8,128)(2,1)} collective-permute-done((bf16[128,2048]{1,0:T(8,128)(2,1)}, bf16[128,2048]{1,0:T(8,128)(2,1)}, u32[]{:S(2)}, u32[]{:S(2)}) %collective-permute-start.1) | collective-permute-done | bytes 524320 | tf_op jit(solution)/shard_map/ppermute | solution.py:25
  21.1 1.7 collective-permute-start.6
  22.8 1.6 collective-permute-start.8
  26.3 7.8 %collective-permute-done.5 = f32[2,512]{1,0:T(2,128)S(1)} collective-permute-done((f32[2,512]{1,0:T(2,128)S(1)}, f32[2,512]{1,0:T(2,128)S(1)}, u32[]{:S(2)}, u32[]{:S(2)}) %collective-permute-start.5) | collective-permute-done | bytes 4128 | tf_op jit(solution)/shard_map/ppermute | solution.py:25
  34.7 2.2 %fusion.3 = (bf16[128,2048]{1,0:T(8,128)(2,1)}, bf16[128,2048]{1,0:T(8,128)(2,1)S(1)}) fusion(bf16[256,2048]{1,0:T(8,128)(2,1)} %refs_0_.1), kind=kLoop, calls=%fused_computation.17 | loop fusion | bytes 2097152 | tf_op jit(solution)/shard_map/slice | solution.py:405
  37.7 1.6 collective-permute-start.9
  41.5 1.5 collective-permute-start.10
  43.0 9.1 %collective-permute-done.9.refs_6_.refs_22_ = bf16[128,2048]{1,0:T(8,128)(2,1)S(1)} collective-permute-done((bf16[128,2048]{1,0:T(8,128)(2,1)}, bf16[128,2048]{1,0:T(8,128)(2,1)S(1)}, u32[]{:S(2)}, u32[]{:S(2)}) %collective-permute-start.9) | collective-permute-done | bytes 524320 | tf_op jit(solution)/shard_map/ppermute | solution.py:29
  53.2 1.9 collective-permute-done.10.refs_2_
  57.7 1.6 collective-permute-start.21
  61.3 11.0 %collective-permute-done.16 = f32[2,1024]{1,0:T(2,128)S(1)} collective-permute-done((f32[2,1024]{1,0:T(2,128)S(1)}, f32[2,1024]{1,0:T(2,128)S(1)}, u32[]{:S(2)}, u32[]{:S(2)}) %collective-permute-start.16) | collective-permute-done | bytes 8224 | tf_op jit(solution)/shard_map/ppermute | solution.py:25
  74.2 7.2 %collective-permute-done.17.refs_12_ = bf16[128,2048]{1,0:T(8,128)(2,1)S(1)} collective-permute-done((bf16[128,2048]{1,0:T(8,128)(2,1)}, bf16[128,2048]{1,0:T(8,128)(2,1)S(1)}, u32[]{:S(2)}, u32[]{:S(2)}) %collective-permute-start.17) | collective-permute-done | bytes 524320 | tf_op jit(solution)/shard_map/ppermute | solution.py:25
  83.5 1.6 collective-permute-start.20
  87.4 9.1 %collective-permute-done.19.refs_3_.refs_19_ = bf16[128,2048]{1,0:T(8,128)(2,1)S(1)} collective-permute-done((bf16[128,2048]{1,0:T(8,128)(2,1)}, bf16[128,2048]{1,0:T(8,128)(2,1)S(1)}, u32[]{:S(2)}, u32[]{:S(2)}) %collective-permute-start.19) | collective-permute-done | bytes 524320 | tf_op jit(solution)/shard_map/ppermute | solution.py:29
  96.5 8.1 %collective-permute-done.20.refs_7_.refs_23_ = bf16[128,2048]{1,0:T(8,128)(2,1)S(1)} collective-permute-done((bf16[128,2048]{1,0:T(8,128)(2,1)}, bf16[128,2048]{1,0:T(8,128)(2,1)S(1)}, u32[]{:S(2)}, u32[]{:S(2)}) %collective-permute-start.20) | collective-permute-done | bytes 524320 | tf_op jit(solution)/shard_map/ppermute | solution.py:29
  105.8 1.5 collective-permute-start.30
  107.7 8.1 %collective-permute-done.29.refs_10_ = bf16[128,2048]{1,0:T(8,128)(2,1)} collective-permute-done((bf16[128,2048]{1,0:T(8,128)(2,1)}, bf16[128,2048]{1,0:T(8,128)(2,1)}, u32[]{:S(2)}, u32[]{:S(2)}) %collective-permute-start.29) | collective-permute-done | bytes 524320 | tf_op jit(solution)/shard_map/ppermute | solution.py:25
  120.7 4.8 %project.2.first_ref = bf16[256,2048]{1,0:T(8,128)(2,1)S(1)} custom-call(bf16[256,2048]{1,0:T(8,128)(2,1)S(1)} %get-tuple-element.103.x_ref, bf16[128,2048]{1,0:T(8,128)(2,1)} %get-tuple-element.139.refs_0_, bf16[128,2048]{1,0:T(8,128)(2,1)} %get-tuple-element.74.refs_1_, bf16[128,2048]{1,0:T(8,128)(2,1)} %collective-permute-done.2.refs_2_, ...), custom_call_target="tpu_custom_call" | custom-call | flops 2147483648 | bytes 8388608 | tf_op jit(solution)/shard_map/project/pallas_call | solution.py:137
  139.9 2.3 %project.3.refs_0_ = f32[256,2048]{1,0:T(8,128)S(1)} custom-call(bf16[256,2048]{1,0:T(8,128)(2,1)S(1)} %get-tuple-element.103.x_ref, bf16[256,2048]{1,0:T(8,128)(2,1)S(1)} %broadcast_select_fusion.refs_0_.refs_16_, bf16[256,2048]{1,0:T(8,128)(2,1)S(1)} %copy-done.5, bf16[128,2048]{1,0:T(8,128)(2,1)S(1)} %copy-done.21, bf16[128,2048]{1,0:T(8,128)(2,1)S(1)} %copy-done.40, ...), custom_call_target="tpu_custom_call" | custom-call | flops 1610612736 | bytes 6291456 | tf_op jit(solution)/shard_map/project/pallas_call | solution.py:137
  142.5 4.5 %back_rows.1.back_ref = bf16[256,2048]{1,0:T(8,128)(2,1)S(1)} custom-call(s32[3]{0:T(128)S(1)} %pad_add_fusion.where_ref, bf16[2048,256]{1,0:T(8,128)(2,1)S(1)} %copy-done.68, bf16[256,2048]{1,0:T(8,128)(2,1)S(1)} %copy-done.3, bf16[256,2048]{1,0:T(8,128)(2,1)S(1)} %copy-done.10, bf16[128,2048]{1,0:T(8,128)(2,1)S(1)} %copy-done.60, ...), custom_call_target="tpu_custom_call" | custom-call | flops 2147483648 | bytes 8388608 | tf_op jit(solution)/shard_map/back_rows/pallas_call | solution.py:161
  147.7 1.7 collective-permute-done.42.refs_4_.refs_29_
  149.4 4.2 %project_totals.1 = (bf16[256,2048]{1,0:T(8,128)(2,1)S(1)}, f32[3,8,2048]{2,1,0:T(8,128)S(1)}, f32[3,2048]{1,0:T(4,128)S(1)}) custom-call(s32[3]{0:T(128)S(1)} %pad_add_fusion.where_ref, bf16[256,2048]{1,0:T(8,128)(2,1)S(1)} %get-tuple-element.103.x_ref, bf16[256,2048]{1,0:T(8,128)(2,1)S(1)} %copy-done.2, bf16[256,2048]{1,0:T(8,128)(2,1)S(1)} %back_rows.1.back_ref, ...), custom_call_target="tpu_custom_call" | custom-call | flops 536870912 | bytes 2097152 | tf_op jit(solution)/shard_map/project_totals/pallas_call | solution.py:228
  153.6 9.5 %all-gather.1.wholes_ref = f32[8,3,2048]{2,1,0:T(4,128)S(1)} all-gather(f32[1,3,2048]{2,1,0:T(4,128)S(1)} %bitcast.17), channel_id=2, replica_groups=mesh['seq'=8,'batch'=4] {'seq'}, dimensions={0}, use_global_device_ids=true | all-gather | bytes 221184 | tf_op jit(solution)/shard_map/all_gather | solution.py:499
  163.1 4.7 %scan_rows.1 = (bf16[256,2048]{1,0:T(8,128)(2,1)S(1)}, bf16[2048,256]{1,0:T(8,128)(2,1)S(1)}, bf16[2048,256]{1,0:T(8,128)(2,1)S(1)}, f32[1,2048]{1,0:T(1,128)S(1)}, f32[1,2048]{1,0:T(1,128)S(1)}) custom-call(s32[3]{0:T(128)S(1)} %pad_add_fusion.where_ref, bf16[256,2048]{1,0:T(8,128)(2,1)S(1)} %copy-done.2, ...), custom_call_target="tpu_custom_call" | custom-call | flops 805306368 | bytes 6291456 | tf_op jit(solution)/shard_map/scan_rows/pallas_call | solution.py:317
  168.4 6.2 %layer_rows.1 = bf16[256,2048]{1,0:T(8,128)(2,1)} custom-call(s32[3]{0:T(128)S(1)} %pad_add_fusion.where_ref, bf16[256,2048]{1,0:T(8,128)(2,1)S(1)} %get-tuple-element.127.x_ref, bf16[256,2048]{1,0:T(8,128)(2,1)S(1)} %bitcast.11, bf16[256,2048]{1,0:T(8,128)(2,1)S(1)} %copy-done.3, bf16[256,2048]{1,0:T(8,128)(2,1)S(1)} %copy-done.10, ...), custom_call_target="tpu_custom_call" | custom-call | flops 2147483648 | bytes 8388608 | tf_op jit(solution)/shard_map/layer_rows/pallas_call | solution.py:345
  176.7 1.5 collective-permute-start.44
  180.3 3.6 %collective-permute-start.49 = (f32[256]{0:T(256)S(1)}, f32[256]{0:T(256)S(1)}, u32[]{:S(2)}, u32[]{:S(2)}) collective-permute-start(f32[256]{0:T(256)S(1)} %bitcast.22), channel_id=1, source_target_pairs={{0,3},{1,2},{2,1},{3,0},{4,7},{5,6},{6,5},{7,4},{8,11},{9,10},{10,... | collective-permute-start | bytes 3080 | tf_op jit(solution)/shard_map/ppermute | solution.py:29
  184.9 10.2 %input_grad_rows.1 = bf16[256,2048]{1,0:T(8,128)(2,1)} custom-call(s32[3]{0:T(128)S(1)} %pad_add_fusion.where_ref, bf16[2048,256]{1,0:T(8,128)(2,1)S(1)} %get-tuple-element.135.one_ref, bf16[2048,256]{1,0:T(8,128)(2,1)S(1)} %get-tuple-element.136.other_ref, bf16[256,2048]{1,0:T(8,128)(2,1)S(1)} %bitcast.12, bf16[256,2048]{1,0:T(8,128)(2,1)S(1)} %bitcast.14, ...), custom_call_target="tpu_custom_call" | custom-call | flops 4294967296 | bytes 16777216 | tf_op jit(solution)/shard_map/input_grad_rows/pallas_call | solution.py:385
  (234 shorter events, 48.5 us)
Async XLA Ops:
  4.0 15.4 %collective-permute-start.1 = (bf16[128,2048]{1,0:T(8,128)(2,1)}, bf16[128,2048]{1,0:T(8,128)(2,1)}, u32[]{:S(2)}, u32[]{:S(2)}) collective-permute-start(bf16[128,2048]{1,0:T(8,128)(2,1)} %get-tuple-element.139.refs_0_), channel_id=1, source_target_pairs={{0,16},{4,20},{8,24},{12,28},{16,0},{20,4},{24,8},{28,12},{1,17},{... | collective-permute-start | bytes 1572872 | tf_op jit(solution)/shard_map/ppermute | solution.py:25
  6.9 13.9 %collective-permute-start = (bf16[128,2048]{1,0:T(8,128)(2,1)}, bf16[128,2048]{1,0:T(8,128)(2,1)}, u32[]{:S(2)}, u32[]{:S(2)}) collective-permute-start(bf16[128,2048]{1,0:T(8,128)(2,1)} %get-tuple-element.139.refs_0_), channel_id=1, source_target_pairs={{0,8},{4,12},{8,0},{12,4},{16,24},{20,28},{24,16},{28,20},{1,9},{5... | collective-permute-start | bytes 1572872 | tf_op jit(solution)/shard_map/ppermute | solution.py:25
  20.8 13.3 %collective-permute-start.7 = (bf16[128,2048]{1,0:T(8,128)(2,1)}, bf16[128,2048]{1,0:T(8,128)(2,1)S(1)}, u32[]{:S(2)}, u32[]{:S(2)}) collective-permute-start(bf16[128,2048]{1,0:T(8,128)(2,1)} %get-tuple-element.74.refs_1_), channel_id=1, source_target_pairs={{0,16},{4,20},{8,24},{12,28},{16,0},{20,4},{24,8},{28,12},{1,17},{... | collective-permute-start | bytes 1572872 | tf_op jit(solution)/shard_map/ppermute | solution.py:25
  21.1 13.5 %collective-permute-start.6 = (bf16[128,2048]{1,0:T(8,128)(2,1)}, bf16[128,2048]{1,0:T(8,128)(2,1)S(1)}, u32[]{:S(2)}, u32[]{:S(2)}) collective-permute-start(bf16[128,2048]{1,0:T(8,128)(2,1)} %get-tuple-element.74.refs_1_), channel_id=1, source_target_pairs={{0,8},{4,12},{8,0},{12,4},{16,24},{20,28},{24,16},{28,20},{1,9},{5... | collective-permute-start | bytes 1572872 | tf_op jit(solution)/shard_map/ppermute | solution.py:25
  22.8 14.1 %collective-permute-start.12 = (bf16[128,2048]{1,0:T(8,128)(2,1)}, bf16[128,2048]{1,0:T(8,128)(2,1)S(1)}, u32[]{:S(2)}, u32[]{:S(2)}) collective-permute-start(bf16[128,2048]{1,0:T(8,128)(2,1)} %collective-permute-done.refs_4_), channel_id=1, source_target_pairs={{0,4},{4,0},{8,12},{12,8},{16,20},{20,16},{24,28},{28,24},{1,5},{5... | collective-permute-start | bytes 1572872 | tf_op jit(solution)/shard_map/ppermute | solution.py:25
  22.8 16.5 %collective-permute-start.8 = (bf16[128,2048]{1,0:T(8,128)(2,1)}, bf16[128,2048]{1,0:T(8,128)(2,1)S(1)}, u32[]{:S(2)}, u32[]{:S(2)}) collective-permute-start(bf16[128,2048]{1,0:T(8,128)(2,1)} %collective-permute-done.refs_4_), channel_id=1, source_target_pairs={{0,1},{1,0},{2,3},{3,2},{4,5},{5,4},{6,7},{7,6},{8,9},{9,8},{10,11... | collective-permute-start | bytes 1572872 | tf_op jit(solution)/shard_map/ppermute | solution.py:29
  34.1 21.0 %collective-permute-start.14 = (bf16[256,2048]{1,0:T(8,128)(2,1)S(1)}, bf16[256,2048]{1,0:T(8,128)(2,1)S(1)}, u32[]{:S(2)}, u32[]{:S(2)}) collective-permute-start(bf16[256,2048]{1,0:T(8,128)(2,1)S(1)} %broadcast_select_fusion.refs_0_.refs_16_), channel_id=1, source_target_pairs={{0,4},{4,0},{8,12},{12,8},{16,20},{20,16},{24,28},{28,24},{1,5},{5... | collective-permute-start | bytes 3145736 | tf_op jit(solution)/shard_map/ppermute | solution.py:25
  34.6 21.5 %collective-permute-start.15 = (bf16[256,2048]{1,0:T(8,128)(2,1)}, bf16[256,2048]{1,0:T(8,128)(2,1)S(1)}, u32[]{:S(2)}, u32[]{:S(2)}) collective-permute-start(bf16[256,2048]{1,0:T(8,128)(2,1)} %refs_0_.1), channel_id=1, source_target_pairs={{0,4},{4,0},{8,12},{12,8},{16,20},{20,16},{24,28},{28,24},{1,5},{5... | collective-permute-start | bytes 3145736 | tf_op jit(solution)/shard_map/ppermute | solution.py:25
  37.7 14.3 %collective-permute-start.9 = (bf16[128,2048]{1,0:T(8,128)(2,1)}, bf16[128,2048]{1,0:T(8,128)(2,1)S(1)}, u32[]{:S(2)}, u32[]{:S(2)}) collective-permute-start(bf16[128,2048]{1,0:T(8,128)(2,1)} %collective-permute-done.1.refs_8_), channel_id=1, source_target_pairs={{0,1},{1,0},{2,3},{3,2},{4,5},{5,4},{6,7},{7,6},{8,9},{9,8},{10,11... | collective-permute-start | bytes 1572872 | tf_op jit(solution)/shard_map/ppermute | solution.py:29
  39.3 13.9 %collective-permute-start.11 = (bf16[128,2048]{1,0:T(8,128)(2,1)S(1)}, bf16[128,2048]{1,0:T(8,128)(2,1)S(1)}, u32[]{:S(2)}, u32[]{:S(2)}) collective-permute-start(bf16[128,2048]{1,0:T(8,128)(2,1)S(1)} %get-tuple-element.141), channel_id=1, source_target_pairs={{0,16},{4,20},{8,24},{12,28},{16,0},{20,4},{24,8},{28,12},{1,17},{... | collective-permute-start | bytes 1572872 | tf_op jit(solution)/shard_map/ppermute | solution.py:25
  41.5 13.6 %collective-permute-start.10 = (bf16[128,2048]{1,0:T(8,128)(2,1)S(1)}, bf16[128,2048]{1,0:T(8,128)(2,1)S(1)}, u32[]{:S(2)}, u32[]{:S(2)}) collective-permute-start(bf16[128,2048]{1,0:T(8,128)(2,1)S(1)} %get-tuple-element.141), channel_id=1, source_target_pairs={{0,8},{4,12},{8,0},{12,4},{16,24},{20,28},{24,16},{28,20},{1,9},{5... | collective-permute-start | bytes 1572872 | tf_op jit(solution)/shard_map/ppermute | solution.py:25
  57.1 15.3 %collective-permute-start.22 = (bf16[128,2048]{1,0:T(8,128)(2,1)}, bf16[128,2048]{1,0:T(8,128)(2,1)}, u32[]{:S(2)}, u32[]{:S(2)}) collective-permute-start(bf16[128,2048]{1,0:T(8,128)(2,1)} %get-tuple-element.85), channel_id=1, source_target_pairs={{0,16},{4,20},{8,24},{12,28},{16,0},{20,4},{24,8},{28,12},{1,17},{... | collective-permute-start | bytes 1572872 | tf_op jit(solution)/shard_map/ppermute | solution.py:25
  57.7 15.1 %collective-permute-start.21 = (bf16[128,2048]{1,0:T(8,128)(2,1)}, bf16[128,2048]{1,0:T(8,128)(2,1)}, u32[]{:S(2)}, u32[]{:S(2)}) collective-permute-start(bf16[128,2048]{1,0:T(8,128)(2,1)} %get-tuple-element.85), channel_id=1, source_target_pairs={{0,8},{4,12},{8,0},{12,4},{16,24},{20,28},{24,16},{28,20},{1,9},{5... | collective-permute-start | bytes 1572872 | tf_op jit(solution)/shard_map/ppermute | solution.py:25
  59.3 13.1 %collective-permute-start.16 = (f32[2,1024]{1,0:T(2,128)S(1)}, f32[2,1024]{1,0:T(2,128)S(1)}, u32[]{:S(2)}, u32[]{:S(2)}) collective-permute-start(f32[2,1024]{1,0:T(2,128)S(1)} %maximum_select_fusion.1), channel_id=1, source_target_pairs={{0,16},{4,20},{8,24},{12,28},{16,0},{20,4},{24,8},{28,12},{1,17},{... | collective-permute-start | bytes 24584 | tf_op jit(solution)/shard_map/ppermute | solution.py:25
  60.7 12.2 %collective-permute-start.27 = (bf16[128,2048]{1,0:T(8,128)(2,1)}, bf16[128,2048]{1,0:T(8,128)(2,1)S(1)}, u32[]{:S(2)}, u32[]{:S(2)}) collective-permute-start(bf16[128,2048]{1,0:T(8,128)(2,1)} %copy-done.59), channel_id=1, source_target_pairs={{0,4},{4,0},{8,12},{12,8},{16,20},{20,16},{24,28},{28,24},{1,5},{5... | collective-permute-start | bytes 1572872 | tf_op jit(solution)/shard_map/ppermute | solution.py:25
  60.7 20.7 %collective-permute-start.17 = (bf16[128,2048]{1,0:T(8,128)(2,1)}, bf16[128,2048]{1,0:T(8,128)(2,1)S(1)}, u32[]{:S(2)}, u32[]{:S(2)}) collective-permute-start(bf16[128,2048]{1,0:T(8,128)(2,1)} %collective-permute-done.refs_4_), channel_id=1, source_target_pairs={{0,16},{4,20},{8,24},{12,28},{16,0},{20,4},{24,8},{28,12},{1,17},{... | collective-permute-start | bytes 1572872 | tf_op jit(solution)/shard_map/ppermute | solution.py:25
  72.9 12.2 %collective-permute-start.28 = (bf16[128,2048]{1,0:T(8,128)(2,1)}, bf16[128,2048]{1,0:T(8,128)(2,1)S(1)}, u32[]{:S(2)}, u32[]{:S(2)}) collective-permute-start(bf16[128,2048]{1,0:T(8,128)(2,1)} %copy-done.57), channel_id=1, source_target_pairs={{0,4},{4,0},{8,12},{12,8},{16,20},{20,16},{24,28},{28,24},{1,5},{5... | collective-permute-start | bytes 1572872 | tf_op jit(solution)/shard_map/ppermute | solution.py:25
  73.8 13.6 %collective-permute-start.23 = (bf16[128,2048]{1,0:T(8,128)(2,1)}, bf16[128,2048]{1,0:T(8,128)(2,1)S(1)}, u32[]{:S(2)}, u32[]{:S(2)}) collective-permute-start(bf16[128,2048]{1,0:T(8,128)(2,1)} %copy-done.14), channel_id=1, source_target_pairs={{0,4},{4,0},{8,12},{12,8},{16,20},{20,16},{24,28},{28,24},{1,5},{5... | collective-permute-start | bytes 1572872 | tf_op jit(solution)/shard_map/ppermute | solution.py:25
  81.5 15.1 %collective-permute-start.19 = (bf16[128,2048]{1,0:T(8,128)(2,1)}, bf16[128,2048]{1,0:T(8,128)(2,1)S(1)}, u32[]{:S(2)}, u32[]{:S(2)}) collective-permute-start(bf16[128,2048]{1,0:T(8,128)(2,1)} %copy-done.14), channel_id=1, source_target_pairs={{0,1},{1,0},{2,3},{3,2},{4,5},{5,4},{6,7},{7,6},{8,9},{9,8},{10,11... | collective-permute-start | bytes 1572872 | tf_op jit(solution)/shard_map/ppermute | solution.py:29
  82.7 13.8 %collective-permute-start.24 = (bf16[128,2048]{1,0:T(8,128)(2,1)}, bf16[128,2048]{1,0:T(8,128)(2,1)S(1)}, u32[]{:S(2)}, u32[]{:S(2)}) collective-permute-start(bf16[128,2048]{1,0:T(8,128)(2,1)} %copy-done.11), channel_id=1, source_target_pairs={{0,4},{4,0},{8,12},{12,8},{16,20},{20,16},{24,28},{28,24},{1,5},{5... | collective-permute-start | bytes 1572872 | tf_op jit(solution)/shard_map/ppermute | solution.py:25
  83.5 21.2 %collective-permute-start.20 = (bf16[128,2048]{1,0:T(8,128)(2,1)}, bf16[128,2048]{1,0:T(8,128)(2,1)S(1)}, u32[]{:S(2)}, u32[]{:S(2)}) collective-permute-start(bf16[128,2048]{1,0:T(8,128)(2,1)} %copy-done.11), channel_id=1, source_target_pairs={{0,1},{1,0},{2,3},{3,2},{4,5},{5,4},{6,7},{7,6},{8,9},{9,8},{10,11... | collective-permute-start | bytes 1572872 | tf_op jit(solution)/shard_map/ppermute | solution.py:29
  85.9 18.8 %collective-permute-start.18 = (bf16[128,2048]{1,0:T(8,128)(2,1)}, bf16[128,2048]{1,0:T(8,128)(2,1)}, u32[]{:S(2)}, u32[]{:S(2)}) collective-permute-start(bf16[128,2048]{1,0:T(8,128)(2,1)} %copy-done.11), channel_id=1, source_target_pairs={{0,8},{4,12},{8,0},{12,4},{16,24},{20,28},{24,16},{28,20},{1,9},{5... | collective-permute-start | bytes 1572872 | tf_op jit(solution)/shard_map/ppermute | solution.py:25
  105.8 20.8 %collective-permute-start.30 = (bf16[128,2048]{1,0:T(8,128)(2,1)}, bf16[128,2048]{1,0:T(8,128)(2,1)}, u32[]{:S(2)}, u32[]{:S(2)}) collective-permute-start(bf16[128,2048]{1,0:T(8,128)(2,1)} %collective-permute-done.22.refs_7_), channel_id=1, source_target_pairs={{0,8},{4,12},{8,0},{12,4},{16,24},{20,28},{24,16},{28,20},{1,9},{5... | collective-permute-start | bytes 1572872 | tf_op jit(solution)/shard_map/ppermute | solution.py:25
  107.3 19.7 %collective-permute-start.31 = (bf16[128,2048]{1,0:T(8,128)(2,1)S(1)}, bf16[128,2048]{1,0:T(8,128)(2,1)}, u32[]{:S(2)}, u32[]{:S(2)}) collective-permute-start(bf16[128,2048]{1,0:T(8,128)(2,1)S(1)} %collective-permute-done.17.refs_12_), channel_id=1, source_target_pairs={{0,1},{1,0},{2,3},{3,2},{4,5},{5,4},{6,7},{7,6},{8,9},{9,8},{10,11... | collective-permute-start | bytes 1572872 | tf_op jit(solution)/shard_map/ppermute | solution.py:29
  115.9 12.4 %collective-permute-start.40 = (bf16[128,2048]{1,0:T(8,128)(2,1)S(1)}, bf16[128,2048]{1,0:T(8,128)(2,1)S(1)}, u32[]{:S(2)}, u32[]{:S(2)}) collective-permute-start(bf16[128,2048]{1,0:T(8,128)(2,1)S(1)} %collective-permute-done.19.refs_3_.refs_19_), channel_id=1, source_target_pairs={{0,4},{4,0},{8,12},{12,8},{16,20},{20,16},{24,28},{28,24},{1,5},{5... | collective-permute-start | bytes 1572872 | tf_op jit(solution)/shard_map/ppermute | solution.py:25
  116.4 13.1 %collective-permute-start.41 = (bf16[128,2048]{1,0:T(8,128)(2,1)S(1)}, bf16[128,2048]{1,0:T(8,128)(2,1)S(1)}, u32[]{:S(2)}, u32[]{:S(2)}) collective-permute-start(bf16[128,2048]{1,0:T(8,128)(2,1)S(1)} %collective-permute-done.20.refs_7_.refs_23_), channel_id=1, source_target_pairs={{0,4},{4,0},{8,12},{12,8},{16,20},{20,16},{24,28},{28,24},{1,5},{5... | collective-permute-start | bytes 1572872 | tf_op jit(solution)/shard_map/ppermute | solution.py:25
  126.6 15.7 %collective-permute-start.37 = (bf16[128,2048]{1,0:T(8,128)(2,1)}, bf16[128,2048]{1,0:T(8,128)(2,1)}, u32[]{:S(2)}, u32[]{:S(2)}) collective-permute-start(bf16[128,2048]{1,0:T(8,128)(2,1)} %collective-permute-done.22.refs_7_), channel_id=1, source_target_pairs={{0,4},{4,0},{8,12},{12,8},{16,20},{20,16},{24,28},{28,24},{1,5},{5... | collective-permute-start | bytes 1572872 | tf_op jit(solution)/shard_map/ppermute | solution.py:25
  126.9 15.3 %collective-permute-start.38 = (bf16[128,2048]{1,0:T(8,128)(2,1)}, bf16[128,2048]{1,0:T(8,128)(2,1)}, u32[]{:S(2)}, u32[]{:S(2)}) collective-permute-start(bf16[128,2048]{1,0:T(8,128)(2,1)} %collective-permute-done.29.refs_10_), channel_id=1, source_target_pairs={{0,4},{4,0},{8,12},{12,8},{16,20},{20,16},{24,28},{28,24},{1,5},{5... | collective-permute-start | bytes 1572872 | tf_op jit(solution)/shard_map/ppermute | solution.py:25
  127.9 14.4 %collective-permute-start.39 = (bf16[128,2048]{1,0:T(8,128)(2,1)}, bf16[128,2048]{1,0:T(8,128)(2,1)}, u32[]{:S(2)}, u32[]{:S(2)}) collective-permute-start(bf16[128,2048]{1,0:T(8,128)(2,1)} %collective-permute-done.30.refs_11_), channel_id=1, source_target_pairs={{0,4},{4,0},{8,12},{12,8},{16,20},{20,16},{24,28},{28,24},{1,5},{5... | collective-permute-start | bytes 1572872 | tf_op jit(solution)/shard_map/ppermute | solution.py:25
  129.1 18.0 %collective-permute-start.34 = (bf16[128,2048]{1,0:T(8,128)(2,1)}, bf16[128,2048]{1,0:T(8,128)(2,1)}, u32[]{:S(2)}, u32[]{:S(2)}) collective-permute-start(bf16[128,2048]{1,0:T(8,128)(2,1)} %collective-permute-done.18.refs_13_), channel_id=1, source_target_pairs={{0,1},{1,0},{2,3},{3,2},{4,5},{5,4},{6,7},{7,6},{8,9},{9,8},{10,11... | collective-permute-start | bytes 1572872 | tf_op jit(solution)/shard_map/ppermute | solution.py:29
  130.3 16.7 %collective-permute-start.35 = (bf16[128,2048]{1,0:T(8,128)(2,1)}, bf16[128,2048]{1,0:T(8,128)(2,1)}, u32[]{:S(2)}, u32[]{:S(2)}) collective-permute-start(bf16[128,2048]{1,0:T(8,128)(2,1)} %collective-permute-done.31.refs_1_.refs_26_), channel_id=1, source_target_pairs={{0,4},{4,0},{8,12},{12,8},{16,20},{20,16},{24,28},{28,24},{1,5},{5... | collective-permute-start | bytes 1572872 | tf_op jit(solution)/shard_map/ppermute | solution.py:25
  180.3 14.8 %collective-permute-start.49 = (f32[256]{0:T(256)S(1)}, f32[256]{0:T(256)S(1)}, u32[]{:S(2)}, u32[]{:S(2)}) collective-permute-start(f32[256]{0:T(256)S(1)} %bitcast.22), channel_id=1, source_target_pairs={{0,3},{1,2},{2,1},{3,0},{4,7},{5,6},{6,5},{7,4},{8,11},{9,10},{10,... | collective-permute-start | bytes 3080 | tf_op jit(solution)/shard_map/ppermute | solution.py:29
  (90 other events, 807.6 us)

commit v2 on v1

--- a/solution.py
+++ b/solution.py
@@ -61,28 +61,43 @@
 
 class Shards:
     def __init__(self, groups):
-        self.groups = groups
-        self.pieces = [piece for group in groups for piece in group]
-        self.depth = sum(piece.shape[0] for piece in groups[0])
-        self.width = groups[0][0].shape[1]
+        self.pieces, self.groups = [], []
+        for group in groups:
+            made = []
+            for piece in group:
+                array, start, rows = piece if isinstance(piece, tuple) else (piece, 0, piece.shape[0])
+                known = [index for index, other in enumerate(self.pieces) if other is array]
+                if not known:
+                    known = [len(self.pieces)]
+                    self.pieces.append(array)
+                made.append((known[0], start, rows))
+            self.groups.append(made)
+        self.depth = sum(rows for _, _, rows in self.groups[0])
+        self.width = self.pieces[0].shape[1]
 
     def operands(self):
         return [pltpu.with_memory_space_constraint(piece, pltpu.VMEM) for piece in self.pieces]
 
     def block(self, refs, index, part, size):
-        position = sum(len(group) for group in self.groups[:index])
-        found, start = [], 0
-        for offset, piece in enumerate(self.groups[index]):
-            rows = piece.shape[0]
-            low, high = max(part, start), min(part + size, start + rows)
+        found, begin = [], 0
+        for which, start, rows in self.groups[index]:
+            low, high = max(part, begin), min(part + size, begin + rows)
             if low < high:
-                found.append(refs[position + offset][low - start : high - start, :])
-            start += rows
+                found.append(refs[which][start + low - begin : start + high - begin, :])
+            begin += rows
         return found[0] if len(found) == 1 else jnp.concatenate(found, axis=0)
 
-    def columns(self, refs, span):
-        found = [ref[:, span] for ref in refs]
-        return found[0] if len(found) == 1 else jnp.concatenate(found, axis=0)
+    def product(self, x_ref, skip, refs, span):
+        total = None
+        joint = max(1, min(len(self.groups), 4))
+        for index in range(0, len(self.groups), joint):
+            groups = self.groups[index : index + joint]
+            found = [refs[which][start : start + rows, span] for group in groups for which, start, rows in group]
+            block = found[0] if len(found) == 1 else jnp.concatenate(found, axis=0)
+            start = skip + index * self.depth
+            term = dot(x_ref[:, start : start + len(groups) * self.depth], block)
+            total = term if total is None else total + term
+        return total
 
 
 VMEM_SPEC = pl.BlockSpec(memory_space=pltpu.VMEM)
@@ -124,13 +139,12 @@
 def project_call(x, shards, tile, dtype, skip=0):
     rows, width = x.shape[0], shards.width
     count, depth = len(shards.groups), shards.depth
-    span_in = slice(skip, skip + count * depth)
 
     def kernel(x_ref, *refs):
         refs, out_ref = refs[:-1], refs[-1]
 
         def body(span):
-            out_ref[:, span] = dot(x_ref[:, span_in], shards.columns(refs, span)).astype(dtype)
+            out_ref[:, span] = shards.product(x_ref, skip, refs, span).astype(dtype)
 
         tiles(width, tile, body)
 
@@ -187,22 +201,25 @@
     return jnp.where(straight, one, other), jnp.where(straight, other, one)
 
 
-def totals_call(where, x, partial, shards, skip, first_pre, back, bias, tile):
+def totals_call(where, x, partial, shards, skip, first_pre, back, both, block, tile):
     rows, width = first_pre.shape
     pairs = rows // (2 * SEGMENTS)
     count, depth = len(shards.groups), shards.depth
     extra = [] if partial is None else [partial]
 
-    def kernel(where_ref, x_ref, first_ref, back_ref, bias_ref, *refs):
+    def kernel(where_ref, x_ref, first_ref, back_ref, both_ref, *refs):
         partial_refs, refs = refs[: len(extra)], refs[len(extra) :]
-        refs, (second_ref, parts_ref, whole_ref) = refs[:-3], refs[-3:]
+        refs, (second_ref, parts_ref, whole_ref, rows_ref) = refs[:-4], refs[-4:]
+        for index in range(width // block):
+            target = pl.multiple_of((where_ref[0] ^ index) * block, block)
+            rows_ref[:, pl.ds(target, block)] = both_ref[:, index * block : (index + 1) * block]
 
         def body(span):
-            total = dot(x_ref[:, skip : skip + count * depth], shards.columns(refs, span))
+            total = shards.product(x_ref, skip, refs, span)
             for ref in partial_refs:
                 total = total + ref[:, span]
             second_ref[:, span] = total.astype(BF16)
-            bias = bias_ref[:, span]
+            bias = rows_ref[0:1, span]
             keep = jnp.ones((SEGMENTS, tile), F32)
             state = leaving = jnp.zeros((SEGMENTS, tile), F32)
             for pair in range(pairs):
@@ -231,27 +248,28 @@
             jax.ShapeDtypeStruct((rows, width), BF16),
             jax.ShapeDtypeStruct((3, SEGMENTS, width), F32),
             jax.ShapeDtypeStruct((3, width), F32),
+            jax.ShapeDtypeStruct((2, width), F32),
         ],
         in_specs=[SMEM_SPEC] + [VMEM_SPEC] * (4 + len(extra)) + [VMEM_SPEC] * len(shards.pieces),
-        out_specs=[VMEM_SPEC] * 3,
+        out_specs=[VMEM_SPEC] * 4,
         compiler_params=params(14),
         cost_estimate=cost(2 * rows * count * depth * width, 2 * count * depth * width),
         name="project_totals",
-    )(where, x, first_pre, back, bias, *extra, *shards.operands())
-
-
-def scan_call(where, first_pre, second_pre, back, bias, initial, parts, wholes, ranks, tile):
+    )(where, x, first_pre, back, both, *extra, *shards.operands())
+
+
+def scan_call(where, first_pre, second_pre, back, both, parts, wholes, ranks, tile):
     rows, width = first_pre.shape
     pairs = rows // (2 * SEGMENTS)
 
-    def kernel(where_ref, first_ref, second_ref, back_ref, bias_ref, initial_ref, parts_ref, wholes_ref, *refs):
+    def kernel(where_ref, first_ref, second_ref, back_ref, both_ref, parts_ref, wholes_ref, *refs):
         (state_ref, one_ref, other_ref, bias_grad_ref, state_grad_ref) = refs[:5]
         kept, updates, slopes, one_hold, other_hold, state_hold = refs[5:]
         me = where_ref[2]
         order = place_back(rows)
 
         def body(span):
-            entering = initial_ref[:, span]
+            entering = both_ref[1:2, span]
             blocks = [wholes_ref[rank, :, span] for rank in range(ranks)]
             for rank in range(ranks):
                 block = blocks[rank]
@@ -271,7 +289,7 @@
                 tails.append(keep[s : s + 1] * tails[-1] + leaves[s : s + 1])
             state = jnp.concatenate(starts, axis=0)
             leaving = jnp.concatenate(tails[::-1], axis=0)
-            bias = bias_ref[:, span]
+            bias = both_ref[0:1, span]
 
             for pair in range(pairs):
                 states, retains, ups, slope = [], [], [], []
@@ -317,13 +335,13 @@
     return pl.pallas_call(
         kernel,
         out_shape=[wide, tall, tall, flat, flat],
-        in_specs=[SMEM_SPEC] + [VMEM_SPEC] * 7,
+        in_specs=[SMEM_SPEC] + [VMEM_SPEC] * 6,
         out_specs=[VMEM_SPEC] * 5,
         scratch_shapes=[pltpu.VMEM((rows, tile), F32)] * 3 + [pltpu.VMEM((rows, tile), BF16)] * 3,
         compiler_params=params(14),
         cost_estimate=cost(6 * rows * rows * width, 12 * rows * width),
         name="scan_rows",
-    )(where, first_pre, second_pre, back, bias, initial, parts, wholes)
+    )(where, first_pre, second_pre, back, both, parts, wholes)
 
 
 def layer_call(where, state_rows, residual, shards, tile):
@@ -337,7 +355,7 @@
             ordered[:, index * depth : (index + 1) * depth] = x_ref[:, source]
 
         def body(span):
-            total = dot(ordered[...], shards.columns(refs, span))
+            total = shards.product(ordered, 0, refs, span)
             out_ref[:, span] = (residual_ref[:, span].astype(F32) + total).astype(BF16)
 
         tiles(width, tile, body)
@@ -394,9 +412,22 @@
     )(where, one, other, x, grads, gain, *first.operands(), *second.operands())
 
 
-def gathered_rows(gate_bias, state_in):
-    both = lax.all_gather(jnp.stack([gate_bias, state_in[0]]), "seq", axis=1, tiled=True)
-    return both[0:1], both[1:2]
+def close_call(where, state_grad, rows, block):
+    def kernel(where_ref, state_ref, *refs):
+        refs, (state_out_ref, bias_out_ref) = refs[:-2], refs[-2:]
+        here = pl.ds(pl.multiple_of(where_ref[2] * block, block), block)
+        state_out_ref[...] = state_ref[:, here]
+        bias_out_ref[...] = sum((ref[:, here] for ref in refs[1:]), refs[0][:, here])
+
+    return pl.pallas_call(
+        kernel,
+        out_shape=[jax.ShapeDtypeStruct((1, block), F32)] * 2,
+        in_specs=[SMEM_SPEC] + [VMEM_SPEC] * (1 + len(rows)),
+        out_specs=[VMEM_SPEC] * 2,
+        compiler_params=params(2),
+        cost_estimate=cost(1, 4 * state_grad.size),
+        name="close_rows",
+    )(where, state_grad, *rows)
 
 
 def front_on_cube(ranks, batches, where, turned, tile, rows_in, grad_rows, gain, gate_bias, state_in, w_gate, w_cand, w_out):
@@ -407,76 +438,80 @@
     send = lambda value, offset: hop(value, offset, ranks)
     core = lambda value: hop(value, 1, ranks)
     over = lambda value: swap_batch(value, 1, batches)
-    me = lax.axis_index("seq")
-
-    def in_order(value, came, offset):
-        low = (me // offset) % 2 == 0
-        return jnp.where(low, jnp.concatenate([value, came], axis=1), jnp.concatenate([came, value], axis=1))
-
-    own_f = [jnp.where(straight, a, b) for a, b in zip(halves(w_gate), halves(w_cand))]
+    f_a = jnp.where(straight, w_gate[:half], w_cand[:half])
+    f_a, where, w_gate, w_cand, own_t = after((f_a, where, w_gate, w_cand, w_out))
+    own_f = [f_a, jnp.where(straight, w_gate[half:], w_cand[half:])]
     f2a, f4a = send(own_f[0], 2), send(own_f[0], 4)
     f1 = [core(v) for v in own_f]
     both = jnp.stack([gate_bias, state_in[0]])
-    came = core(both)
+    both = jnp.concatenate([both, core(both)], axis=1)
     normed, grads = norm_call(where, rows_in, grad_rows, gain, depth)
-    f2a, f4a, f1a, f1b, came, normed, grads, f_b, own_t, own_s0, own_s1 = after(
-        (f2a, f4a, f1[0], f1[1], came, normed, grads, own_f[1], w_out, w_gate, w_cand)
+    own_s = jnp.where(straight, w_cand, w_gate)
+    t_a, t_b = halves(own_t)
+    f2a, f4a, f1a, f1b, both, normed, grads, f_b, own_s, own_t, t_a, t_b = after(
+        (f2a, f4a, f1[0], f1[1], both, normed, grads, own_f[1], own_s, own_t, t_a, t_b)
     )
     f1 = [f1a, f1b]
-    both = in_order(both, came, 1)
-    t_a, t_b = halves(own_t)
-    came = send(both, 2)
     f2b, f4b = send(f_b, 2), send(f_b, 4)
-    s2a, s4a = over(f2a), over(f4a)
     t2a, t4a = send(t_a, 2), send(t_a, 4)
-    f3a, f5a = core(f2a), core(f4a)
-    own_s = jnp.where(straight, own_s1, own_s0)
-    s1, t1 = core(own_s), core(own_t)
-    came, f2b, f4b, s2a, s4a, t2a, t4a, f3a, f5a, s1, t1, own_s, t_b, f2a, both = after(
-        (came, f2b, f4b, s2a, s4a, t2a, t4a, f3a, f5a, s1, t1, own_s, t_b, f2a, both)
-    )
-    both = in_order(both, came, 2)
-    came = send(both, 4)
+    sa = over(jnp.concatenate([f2a, f4a], axis=0))
+    f2b, f4b, both, f3a, f5a, s1, t1 = after((f2b, f4b, both, f2a, f4a, own_s, own_t))
+    came, f3a, f5a, s1, t1 = send(both, 2), core(f3a), core(f5a), core(s1), core(t1)
+    both = jnp.concatenate([both, came], axis=1)
+    both, f2b, f4b, sa, t2a, t4a, f3a, f5a, s1, t1, t_b, f2a = after(
+        (both, f2b, f4b, sa, t2a, t4a, f3a, f5a, s1, t1, t_b, f2a)
+    )
     f6a, f6b = send(f2a, 4), send(f4b, 2)
-    s2b, s4b = over(f2b), over(f4b)
     t2b, t4b = send(t_b, 2), send(t_b, 4)
-    f3b, f5b, s3a, s5a, t3a, t5a = core(f2b), core(f4b), core(s2a), core(s4a), core(t2a), core(t4a)
-    came, f6a, f6b, s2b, s4b, t2b, t4b, f3b, f5b, s3a, s5a, t3a, t5a, both, t2a = after(
-        (came, f6a, f6b, s2b, s4b, t2b, t4b, f3b, f5b, s3a, s5a, t3a, t5a, both, t2a)
-    )
-    both = in_order(both, came, 4)
-    bias, initial = both[0:1], both[1:2]
-    s6a, s6b = over(f6a), over(f6b)
+    sb = over(jnp.concatenate([f2b, f4b], axis=0))
+    f6a, f6b, both, f3b, f5b, t3a, t5a, ca = after((f6a, f6b, both, f2b, f4b, t2a, t4a, sa))
+    came, f3b, f5b, t3a, t5a, ca = send(both, 4), core(f3b), core(f5b), core(t3a), core(t5a), core(ca)
+    f7a, f7b = core(f6a), core(f6b)
+    both = jnp.concatenate([both, came], axis=1)
+    both, f6a, f6b, f7a, f7b, sb, t2b, t4b, f3b, f5b, t3a, t5a, ca, t2a = after(
+        (both, f6a, f6b, f7a, f7b, sb, t2b, t4b, f3b, f5b, t3a, t5a, ca, t2a)
+    )
     t6a, t6b = send(t2a, 4), send(t4b, 2)
-    f7a, f7b, s3b, s5b, t3b, t5b = core(f6a), core(f6b), core(s2b), core(s4b), core(t2b), core(t4b)
+    s6 = over(jnp.concatenate([f6a, f6b], axis=0))
     first = Shards([own_f, f1, [f2a, f2b], [f3a, f3b], [f4a, f4b], [f5a, f5b], [f6a, f6b], [f7a, f7b]])
-    most = [[own_s], [s1], [s2a, s2b], [s3a, s3b], [s4a, s4b], [s5a, s5b]]
     first_pre = project_call(normed, first, tile, BF16)
-    t6a, t6b, s6a, first_pre, normed, grads = after((t6a, t6b, s6a, first_pre, normed, grads))
-    t7a, t7b, s7a = core(t6a), core(t6b), core(s6a)
+    first_pre, t3b, t5b, cb = after((first_pre, t2b, t4b, sb))
+    t3b, t5b, cb = core(t3b), core(t5b), core(cb)
+    pairs = lambda one, two, row: [(one, row, half), (two, row, half)]
+    most = [
+        [own_s],
+        [s1],
+        pairs(sa, sb, 0),
+        pairs(ca, cb, 0),
+        pairs(sa, sb, half),
+        pairs(ca, cb, half),
+    ]
+    partial = project_call(normed, Shards(most), tile, F32)
+    t6a, t6b, t3b, t5b, partial = after((t6a, t6b, t3b, t5b, partial))
+    t7a, t7b = core(t6a), core(t6b)
     third = Shards([[own_t], [t1], [t2a, t2b], [t3a, t3b], [t4a, t4b], [t5a, t5b], [t6a, t6b], [t7a, t7b]])
-    partial = project_call(normed, Shards(most), tile, F32)
     back = back_call(where, grads, third)
-    s6b, s7a, back, partial = after((s6b, s7a, back, partial))
-    s7b = core(s6b)
-    last = [[s6a, s6b], [s7a, s7b]]
+    s6, back = after((s6, back))
+    last = [[s6], [core(s6)]]
     second = Shards(most + last)
-    second_pre, parts, whole = totals_call(
-        where, normed, partial, Shards(last), len(most) * depth, first_pre, back, bias, tile
-    )
-    return first, second, third, first_pre, second_pre, back, bias, initial, parts, whole
+    second_pre, parts, whole, both = totals_call(
+        where, normed, partial, Shards(last), len(most) * depth, first_pre, back, both, depth, tile
+    )
+    return where, first, second, third, first_pre, second_pre, back, both, parts, whole
 
 
 def front(where, tile, rows_in, grad_rows, gain, gate_bias, state_in, w_gate, w_cand, w_out):
     first, second, third = (
         Shards([[lax.all_gather(w, "seq", tiled=True)]]) for w in (w_gate, w_cand, w_out)
     )
-    bias, initial = gathered_rows(gate_bias, state_in)
+    both = lax.all_gather(jnp.stack([gate_bias, state_in[0]]), "seq", axis=1, tiled=True)
     normed, grads = norm_call(where, rows_in, grad_rows, gain, first.depth)
     first_pre = project_call(normed, first, tile, BF16)
     back = back_call(where, grads, third)
-    second_pre, parts, whole = totals_call(where, normed, None, second, 0, first_pre, back, bias, tile)
-    return first, second, third, first_pre, second_pre, back, bias, initial, parts, whole
+    second_pre, parts, whole, both = totals_call(
+        where, normed, None, second, 0, first_pre, back, both, first.depth, tile
+    )
+    return where, first, second, third, first_pre, second_pre, back, both, parts, whole
 
 
 def on_device(ranks, batches, inputs, output_grad, norm_gain, gate_bias, state_in, w_gate, w_cand, w_out):
@@ -495,28 +530,29 @@
         nought = jnp.zeros_like(me)
         where = jnp.stack([nought, nought, me]).astype(jnp.int32)
         found = front(where, tile, *given)
-    first, second, third, first_pre, second_pre, back, bias, initial, parts, whole = found
+    where, first, second, third, first_pre, second_pre, back, both, parts, whole = found
     wholes = lax.all_gather(whole, "seq")
     state_rows, one, other, bias_part, state_grad = scan_call(
-        where, first_pre, second_pre, back, bias, initial, parts, wholes, ranks, tile
+        where, first_pre, second_pre, back, both, parts, wholes, ranks, tile
     )
     width = hidden // ranks
-    own_width = lambda row: lax.dynamic_slice_in_dim(row, me * width, width, 0)
     if cube:
         pair = bias_part + hop(bias_part, 1, ranks)
+        layer_out = layer_call(where, state_rows, rows_in, third, tile)
         near = [hop(pair, offset, ranks) for offset in (2, 4, 6)]
-        layer_out = layer_call(where, state_rows, rows_in, third, tile)
-        layer_out, *near = after((layer_out,) + tuple(near))
-        plane = own_width((pair + near[0] + near[1] + near[2])[0])
+        layer_out, pair, *near = after((layer_out, pair) + tuple(near))
+        plane = pair + near[0] + near[1] + near[2]
         far = [swap_batch(plane, offset, batches) for offset in range(1, batches)]
-        bias_grad = plane + sum(far[1:], far[0])
         one, other, plane = after((one, other, plane), layer_out)
+        input_grad = input_grad_call(where, one, other, first, second, rows_in, grad_rows, gain)
+        state_out, bias_grad = close_call(where, state_grad, [plane] + far, width)
+        bias_grad = bias_grad[0]
     else:
         over_seq = lax.psum_scatter(bias_part[0], "seq", scatter_dimension=0, tiled=True)
         bias_grad = lax.psum(over_seq, "batch")
         layer_out = layer_call(where, state_rows, rows_in, third, tile)
-    input_grad = input_grad_call(where, one, other, first, second, rows_in, grad_rows, gain)
-    state_out = lax.dynamic_slice_in_dim(state_grad, me * width, width, 1)
+        input_grad = input_grad_call(where, one, other, first, second, rows_in, grad_rows, gain)
+        state_out = lax.dynamic_slice_in_dim(state_grad, me * width, width, 1)
     return (layer_out[None], input_grad[None], state_out, bias_grad)
 
 

time: 197 us -> 157 us (0.80)
  local copies, waits for them, and re-layouts: 28.2 us -> 0.93 us
  Pallas kernels: 40.3 us -> 33.7 us
    unnamed x144 -> x16, local copies, waits for them, and re-layouts: 25.4 us -> 0.86 us
    ppermute x9 -> x6, waiting for transfers between devices: 26.3 us -> 7.48 us  [swap_batch(): return lax.ppermute(value, 'batch', [(i, i ^ offset) for i in range(count)])]
    ppermute x41 -> x38, waiting for transfers between devices: 48.4 us -> 65.8 us  [hop(): return lax.ppermute(value, 'seq', [(i, i ^ offset) for i in range(count)])]
    slice x1, local copies, waits for them, and re-layouts: 2.2 us -> 0.07 us  [front_on_cube(): halves = lambda w: (w[:half], w[half:])]
    pallas_call x2, Pallas kernels: 7.15 us -> 5.15 us  [project_call(): pl.pallas_call(kernel, out_shape=jax.ShapeDtypeStruct((rows, width), dtyp...]
    select_n x5 -> x3, other arithmetic: 4.11 us -> 2.83 us  [the longest x1 1.39 us: front_on_cube(): f_a = jnp.where(straight, w_gate[:half], w_cand[:half])]
    ppermute x9 -> x6, starting transfers between devices: 10.5 us -> 9.38 us  [swap_batch(): return lax.ppermute(value, 'batch', [(i, i ^ offset) for i in range(count)])]
    ppermute x41 -> x38, starting transfers between devices: 26.4 us -> 26.5 us  [hop(): return lax.ppermute(value, 'seq', [(i, i ^ offset) for i in range(count)])]
  transfers between devices with their start and end apart: 50 -> 44, of which waited for: 15 -> 22; matrix products, arithmetic and copies ran while one was open for 2% -> 2% of each run, Pallas kernels for 16% -> 14%
where the time goes in v2:
time: 157 us
  waiting for transfers between devices  73.3 us (47%)
  starting transfers between devices  35.8 us (23%)
  Pallas kernels  33.7 us (21%)
  blocking collectives  8.59 us (5%)
  other arithmetic  3.9 us (2%)
    ppermute x38, waiting for transfers between devices, hop(): return lax.ppermute(value, 'seq', [(i, i ^ offset) for i in range(count)])  65.8 us
    ppermute x38, starting transfers between devices, hop(): return lax.ppermute(value, 'seq', [(i, i ^ offset) for i in range(count)])  26.5 us
    ppermute x6, starting transfers between devices, swap_batch(): return lax.ppermute(value, 'batch', [(i, i ^ offset) for i in range(count)])  9.38 us
    all_gather x1, blocking collectives, on_device(): wholes = lax.all_gather(whole, 'seq')  8.59 us
    pallas_call x1, Pallas kernels, input_grad_call(): pl.pallas_call(kernel, out_shape=jax.ShapeDtypeStruct((rows, width), BF16...  8.35 us
    ppermute x6, waiting for transfers between devices, swap_batch(): return lax.ppermute(value, 'batch', [(i, i ^ offset) for i in range(count)])  7.48 us
    pallas_call x2, Pallas kernels, project_call(): pl.pallas_call(kernel, out_shape=jax.ShapeDtypeStruct((rows, width), dtyp...  5.15 us
    pallas_call x1, Pallas kernels, scan_call(): pl.pallas_call(kernel, out_shape=[wide, tall, tall, flat, flat], in_specs...  4.76 us
  transfers between devices with their start and end apart: 44, of which 22 were waited for; matrix products, arithmetic and copies ran while one was open for 2% of the time, Pallas kernels for 14%

profile of v2, /device:TPU:0, one launch (start us, length us, event | category | flops | bytes accessed | tf_op | source)
XLA Modules:
  0.0 157.1 jit_solution(4823795469996215831)
XLA Ops:
  2.7 2.6 %collective-permute-start.1 = (bf16[128,2048]{1,0:T(8,128)(2,1)S(1)}, bf16[128,2048]{1,0:T(8,128)(2,1)S(1)}, u32[]{:S(2)}, u32[]{:S(2)}) collective-permute-start(bf16[128,2048]{1,0:T(8,128)(2,1)S(1)} %slice_select_fusion.1.refs_0_), channel_id=1, source_target_pairs={{0,16},{4,20},{8,24},{12,28},{16,0},{20,4},{24,8},{28,12},{1,17},{... | collective-permute-start | bytes 1572872 | tf_op jit(solution)/shard_map/ppermute | solution.py:25
  5.2 1.5 collective-permute-start
  10.4 3.3 %norm_rows.1 = (bf16[256,2048]{1,0:T(8,128)(2,1)S(1)}, bf16[2048,256]{1,0:T(8,128)(2,1)S(1)}) custom-call(s32[3]{0:T(128)S(1)} %pad_add_fusion.where_ref, bf16[256,2048]{1,0:T(8,128)(2,1)S(1)} %bitcast.10, bf16[256,2048]{1,0:T(8,128)(2,1)S(1)} %bitcast.13, f32[1,2048]{1,0:T(1,128)S(1)} %bitcast.15), custom_call_target="tpu_custom_call" | custom-call | flops 536870912 | bytes 4194304 | tf_op jit(solution)/shard_map/norm_rows/pallas_call | solution.py:127
  13.8 4.0 %collective-permute-done.1.refs_8_ = bf16[128,2048]{1,0:T(8,128)(2,1)S(1)} collective-permute-done((bf16[128,2048]{1,0:T(8,128)(2,1)S(1)}, bf16[128,2048]{1,0:T(8,128)(2,1)S(1)}, u32[]{:S(2)}, u32[]{:S(2)}) %collective-permute-start.1) | collective-permute-done | bytes 524320 | tf_op jit(solution)/shard_map/ppermute | solution.py:25
  19.5 1.7 %collective-permute-start.5 = (bf16[128,2048]{1,0:T(8,128)(2,1)S(1)}, bf16[128,2048]{1,0:T(8,128)(2,1)S(1)}, u32[]{:S(2)}, u32[]{:S(2)}) collective-permute-start(bf16[128,2048]{1,0:T(8,128)(2,1)S(1)} %slice_select_fusion.refs_1_), channel_id=1, source_target_pairs={{0,8},{4,12},{8,0},{12,4},{16,24},{20,28},{24,16},{28,20},{1,9},{5... | collective-permute-start | bytes 1572872 | tf_op jit(solution)/shard_map/ppermute | solution.py:25
  21.2 1.5 collective-permute-start.10
  23.4 1.6 %collective-permute-start.8 = (bf16[256,2048]{1,0:T(8,128)(2,1)S(1)}, bf16[256,2048]{1,0:T(8,128)(2,1)S(1)}, u32[]{:S(2)}, u32[]{:S(2)}) collective-permute-start(bf16[256,2048]{1,0:T(8,128)(2,1)S(1)} %pad_maximum_fusion), channel_id=1, source_target_pairs={{0,1},{1,0},{2,3},{3,2},{4,5},{5,4},{6,7},{7,6},{8,9},{9,8},{10,11... | collective-permute-start | bytes 3145736 | tf_op jit(solution)/shard_map/ppermute | solution.py:29
  25.0 9.1 %collective-permute-done.6.refs_9_ = bf16[128,2048]{1,0:T(8,128)(2,1)S(1)} collective-permute-done((bf16[128,2048]{1,0:T(8,128)(2,1)S(1)}, bf16[128,2048]{1,0:T(8,128)(2,1)S(1)}, u32[]{:S(2)}, u32[]{:S(2)}) %collective-permute-start.6) | collective-permute-done | bytes 524320 | tf_op jit(solution)/shard_map/ppermute | solution.py:25
  34.9 8.7 %collective-permute-done.10.refs_6_ = bf16[128,2048]{1,0:T(8,128)(2,1)S(1)} collective-permute-done((bf16[128,2048]{1,0:T(8,128)(2,1)S(1)}, bf16[128,2048]{1,0:T(8,128)(2,1)S(1)}, u32[]{:S(2)}, u32[]{:S(2)}) %collective-permute-start.10) | collective-permute-done | bytes 524320 | tf_op jit(solution)/shard_map/ppermute | solution.py:25
  43.6 1.5 collective-permute-start.7
  45.1 2.1 %collective-permute-done.7 = f32[2,512]{1,0:T(2,128)S(1)} collective-permute-done((f32[2,512]{1,0:T(2,128)S(1)}, f32[2,512]{1,0:T(2,128)S(1)}, u32[]{:S(2)}, u32[]{:S(2)}) %collective-permute-start.7) | collective-permute-done | bytes 4128 | tf_op jit(solution)/shard_map/ppermute | solution.py:25
  47.3 1.9 %collective-permute-done.12.refs_10_ = bf16[128,2048]{1,0:T(8,128)(2,1)S(1)} collective-permute-done((bf16[128,2048]{1,0:T(8,128)(2,1)S(1)}, bf16[128,2048]{1,0:T(8,128)(2,1)S(1)}, u32[]{:S(2)}, u32[]{:S(2)}) %collective-permute-start.12) | collective-permute-done | bytes 524320 | tf_op jit(solution)/shard_map/ppermute | solution.py:25
  49.8 1.5 collective-permute-start.16
  51.4 1.6 %collective-permute-start.20 = (bf16[256,2048]{1,0:T(8,128)(2,1)S(1)}, bf16[256,2048]{1,0:T(8,128)(2,1)S(1)}, u32[]{:S(2)}, u32[]{:S(2)}) collective-permute-start(bf16[256,2048]{1,0:T(8,128)(2,1)S(1)} %pad_maximum_fusion.1), channel_id=1, source_target_pairs={{0,1},{1,0},{2,3},{3,2},{4,5},{5,4},{6,7},{7,6},{8,9},{9,8},{10,11... | collective-permute-start | bytes 3145736 | tf_op jit(solution)/shard_map/ppermute | solution.py:29
  55.0 9.0 %collective-permute-done.15.refs_12_ = bf16[128,2048]{1,0:T(8,128)(2,1)S(1)} collective-permute-done((bf16[128,2048]{1,0:T(8,128)(2,1)S(1)}, bf16[128,2048]{1,0:T(8,128)(2,1)S(1)}, u32[]{:S(2)}, u32[]{:S(2)}) %collective-permute-start.15) | collective-permute-done | bytes 524320 | tf_op jit(solution)/shard_map/ppermute | solution.py:25
  65.2 9.3 %collective-permute-done.22.refs_7_ = bf16[128,2048]{1,0:T(8,128)(2,1)S(1)} collective-permute-done((bf16[128,2048]{1,0:T(8,128)(2,1)S(1)}, bf16[128,2048]{1,0:T(8,128)(2,1)S(1)}, u32[]{:S(2)}, u32[]{:S(2)}) %collective-permute-start.22) | collective-permute-done | bytes 524320 | tf_op jit(solution)/shard_map/ppermute | solution.py:25
  76.2 2.2 %collective-permute-done.17 = f32[2,1024]{1,0:T(2,128)S(1)} collective-permute-done((f32[2,1024]{1,0:T(2,128)S(1)}, f32[2,1024]{1,0:T(2,128)S(1)}, u32[]{:S(2)}, u32[]{:S(2)}) %collective-permute-start.17) | collective-permute-done | bytes 8224 | tf_op jit(solution)/shard_map/ppermute | solution.py:25
  82.6 2.9 %project.2.first_ref = bf16[256,2048]{1,0:T(8,128)(2,1)S(1)} custom-call(bf16[256,2048]{1,0:T(8,128)(2,1)S(1)} %get-tuple-element.101.x_ref, bf16[128,2048]{1,0:T(8,128)(2,1)S(1)} %slice_select_fusion.1.refs_0_, bf16[128,2048]{1,0:T(8,128)(2,1)S(1)} %slice_select_fusion.refs_1_, bf16[128,2048]{1,0:T(8,128)(2,1)S(1)} %collective-permute-done.2.refs_2_, ...), custom_call_target="tpu_custom_call" | custom-call | flops 2147483648 | bytes 8388608 | tf_op jit(solution)/shard_map/project/pallas_call | solution.py:151
  85.6 1.5 collective-permute-start.30
  89.2 1.6 %collective-permute-start.28 = (bf16[256,2048]{1,0:T(8,128)(2,1)S(1)}, bf16[256,2048]{1,0:T(8,128)(2,1)S(1)}, u32[]{:S(2)}, u32[]{:S(2)}) collective-permute-start(bf16[256,2048]{1,0:T(8,128)(2,1)S(1)} %pad_maximum_fusion.2), channel_id=1, source_target_pairs={{0,1},{1,0},{2,3},{3,2},{4,5},{5,4},{6,7},{7,6},{8,9},{9,8},{10,11... | collective-permute-start | bytes 3145736 | tf_op jit(solution)/shard_map/ppermute | solution.py:29
  90.8 2.3 %project.3.refs_0_ = f32[256,2048]{1,0:T(8,128)S(1)} custom-call(bf16[256,2048]{1,0:T(8,128)(2,1)S(1)} %get-tuple-element.101.x_ref, bf16[256,2048]{1,0:T(8,128)(2,1)S(1)} %broadcast_select_fusion.refs_0_.refs_16_, bf16[256,2048]{1,0:T(8,128)(2,1)S(1)} %collective-permute-done.13.refs_1_.refs_17_, ...), custom_call_target="tpu_custom_call" | custom-call | flops 1610612736 | bytes 6291456 | tf_op jit(solution)/shard_map/project/pallas_call | solution.py:151
  93.1 7.9 %collective-permute-done.29.refs_10_ = bf16[128,2048]{1,0:T(8,128)(2,1)S(1)} collective-permute-done((bf16[128,2048]{1,0:T(8,128)(2,1)S(1)}, bf16[128,2048]{1,0:T(8,128)(2,1)S(1)}, u32[]{:S(2)}, u32[]{:S(2)}) %collective-permute-start.29) | collective-permute-done | bytes 524320 | tf_op jit(solution)/shard_map/ppermute | solution.py:25
  103.8 3.0 %back_rows.1.back_ref = bf16[256,2048]{1,0:T(8,128)(2,1)S(1)} custom-call(s32[3]{0:T(128)S(1)} %pad_add_fusion.where_ref, bf16[2048,256]{1,0:T(8,128)(2,1)S(1)} %get-tuple-element.147.g_ref, bf16[256,2048]{1,0:T(8,128)(2,1)S(1)} %copy-done.1, bf16[256,2048]{1,0:T(8,128)(2,1)S(1)} %collective-permute-done.14.refs_1_, ...), custom_call_target="tpu_custom_call" | custom-call | flops 2147483648 | bytes 8388608 | tf_op jit(solution)/shard_map/back_rows/pallas_call | solution.py:175
  106.8 7.5 %collective-permute-done.28.refs_1_.refs_22_ = bf16[256,2048]{1,0:T(8,128)(2,1)S(1)} collective-permute-done((bf16[256,2048]{1,0:T(8,128)(2,1)S(1)}, bf16[256,2048]{1,0:T(8,128)(2,1)S(1)}, u32[]{:S(2)}, u32[]{:S(2)}) %collective-permute-start.28) | collective-permute-done | bytes 1048608 | tf_op jit(solution)/shard_map/ppermute | solution.py:29
  114.3 2.7 %collective-permute-done.36.refs_2_.refs_23_ = bf16[256,2048]{1,0:T(8,128)(2,1)S(1)} collective-permute-done((bf16[256,2048]{1,0:T(8,128)(2,1)S(1)}, bf16[256,2048]{1,0:T(8,128)(2,1)S(1)}, u32[]{:S(2)}, u32[]{:S(2)}) %collective-permute-start.36) | collective-permute-done | bytes 1048608 | tf_op jit(solution)/shard_map/ppermute | solution.py:25
  117.0 3.4 %project_totals.1 = (bf16[256,2048]{1,0:T(8,128)(2,1)S(1)}, f32[3,8,2048]{2,1,0:T(8,128)S(1)}, f32[3,2048]{1,0:T(4,128)S(1)}, f32[2,2048]{1,0:T(2,128)S(1)}) custom-call(s32[3]{0:T(128)S(1)} %pad_add_fusion.where_ref, bf16[256,2048]{1,0:T(8,128)(2,1)S(1)} %get-tuple-element.101.x_ref, bf16[256,2048]{1,0:T(8,128)(2,1)S(1)} %project.2.first_ref, ...), custom_call_target="tpu_custom_call" | custom-call | flops 536870912 | bytes 2097152 | tf_op jit(solution)/shard_map/project_totals/pallas_call | solution.py:245
  120.4 8.6 %all-gather.1.wholes_ref = f32[8,3,2048]{2,1,0:T(4,128)S(1)} all-gather(f32[1,3,2048]{2,1,0:T(4,128)S(1)} %bitcast.17), channel_id=2, replica_groups=mesh['seq'=8,'batch'=4] {'seq'}, dimensions={0}, use_global_device_ids=true | all-gather | bytes 221184 | tf_op jit(solution)/shard_map/all_gather | solution.py:534
  129.0 4.8 %scan_rows.1 = (bf16[256,2048]{1,0:T(8,128)(2,1)S(1)}, bf16[2048,256]{1,0:T(8,128)(2,1)S(1)}, bf16[2048,256]{1,0:T(8,128)(2,1)S(1)}, f32[1,2048]{1,0:T(1,128)S(1)}, f32[1,2048]{1,0:T(1,128)S(1)}) custom-call(s32[3]{0:T(128)S(1)} %pad_add_fusion.where_ref, bf16[256,2048]{1,0:T(8,128)(2,1)S(1)} %project.2.first_ref, ...), custom_call_target="tpu_custom_call" | custom-call | flops 805306368 | bytes 6291456 | tf_op jit(solution)/shard_map/scan_rows/pallas_call | solution.py:335
  135.0 1.5 collective-permute-start.40
  138.6 4.6 %layer_rows.1 = bf16[256,2048]{1,0:T(8,128)(2,1)} custom-call(s32[3]{0:T(128)S(1)} %pad_add_fusion.where_ref, bf16[256,2048]{1,0:T(8,128)(2,1)S(1)} %get-tuple-element.169.x_ref, bf16[256,2048]{1,0:T(8,128)(2,1)S(1)} %bitcast.11, bf16[256,2048]{1,0:T(8,128)(2,1)S(1)} %copy-done.1, bf16[256,2048]{1,0:T(8,128)(2,1)S(1)} %collective-permute-done.14.refs_1_, ...), custom_call_target="tpu_custom_call" | custom-call | flops 2147483648 | bytes 8388608 | tf_op jit(solution)/shard_map/layer_rows/pallas_call | solution.py:363
  143.2 3.7 %collective-permute-start.43 = (f32[1,2048]{1,0:T(1,128)S(1)}, f32[1,2048]{1,0:T(1,128)S(1)}, u32[]{:S(2)}, u32[]{:S(2)}) collective-permute-start(f32[1,2048]{1,0:T(1,128)S(1)} %add_add_fusion.refs_0_), channel_id=1, source_target_pairs={{0,3},{1,2},{2,1},{3,0},{4,7},{5,6},{6,5},{7,4},{8,11},{9,10},{10,... | collective-permute-start | bytes 24584 | tf_op jit(solution)/shard_map/ppermute | solution.py:29
  147.6 8.4 %input_grad_rows.1 = bf16[256,2048]{1,0:T(8,128)(2,1)} custom-call(s32[3]{0:T(128)S(1)} %pad_add_fusion.where_ref, bf16[2048,256]{1,0:T(8,128)(2,1)S(1)} %get-tuple-element.178.one_ref, bf16[2048,256]{1,0:T(8,128)(2,1)S(1)} %get-tuple-element.179.other_ref, bf16[256,2048]{1,0:T(8,128)(2,1)S(1)} %bitcast.12, bf16[256,2048]{1,0:T(8,128)(2,1)S(1)} %bitcast.14, ...), custom_call_target="tpu_custom_call" | custom-call | flops 4294967296 | bytes 16777216 | tf_op jit(solution)/shard_map/input_grad_rows/pallas_call | solution.py:403
  (96 shorter events, 28.7 us)
Async XLA Ops:
  2.1 11.6 %collective-permute-start.2 = (bf16[128,2048]{1,0:T(8,128)(2,1)S(1)}, bf16[128,2048]{1,0:T(8,128)(2,1)S(1)}, u32[]{:S(2)}, u32[]{:S(2)}) collective-permute-start(bf16[128,2048]{1,0:T(8,128)(2,1)S(1)} %slice_select_fusion.1.refs_0_), channel_id=1, source_target_pairs={{0,4},{4,0},{8,12},{12,8},{16,20},{20,16},{24,28},{28,24},{1,5},{5... | collective-permute-start | bytes 1572872 | tf_op jit(solution)/shard_map/ppermute | solution.py:25
  2.7 15.1 %collective-permute-start.1 = (bf16[128,2048]{1,0:T(8,128)(2,1)S(1)}, bf16[128,2048]{1,0:T(8,128)(2,1)S(1)}, u32[]{:S(2)}, u32[]{:S(2)}) collective-permute-start(bf16[128,2048]{1,0:T(8,128)(2,1)S(1)} %slice_select_fusion.1.refs_0_), channel_id=1, source_target_pairs={{0,16},{4,20},{8,24},{12,28},{16,0},{20,4},{24,8},{28,12},{1,17},{... | collective-permute-start | bytes 1572872 | tf_op jit(solution)/shard_map/ppermute | solution.py:25
  5.2 14.0 %collective-permute-start = (bf16[128,2048]{1,0:T(8,128)(2,1)S(1)}, bf16[128,2048]{1,0:T(8,128)(2,1)S(1)}, u32[]{:S(2)}, u32[]{:S(2)}) collective-permute-start(bf16[128,2048]{1,0:T(8,128)(2,1)S(1)} %slice_select_fusion.1.refs_0_), channel_id=1, source_target_pairs={{0,8},{4,12},{8,0},{12,4},{16,24},{20,28},{24,16},{28,20},{1,9},{5... | collective-permute-start | bytes 1572872 | tf_op jit(solution)/shard_map/ppermute | solution.py:25
  7.4 6.3 %collective-permute-start.4 = (f32[2,256]{1,0:T(2,128)S(1)}, f32[2,256]{1,0:T(2,128)S(1)}, u32[]{:S(2)}, u32[]{:S(2)}) collective-permute-start(f32[2,256]{1,0:T(2,128)S(1)} %pad_maximum_fusion.6), channel_id=1, source_target_pairs={{0,4},{4,0},{8,12},{12,8},{16,20},{20,16},{24,28},{28,24},{1,5},{5... | collective-permute-start | bytes 6152 | tf_op jit(solution)/shard_map/ppermute | solution.py:25
  8.9 4.9 %collective-permute-start.3 = (bf16[128,2048]{1,0:T(8,128)(2,1)S(1)}, bf16[128,2048]{1,0:T(8,128)(2,1)S(1)}, u32[]{:S(2)}, u32[]{:S(2)}) collective-permute-start(bf16[128,2048]{1,0:T(8,128)(2,1)S(1)} %slice_select_fusion.refs_1_), channel_id=1, source_target_pairs={{0,4},{4,0},{8,12},{12,8},{16,20},{20,16},{24,28},{28,24},{1,5},{5... | collective-permute-start | bytes 1572872 | tf_op jit(solution)/shard_map/ppermute | solution.py:25
  19.2 14.9 %collective-permute-start.6 = (bf16[128,2048]{1,0:T(8,128)(2,1)S(1)}, bf16[128,2048]{1,0:T(8,128)(2,1)S(1)}, u32[]{:S(2)}, u32[]{:S(2)}) collective-permute-start(bf16[128,2048]{1,0:T(8,128)(2,1)S(1)} %slice_select_fusion.refs_1_), channel_id=1, source_target_pairs={{0,16},{4,20},{8,24},{12,28},{16,0},{20,4},{24,8},{28,12},{1,17},{... | collective-permute-start | bytes 1572872 | tf_op jit(solution)/shard_map/ppermute | solution.py:25
  19.5 14.9 %collective-permute-start.5 = (bf16[128,2048]{1,0:T(8,128)(2,1)S(1)}, bf16[128,2048]{1,0:T(8,128)(2,1)S(1)}, u32[]{:S(2)}, u32[]{:S(2)}) collective-permute-start(bf16[128,2048]{1,0:T(8,128)(2,1)S(1)} %slice_select_fusion.refs_1_), channel_id=1, source_target_pairs={{0,8},{4,12},{8,0},{12,4},{16,24},{20,28},{24,16},{28,20},{1,9},{5... | collective-permute-start | bytes 1572872 | tf_op jit(solution)/shard_map/ppermute | solution.py:25
  21.2 22.4 %collective-permute-start.10 = (bf16[128,2048]{1,0:T(8,128)(2,1)S(1)}, bf16[128,2048]{1,0:T(8,128)(2,1)S(1)}, u32[]{:S(2)}, u32[]{:S(2)}) collective-permute-start(bf16[128,2048]{1,0:T(8,128)(2,1)S(1)} %get-tuple-element.113), channel_id=1, source_target_pairs={{0,16},{4,20},{8,24},{12,28},{16,0},{20,4},{24,8},{28,12},{1,17},{... | collective-permute-start | bytes 1572872 | tf_op jit(solution)/shard_map/ppermute | solution.py:25
  22.8 22.4 %collective-permute-start.9 = (bf16[128,2048]{1,0:T(8,128)(2,1)S(1)}, bf16[128,2048]{1,0:T(8,128)(2,1)S(1)}, u32[]{:S(2)}, u32[]{:S(2)}) collective-permute-start(bf16[128,2048]{1,0:T(8,128)(2,1)S(1)} %get-tuple-element.113), channel_id=1, source_target_pairs={{0,8},{4,12},{8,0},{12,4},{16,24},{20,28},{24,16},{28,20},{1,9},{5... | collective-permute-start | bytes 1572872 | tf_op jit(solution)/shard_map/ppermute | solution.py:25
  23.4 25.8 %collective-permute-start.8 = (bf16[256,2048]{1,0:T(8,128)(2,1)S(1)}, bf16[256,2048]{1,0:T(8,128)(2,1)S(1)}, u32[]{:S(2)}, u32[]{:S(2)}) collective-permute-start(bf16[256,2048]{1,0:T(8,128)(2,1)S(1)} %pad_maximum_fusion), channel_id=1, source_target_pairs={{0,1},{1,0},{2,3},{3,2},{4,5},{5,4},{6,7},{7,6},{8,9},{9,8},{10,11... | collective-permute-start | bytes 3145736 | tf_op jit(solution)/shard_map/ppermute | solution.py:29
  34.4 14.8 %collective-permute-start.13 = (bf16[256,2048]{1,0:T(8,128)(2,1)S(1)}, bf16[256,2048]{1,0:T(8,128)(2,1)S(1)}, u32[]{:S(2)}, u32[]{:S(2)}) collective-permute-start(bf16[256,2048]{1,0:T(8,128)(2,1)S(1)} %broadcast_select_fusion.refs_0_.refs_16_), channel_id=1, source_target_pairs={{0,4},{4,0},{8,12},{12,8},{16,20},{20,16},{24,28},{28,24},{1,5},{5... | collective-permute-start | bytes 3145736 | tf_op jit(solution)/shard_map/ppermute | solution.py:25
  34.4 14.8 %collective-permute-start.14 = (bf16[256,2048]{1,0:T(8,128)(2,1)S(1)}, bf16[256,2048]{1,0:T(8,128)(2,1)S(1)}, u32[]{:S(2)}, u32[]{:S(2)}) collective-permute-start(bf16[256,2048]{1,0:T(8,128)(2,1)S(1)} %copy-done.1), channel_id=1, source_target_pairs={{0,4},{4,0},{8,12},{12,8},{16,20},{20,16},{24,28},{28,24},{1,5},{5... | collective-permute-start | bytes 3145736 | tf_op jit(solution)/shard_map/ppermute | solution.py:25
  49.2 14.8 %collective-permute-start.15 = (bf16[128,2048]{1,0:T(8,128)(2,1)S(1)}, bf16[128,2048]{1,0:T(8,128)(2,1)S(1)}, u32[]{:S(2)}, u32[]{:S(2)}) collective-permute-start(bf16[128,2048]{1,0:T(8,128)(2,1)S(1)} %collective-permute-done.refs_4_), channel_id=1, source_target_pairs={{0,16},{4,20},{8,24},{12,28},{16,0},{20,4},{24,8},{28,12},{1,17},{... | collective-permute-start | bytes 1572872 | tf_op jit(solution)/shard_map/ppermute | solution.py:25
  49.8 14.8 %collective-permute-start.16 = (bf16[128,2048]{1,0:T(8,128)(2,1)S(1)}, bf16[128,2048]{1,0:T(8,128)(2,1)S(1)}, u32[]{:S(2)}, u32[]{:S(2)}) collective-permute-start(bf16[128,2048]{1,0:T(8,128)(2,1)S(1)} %collective-permute-done.6.refs_9_), channel_id=1, source_target_pairs={{0,8},{4,12},{8,0},{12,4},{16,24},{20,28},{24,16},{28,20},{1,9},{5... | collective-permute-start | bytes 1572872 | tf_op jit(solution)/shard_map/ppermute | solution.py:25
  51.4 27.0 %collective-permute-start.20 = (bf16[256,2048]{1,0:T(8,128)(2,1)S(1)}, bf16[256,2048]{1,0:T(8,128)(2,1)S(1)}, u32[]{:S(2)}, u32[]{:S(2)}) collective-permute-start(bf16[256,2048]{1,0:T(8,128)(2,1)S(1)} %pad_maximum_fusion.1), channel_id=1, source_target_pairs={{0,1},{1,0},{2,3},{3,2},{4,5},{5,4},{6,7},{7,6},{8,9},{9,8},{10,11... | collective-permute-start | bytes 3145736 | tf_op jit(solution)/shard_map/ppermute | solution.py:29
  53.1 21.4 %collective-permute-start.22 = (bf16[128,2048]{1,0:T(8,128)(2,1)S(1)}, bf16[128,2048]{1,0:T(8,128)(2,1)S(1)}, u32[]{:S(2)}, u32[]{:S(2)}) collective-permute-start(bf16[128,2048]{1,0:T(8,128)(2,1)S(1)} %get-tuple-element.130), channel_id=1, source_target_pairs={{0,16},{4,20},{8,24},{12,28},{16,0},{20,4},{24,8},{28,12},{1,17},{... | collective-permute-start | bytes 1572872 | tf_op jit(solution)/shard_map/ppermute | solution.py:25
  54.5 20.3 %collective-permute-start.21 = (bf16[128,2048]{1,0:T(8,128)(2,1)S(1)}, bf16[128,2048]{1,0:T(8,128)(2,1)S(1)}, u32[]{:S(2)}, u32[]{:S(2)}) collective-permute-start(bf16[128,2048]{1,0:T(8,128)(2,1)S(1)} %get-tuple-element.130), channel_id=1, source_target_pairs={{0,8},{4,12},{8,0},{12,4},{16,24},{20,28},{24,16},{28,20},{1,9},{5... | collective-permute-start | bytes 1572872 | tf_op jit(solution)/shard_map/ppermute | solution.py:25
  64.7 14.3 %collective-permute-start.23 = (bf16[128,2048]{1,0:T(8,128)(2,1)S(1)}, bf16[128,2048]{1,0:T(8,128)(2,1)S(1)}, u32[]{:S(2)}, u32[]{:S(2)}) collective-permute-start(bf16[128,2048]{1,0:T(8,128)(2,1)S(1)} %collective-permute-done.5.refs_5_), channel_id=1, source_target_pairs={{0,4},{4,0},{8,12},{12,8},{16,20},{20,16},{24,28},{28,24},{1,5},{5... | collective-permute-start | bytes 1572872 | tf_op jit(solution)/shard_map/ppermute | solution.py:25
  64.7 14.3 %collective-permute-start.24 = (bf16[128,2048]{1,0:T(8,128)(2,1)S(1)}, bf16[128,2048]{1,0:T(8,128)(2,1)S(1)}, u32[]{:S(2)}, u32[]{:S(2)}) collective-permute-start(bf16[128,2048]{1,0:T(8,128)(2,1)S(1)} %collective-permute-done.6.refs_9_), channel_id=1, source_target_pairs={{0,4},{4,0},{8,12},{12,8},{16,20},{20,16},{24,28},{28,24},{1,5},{5... | collective-permute-start | bytes 1572872 | tf_op jit(solution)/shard_map/ppermute | solution.py:25
  74.4 8.1 %collective-permute-start.27 = (bf16[256,2048]{1,0:T(8,128)(2,1)S(1)}, bf16[256,2048]{1,0:T(8,128)(2,1)S(1)}, u32[]{:S(2)}, u32[]{:S(2)}) collective-permute-start(bf16[256,2048]{1,0:T(8,128)(2,1)S(1)} %collective-permute-done.8.refs_2_.refs_18_), channel_id=1, source_target_pairs={{0,4},{4,0},{8,12},{12,8},{16,20},{20,16},{24,28},{28,24},{1,5},{5... | collective-permute-start | bytes 3145736 | tf_op jit(solution)/shard_map/ppermute | solution.py:25
  85.4 3.7 %collective-permute-start.33 = (bf16[256,2048]{1,0:T(8,128)(2,1)S(1)}, bf16[256,2048]{1,0:T(8,128)(2,1)S(1)}, u32[]{:S(2)}, u32[]{:S(2)}) collective-permute-start(bf16[256,2048]{1,0:T(8,128)(2,1)S(1)} %collective-permute-done.20.refs_3_.refs_19_), channel_id=1, source_target_pairs={{0,4},{4,0},{8,12},{12,8},{16,20},{20,16},{24,28},{28,24},{1,5},{5... | collective-permute-start | bytes 3145736 | tf_op jit(solution)/shard_map/ppermute | solution.py:25
  85.6 15.4 %collective-permute-start.30 = (bf16[128,2048]{1,0:T(8,128)(2,1)S(1)}, bf16[128,2048]{1,0:T(8,128)(2,1)S(1)}, u32[]{:S(2)}, u32[]{:S(2)}) collective-permute-start(bf16[128,2048]{1,0:T(8,128)(2,1)S(1)} %collective-permute-done.22.refs_7_), channel_id=1, source_target_pairs={{0,8},{4,12},{8,0},{12,4},{16,24},{20,28},{24,16},{28,20},{1,9},{5... | collective-permute-start | bytes 1572872 | tf_op jit(solution)/shard_map/ppermute | solution.py:25
  87.1 13.9 %collective-permute-start.29 = (bf16[128,2048]{1,0:T(8,128)(2,1)S(1)}, bf16[128,2048]{1,0:T(8,128)(2,1)S(1)}, u32[]{:S(2)}, u32[]{:S(2)}) collective-permute-start(bf16[128,2048]{1,0:T(8,128)(2,1)S(1)} %collective-permute-done.9.refs_2_), channel_id=1, source_target_pairs={{0,16},{4,20},{8,24},{12,28},{16,0},{20,4},{24,8},{28,12},{1,17},{... | collective-permute-start | bytes 1572872 | tf_op jit(solution)/shard_map/ppermute | solution.py:25
  88.6 12.5 %collective-permute-start.31 = (bf16[128,2048]{1,0:T(8,128)(2,1)S(1)}, bf16[128,2048]{1,0:T(8,128)(2,1)S(1)}, u32[]{:S(2)}, u32[]{:S(2)}) collective-permute-start(bf16[128,2048]{1,0:T(8,128)(2,1)S(1)} %collective-permute-done.21.refs_3_), channel_id=1, source_target_pairs={{0,4},{4,0},{8,12},{12,8},{16,20},{20,16},{24,28},{28,24},{1,5},{5... | collective-permute-start | bytes 1572872 | tf_op jit(solution)/shard_map/ppermute | solution.py:25
  88.6 12.5 %collective-permute-start.32 = (bf16[128,2048]{1,0:T(8,128)(2,1)S(1)}, bf16[128,2048]{1,0:T(8,128)(2,1)S(1)}, u32[]{:S(2)}, u32[]{:S(2)}) collective-permute-start(bf16[128,2048]{1,0:T(8,128)(2,1)S(1)} %collective-permute-done.22.refs_7_), channel_id=1, source_target_pairs={{0,4},{4,0},{8,12},{12,8},{16,20},{20,16},{24,28},{28,24},{1,5},{5... | collective-permute-start | bytes 1572872 | tf_op jit(solution)/shard_map/ppermute | solution.py:25
  89.2 25.1 %collective-permute-start.28 = (bf16[256,2048]{1,0:T(8,128)(2,1)S(1)}, bf16[256,2048]{1,0:T(8,128)(2,1)S(1)}, u32[]{:S(2)}, u32[]{:S(2)}) collective-permute-start(bf16[256,2048]{1,0:T(8,128)(2,1)S(1)} %pad_maximum_fusion.2), channel_id=1, source_target_pairs={{0,1},{1,0},{2,3},{3,2},{4,5},{5,4},{6,7},{7,6},{8,9},{9,8},{10,11... | collective-permute-start | bytes 3145736 | tf_op jit(solution)/shard_map/ppermute | solution.py:29
  135.0 8.1 %collective-permute-start.40 = (f32[1,2048]{1,0:T(1,128)S(1)}, f32[1,2048]{1,0:T(1,128)S(1)}, u32[]{:S(2)}, u32[]{:S(2)}) collective-permute-start(f32[1,2048]{1,0:T(1,128)S(1)} %add.17), channel_id=1, source_target_pairs={{0,24},{4,28},{8,16},{12,20},{16,8},{20,12},{24,0},{28,4},{1,25},{... | collective-permute-start | bytes 24584 | tf_op jit(solution)/shard_map/ppermute | solution.py:25
  136.5 6.6 %collective-permute-start.39 = (f32[1,2048]{1,0:T(1,128)S(1)}, f32[1,2048]{1,0:T(1,128)S(1)}, u32[]{:S(2)}, u32[]{:S(2)}) collective-permute-start(f32[1,2048]{1,0:T(1,128)S(1)} %add.17), channel_id=1, source_target_pairs={{0,16},{4,20},{8,24},{12,28},{16,0},{20,4},{24,8},{28,12},{1,17},{... | collective-permute-start | bytes 24584 | tf_op jit(solution)/shard_map/ppermute | solution.py:25
  138.0 5.2 %collective-permute-start.38 = (f32[1,2048]{1,0:T(1,128)S(1)}, f32[1,2048]{1,0:T(1,128)S(1)}, u32[]{:S(2)}, u32[]{:S(2)}) collective-permute-start(f32[1,2048]{1,0:T(1,128)S(1)} %add.17), channel_id=1, source_target_pairs={{0,8},{4,12},{8,0},{12,4},{16,24},{20,28},{24,16},{28,20},{1,9},{5... | collective-permute-start | bytes 24584 | tf_op jit(solution)/shard_map/ppermute | solution.py:25
  143.2 12.8 %collective-permute-start.43 = (f32[1,2048]{1,0:T(1,128)S(1)}, f32[1,2048]{1,0:T(1,128)S(1)}, u32[]{:S(2)}, u32[]{:S(2)}) collective-permute-start(f32[1,2048]{1,0:T(1,128)S(1)} %add_add_fusion.refs_0_), channel_id=1, source_target_pairs={{0,3},{1,2},{2,1},{3,0},{4,7},{5,6},{6,5},{7,4},{8,11},{9,10},{10,... | collective-permute-start | bytes 24584 | tf_op jit(solution)/shard_map/ppermute | solution.py:29
  146.8 9.2 %collective-permute-start.42 = (f32[1,2048]{1,0:T(1,128)S(1)}, f32[1,2048]{1,0:T(1,128)S(1)}, u32[]{:S(2)}, u32[]{:S(2)}) collective-permute-start(f32[1,2048]{1,0:T(1,128)S(1)} %add_add_fusion.refs_0_), channel_id=1, source_target_pairs={{0,2},{1,3},{2,0},{3,1},{4,6},{5,7},{6,4},{7,5},{8,10},{9,11},{10,... | collective-permute-start | bytes 24584 | tf_op jit(solution)/shard_map/ppermute | solution.py:29
  146.8 9.2 %collective-permute-start.41 = (f32[1,2048]{1,0:T(1,128)S(1)}, f32[1,2048]{1,0:T(1,128)S(1)}, u32[]{:S(2)}, u32[]{:S(2)}) collective-permute-start(f32[1,2048]{1,0:T(1,128)S(1)} %add_add_fusion.refs_0_), channel_id=1, source_target_pairs={{0,1},{1,0},{2,3},{3,2},{4,5},{5,4},{6,7},{7,6},{8,9},{9,8},{10,11... | collective-permute-start | bytes 24584 | tf_op jit(solution)/shard_map/ppermute | solution.py:29
  (20 other events, 63.2 us)

commit v3 on v2

--- a/solution.py
+++ b/solution.py
@@ -100,6 +100,10 @@
         return total
 
 
+def near(value):
+    return pltpu.with_memory_space_constraint(value, pltpu.VMEM)
+
+
 VMEM_SPEC = pl.BlockSpec(memory_space=pltpu.VMEM)
 SMEM_SPEC = pl.BlockSpec(memory_space=pltpu.SMEM)
 
@@ -133,7 +137,7 @@
         compiler_params=params(14),
         cost_estimate=cost(4 * rows * x.size, 8 * x.size),
         name="norm_rows",
-    )(where, x, g, gain)
+    )(where, near(x), near(g), near(gain))
 
 
 def project_call(x, shards, tile, dtype, skip=0):
@@ -156,7 +160,7 @@
         compiler_params=params(14),
         cost_estimate=cost(2 * rows * count * depth * width, 2 * count * depth * width),
         name="project",
-    )(x, *shards.operands())
+    )(near(x), *shards.operands())
 
 
 def back_call(where, grads, shards):
@@ -180,7 +184,7 @@
         compiler_params=params(14),
         cost_estimate=cost(2 * rows * count * depth * width, 2 * count * depth * width),
         name="back_rows",
-    )(where, grads, *shards.operands())
+    )(where, near(grads), *shards.operands())
 
 
 def gates(x):
@@ -255,7 +259,7 @@
         compiler_params=params(14),
         cost_estimate=cost(2 * rows * count * depth * width, 2 * count * depth * width),
         name="project_totals",
-    )(where, x, first_pre, back, both, *extra, *shards.operands())
+    )(where, *map(near, (x, first_pre, back, both, *extra)), *shards.operands())
 
 
 def scan_call(where, first_pre, second_pre, back, both, parts, wholes, ranks, tile):
@@ -341,7 +345,7 @@
         compiler_params=params(14),
         cost_estimate=cost(6 * rows * rows * width, 12 * rows * width),
         name="scan_rows",
-    )(where, first_pre, second_pre, back, both, parts, wholes)
+    )(where, *map(near, (first_pre, second_pre, back, both, parts, wholes)))
 
 
 def layer_call(where, state_rows, residual, shards, tile):
@@ -369,7 +373,7 @@
         compiler_params=params(14),
         cost_estimate=cost(2 * rows * count * depth * width, 2 * count * depth * width),
         name="layer_rows",
-    )(where, state_rows, residual, *shards.operands())
+    )(where, near(state_rows), near(residual), *shards.operands())
 
 
 def input_grad_call(where, one, other, first, second, x, grads, gain):
@@ -409,7 +413,7 @@
         compiler_params=params(14),
         cost_estimate=cost(4 * one.size * width, 4 * hidden * width),
         name="input_grad_rows",
-    )(where, one, other, x, grads, gain, *first.operands(), *second.operands())
+    )(where, *map(near, (one, other, x, grads, gain)), *first.operands(), *second.operands())
 
 
 def close_call(where, state_grad, rows, block):
@@ -441,58 +445,54 @@
     f_a = jnp.where(straight, w_gate[:half], w_cand[:half])
     f_a, where, w_gate, w_cand, own_t = after((f_a, where, w_gate, w_cand, w_out))
     own_f = [f_a, jnp.where(straight, w_gate[half:], w_cand[half:])]
+    stack = lambda *parts: jnp.concatenate(parts, axis=0)
+    cut = lambda held, *starts: [(held, start * half, half) for start in starts]
     f2a, f4a = send(own_f[0], 2), send(own_f[0], 4)
     f1 = [core(v) for v in own_f]
     both = jnp.stack([gate_bias, state_in[0]])
     both = jnp.concatenate([both, core(both)], axis=1)
+    both = jnp.concatenate([both, send(both, 2)], axis=1)
     normed, grads = norm_call(where, rows_in, grad_rows, gain, depth)
     own_s = jnp.where(straight, w_cand, w_gate)
     t_a, t_b = halves(own_t)
     f2a, f4a, f1a, f1b, both, normed, grads, f_b, own_s, own_t, t_a, t_b = after(
         (f2a, f4a, f1[0], f1[1], both, normed, grads, own_f[1], own_s, own_t, t_a, t_b)
     )
-    f1 = [f1a, f1b]
     f2b, f4b = send(f_b, 2), send(f_b, 4)
     t2a, t4a = send(t_a, 2), send(t_a, 4)
-    sa = over(jnp.concatenate([f2a, f4a], axis=0))
-    f2b, f4b, both, f3a, f5a, s1, t1 = after((f2b, f4b, both, f2a, f4a, own_s, own_t))
-    came, f3a, f5a, s1, t1 = send(both, 2), core(f3a), core(f5a), core(s1), core(t1)
-    both = jnp.concatenate([both, came], axis=1)
-    both, f2b, f4b, sa, t2a, t4a, f3a, f5a, s1, t1, t_b, f2a = after(
-        (both, f2b, f4b, sa, t2a, t4a, f3a, f5a, s1, t1, t_b, f2a)
-    )
+    sa = over(stack(f2a, f4a))
+    f2b, f4b, f3a, f5a, s1 = after((f2b, f4b, f2a, f4a, own_s))
+    f3a, f5a, s1 = core(f3a), core(f5a), core(s1)
+    f2b, f4b, sa, t2a, t4a, f3a, f5a, s1, t_b, f2a = after((f2b, f4b, sa, t2a, t4a, f3a, f5a, s1, t_b, f2a))
     f6a, f6b = send(f2a, 4), send(f4b, 2)
     t2b, t4b = send(t_b, 2), send(t_b, 4)
-    sb = over(jnp.concatenate([f2b, f4b], axis=0))
-    f6a, f6b, both, f3b, f5b, t3a, t5a, ca = after((f6a, f6b, both, f2b, f4b, t2a, t4a, sa))
-    came, f3b, f5b, t3a, t5a, ca = send(both, 4), core(f3b), core(f5b), core(t3a), core(t5a), core(ca)
-    f7a, f7b = core(f6a), core(f6b)
-    both = jnp.concatenate([both, came], axis=1)
-    both, f6a, f6b, f7a, f7b, sb, t2b, t4b, f3b, f5b, t3a, t5a, ca, t2a = after(
-        (both, f6a, f6b, f7a, f7b, sb, t2b, t4b, f3b, f5b, t3a, t5a, ca, t2a)
+    sb = over(stack(f2b, f4b))
+    f6a, f6b, f3b, f5b, t3a, t5a, ca = after((f6a, f6b, f2b, f4b, t2a, t4a, sa))
+    f3b, f5b, t3a, t5a, ca = core(f3b), core(f5b), core(t3a), core(t5a), core(ca)
+    both, f6a, f6b, sb, t2b, t4b, f3b, f5b, t3a, t5a, ca, t2a = after(
+        (both, f6a, f6b, sb, t2b, t4b, f3b, f5b, t3a, t5a, ca, t2a)
     )
     t6a, t6b = send(t2a, 4), send(t4b, 2)
-    s6 = over(jnp.concatenate([f6a, f6b], axis=0))
-    first = Shards([own_f, f1, [f2a, f2b], [f3a, f3b], [f4a, f4b], [f5a, f5b], [f6a, f6b], [f7a, f7b]])
+    s6a = over(f6a)
+    f7, cb = core(stack(f6a, f6b)), core(sb)
+    first = Shards([own_f, [f1a, f1b], [f2a, f2b], [f3a, f3b], [f4a, f4b], [f5a, f5b], [f6a, f6b], [f7]])
+    pairs = lambda one, two, row: cut(one, row) + cut(two, row)
+    most = [[own_s], [s1], pairs(sa, sb, 0), pairs(ca, cb, 0), pairs(sa, sb, 1), pairs(ca, cb, 1)]
     first_pre = project_call(normed, first, tile, BF16)
-    first_pre, t3b, t5b, cb = after((first_pre, t2b, t4b, sb))
-    t3b, t5b, cb = core(t3b), core(t5b), core(cb)
-    pairs = lambda one, two, row: [(one, row, half), (two, row, half)]
-    most = [
-        [own_s],
-        [s1],
-        pairs(sa, sb, 0),
-        pairs(ca, cb, 0),
-        pairs(sa, sb, half),
-        pairs(ca, cb, half),
-    ]
     partial = project_call(normed, Shards(most), tile, F32)
-    t6a, t6b, t3b, t5b, partial = after((t6a, t6b, t3b, t5b, partial))
-    t7a, t7b = core(t6a), core(t6b)
-    third = Shards([[own_t], [t1], [t2a, t2b], [t3a, t3b], [t4a, t4b], [t5a, t5b], [t6a, t6b], [t7a, t7b]])
+    t6a, t6b, s6a, f6b, first_pre, partial, own_t, both = after(
+        (t6a, t6b, s6a, f6b, first_pre, partial, own_t, both)
+    )
+    s6b, s7a = over(f6b), core(s6a)
+    c4 = core(stack(t6a, t6b, t2b, t4b, own_t))
+    third = Shards(
+        [[own_t], cut(c4, 4, 5), [t2a, t2b], [t3a, (c4, 2 * half, half)], [t4a, t4b], [t5a, (c4, 3 * half, half)]]
+        + [[t6a, t6b], cut(c4, 0, 1)]
+    )
+    both = jnp.concatenate([both, send(both, 4)], axis=1)
     back = back_call(where, grads, third)
-    s6, back = after((s6, back))
-    last = [[s6], [core(s6)]]
+    s6b, s7a, back, both = after((s6b, s7a, back, both))
+    last = [[s6a, s6b], [s7a, core(s6b)]]
     second = Shards(most + last)
     second_pre, parts, whole, both = totals_call(
         where, normed, partial, Shards(last), len(most) * depth, first_pre, back, both, depth, tile
@@ -539,9 +539,9 @@
     if cube:
         pair = bias_part + hop(bias_part, 1, ranks)
         layer_out = layer_call(where, state_rows, rows_in, third, tile)
-        near = [hop(pair, offset, ranks) for offset in (2, 4, 6)]
-        layer_out, pair, *near = after((layer_out, pair) + tuple(near))
-        plane = pair + near[0] + near[1] + near[2]
+        plane = [hop(pair, offset, ranks) for offset in (2, 4, 6)]
+        layer_out, pair, *plane = after((layer_out, pair) + tuple(plane))
+        plane = pair + plane[0] + plane[1] + plane[2]
         far = [swap_batch(plane, offset, batches) for offset in range(1, batches)]
         one, other, plane = after((one, other, plane), layer_out)
         input_grad = input_grad_call(where, one, other, first, second, rows_in, grad_rows, gain)

time: 157 us -> 152 us (0.968)
  waiting for transfers between devices: 73.3 us -> 69.5 us
    ppermute x38 -> x34, waiting for transfers between devices: 65.8 us -> 61.7 us  [hop(): return lax.ppermute(value, 'seq', [(i, i ^ offset) for i in range(count)])]
    ppermute x38 -> x34, starting transfers between devices: 26.5 us -> 23.6 us  [hop(): return lax.ppermute(value, 'seq', [(i, i ^ offset) for i in range(count)])]
    ppermute x6 -> x7, starting transfers between devices: 9.38 us -> 11 us  [swap_batch(): return lax.ppermute(value, 'batch', [(i, i ^ offset) for i in range(count)])]
    ppermute x6 -> x7, waiting for transfers between devices: 7.48 us -> 7.8 us  [swap_batch(): return lax.ppermute(value, 'batch', [(i, i ^ offset) for i in range(count)])]
  transfers between devices with their start and end apart: 44 -> 41, of which waited for: 22 -> 22; matrix products, arithmetic and copies ran while one was open for 2% -> 1% of each run, Pallas kernels for 14% -> 16%
where the time goes in v3:
time: 152 us
  waiting for transfers between devices  69.5 us (46%)
  starting transfers between devices  34.5 us (23%)
  Pallas kernels  33.7 us (22%)
  blocking collectives  9.5 us (6%)
  other arithmetic  3.15 us (2%)
    ppermute x34, waiting for transfers between devices, hop(): return lax.ppermute(value, 'seq', [(i, i ^ offset) for i in range(count)])  61.7 us
    ppermute x34, starting transfers between devices, hop(): return lax.ppermute(value, 'seq', [(i, i ^ offset) for i in range(count)])  23.6 us
    ppermute x7, starting transfers between devices, swap_batch(): return lax.ppermute(value, 'batch', [(i, i ^ offset) for i in range(count)])  11 us
    all_gather x1, blocking collectives, on_device(): wholes = lax.all_gather(whole, 'seq')  9.5 us
    pallas_call x1, Pallas kernels, input_grad_call(): pl.pallas_call(kernel, out_shape=jax.ShapeDtypeStruct((rows, width), BF16...  8.38 us
    ppermute x7, waiting for transfers between devices, swap_batch(): return lax.ppermute(value, 'batch', [(i, i ^ offset) for i in range(count)])  7.8 us
    pallas_call x2, Pallas kernels, project_call(): pl.pallas_call(kernel, out_shape=jax.ShapeDtypeStruct((rows, width), dtyp...  5.16 us
    pallas_call x1, Pallas kernels, scan_call(): pl.pallas_call(kernel, out_shape=[wide, tall, tall, flat, flat], in_specs...  4.76 us
  transfers between devices with their start and end apart: 41, of which 22 were waited for; matrix products, arithmetic and copies ran while one was open for 1% of the time, Pallas kernels for 16%

profile of v3, /device:TPU:0, one launch (start us, length us, event | category | flops | bytes accessed | tf_op | source)
XLA Modules:
  0.0 151.6 jit_solution(11432956817145533460)
XLA Ops:
  2.2 3.0 %collective-permute-start = (bf16[128,2048]{1,0:T(8,128)(2,1)S(1)}, bf16[128,2048]{1,0:T(8,128)(2,1)S(1)}, u32[]{:S(2)}, u32[]{:S(2)}) collective-permute-start(bf16[128,2048]{1,0:T(8,128)(2,1)S(1)} %slice_select_fusion.1.refs_0_), channel_id=1, source_target_pairs={{0,8},{4,12},{8,0},{12,4},{16,24},{20,28},{24,16},{28,20},{1,9},{5... | collective-permute-start | bytes 1572872 | tf_op jit(solution)/shard_map/ppermute | solution.py:25
  10.7 3.3 %norm_rows.1 = (bf16[256,2048]{1,0:T(8,128)(2,1)S(1)}, bf16[2048,256]{1,0:T(8,128)(2,1)S(1)}) custom-call(s32[3]{0:T(128)S(1)} %pad_add_fusion.where_ref, bf16[256,2048]{1,0:T(8,128)(2,1)S(1)} %bitcast.10, bf16[256,2048]{1,0:T(8,128)(2,1)S(1)} %bitcast.13, f32[1,2048]{1,0:T(1,128)S(1)} %bitcast.15), custom_call_target="tpu_custom_call" | custom-call | flops 536870912 | bytes 4194304 | tf_op jit(solution)/shard_map/norm_rows/pallas_call | solution.py:131
  13.9 3.3 %collective-permute-done.5 = f32[2,512]{1,0:T(2,128)S(1)} collective-permute-done((f32[2,512]{1,0:T(2,128)S(1)}, f32[2,512]{1,0:T(2,128)S(1)}, u32[]{:S(2)}, u32[]{:S(2)}) %collective-permute-start.5) | collective-permute-done | bytes 4128 | tf_op jit(solution)/shard_map/ppermute | solution.py:25
  19.1 1.6 %collective-permute-start.7 = (bf16[128,2048]{1,0:T(8,128)(2,1)S(1)}, bf16[128,2048]{1,0:T(8,128)(2,1)S(1)}, u32[]{:S(2)}, u32[]{:S(2)}) collective-permute-start(bf16[128,2048]{1,0:T(8,128)(2,1)S(1)} %slice_select_fusion.refs_1_), channel_id=1, source_target_pairs={{0,16},{4,20},{8,24},{12,28},{16,0},{20,4},{24,8},{28,12},{1,17},{... | collective-permute-start | bytes 1572872 | tf_op jit(solution)/shard_map/ppermute | solution.py:25
  20.8 1.6 %collective-permute-start.8 = (bf16[256,2048]{1,0:T(8,128)(2,1)S(1)}, bf16[256,2048]{1,0:T(8,128)(2,1)S(1)}, u32[]{:S(2)}, u32[]{:S(2)}) collective-permute-start(bf16[256,2048]{1,0:T(8,128)(2,1)S(1)} %pad_maximum_fusion), channel_id=1, source_target_pairs={{0,1},{1,0},{2,3},{3,2},{4,5},{5,4},{6,7},{7,6},{8,9},{9,8},{10,11... | collective-permute-start | bytes 3145736 | tf_op jit(solution)/shard_map/ppermute | solution.py:29
  22.9 8.2 %collective-permute-done.6.refs_5_ = bf16[128,2048]{1,0:T(8,128)(2,1)S(1)} collective-permute-done((bf16[128,2048]{1,0:T(8,128)(2,1)S(1)}, bf16[128,2048]{1,0:T(8,128)(2,1)S(1)}, u32[]{:S(2)}, u32[]{:S(2)}) %collective-permute-start.6) | collective-permute-done | bytes 524320 | tf_op jit(solution)/shard_map/ppermute | solution.py:25
  31.1 2.9 %collective-permute-done.7.refs_9_ = bf16[128,2048]{1,0:T(8,128)(2,1)S(1)} collective-permute-done((bf16[128,2048]{1,0:T(8,128)(2,1)S(1)}, bf16[128,2048]{1,0:T(8,128)(2,1)S(1)}, u32[]{:S(2)}, u32[]{:S(2)}) %collective-permute-start.7) | collective-permute-done | bytes 524320 | tf_op jit(solution)/shard_map/ppermute | solution.py:25
  34.0 1.5 %collective-permute-start.9 = (bf16[128,2048]{1,0:T(8,128)(2,1)S(1)}, bf16[128,2048]{1,0:T(8,128)(2,1)S(1)}, u32[]{:S(2)}, u32[]{:S(2)}) collective-permute-start(bf16[128,2048]{1,0:T(8,128)(2,1)S(1)} %get-tuple-element.102), channel_id=1, source_target_pairs={{0,8},{4,12},{8,0},{12,4},{16,24},{20,28},{24,16},{28,20},{1,9},{5... | collective-permute-start | bytes 1572872 | tf_op jit(solution)/shard_map/ppermute | solution.py:25
  35.7 7.1 %collective-permute-done.10.refs_5_ = bf16[128,2048]{1,0:T(8,128)(2,1)S(1)} collective-permute-done((bf16[128,2048]{1,0:T(8,128)(2,1)S(1)}, bf16[128,2048]{1,0:T(8,128)(2,1)S(1)}, u32[]{:S(2)}, u32[]{:S(2)}) %collective-permute-start.10) | collective-permute-done | bytes 524320 | tf_op jit(solution)/shard_map/ppermute | solution.py:25
  42.8 5.4 %collective-permute-done.9.refs_2_ = bf16[128,2048]{1,0:T(8,128)(2,1)S(1)} collective-permute-done((bf16[128,2048]{1,0:T(8,128)(2,1)S(1)}, bf16[128,2048]{1,0:T(8,128)(2,1)S(1)}, u32[]{:S(2)}, u32[]{:S(2)}) %collective-permute-start.9) | collective-permute-done | bytes 524320 | tf_op jit(solution)/shard_map/ppermute | solution.py:25
  48.3 1.6 %collective-permute-start.14 = (bf16[128,2048]{1,0:T(8,128)(2,1)S(1)}, bf16[128,2048]{1,0:T(8,128)(2,1)S(1)}, u32[]{:S(2)}, u32[]{:S(2)}) collective-permute-start(bf16[128,2048]{1,0:T(8,128)(2,1)S(1)} %collective-permute-done.refs_4_), channel_id=1, source_target_pairs={{0,16},{4,20},{8,24},{12,28},{16,0},{20,4},{24,8},{28,12},{1,17},{... | collective-permute-start | bytes 1572872 | tf_op jit(solution)/shard_map/ppermute | solution.py:25
  51.5 1.6 %collective-permute-start.16 = (bf16[256,2048]{1,0:T(8,128)(2,1)S(1)}, bf16[256,2048]{1,0:T(8,128)(2,1)S(1)}, u32[]{:S(2)}, u32[]{:S(2)}) collective-permute-start(bf16[256,2048]{1,0:T(8,128)(2,1)S(1)} %pad_maximum_fusion.1), channel_id=1, source_target_pairs={{0,1},{1,0},{2,3},{3,2},{4,5},{5,4},{6,7},{7,6},{8,9},{9,8},{10,11... | collective-permute-start | bytes 3145736 | tf_op jit(solution)/shard_map/ppermute | solution.py:29
  54.2 9.0 %collective-permute-done.14.refs_12_ = bf16[128,2048]{1,0:T(8,128)(2,1)S(1)} collective-permute-done((bf16[128,2048]{1,0:T(8,128)(2,1)S(1)}, bf16[128,2048]{1,0:T(8,128)(2,1)S(1)}, u32[]{:S(2)}, u32[]{:S(2)}) %collective-permute-start.14) | collective-permute-done | bytes 524320 | tf_op jit(solution)/shard_map/ppermute | solution.py:25
  63.2 1.6 %collective-permute-done.15.refs_13_ = bf16[128,2048]{1,0:T(8,128)(2,1)S(1)} collective-permute-done((bf16[128,2048]{1,0:T(8,128)(2,1)S(1)}, bf16[128,2048]{1,0:T(8,128)(2,1)S(1)}, u32[]{:S(2)}, u32[]{:S(2)}) %collective-permute-start.15) | collective-permute-done | bytes 524320 | tf_op jit(solution)/shard_map/ppermute | solution.py:25
  65.3 9.1 %collective-permute-done.17.refs_3_ = bf16[128,2048]{1,0:T(8,128)(2,1)S(1)} collective-permute-done((bf16[128,2048]{1,0:T(8,128)(2,1)S(1)}, bf16[128,2048]{1,0:T(8,128)(2,1)S(1)}, u32[]{:S(2)}, u32[]{:S(2)}) %collective-permute-start.17) | collective-permute-done | bytes 524320 | tf_op jit(solution)/shard_map/ppermute | solution.py:25
  79.0 1.5 %collective-permute-start.25 = (bf16[128,2048]{1,0:T(8,128)(2,1)S(1)}, bf16[128,2048]{1,0:T(8,128)(2,1)S(1)}, u32[]{:S(2)}, u32[]{:S(2)}) collective-permute-start(bf16[128,2048]{1,0:T(8,128)(2,1)S(1)} %collective-permute-done.18.refs_6_), channel_id=1, source_target_pairs={{0,8},{4,12},{8,0},{12,4},{16,24},{20,28},{24,16},{28,20},{1,9},{5... | collective-permute-start | bytes 1572872 | tf_op jit(solution)/shard_map/ppermute | solution.py:25
  80.5 1.6 %collective-permute-start.26 = (bf16[128,2048]{1,0:T(8,128)(2,1)S(1)}, bf16[128,2048]{1,0:T(8,128)(2,1)S(1)}, u32[]{:S(2)}, u32[]{:S(2)}) collective-permute-start(bf16[128,2048]{1,0:T(8,128)(2,1)S(1)} %collective-permute-done.14.refs_12_), channel_id=1, source_target_pairs={{0,1},{1,0},{2,3},{3,2},{4,5},{5,4},{6,7},{7,6},{8,9},{9,8},{10,11... | collective-permute-start | bytes 1572872 | tf_op jit(solution)/shard_map/ppermute | solution.py:29
  82.1 2.3 %project.3.refs_0_ = f32[256,2048]{1,0:T(8,128)S(1)} custom-call(bf16[256,2048]{1,0:T(8,128)(2,1)S(1)} %get-tuple-element.125.x_ref, bf16[256,2048]{1,0:T(8,128)(2,1)S(1)} %broadcast_select_fusion.refs_0_.refs_15_, bf16[256,2048]{1,0:T(8,128)(2,1)S(1)} %collective-permute-done.13.refs_1_.refs_16_, ...), custom_call_target="tpu_custom_call" | custom-call | flops 1610612736 | bytes 6291456 | tf_op jit(solution)/shard_map/project/pallas_call | solution.py:155
  84.4 2.9 %project.2.first_ref = bf16[256,2048]{1,0:T(8,128)(2,1)S(1)} custom-call(bf16[256,2048]{1,0:T(8,128)(2,1)S(1)} %get-tuple-element.125.x_ref, bf16[128,2048]{1,0:T(8,128)(2,1)S(1)} %slice_select_fusion.1.refs_0_, bf16[128,2048]{1,0:T(8,128)(2,1)S(1)} %slice_select_fusion.refs_1_, bf16[128,2048]{1,0:T(8,128)(2,1)S(1)} %collective-permute-done.2.refs_2_, ...), custom_call_target="tpu_custom_call" | custom-call | flops 2147483648 | bytes 8388608 | tf_op jit(solution)/shard_map/project/pallas_call | solution.py:155
  87.3 5.2 %collective-permute-done.24.refs_8_ = bf16[128,2048]{1,0:T(8,128)(2,1)S(1)} collective-permute-done((bf16[128,2048]{1,0:T(8,128)(2,1)S(1)}, bf16[128,2048]{1,0:T(8,128)(2,1)S(1)}, u32[]{:S(2)}, u32[]{:S(2)}) %collective-permute-start.24) | collective-permute-done | bytes 524320 | tf_op jit(solution)/shard_map/ppermute | solution.py:25
  94.3 1.6 %collective-permute-start.29 = (bf16[128,2048]{1,0:T(8,128)(2,1)S(1)}, bf16[128,2048]{1,0:T(8,128)(2,1)S(1)}, u32[]{:S(2)}, u32[]{:S(2)}) collective-permute-start(bf16[128,2048]{1,0:T(8,128)(2,1)S(1)} %collective-permute-done.15.refs_13_), channel_id=1, source_target_pairs={{0,1},{1,0},{2,3},{3,2},{4,5},{5,4},{6,7},{7,6},{8,9},{9,8},{10,11... | collective-permute-start | bytes 1572872 | tf_op jit(solution)/shard_map/ppermute | solution.py:29
  97.6 2.1 %collective-permute-done.32 = f32[2,1024]{1,0:T(2,128)S(1)} collective-permute-done((f32[2,1024]{1,0:T(2,128)S(1)}, f32[2,1024]{1,0:T(2,128)S(1)}, u32[]{:S(2)}, u32[]{:S(2)}) %collective-permute-start.32) | collective-permute-done | bytes 8224 | tf_op jit(solution)/shard_map/ppermute | solution.py:25
  99.9 3.0 %back_rows.1.back_ref = bf16[256,2048]{1,0:T(8,128)(2,1)S(1)} custom-call(s32[3]{0:T(128)S(1)} %pad_add_fusion.where_ref, bf16[2048,256]{1,0:T(8,128)(2,1)S(1)} %get-tuple-element.140.g_ref, bf16[256,2048]{1,0:T(8,128)(2,1)S(1)} %copy-done, bf16[768,2048]{1,0:T(8,128)(2,1)S(1)} %collective-permute-done.31.refs_1_, ...), custom_call_target="tpu_custom_call" | custom-call | flops 2147483648 | bytes 8388608 | tf_op jit(solution)/shard_map/back_rows/pallas_call | solution.py:179
  102.9 5.7 %collective-permute-done.29.refs_2_.refs_22_ = bf16[128,2048]{1,0:T(8,128)(2,1)S(1)} collective-permute-done((bf16[128,2048]{1,0:T(8,128)(2,1)S(1)}, bf16[128,2048]{1,0:T(8,128)(2,1)S(1)}, u32[]{:S(2)}, u32[]{:S(2)}) %collective-permute-start.29) | collective-permute-done | bytes 524320 | tf_op jit(solution)/shard_map/ppermute | solution.py:29
  108.6 1.9 %collective-permute-done.33.refs_4_.refs_24_ = bf16[128,2048]{1,0:T(8,128)(2,1)S(1)} collective-permute-done((bf16[128,2048]{1,0:T(8,128)(2,1)S(1)}, bf16[128,2048]{1,0:T(8,128)(2,1)S(1)}, u32[]{:S(2)}, u32[]{:S(2)}) %collective-permute-start.33) | collective-permute-done | bytes 524320 | tf_op jit(solution)/shard_map/ppermute | solution.py:25
  110.5 3.4 %project_totals.1 = (bf16[256,2048]{1,0:T(8,128)(2,1)S(1)}, f32[3,8,2048]{2,1,0:T(8,128)S(1)}, f32[3,2048]{1,0:T(4,128)S(1)}, f32[2,2048]{1,0:T(2,128)S(1)}) custom-call(s32[3]{0:T(128)S(1)} %pad_add_fusion.where_ref, bf16[256,2048]{1,0:T(8,128)(2,1)S(1)} %get-tuple-element.125.x_ref, bf16[256,2048]{1,0:T(8,128)(2,1)S(1)} %project.2.first_ref, ...), custom_call_target="tpu_custom_call" | custom-call | flops 536870912 | bytes 2097152 | tf_op jit(solution)/shard_map/project_totals/pallas_call | solution.py:249
  114.0 9.5 %all-gather.1.wholes_ref = f32[8,3,2048]{2,1,0:T(4,128)S(1)} all-gather(f32[1,3,2048]{2,1,0:T(4,128)S(1)} %bitcast.17), channel_id=2, replica_groups=mesh['seq'=8,'batch'=4] {'seq'}, dimensions={0}, use_global_device_ids=true | all-gather | bytes 221184 | tf_op jit(solution)/shard_map/all_gather | solution.py:534
  123.5 4.8 %scan_rows.1 = (bf16[256,2048]{1,0:T(8,128)(2,1)S(1)}, bf16[2048,256]{1,0:T(8,128)(2,1)S(1)}, bf16[2048,256]{1,0:T(8,128)(2,1)S(1)}, f32[1,2048]{1,0:T(1,128)S(1)}, f32[1,2048]{1,0:T(1,128)S(1)}) custom-call(s32[3]{0:T(128)S(1)} %pad_add_fusion.where_ref, bf16[256,2048]{1,0:T(8,128)(2,1)S(1)} %project.2.first_ref, ...), custom_call_target="tpu_custom_call" | custom-call | flops 805306368 | bytes 6291456 | tf_op jit(solution)/shard_map/scan_rows/pallas_call | solution.py:339
  133.0 4.5 %layer_rows.1 = bf16[256,2048]{1,0:T(8,128)(2,1)} custom-call(s32[3]{0:T(128)S(1)} %pad_add_fusion.where_ref, bf16[256,2048]{1,0:T(8,128)(2,1)S(1)} %get-tuple-element.157.x_ref, bf16[256,2048]{1,0:T(8,128)(2,1)S(1)} %bitcast.11, bf16[256,2048]{1,0:T(8,128)(2,1)S(1)} %copy-done, bf16[768,2048]{1,0:T(8,128)(2,1)S(1)} %collective-permute-done.31.refs_1_, ...), custom_call_target="tpu_custom_call" | custom-call | flops 2147483648 | bytes 8388608 | tf_op jit(solution)/shard_map/layer_rows/pallas_call | solution.py:367
  137.6 1.6 %collective-permute-start.38 = (f32[1,2048]{1,0:T(1,128)S(1)}, f32[1,2048]{1,0:T(1,128)S(1)}, u32[]{:S(2)}, u32[]{:S(2)}) collective-permute-start(f32[1,2048]{1,0:T(1,128)S(1)} %add_add_fusion.refs_0_), channel_id=1, source_target_pairs={{0,1},{1,0},{2,3},{3,2},{4,5},{5,4},{6,7},{7,6},{8,9},{9,8},{10,11... | collective-permute-start | bytes 24584 | tf_op jit(solution)/shard_map/ppermute | solution.py:29
  139.3 2.6 %collective-permute-start.39 = (f32[1,2048]{1,0:T(1,128)S(1)}, f32[1,2048]{1,0:T(1,128)S(1)}, u32[]{:S(2)}, u32[]{:S(2)}) collective-permute-start(f32[1,2048]{1,0:T(1,128)S(1)} %add_add_fusion.refs_0_), channel_id=1, source_target_pairs={{0,2},{1,3},{2,0},{3,1},{4,6},{5,7},{6,4},{7,5},{8,10},{9,11},{10,... | collective-permute-start | bytes 24584 | tf_op jit(solution)/shard_map/ppermute | solution.py:29
  142.1 8.4 %input_grad_rows.1 = bf16[256,2048]{1,0:T(8,128)(2,1)} custom-call(s32[3]{0:T(128)S(1)} %pad_add_fusion.where_ref, bf16[2048,256]{1,0:T(8,128)(2,1)S(1)} %get-tuple-element.166.one_ref, bf16[2048,256]{1,0:T(8,128)(2,1)S(1)} %get-tuple-element.167.other_ref, bf16[256,2048]{1,0:T(8,128)(2,1)S(1)} %bitcast.12, bf16[256,2048]{1,0:T(8,128)(2,1)S(1)} %bitcast.14, ...), custom_call_target="tpu_custom_call" | custom-call | flops 4294967296 | bytes 16777216 | tf_op jit(solution)/shard_map/input_grad_rows/pallas_call | solution.py:407
  (95 shorter events, 27.0 us)
Async XLA Ops:
  2.2 15.0 %collective-permute-start = (bf16[128,2048]{1,0:T(8,128)(2,1)S(1)}, bf16[128,2048]{1,0:T(8,128)(2,1)S(1)}, u32[]{:S(2)}, u32[]{:S(2)}) collective-permute-start(bf16[128,2048]{1,0:T(8,128)(2,1)S(1)} %slice_select_fusion.1.refs_0_), channel_id=1, source_target_pairs={{0,8},{4,12},{8,0},{12,4},{16,24},{20,28},{24,16},{28,20},{1,9},{5... | collective-permute-start | bytes 1572872 | tf_op jit(solution)/shard_map/ppermute | solution.py:25
  5.2 13.4 %collective-permute-start.1 = (bf16[128,2048]{1,0:T(8,128)(2,1)S(1)}, bf16[128,2048]{1,0:T(8,128)(2,1)S(1)}, u32[]{:S(2)}, u32[]{:S(2)}) collective-permute-start(bf16[128,2048]{1,0:T(8,128)(2,1)S(1)} %slice_select_fusion.1.refs_0_), channel_id=1, source_target_pairs={{0,16},{4,20},{8,24},{12,28},{16,0},{20,4},{24,8},{28,12},{1,17},{... | collective-permute-start | bytes 1572872 | tf_op jit(solution)/shard_map/ppermute | solution.py:25
  6.7 11.9 %collective-permute-start.2 = (bf16[128,2048]{1,0:T(8,128)(2,1)S(1)}, bf16[128,2048]{1,0:T(8,128)(2,1)S(1)}, u32[]{:S(2)}, u32[]{:S(2)}) collective-permute-start(bf16[128,2048]{1,0:T(8,128)(2,1)S(1)} %slice_select_fusion.1.refs_0_), channel_id=1, source_target_pairs={{0,4},{4,0},{8,12},{12,8},{16,20},{20,16},{24,28},{28,24},{1,5},{5... | collective-permute-start | bytes 1572872 | tf_op jit(solution)/shard_map/ppermute | solution.py:25
  8.0 9.2 %collective-permute-start.3 = (bf16[128,2048]{1,0:T(8,128)(2,1)S(1)}, bf16[128,2048]{1,0:T(8,128)(2,1)S(1)}, u32[]{:S(2)}, u32[]{:S(2)}) collective-permute-start(bf16[128,2048]{1,0:T(8,128)(2,1)S(1)} %slice_select_fusion.refs_1_), channel_id=1, source_target_pairs={{0,4},{4,0},{8,12},{12,8},{16,20},{20,16},{24,28},{28,24},{1,5},{5... | collective-permute-start | bytes 1572872 | tf_op jit(solution)/shard_map/ppermute | solution.py:25
  10.1 7.1 %collective-permute-start.5 = (f32[2,512]{1,0:T(2,128)S(1)}, f32[2,512]{1,0:T(2,128)S(1)}, u32[]{:S(2)}, u32[]{:S(2)}) collective-permute-start(f32[2,512]{1,0:T(2,128)S(1)} %pad_maximum_fusion.5), channel_id=1, source_target_pairs={{0,8},{4,12},{8,0},{12,4},{16,24},{20,28},{24,16},{28,20},{1,9},{5... | collective-permute-start | bytes 12296 | tf_op jit(solution)/shard_map/ppermute | solution.py:25
  18.6 12.5 %collective-permute-start.6 = (bf16[128,2048]{1,0:T(8,128)(2,1)S(1)}, bf16[128,2048]{1,0:T(8,128)(2,1)S(1)}, u32[]{:S(2)}, u32[]{:S(2)}) collective-permute-start(bf16[128,2048]{1,0:T(8,128)(2,1)S(1)} %slice_select_fusion.refs_1_), channel_id=1, source_target_pairs={{0,8},{4,12},{8,0},{12,4},{16,24},{20,28},{24,16},{28,20},{1,9},{5... | collective-permute-start | bytes 1572872 | tf_op jit(solution)/shard_map/ppermute | solution.py:25
  19.1 14.9 %collective-permute-start.7 = (bf16[128,2048]{1,0:T(8,128)(2,1)S(1)}, bf16[128,2048]{1,0:T(8,128)(2,1)S(1)}, u32[]{:S(2)}, u32[]{:S(2)}) collective-permute-start(bf16[128,2048]{1,0:T(8,128)(2,1)S(1)} %slice_select_fusion.refs_1_), channel_id=1, source_target_pairs={{0,16},{4,20},{8,24},{12,28},{16,0},{20,4},{24,8},{28,12},{1,17},{... | collective-permute-start | bytes 1572872 | tf_op jit(solution)/shard_map/ppermute | solution.py:25
  20.8 27.5 %collective-permute-start.8 = (bf16[256,2048]{1,0:T(8,128)(2,1)S(1)}, bf16[256,2048]{1,0:T(8,128)(2,1)S(1)}, u32[]{:S(2)}, u32[]{:S(2)}) collective-permute-start(bf16[256,2048]{1,0:T(8,128)(2,1)S(1)} %pad_maximum_fusion), channel_id=1, source_target_pairs={{0,1},{1,0},{2,3},{3,2},{4,5},{5,4},{6,7},{7,6},{8,9},{9,8},{10,11... | collective-permute-start | bytes 3145736 | tf_op jit(solution)/shard_map/ppermute | solution.py:29
  22.4 20.4 %collective-permute-start.10 = (bf16[128,2048]{1,0:T(8,128)(2,1)S(1)}, bf16[128,2048]{1,0:T(8,128)(2,1)S(1)}, u32[]{:S(2)}, u32[]{:S(2)}) collective-permute-start(bf16[128,2048]{1,0:T(8,128)(2,1)S(1)} %get-tuple-element.102), channel_id=1, source_target_pairs={{0,16},{4,20},{8,24},{12,28},{16,0},{20,4},{24,8},{28,12},{1,17},{... | collective-permute-start | bytes 1572872 | tf_op jit(solution)/shard_map/ppermute | solution.py:25
  34.0 14.4 %collective-permute-start.13 = (bf16[256,2048]{1,0:T(8,128)(2,1)S(1)}, bf16[256,2048]{1,0:T(8,128)(2,1)S(1)}, u32[]{:S(2)}, u32[]{:S(2)}) collective-permute-start(bf16[256,2048]{1,0:T(8,128)(2,1)S(1)} %broadcast_select_fusion.refs_0_.refs_15_), channel_id=1, source_target_pairs={{0,4},{4,0},{8,12},{12,8},{16,20},{20,16},{24,28},{28,24},{1,5},{5... | collective-permute-start | bytes 3145736 | tf_op jit(solution)/shard_map/ppermute | solution.py:25
  34.0 14.3 %collective-permute-start.9 = (bf16[128,2048]{1,0:T(8,128)(2,1)S(1)}, bf16[128,2048]{1,0:T(8,128)(2,1)S(1)}, u32[]{:S(2)}, u32[]{:S(2)}) collective-permute-start(bf16[128,2048]{1,0:T(8,128)(2,1)S(1)} %get-tuple-element.102), channel_id=1, source_target_pairs={{0,8},{4,12},{8,0},{12,4},{16,24},{20,28},{24,16},{28,20},{1,9},{5... | collective-permute-start | bytes 1572872 | tf_op jit(solution)/shard_map/ppermute | solution.py:25
  35.5 12.8 %collective-permute-start.11 = (bf16[128,2048]{1,0:T(8,128)(2,1)S(1)}, bf16[128,2048]{1,0:T(8,128)(2,1)S(1)}, u32[]{:S(2)}, u32[]{:S(2)}) collective-permute-start(bf16[128,2048]{1,0:T(8,128)(2,1)S(1)} %collective-permute-done.refs_4_), channel_id=1, source_target_pairs={{0,4},{4,0},{8,12},{12,8},{16,20},{20,16},{24,28},{28,24},{1,5},{5... | collective-permute-start | bytes 1572872 | tf_op jit(solution)/shard_map/ppermute | solution.py:25
  48.3 14.9 %collective-permute-start.14 = (bf16[128,2048]{1,0:T(8,128)(2,1)S(1)}, bf16[128,2048]{1,0:T(8,128)(2,1)S(1)}, u32[]{:S(2)}, u32[]{:S(2)}) collective-permute-start(bf16[128,2048]{1,0:T(8,128)(2,1)S(1)} %collective-permute-done.refs_4_), channel_id=1, source_target_pairs={{0,16},{4,20},{8,24},{12,28},{16,0},{20,4},{24,8},{28,12},{1,17},{... | collective-permute-start | bytes 1572872 | tf_op jit(solution)/shard_map/ppermute | solution.py:25
  50.0 14.9 %collective-permute-start.15 = (bf16[128,2048]{1,0:T(8,128)(2,1)S(1)}, bf16[128,2048]{1,0:T(8,128)(2,1)S(1)}, u32[]{:S(2)}, u32[]{:S(2)}) collective-permute-start(bf16[128,2048]{1,0:T(8,128)(2,1)S(1)} %collective-permute-done.7.refs_9_), channel_id=1, source_target_pairs={{0,8},{4,12},{8,0},{12,4},{16,24},{20,28},{24,16},{28,20},{1,9},{5... | collective-permute-start | bytes 1572872 | tf_op jit(solution)/shard_map/ppermute | solution.py:25
  51.5 24.3 %collective-permute-start.16 = (bf16[256,2048]{1,0:T(8,128)(2,1)S(1)}, bf16[256,2048]{1,0:T(8,128)(2,1)S(1)}, u32[]{:S(2)}, u32[]{:S(2)}) collective-permute-start(bf16[256,2048]{1,0:T(8,128)(2,1)S(1)} %pad_maximum_fusion.1), channel_id=1, source_target_pairs={{0,1},{1,0},{2,3},{3,2},{4,5},{5,4},{6,7},{7,6},{8,9},{9,8},{10,11... | collective-permute-start | bytes 3145736 | tf_op jit(solution)/shard_map/ppermute | solution.py:29
  53.2 21.3 %collective-permute-start.17 = (bf16[128,2048]{1,0:T(8,128)(2,1)S(1)}, bf16[128,2048]{1,0:T(8,128)(2,1)S(1)}, u32[]{:S(2)}, u32[]{:S(2)}) collective-permute-start(bf16[128,2048]{1,0:T(8,128)(2,1)S(1)} %get-tuple-element.115), channel_id=1, source_target_pairs={{0,8},{4,12},{8,0},{12,4},{16,24},{20,28},{24,16},{28,20},{1,9},{5... | collective-permute-start | bytes 1572872 | tf_op jit(solution)/shard_map/ppermute | solution.py:25
  53.7 20.8 %collective-permute-start.18 = (bf16[128,2048]{1,0:T(8,128)(2,1)S(1)}, bf16[128,2048]{1,0:T(8,128)(2,1)S(1)}, u32[]{:S(2)}, u32[]{:S(2)}) collective-permute-start(bf16[128,2048]{1,0:T(8,128)(2,1)S(1)} %get-tuple-element.115), channel_id=1, source_target_pairs={{0,16},{4,20},{8,24},{12,28},{16,0},{20,4},{24,8},{28,12},{1,17},{... | collective-permute-start | bytes 1572872 | tf_op jit(solution)/shard_map/ppermute | solution.py:25
  64.8 13.1 %collective-permute-start.23 = (bf16[256,2048]{1,0:T(8,128)(2,1)S(1)}, bf16[256,2048]{1,0:T(8,128)(2,1)S(1)}, u32[]{:S(2)}, u32[]{:S(2)}) collective-permute-start(bf16[256,2048]{1,0:T(8,128)(2,1)S(1)} %collective-permute-done.8.refs_2_.refs_17_), channel_id=1, source_target_pairs={{0,4},{4,0},{8,12},{12,8},{16,20},{20,16},{24,28},{28,24},{1,5},{5... | collective-permute-start | bytes 3145736 | tf_op jit(solution)/shard_map/ppermute | solution.py:25
  64.8 11.0 %collective-permute-start.19 = (bf16[128,2048]{1,0:T(8,128)(2,1)S(1)}, bf16[128,2048]{1,0:T(8,128)(2,1)S(1)}, u32[]{:S(2)}, u32[]{:S(2)}) collective-permute-start(bf16[128,2048]{1,0:T(8,128)(2,1)S(1)} %collective-permute-done.6.refs_5_), channel_id=1, source_target_pairs={{0,4},{4,0},{8,12},{12,8},{16,20},{20,16},{24,28},{28,24},{1,5},{5... | collective-permute-start | bytes 1572872 | tf_op jit(solution)/shard_map/ppermute | solution.py:25
  78.1 6.3 %collective-permute-start.27 = (bf16[256,2048]{1,0:T(8,128)(2,1)S(1)}, bf16[256,2048]{1,0:T(8,128)(2,1)S(1)}, u32[]{:S(2)}, u32[]{:S(2)}) collective-permute-start(bf16[256,2048]{1,0:T(8,128)(2,1)S(1)} %pad_maximum_fusion.2), channel_id=1, source_target_pairs={{0,4},{4,0},{8,12},{12,8},{16,20},{20,16},{24,28},{28,24},{1,5},{5... | collective-permute-start | bytes 3145736 | tf_op jit(solution)/shard_map/ppermute | solution.py:25
  78.5 14.0 %collective-permute-start.24 = (bf16[128,2048]{1,0:T(8,128)(2,1)S(1)}, bf16[128,2048]{1,0:T(8,128)(2,1)S(1)}, u32[]{:S(2)}, u32[]{:S(2)}) collective-permute-start(bf16[128,2048]{1,0:T(8,128)(2,1)S(1)} %collective-permute-done.9.refs_2_), channel_id=1, source_target_pairs={{0,16},{4,20},{8,24},{12,28},{16,0},{20,4},{24,8},{28,12},{1,17},{... | collective-permute-start | bytes 1572872 | tf_op jit(solution)/shard_map/ppermute | solution.py:25
  79.0 13.7 %collective-permute-start.25 = (bf16[128,2048]{1,0:T(8,128)(2,1)S(1)}, bf16[128,2048]{1,0:T(8,128)(2,1)S(1)}, u32[]{:S(2)}, u32[]{:S(2)}) collective-permute-start(bf16[128,2048]{1,0:T(8,128)(2,1)S(1)} %collective-permute-done.18.refs_6_), channel_id=1, source_target_pairs={{0,8},{4,12},{8,0},{12,4},{16,24},{20,28},{24,16},{28,20},{1,9},{5... | collective-permute-start | bytes 1572872 | tf_op jit(solution)/shard_map/ppermute | solution.py:25
  80.5 13.4 %collective-permute-start.26 = (bf16[128,2048]{1,0:T(8,128)(2,1)S(1)}, bf16[128,2048]{1,0:T(8,128)(2,1)S(1)}, u32[]{:S(2)}, u32[]{:S(2)}) collective-permute-start(bf16[128,2048]{1,0:T(8,128)(2,1)S(1)} %collective-permute-done.14.refs_12_), channel_id=1, source_target_pairs={{0,1},{1,0},{2,3},{3,2},{4,5},{5,4},{6,7},{7,6},{8,9},{9,8},{10,11... | collective-permute-start | bytes 1572872 | tf_op jit(solution)/shard_map/ppermute | solution.py:29
  94.2 5.7 %collective-permute-start.31 = (bf16[768,2048]{1,0:T(8,128)(2,1)S(1)}, bf16[768,2048]{1,0:T(8,128)(2,1)S(1)}, u32[]{:S(2)}, u32[]{:S(2)}) collective-permute-start(bf16[768,2048]{1,0:T(8,128)(2,1)S(1)} %constant_dynamic-update-slice_fusion), channel_id=1, source_target_pairs={{0,4},{4,0},{8,12},{12,8},{16,20},{20,16},{24,28},{28,24},{1,5},{5... | collective-permute-start | bytes 9437192 | tf_op jit(solution)/shard_map/ppermute | solution.py:25
  94.3 14.3 %collective-permute-start.29 = (bf16[128,2048]{1,0:T(8,128)(2,1)S(1)}, bf16[128,2048]{1,0:T(8,128)(2,1)S(1)}, u32[]{:S(2)}, u32[]{:S(2)}) collective-permute-start(bf16[128,2048]{1,0:T(8,128)(2,1)S(1)} %collective-permute-done.15.refs_13_), channel_id=1, source_target_pairs={{0,1},{1,0},{2,3},{3,2},{4,5},{5,4},{6,7},{7,6},{8,9},{9,8},{10,11... | collective-permute-start | bytes 1572872 | tf_op jit(solution)/shard_map/ppermute | solution.py:29
  95.9 12.7 %collective-permute-start.30 = (bf16[128,2048]{1,0:T(8,128)(2,1)S(1)}, bf16[128,2048]{1,0:T(8,128)(2,1)S(1)}, u32[]{:S(2)}, u32[]{:S(2)}) collective-permute-start(bf16[128,2048]{1,0:T(8,128)(2,1)S(1)} %collective-permute-done.26.refs_1_.refs_21_), channel_id=1, source_target_pairs={{0,4},{4,0},{8,12},{12,8},{16,20},{20,16},{24,28},{28,24},{1,5},{5... | collective-permute-start | bytes 1572872 | tf_op jit(solution)/shard_map/ppermute | solution.py:25
  129.5 8.1 %collective-permute-start.35 = (f32[1,2048]{1,0:T(1,128)S(1)}, f32[1,2048]{1,0:T(1,128)S(1)}, u32[]{:S(2)}, u32[]{:S(2)}) collective-permute-start(f32[1,2048]{1,0:T(1,128)S(1)} %add.17), channel_id=1, source_target_pairs={{0,8},{4,12},{8,0},{12,4},{16,24},{20,28},{24,16},{28,20},{1,9},{5... | collective-permute-start | bytes 24584 | tf_op jit(solution)/shard_map/ppermute | solution.py:25
  130.1 7.5 %collective-permute-start.36 = (f32[1,2048]{1,0:T(1,128)S(1)}, f32[1,2048]{1,0:T(1,128)S(1)}, u32[]{:S(2)}, u32[]{:S(2)}) collective-permute-start(f32[1,2048]{1,0:T(1,128)S(1)} %add.17), channel_id=1, source_target_pairs={{0,16},{4,20},{8,24},{12,28},{16,0},{20,4},{24,8},{28,12},{1,17},{... | collective-permute-start | bytes 24584 | tf_op jit(solution)/shard_map/ppermute | solution.py:25
  131.6 6.0 %collective-permute-start.37 = (f32[1,2048]{1,0:T(1,128)S(1)}, f32[1,2048]{1,0:T(1,128)S(1)}, u32[]{:S(2)}, u32[]{:S(2)}) collective-permute-start(f32[1,2048]{1,0:T(1,128)S(1)} %add.17), channel_id=1, source_target_pairs={{0,24},{4,28},{8,16},{12,20},{16,8},{20,12},{24,0},{28,4},{1,25},{... | collective-permute-start | bytes 24584 | tf_op jit(solution)/shard_map/ppermute | solution.py:25
  137.6 12.8 %collective-permute-start.38 = (f32[1,2048]{1,0:T(1,128)S(1)}, f32[1,2048]{1,0:T(1,128)S(1)}, u32[]{:S(2)}, u32[]{:S(2)}) collective-permute-start(f32[1,2048]{1,0:T(1,128)S(1)} %add_add_fusion.refs_0_), channel_id=1, source_target_pairs={{0,1},{1,0},{2,3},{3,2},{4,5},{5,4},{6,7},{7,6},{8,9},{9,8},{10,11... | collective-permute-start | bytes 24584 | tf_op jit(solution)/shard_map/ppermute | solution.py:29
  139.3 11.2 %collective-permute-start.39 = (f32[1,2048]{1,0:T(1,128)S(1)}, f32[1,2048]{1,0:T(1,128)S(1)}, u32[]{:S(2)}, u32[]{:S(2)}) collective-permute-start(f32[1,2048]{1,0:T(1,128)S(1)} %add_add_fusion.refs_0_), channel_id=1, source_target_pairs={{0,2},{1,3},{2,0},{3,1},{4,6},{5,7},{6,4},{7,5},{8,10},{9,11},{10,... | collective-permute-start | bytes 24584 | tf_op jit(solution)/shard_map/ppermute | solution.py:29
  141.9 8.6 %collective-permute-start.40 = (f32[1,2048]{1,0:T(1,128)S(1)}, f32[1,2048]{1,0:T(1,128)S(1)}, u32[]{:S(2)}, u32[]{:S(2)}) collective-permute-start(f32[1,2048]{1,0:T(1,128)S(1)} %add_add_fusion.refs_0_), channel_id=1, source_target_pairs={{0,3},{1,2},{2,1},{3,0},{4,7},{5,6},{6,5},{7,4},{8,11},{9,10},{10,... | collective-permute-start | bytes 24584 | tf_op jit(solution)/shard_map/ppermute | solution.py:29
  (17 other events, 90.1 us)

commit v4 on v3

--- a/solution.py
+++ b/solution.py
@@ -266,15 +266,21 @@
     rows, width = first_pre.shape
     pairs = rows // (2 * SEGMENTS)
 
-    def kernel(where_ref, first_ref, second_ref, back_ref, both_ref, parts_ref, wholes_ref, *refs):
+    def kernel(where_ref, first_ref, second_ref, back_ref, both_ref, parts_ref, *refs):
+        whole_refs, refs = refs[: len(wholes)], refs[len(wholes) :]
         (state_ref, one_ref, other_ref, bias_grad_ref, state_grad_ref) = refs[:5]
-        kept, updates, slopes, one_hold, other_hold, state_hold = refs[5:]
+        hold, kept, updates, slopes, one_hold, other_hold, state_hold = refs[5:]
         me = where_ref[2]
         order = place_back(rows)
 
         def body(span):
             entering = both_ref[1:2, span]
-            blocks = [wholes_ref[rank, :, span] for rank in range(ranks)]
+            per = ranks // len(wholes)
+            for index, ref in enumerate(whole_refs):
+                for member in range(per):
+                    offset = index * per + member
+                    hold[me ^ offset if len(wholes) > 1 else offset, 0:3, :] = ref[member, :, span]
+            blocks = [hold[rank] for rank in range(ranks)]
             for rank in range(ranks):
                 block = blocks[rank]
                 entering = jnp.where(rank < me, block[0:1] * entering + block[1:2], entering)
@@ -339,13 +345,15 @@
     return pl.pallas_call(
         kernel,
         out_shape=[wide, tall, tall, flat, flat],
-        in_specs=[SMEM_SPEC] + [VMEM_SPEC] * 6,
+        in_specs=[SMEM_SPEC] + [VMEM_SPEC] * (5 + len(wholes)),
         out_specs=[VMEM_SPEC] * 5,
-        scratch_shapes=[pltpu.VMEM((rows, tile), F32)] * 3 + [pltpu.VMEM((rows, tile), BF16)] * 3,
+        scratch_shapes=[pltpu.VMEM((ranks, SEGMENTS, tile), F32)]
+        + [pltpu.VMEM((rows, tile), F32)] * 3
+        + [pltpu.VMEM((rows, tile), BF16)] * 3,
         compiler_params=params(14),
         cost_estimate=cost(6 * rows * rows * width, 12 * rows * width),
         name="scan_rows",
-    )(where, *map(near, (first_pre, second_pre, back, both, parts, wholes)))
+    )(where, *map(near, (first_pre, second_pre, back, both, parts, *wholes)))
 
 
 def layer_call(where, state_rows, residual, shards, tile):
@@ -467,23 +475,25 @@
     f6a, f6b = send(f2a, 4), send(f4b, 2)
     t2b, t4b = send(t_b, 2), send(t_b, 4)
     sb = over(stack(f2b, f4b))
-    f6a, f6b, f3b, f5b, t3a, t5a, ca = after((f6a, f6b, f2b, f4b, t2a, t4a, sa))
-    f3b, f5b, t3a, t5a, ca = core(f3b), core(f5b), core(t3a), core(t5a), core(ca)
-    both, f6a, f6b, sb, t2b, t4b, f3b, f5b, t3a, t5a, ca, t2a = after(
-        (both, f6a, f6b, sb, t2b, t4b, f3b, f5b, t3a, t5a, ca, t2a)
+    f6a, f6b, f3b, f5b, t3a, t5a = after((f6a, f6b, f2b, f4b, t2a, t4a))
+    f3b, f5b, t3a, t5a = core(f3b), core(f5b), core(t3a), core(t5a)
+    both, f6a, f6b, sb, t2b, t4b, f3b, f5b, t3a, t5a, sa, t2a = after(
+        (both, f6a, f6b, sb, t2b, t4b, f3b, f5b, t3a, t5a, sa, t2a)
     )
     t6a, t6b = send(t2a, 4), send(t4b, 2)
     s6a = over(f6a)
-    f7, cb = core(stack(f6a, f6b)), core(sb)
+    f7, cs = core(stack(f6a, f6b)), core(stack(sa, sb))
     first = Shards([own_f, [f1a, f1b], [f2a, f2b], [f3a, f3b], [f4a, f4b], [f5a, f5b], [f6a, f6b], [f7]])
     pairs = lambda one, two, row: cut(one, row) + cut(two, row)
-    most = [[own_s], [s1], pairs(sa, sb, 0), pairs(ca, cb, 0), pairs(sa, sb, 1), pairs(ca, cb, 1)]
+    most = [[own_s], [s1], pairs(sa, sb, 0), cut(cs, 0, 2), pairs(sa, sb, 1), cut(cs, 1, 3)]
     first_pre = project_call(normed, first, tile, BF16)
     partial = project_call(normed, Shards(most), tile, F32)
-    t6a, t6b, s6a, f6b, first_pre, partial, own_t, both = after(
-        (t6a, t6b, s6a, f6b, first_pre, partial, own_t, both)
-    )
-    s6b, s7a = over(f6b), core(s6a)
+    t6a, t6b, s6a, sb_out, first_pre, partial, own_t, both = after(
+        (t6a, t6b, s6a, sb, first_pre, partial, own_t, both)
+    )
+    quarter = half // 2
+    s6b = [send(sb_out[half : half + quarter], 2), send(sb_out[quarter:half], 4)]
+    s7a = core(s6a)
     c4 = core(stack(t6a, t6b, t2b, t4b, own_t))
     third = Shards(
         [[own_t], cut(c4, 4, 5), [t2a, t2b], [t3a, (c4, 2 * half, half)], [t4a, t4b], [t5a, (c4, 3 * half, half)]]
@@ -491,8 +501,8 @@
     )
     both = jnp.concatenate([both, send(both, 4)], axis=1)
     back = back_call(where, grads, third)
-    s6b, s7a, back, both = after((s6b, s7a, back, both))
-    last = [[s6a, s6b], [s7a, core(s6b)]]
+    s6b_low, s6b_high, s7a, back, both = after((*s6b, s7a, back, both))
+    last = [[s6a, s6b_low, s6b_high], [s7a, core(stack(s6b_low, s6b_high))]]
     second = Shards(most + last)
     second_pre, parts, whole, both = totals_call(
         where, normed, partial, Shards(last), len(most) * depth, first_pre, back, both, depth, tile
@@ -531,7 +541,11 @@
         where = jnp.stack([nought, nought, me]).astype(jnp.int32)
         found = front(where, tile, *given)
     where, first, second, third, first_pre, second_pre, back, both, parts, whole = found
-    wholes = lax.all_gather(whole, "seq")
+    if cube:
+        chip = jnp.stack([whole, hop(whole, 1, ranks)])
+        wholes = [chip] + [hop(chip, offset, ranks) for offset in (2, 4, 6)]
+    else:
+        wholes = [lax.all_gather(whole, "seq")]
     state_rows, one, other, bias_part, state_grad = scan_call(
         where, first_pre, second_pre, back, both, parts, wholes, ranks, tile
     )

time: 152 us -> 147 us (0.967)
  blocking collectives: 9.5 us -> 0 us
  starting transfers between devices: 34.5 us -> 37.5 us
    all_gather x1 -> x0, blocking collectives: 9.5 us -> none  [on_device(): wholes = lax.all_gather(whole, 'seq')]
    ppermute x34 -> x39, waiting for transfers between devices: 61.7 us -> 68.2 us  [hop(): return lax.ppermute(value, 'seq', [(i, i ^ offset) for i in range(count)])]
    ppermute x7 -> x6, waiting for transfers between devices: 7.8 us -> 2.36 us  [swap_batch(): return lax.ppermute(value, 'batch', [(i, i ^ offset) for i in range(count)])]
    ppermute x34 -> x39, starting transfers between devices: 23.6 us -> 28.2 us  [hop(): return lax.ppermute(value, 'seq', [(i, i ^ offset) for i in range(count)])]
    ppermute x7 -> x6, starting transfers between devices: 11 us -> 9.31 us  [swap_batch(): return lax.ppermute(value, 'batch', [(i, i ^ offset) for i in range(count)])]
  transfers between devices with their start and end apart: 41 -> 45, of which waited for: 22 -> 27; matrix products, arithmetic and copies ran while one was open for 1% -> 1% of each run, Pallas kernels for 16% -> 17%
where the time goes in v4:
time: 147 us
  waiting for transfers between devices  70.6 us (48%)
  starting transfers between devices  37.5 us (26%)
  Pallas kernels  33.9 us (23%)
  other arithmetic  3.31 us (2%)
    ppermute x39, waiting for transfers between devices, hop(): return lax.ppermute(value, 'seq', [(i, i ^ offset) for i in range(count)])  68.2 us
    ppermute x39, starting transfers between devices, hop(): return lax.ppermute(value, 'seq', [(i, i ^ offset) for i in range(count)])  28.2 us
    ppermute x6, starting transfers between devices, swap_batch(): return lax.ppermute(value, 'batch', [(i, i ^ offset) for i in range(count)])  9.31 us
    pallas_call x1, Pallas kernels, input_grad_call(): pl.pallas_call(kernel, out_shape=jax.ShapeDtypeStruct((rows, width), BF16...  8.37 us
    pallas_call x2, Pallas kernels, project_call(): pl.pallas_call(kernel, out_shape=jax.ShapeDtypeStruct((rows, width), dtyp...  5.16 us
    pallas_call x1, Pallas kernels, scan_call(): pl.pallas_call(kernel, out_shape=[wide, tall, tall, flat, flat], in_specs...  4.75 us
    pallas_call x1, Pallas kernels, layer_call(): pl.pallas_call(kernel, out_shape=jax.ShapeDtypeStruct((rows, width), BF16...  4.72 us
    pallas_call x1, Pallas kernels, totals_call(): pl.pallas_call(kernel, out_shape=[jax.ShapeDtypeStruct((rows, width), BF1...  3.45 us
  transfers between devices with their start and end apart: 45, of which 27 were waited for; matrix products, arithmetic and copies ran while one was open for 1% of the time, Pallas kernels for 17%

profile of v4, /device:TPU:0, one launch (start us, length us, event | category | flops | bytes accessed | tf_op | source)
XLA Modules:
  0.0 146.7 jit_solution(7684830085626415708)
XLA Ops:
  2.2 3.0 %collective-permute-start = (bf16[128,2048]{1,0:T(8,128)(2,1)S(1)}, bf16[128,2048]{1,0:T(8,128)(2,1)S(1)}, u32[]{:S(2)}, u32[]{:S(2)}) collective-permute-start(bf16[128,2048]{1,0:T(8,128)(2,1)S(1)} %slice_select_fusion.1.refs_0_), channel_id=1, source_target_pairs={{0,8},{4,12},{8,0},{12,4},{16,24},{20,28},{24,16},{28,20},{1,9},{5... | collective-permute-start | bytes 1572872 | tf_op jit(solution)/shard_map/ppermute | solution.py:25
  10.7 3.3 %norm_rows.1 = (bf16[256,2048]{1,0:T(8,128)(2,1)S(1)}, bf16[2048,256]{1,0:T(8,128)(2,1)S(1)}) custom-call(s32[3]{0:T(128)S(1)} %pad_add_fusion.where_ref, bf16[256,2048]{1,0:T(8,128)(2,1)S(1)} %bitcast.11, bf16[256,2048]{1,0:T(8,128)(2,1)S(1)} %bitcast.14, f32[1,2048]{1,0:T(1,128)S(1)} %bitcast.16), custom_call_target="tpu_custom_call" | custom-call | flops 536870912 | bytes 4194304 | tf_op jit(solution)/shard_map/norm_rows/pallas_call | solution.py:131
  13.9 3.3 %collective-permute-done.5 = f32[2,512]{1,0:T(2,128)S(1)} collective-permute-done((f32[2,512]{1,0:T(2,128)S(1)}, f32[2,512]{1,0:T(2,128)S(1)}, u32[]{:S(2)}, u32[]{:S(2)}) %collective-permute-start.5) | collective-permute-done | bytes 4128 | tf_op jit(solution)/shard_map/ppermute | solution.py:25
  19.1 1.6 %collective-permute-start.7 = (bf16[128,2048]{1,0:T(8,128)(2,1)S(1)}, bf16[128,2048]{1,0:T(8,128)(2,1)S(1)}, u32[]{:S(2)}, u32[]{:S(2)}) collective-permute-start(bf16[128,2048]{1,0:T(8,128)(2,1)S(1)} %slice_select_fusion.refs_1_), channel_id=1, source_target_pairs={{0,16},{4,20},{8,24},{12,28},{16,0},{20,4},{24,8},{28,12},{1,17},{... | collective-permute-start | bytes 1572872 | tf_op jit(solution)/shard_map/ppermute | solution.py:25
  20.7 1.6 %collective-permute-start.8 = (bf16[256,2048]{1,0:T(8,128)(2,1)S(1)}, bf16[256,2048]{1,0:T(8,128)(2,1)S(1)}, u32[]{:S(2)}, u32[]{:S(2)}) collective-permute-start(bf16[256,2048]{1,0:T(8,128)(2,1)S(1)} %pad_maximum_fusion.1), channel_id=1, source_target_pairs={{0,1},{1,0},{2,3},{3,2},{4,5},{5,4},{6,7},{7,6},{8,9},{9,8},{10,11... | collective-permute-start | bytes 3145736 | tf_op jit(solution)/shard_map/ppermute | solution.py:29
  22.9 8.2 %collective-permute-done.6.refs_5_ = bf16[128,2048]{1,0:T(8,128)(2,1)S(1)} collective-permute-done((bf16[128,2048]{1,0:T(8,128)(2,1)S(1)}, bf16[128,2048]{1,0:T(8,128)(2,1)S(1)}, u32[]{:S(2)}, u32[]{:S(2)}) %collective-permute-start.6) | collective-permute-done | bytes 524320 | tf_op jit(solution)/shard_map/ppermute | solution.py:25
  31.1 2.9 %collective-permute-done.7.refs_9_ = bf16[128,2048]{1,0:T(8,128)(2,1)S(1)} collective-permute-done((bf16[128,2048]{1,0:T(8,128)(2,1)S(1)}, bf16[128,2048]{1,0:T(8,128)(2,1)S(1)}, u32[]{:S(2)}, u32[]{:S(2)}) %collective-permute-start.7) | collective-permute-done | bytes 524320 | tf_op jit(solution)/shard_map/ppermute | solution.py:25
  34.0 1.5 %collective-permute-start.9 = (bf16[128,2048]{1,0:T(8,128)(2,1)S(1)}, bf16[128,2048]{1,0:T(8,128)(2,1)S(1)}, u32[]{:S(2)}, u32[]{:S(2)}) collective-permute-start(bf16[128,2048]{1,0:T(8,128)(2,1)S(1)} %get-tuple-element.102), channel_id=1, source_target_pairs={{0,8},{4,12},{8,0},{12,4},{16,24},{20,28},{24,16},{28,20},{1,9},{5... | collective-permute-start | bytes 1572872 | tf_op jit(solution)/shard_map/ppermute | solution.py:25
  35.7 7.1 %collective-permute-done.10.refs_5_ = bf16[128,2048]{1,0:T(8,128)(2,1)S(1)} collective-permute-done((bf16[128,2048]{1,0:T(8,128)(2,1)S(1)}, bf16[128,2048]{1,0:T(8,128)(2,1)S(1)}, u32[]{:S(2)}, u32[]{:S(2)}) %collective-permute-start.10) | collective-permute-done | bytes 524320 | tf_op jit(solution)/shard_map/ppermute | solution.py:25
  42.8 5.4 %collective-permute-done.9.refs_2_ = bf16[128,2048]{1,0:T(8,128)(2,1)S(1)} collective-permute-done((bf16[128,2048]{1,0:T(8,128)(2,1)S(1)}, bf16[128,2048]{1,0:T(8,128)(2,1)S(1)}, u32[]{:S(2)}, u32[]{:S(2)}) %collective-permute-start.9) | collective-permute-done | bytes 524320 | tf_op jit(solution)/shard_map/ppermute | solution.py:25
  48.3 1.6 %collective-permute-start.14 = (bf16[128,2048]{1,0:T(8,128)(2,1)S(1)}, bf16[128,2048]{1,0:T(8,128)(2,1)S(1)}, u32[]{:S(2)}, u32[]{:S(2)}) collective-permute-start(bf16[128,2048]{1,0:T(8,128)(2,1)S(1)} %collective-permute-done.refs_4_), channel_id=1, source_target_pairs={{0,16},{4,20},{8,24},{12,28},{16,0},{20,4},{24,8},{28,12},{1,17},{... | collective-permute-start | bytes 1572872 | tf_op jit(solution)/shard_map/ppermute | solution.py:25
  52.1 1.6 %collective-permute-start.16 = (bf16[256,2048]{1,0:T(8,128)(2,1)S(1)}, bf16[256,2048]{1,0:T(8,128)(2,1)S(1)}, u32[]{:S(2)}, u32[]{:S(2)}) collective-permute-start(bf16[256,2048]{1,0:T(8,128)(2,1)S(1)} %pad_maximum_fusion.2), channel_id=1, source_target_pairs={{0,1},{1,0},{2,3},{3,2},{4,5},{5,4},{6,7},{7,6},{8,9},{9,8},{10,11... | collective-permute-start | bytes 3145736 | tf_op jit(solution)/shard_map/ppermute | solution.py:29
  54.2 9.0 %collective-permute-done.14.refs_12_ = bf16[128,2048]{1,0:T(8,128)(2,1)S(1)} collective-permute-done((bf16[128,2048]{1,0:T(8,128)(2,1)S(1)}, bf16[128,2048]{1,0:T(8,128)(2,1)S(1)}, u32[]{:S(2)}, u32[]{:S(2)}) %collective-permute-start.14) | collective-permute-done | bytes 524320 | tf_op jit(solution)/shard_map/ppermute | solution.py:25
  63.2 1.6 %collective-permute-done.15.refs_13_ = bf16[128,2048]{1,0:T(8,128)(2,1)S(1)} collective-permute-done((bf16[128,2048]{1,0:T(8,128)(2,1)S(1)}, bf16[128,2048]{1,0:T(8,128)(2,1)S(1)}, u32[]{:S(2)}, u32[]{:S(2)}) %collective-permute-start.15) | collective-permute-done | bytes 524320 | tf_op jit(solution)/shard_map/ppermute | solution.py:25
  65.3 9.1 %collective-permute-done.17.refs_3_ = bf16[128,2048]{1,0:T(8,128)(2,1)S(1)} collective-permute-done((bf16[128,2048]{1,0:T(8,128)(2,1)S(1)}, bf16[128,2048]{1,0:T(8,128)(2,1)S(1)}, u32[]{:S(2)}, u32[]{:S(2)}) %collective-permute-start.17) | collective-permute-done | bytes 524320 | tf_op jit(solution)/shard_map/ppermute | solution.py:25
  80.0 1.6 %collective-permute-start.25 = (bf16[128,2048]{1,0:T(8,128)(2,1)S(1)}, bf16[128,2048]{1,0:T(8,128)(2,1)S(1)}, u32[]{:S(2)}, u32[]{:S(2)}) collective-permute-start(bf16[128,2048]{1,0:T(8,128)(2,1)S(1)} %collective-permute-done.14.refs_12_), channel_id=1, source_target_pairs={{0,1},{1,0},{2,3},{3,2},{4,5},{5,4},{6,7},{7,6},{8,9},{9,8},{10,11... | collective-permute-start | bytes 1572872 | tf_op jit(solution)/shard_map/ppermute | solution.py:29
  83.0 2.9 %project.2.first_ref = bf16[256,2048]{1,0:T(8,128)(2,1)S(1)} custom-call(bf16[256,2048]{1,0:T(8,128)(2,1)S(1)} %get-tuple-element.124.x_ref, bf16[128,2048]{1,0:T(8,128)(2,1)S(1)} %slice_select_fusion.1.refs_0_, bf16[128,2048]{1,0:T(8,128)(2,1)S(1)} %slice_select_fusion.refs_1_, bf16[128,2048]{1,0:T(8,128)(2,1)S(1)} %collective-permute-done.2.refs_2_, ...), custom_call_target="tpu_custom_call" | custom-call | flops 2147483648 | bytes 8388608 | tf_op jit(solution)/shard_map/project/pallas_call | solution.py:155
  85.9 2.3 %project.3.refs_0_ = f32[256,2048]{1,0:T(8,128)S(1)} custom-call(bf16[256,2048]{1,0:T(8,128)(2,1)S(1)} %get-tuple-element.124.x_ref, bf16[256,2048]{1,0:T(8,128)(2,1)S(1)} %broadcast_select_fusion.refs_0_.refs_15_, bf16[256,2048]{1,0:T(8,128)(2,1)S(1)} %collective-permute-done.13.refs_1_.refs_16_, ...), custom_call_target="tpu_custom_call" | custom-call | flops 1610612736 | bytes 6291456 | tf_op jit(solution)/shard_map/project/pallas_call | solution.py:155
  88.2 3.8 %collective-permute-done.23.refs_8_ = bf16[128,2048]{1,0:T(8,128)(2,1)S(1)} collective-permute-done((bf16[128,2048]{1,0:T(8,128)(2,1)S(1)}, bf16[128,2048]{1,0:T(8,128)(2,1)S(1)}, u32[]{:S(2)}, u32[]{:S(2)}) %collective-permute-start.23) | collective-permute-done | bytes 524320 | tf_op jit(solution)/shard_map/ppermute | solution.py:25
  93.7 1.6 %collective-permute-start.32 = (f32[2,1024]{1,0:T(2,128)S(1)}, f32[2,1024]{1,0:T(2,128)S(1)}, u32[]{:S(2)}, u32[]{:S(2)}) collective-permute-start(f32[2,1024]{1,0:T(2,128)S(1)} %pad_maximum_fusion.7), channel_id=1, source_target_pairs={{0,16},{4,20},{8,24},{12,28},{16,0},{20,4},{24,8},{28,12},{1,17},{... | collective-permute-start | bytes 24584 | tf_op jit(solution)/shard_map/ppermute | solution.py:25
  97.5 1.9 %collective-permute-done.31.refs_1_ = bf16[768,2048]{1,0:T(8,128)(2,1)S(1)} collective-permute-done((bf16[768,2048]{1,0:T(8,128)(2,1)S(1)}, bf16[768,2048]{1,0:T(8,128)(2,1)S(1)}, u32[]{:S(2)}, u32[]{:S(2)}) %collective-permute-start.31) | collective-permute-done | bytes 3145760 | tf_op jit(solution)/shard_map/ppermute | solution.py:25
  99.4 3.1 %back_rows.1.back_ref = bf16[256,2048]{1,0:T(8,128)(2,1)S(1)} custom-call(s32[3]{0:T(128)S(1)} %pad_add_fusion.where_ref, bf16[2048,256]{1,0:T(8,128)(2,1)S(1)} %get-tuple-element.139.g_ref, bf16[256,2048]{1,0:T(8,128)(2,1)S(1)} %copy-done, bf16[768,2048]{1,0:T(8,128)(2,1)S(1)} %collective-permute-done.31.refs_1_, ...), custom_call_target="tpu_custom_call" | custom-call | flops 2147483648 | bytes 8388608 | tf_op jit(solution)/shard_map/back_rows/pallas_call | solution.py:179
  102.5 1.7 %collective-permute-done.28.refs_2_.refs_21_ = bf16[64,2048]{1,0:T(8,128)(2,1)S(1)} collective-permute-done((bf16[64,2048]{1,0:T(8,128)(2,1)S(1)}, bf16[64,2048]{1,0:T(8,128)(2,1)S(1)}, u32[]{:S(2)}, u32[]{:S(2)}) %collective-permute-start.28) | collective-permute-done | bytes 262176 | tf_op jit(solution)/shard_map/ppermute | solution.py:25
  104.5 1.9 %collective-permute-done.33.refs_5_.refs_24_ = bf16[128,2048]{1,0:T(8,128)(2,1)S(1)} collective-permute-done((bf16[128,2048]{1,0:T(8,128)(2,1)S(1)}, bf16[128,2048]{1,0:T(8,128)(2,1)S(1)}, u32[]{:S(2)}, u32[]{:S(2)}) %collective-permute-start.33) | collective-permute-done | bytes 524320 | tf_op jit(solution)/shard_map/ppermute | solution.py:25
  106.4 3.5 %project_totals.1 = (bf16[256,2048]{1,0:T(8,128)(2,1)S(1)}, f32[3,8,2048]{2,1,0:T(8,128)S(1)}, f32[3,2048]{1,0:T(4,128)S(1)}, f32[2,2048]{1,0:T(2,128)S(1)}) custom-call(s32[3]{0:T(128)S(1)} %pad_add_fusion.where_ref, bf16[256,2048]{1,0:T(8,128)(2,1)S(1)} %get-tuple-element.124.x_ref, bf16[256,2048]{1,0:T(8,128)(2,1)S(1)} %project.2.first_ref, ...), custom_call_target="tpu_custom_call" | custom-call | flops 536870912 | bytes 2097152 | tf_op jit(solution)/shard_map/project_totals/pallas_call | solution.py:249
  111.2 1.6 %collective-permute-start.35 = (f32[2,3,2048]{2,1,0:T(4,128)S(1)}, f32[2,3,2048]{2,1,0:T(4,128)S(1)}, u32[]{:S(2)}, u32[]{:S(2)}) collective-permute-start(f32[2,3,2048]{2,1,0:T(4,128)S(1)} %pad_maximum_fusion.5.refs_0_), channel_id=1, source_target_pairs={{0,8},{4,12},{8,0},{12,4},{16,24},{20,28},{24,16},{28,20},{1,9},{5... | collective-permute-start | bytes 147464 | tf_op jit(solution)/shard_map/ppermute | solution.py:25
  115.5 2.2 %collective-permute-done.36.refs_2_ = f32[2,3,2048]{2,1,0:T(4,128)S(1)} collective-permute-done((f32[2,3,2048]{2,1,0:T(4,128)S(1)}, f32[2,3,2048]{2,1,0:T(4,128)S(1)}, u32[]{:S(2)}, u32[]{:S(2)}) %collective-permute-start.36) | collective-permute-done | bytes 49184 | tf_op jit(solution)/shard_map/ppermute | solution.py:25
  118.4 4.7 %scan_rows.1 = (bf16[256,2048]{1,0:T(8,128)(2,1)S(1)}, bf16[2048,256]{1,0:T(8,128)(2,1)S(1)}, bf16[2048,256]{1,0:T(8,128)(2,1)S(1)}, f32[1,2048]{1,0:T(1,128)S(1)}, f32[1,2048]{1,0:T(1,128)S(1)}) custom-call(s32[3]{0:T(128)S(1)} %pad_add_fusion.where_ref, bf16[256,2048]{1,0:T(8,128)(2,1)S(1)} %project.2.first_ref, ...), custom_call_target="tpu_custom_call" | custom-call | flops 805306368 | bytes 6291456 | tf_op jit(solution)/shard_map/scan_rows/pallas_call | solution.py:345
  128.0 4.7 %layer_rows.1 = bf16[256,2048]{1,0:T(8,128)(2,1)} custom-call(s32[3]{0:T(128)S(1)} %pad_add_fusion.where_ref, bf16[256,2048]{1,0:T(8,128)(2,1)S(1)} %get-tuple-element.157.x_ref, bf16[256,2048]{1,0:T(8,128)(2,1)S(1)} %bitcast.12, bf16[256,2048]{1,0:T(8,128)(2,1)S(1)} %copy-done, bf16[768,2048]{1,0:T(8,128)(2,1)S(1)} %collective-permute-done.31.refs_1_, ...), custom_call_target="tpu_custom_call" | custom-call | flops 2147483648 | bytes 8388608 | tf_op jit(solution)/shard_map/layer_rows/pallas_call | solution.py:375
  132.7 1.6 %collective-permute-start.42 = (f32[1,2048]{1,0:T(1,128)S(1)}, f32[1,2048]{1,0:T(1,128)S(1)}, u32[]{:S(2)}, u32[]{:S(2)}) collective-permute-start(f32[1,2048]{1,0:T(1,128)S(1)} %add_add_fusion.refs_0_), channel_id=1, source_target_pairs={{0,1},{1,0},{2,3},{3,2},{4,5},{5,4},{6,7},{7,6},{8,9},{9,8},{10,11... | collective-permute-start | bytes 24584 | tf_op jit(solution)/shard_map/ppermute | solution.py:29
  134.4 2.6 %collective-permute-start.43 = (f32[1,2048]{1,0:T(1,128)S(1)}, f32[1,2048]{1,0:T(1,128)S(1)}, u32[]{:S(2)}, u32[]{:S(2)}) collective-permute-start(f32[1,2048]{1,0:T(1,128)S(1)} %add_add_fusion.refs_0_), channel_id=1, source_target_pairs={{0,2},{1,3},{2,0},{3,1},{4,6},{5,7},{6,4},{7,5},{8,10},{9,11},{10,... | collective-permute-start | bytes 24584 | tf_op jit(solution)/shard_map/ppermute | solution.py:29
  137.2 8.4 %input_grad_rows.1 = bf16[256,2048]{1,0:T(8,128)(2,1)} custom-call(s32[3]{0:T(128)S(1)} %pad_add_fusion.where_ref, bf16[2048,256]{1,0:T(8,128)(2,1)S(1)} %get-tuple-element.166.one_ref, bf16[2048,256]{1,0:T(8,128)(2,1)S(1)} %get-tuple-element.167.other_ref, bf16[256,2048]{1,0:T(8,128)(2,1)S(1)} %bitcast.13, bf16[256,2048]{1,0:T(8,128)(2,1)S(1)} %bitcast.15, ...), custom_call_target="tpu_custom_call" | custom-call | flops 4294967296 | bytes 16777216 | tf_op jit(solution)/shard_map/input_grad_rows/pallas_call | solution.py:415
  (106 shorter events, 34.8 us)
Async XLA Ops:
  2.2 15.0 %collective-permute-start = (bf16[128,2048]{1,0:T(8,128)(2,1)S(1)}, bf16[128,2048]{1,0:T(8,128)(2,1)S(1)}, u32[]{:S(2)}, u32[]{:S(2)}) collective-permute-start(bf16[128,2048]{1,0:T(8,128)(2,1)S(1)} %slice_select_fusion.1.refs_0_), channel_id=1, source_target_pairs={{0,8},{4,12},{8,0},{12,4},{16,24},{20,28},{24,16},{28,20},{1,9},{5... | collective-permute-start | bytes 1572872 | tf_op jit(solution)/shard_map/ppermute | solution.py:25
  5.2 13.4 %collective-permute-start.1 = (bf16[128,2048]{1,0:T(8,128)(2,1)S(1)}, bf16[128,2048]{1,0:T(8,128)(2,1)S(1)}, u32[]{:S(2)}, u32[]{:S(2)}) collective-permute-start(bf16[128,2048]{1,0:T(8,128)(2,1)S(1)} %slice_select_fusion.1.refs_0_), channel_id=1, source_target_pairs={{0,16},{4,20},{8,24},{12,28},{16,0},{20,4},{24,8},{28,12},{1,17},{... | collective-permute-start | bytes 1572872 | tf_op jit(solution)/shard_map/ppermute | solution.py:25
  6.7 11.9 %collective-permute-start.2 = (bf16[128,2048]{1,0:T(8,128)(2,1)S(1)}, bf16[128,2048]{1,0:T(8,128)(2,1)S(1)}, u32[]{:S(2)}, u32[]{:S(2)}) collective-permute-start(bf16[128,2048]{1,0:T(8,128)(2,1)S(1)} %slice_select_fusion.1.refs_0_), channel_id=1, source_target_pairs={{0,4},{4,0},{8,12},{12,8},{16,20},{20,16},{24,28},{28,24},{1,5},{5... | collective-permute-start | bytes 1572872 | tf_op jit(solution)/shard_map/ppermute | solution.py:25
  8.0 9.2 %collective-permute-start.3 = (bf16[128,2048]{1,0:T(8,128)(2,1)S(1)}, bf16[128,2048]{1,0:T(8,128)(2,1)S(1)}, u32[]{:S(2)}, u32[]{:S(2)}) collective-permute-start(bf16[128,2048]{1,0:T(8,128)(2,1)S(1)} %slice_select_fusion.refs_1_), channel_id=1, source_target_pairs={{0,4},{4,0},{8,12},{12,8},{16,20},{20,16},{24,28},{28,24},{1,5},{5... | collective-permute-start | bytes 1572872 | tf_op jit(solution)/shard_map/ppermute | solution.py:25
  10.1 7.1 %collective-permute-start.5 = (f32[2,512]{1,0:T(2,128)S(1)}, f32[2,512]{1,0:T(2,128)S(1)}, u32[]{:S(2)}, u32[]{:S(2)}) collective-permute-start(f32[2,512]{1,0:T(2,128)S(1)} %pad_maximum_fusion.8), channel_id=1, source_target_pairs={{0,8},{4,12},{8,0},{12,4},{16,24},{20,28},{24,16},{28,20},{1,9},{5... | collective-permute-start | bytes 12296 | tf_op jit(solution)/shard_map/ppermute | solution.py:25
  18.6 12.5 %collective-permute-start.6 = (bf16[128,2048]{1,0:T(8,128)(2,1)S(1)}, bf16[128,2048]{1,0:T(8,128)(2,1)S(1)}, u32[]{:S(2)}, u32[]{:S(2)}) collective-permute-start(bf16[128,2048]{1,0:T(8,128)(2,1)S(1)} %slice_select_fusion.refs_1_), channel_id=1, source_target_pairs={{0,8},{4,12},{8,0},{12,4},{16,24},{20,28},{24,16},{28,20},{1,9},{5... | collective-permute-start | bytes 1572872 | tf_op jit(solution)/shard_map/ppermute | solution.py:25
  19.1 14.9 %collective-permute-start.7 = (bf16[128,2048]{1,0:T(8,128)(2,1)S(1)}, bf16[128,2048]{1,0:T(8,128)(2,1)S(1)}, u32[]{:S(2)}, u32[]{:S(2)}) collective-permute-start(bf16[128,2048]{1,0:T(8,128)(2,1)S(1)} %slice_select_fusion.refs_1_), channel_id=1, source_target_pairs={{0,16},{4,20},{8,24},{12,28},{16,0},{20,4},{24,8},{28,12},{1,17},{... | collective-permute-start | bytes 1572872 | tf_op jit(solution)/shard_map/ppermute | solution.py:25
  20.7 27.6 %collective-permute-start.8 = (bf16[256,2048]{1,0:T(8,128)(2,1)S(1)}, bf16[256,2048]{1,0:T(8,128)(2,1)S(1)}, u32[]{:S(2)}, u32[]{:S(2)}) collective-permute-start(bf16[256,2048]{1,0:T(8,128)(2,1)S(1)} %pad_maximum_fusion.1), channel_id=1, source_target_pairs={{0,1},{1,0},{2,3},{3,2},{4,5},{5,4},{6,7},{7,6},{8,9},{9,8},{10,11... | collective-permute-start | bytes 3145736 | tf_op jit(solution)/shard_map/ppermute | solution.py:29
  22.4 20.5 %collective-permute-start.10 = (bf16[128,2048]{1,0:T(8,128)(2,1)S(1)}, bf16[128,2048]{1,0:T(8,128)(2,1)S(1)}, u32[]{:S(2)}, u32[]{:S(2)}) collective-permute-start(bf16[128,2048]{1,0:T(8,128)(2,1)S(1)} %get-tuple-element.102), channel_id=1, source_target_pairs={{0,16},{4,20},{8,24},{12,28},{16,0},{20,4},{24,8},{28,12},{1,17},{... | collective-permute-start | bytes 1572872 | tf_op jit(solution)/shard_map/ppermute | solution.py:25
  34.0 14.4 %collective-permute-start.13 = (bf16[256,2048]{1,0:T(8,128)(2,1)S(1)}, bf16[256,2048]{1,0:T(8,128)(2,1)S(1)}, u32[]{:S(2)}, u32[]{:S(2)}) collective-permute-start(bf16[256,2048]{1,0:T(8,128)(2,1)S(1)} %broadcast_select_fusion.refs_0_.refs_15_), channel_id=1, source_target_pairs={{0,4},{4,0},{8,12},{12,8},{16,20},{20,16},{24,28},{28,24},{1,5},{5... | collective-permute-start | bytes 3145736 | tf_op jit(solution)/shard_map/ppermute | solution.py:25
  34.0 14.3 %collective-permute-start.9 = (bf16[128,2048]{1,0:T(8,128)(2,1)S(1)}, bf16[128,2048]{1,0:T(8,128)(2,1)S(1)}, u32[]{:S(2)}, u32[]{:S(2)}) collective-permute-start(bf16[128,2048]{1,0:T(8,128)(2,1)S(1)} %get-tuple-element.102), channel_id=1, source_target_pairs={{0,8},{4,12},{8,0},{12,4},{16,24},{20,28},{24,16},{28,20},{1,9},{5... | collective-permute-start | bytes 1572872 | tf_op jit(solution)/shard_map/ppermute | solution.py:25
  35.5 12.8 %collective-permute-start.11 = (bf16[128,2048]{1,0:T(8,128)(2,1)S(1)}, bf16[128,2048]{1,0:T(8,128)(2,1)S(1)}, u32[]{:S(2)}, u32[]{:S(2)}) collective-permute-start(bf16[128,2048]{1,0:T(8,128)(2,1)S(1)} %collective-permute-done.refs_4_), channel_id=1, source_target_pairs={{0,4},{4,0},{8,12},{12,8},{16,20},{20,16},{24,28},{28,24},{1,5},{5... | collective-permute-start | bytes 1572872 | tf_op jit(solution)/shard_map/ppermute | solution.py:25
  48.3 14.9 %collective-permute-start.14 = (bf16[128,2048]{1,0:T(8,128)(2,1)S(1)}, bf16[128,2048]{1,0:T(8,128)(2,1)S(1)}, u32[]{:S(2)}, u32[]{:S(2)}) collective-permute-start(bf16[128,2048]{1,0:T(8,128)(2,1)S(1)} %collective-permute-done.refs_4_), channel_id=1, source_target_pairs={{0,16},{4,20},{8,24},{12,28},{16,0},{20,4},{24,8},{28,12},{1,17},{... | collective-permute-start | bytes 1572872 | tf_op jit(solution)/shard_map/ppermute | solution.py:25
  50.0 14.9 %collective-permute-start.15 = (bf16[128,2048]{1,0:T(8,128)(2,1)S(1)}, bf16[128,2048]{1,0:T(8,128)(2,1)S(1)}, u32[]{:S(2)}, u32[]{:S(2)}) collective-permute-start(bf16[128,2048]{1,0:T(8,128)(2,1)S(1)} %collective-permute-done.7.refs_9_), channel_id=1, source_target_pairs={{0,8},{4,12},{8,0},{12,4},{16,24},{20,28},{24,16},{28,20},{1,9},{5... | collective-permute-start | bytes 1572872 | tf_op jit(solution)/shard_map/ppermute | solution.py:25
  51.4 23.0 %collective-permute-start.17 = (bf16[128,2048]{1,0:T(8,128)(2,1)S(1)}, bf16[128,2048]{1,0:T(8,128)(2,1)S(1)}, u32[]{:S(2)}, u32[]{:S(2)}) collective-permute-start(bf16[128,2048]{1,0:T(8,128)(2,1)S(1)} %get-tuple-element.114), channel_id=1, source_target_pairs={{0,8},{4,12},{8,0},{12,4},{16,24},{20,28},{24,16},{28,20},{1,9},{5... | collective-permute-start | bytes 1572872 | tf_op jit(solution)/shard_map/ppermute | solution.py:25
  52.1 24.0 %collective-permute-start.16 = (bf16[256,2048]{1,0:T(8,128)(2,1)S(1)}, bf16[256,2048]{1,0:T(8,128)(2,1)S(1)}, u32[]{:S(2)}, u32[]{:S(2)}) collective-permute-start(bf16[256,2048]{1,0:T(8,128)(2,1)S(1)} %pad_maximum_fusion.2), channel_id=1, source_target_pairs={{0,1},{1,0},{2,3},{3,2},{4,5},{5,4},{6,7},{7,6},{8,9},{9,8},{10,11... | collective-permute-start | bytes 3145736 | tf_op jit(solution)/shard_map/ppermute | solution.py:29
  53.7 20.8 %collective-permute-start.18 = (bf16[128,2048]{1,0:T(8,128)(2,1)S(1)}, bf16[128,2048]{1,0:T(8,128)(2,1)S(1)}, u32[]{:S(2)}, u32[]{:S(2)}) collective-permute-start(bf16[128,2048]{1,0:T(8,128)(2,1)S(1)} %get-tuple-element.114), channel_id=1, source_target_pairs={{0,16},{4,20},{8,24},{12,28},{16,0},{20,4},{24,8},{28,12},{1,17},{... | collective-permute-start | bytes 1572872 | tf_op jit(solution)/shard_map/ppermute | solution.py:25
  64.8 11.3 %collective-permute-start.19 = (bf16[128,2048]{1,0:T(8,128)(2,1)S(1)}, bf16[128,2048]{1,0:T(8,128)(2,1)S(1)}, u32[]{:S(2)}, u32[]{:S(2)}) collective-permute-start(bf16[128,2048]{1,0:T(8,128)(2,1)S(1)} %collective-permute-done.6.refs_5_), channel_id=1, source_target_pairs={{0,4},{4,0},{8,12},{12,8},{16,20},{20,16},{24,28},{28,24},{1,5},{5... | collective-permute-start | bytes 1572872 | tf_op jit(solution)/shard_map/ppermute | solution.py:25
  64.8 11.3 %collective-permute-start.20 = (bf16[128,2048]{1,0:T(8,128)(2,1)S(1)}, bf16[128,2048]{1,0:T(8,128)(2,1)S(1)}, u32[]{:S(2)}, u32[]{:S(2)}) collective-permute-start(bf16[128,2048]{1,0:T(8,128)(2,1)S(1)} %collective-permute-done.7.refs_9_), channel_id=1, source_target_pairs={{0,4},{4,0},{8,12},{12,8},{16,20},{20,16},{24,28},{28,24},{1,5},{5... | collective-permute-start | bytes 1572872 | tf_op jit(solution)/shard_map/ppermute | solution.py:25
  77.3 8.6 %collective-permute-start.27 = (bf16[512,2048]{1,0:T(8,128)(2,1)S(1)}, bf16[512,2048]{1,0:T(8,128)(2,1)S(1)}, u32[]{:S(2)}, u32[]{:S(2)}) collective-permute-start(bf16[512,2048]{1,0:T(8,128)(2,1)S(1)} %pad_maximum_fusion), channel_id=1, source_target_pairs={{0,4},{4,0},{8,12},{12,8},{16,20},{20,16},{24,28},{28,24},{1,5},{5... | collective-permute-start | bytes 6291464 | tf_op jit(solution)/shard_map/ppermute | solution.py:25
  78.0 14.0 %collective-permute-start.23 = (bf16[128,2048]{1,0:T(8,128)(2,1)S(1)}, bf16[128,2048]{1,0:T(8,128)(2,1)S(1)}, u32[]{:S(2)}, u32[]{:S(2)}) collective-permute-start(bf16[128,2048]{1,0:T(8,128)(2,1)S(1)} %collective-permute-done.9.refs_2_), channel_id=1, source_target_pairs={{0,16},{4,20},{8,24},{12,28},{16,0},{20,4},{24,8},{28,12},{1,17},{... | collective-permute-start | bytes 1572872 | tf_op jit(solution)/shard_map/ppermute | solution.py:25
  78.4 13.7 %collective-permute-start.24 = (bf16[128,2048]{1,0:T(8,128)(2,1)S(1)}, bf16[128,2048]{1,0:T(8,128)(2,1)S(1)}, u32[]{:S(2)}, u32[]{:S(2)}) collective-permute-start(bf16[128,2048]{1,0:T(8,128)(2,1)S(1)} %collective-permute-done.18.refs_6_), channel_id=1, source_target_pairs={{0,8},{4,12},{8,0},{12,4},{16,24},{20,28},{24,16},{28,20},{1,9},{5... | collective-permute-start | bytes 1572872 | tf_op jit(solution)/shard_map/ppermute | solution.py:25
  80.0 13.4 %collective-permute-start.25 = (bf16[128,2048]{1,0:T(8,128)(2,1)S(1)}, bf16[128,2048]{1,0:T(8,128)(2,1)S(1)}, u32[]{:S(2)}, u32[]{:S(2)}) collective-permute-start(bf16[128,2048]{1,0:T(8,128)(2,1)S(1)} %collective-permute-done.14.refs_12_), channel_id=1, source_target_pairs={{0,1},{1,0},{2,3},{3,2},{4,5},{5,4},{6,7},{7,6},{8,9},{9,8},{10,11... | collective-permute-start | bytes 1572872 | tf_op jit(solution)/shard_map/ppermute | solution.py:29
  95.3 9.1 %collective-permute-start.30 = (bf16[128,2048]{1,0:T(8,128)(2,1)S(1)}, bf16[128,2048]{1,0:T(8,128)(2,1)S(1)}, u32[]{:S(2)}, u32[]{:S(2)}) collective-permute-start(bf16[128,2048]{1,0:T(8,128)(2,1)S(1)} %collective-permute-done.25.refs_1_.refs_20_), channel_id=1, source_target_pairs={{0,4},{4,0},{8,12},{12,8},{16,20},{20,16},{24,28},{28,24},{1,5},{5... | collective-permute-start | bytes 1572872 | tf_op jit(solution)/shard_map/ppermute | solution.py:25
  95.5 8.6 %collective-permute-start.28 = (bf16[64,2048]{1,0:T(8,128)(2,1)S(1)}, bf16[64,2048]{1,0:T(8,128)(2,1)S(1)}, u32[]{:S(2)}, u32[]{:S(2)}) collective-permute-start(bf16[64,2048]{1,0:T(8,128)(2,1)S(1)} %get-tuple-element.173), channel_id=1, source_target_pairs={{0,8},{4,12},{8,0},{12,4},{16,24},{20,28},{24,16},{28,20},{1,9},{5... | collective-permute-start | bytes 786440 | tf_op jit(solution)/shard_map/ppermute | solution.py:25
  96.1 8.3 %collective-permute-start.29 = (bf16[64,2048]{1,0:T(8,128)(2,1)S(1)}, bf16[64,2048]{1,0:T(8,128)(2,1)S(1)}, u32[]{:S(2)}, u32[]{:S(2)}) collective-permute-start(bf16[64,2048]{1,0:T(8,128)(2,1)S(1)} %get-tuple-element.172), channel_id=1, source_target_pairs={{0,16},{4,20},{8,24},{12,28},{16,0},{20,4},{24,8},{28,12},{1,17},{... | collective-permute-start | bytes 786440 | tf_op jit(solution)/shard_map/ppermute | solution.py:25
  124.4 8.3 %collective-permute-start.39 = (f32[1,2048]{1,0:T(1,128)S(1)}, f32[1,2048]{1,0:T(1,128)S(1)}, u32[]{:S(2)}, u32[]{:S(2)}) collective-permute-start(f32[1,2048]{1,0:T(1,128)S(1)} %add.17), channel_id=1, source_target_pairs={{0,8},{4,12},{8,0},{12,4},{16,24},{20,28},{24,16},{28,20},{1,9},{5... | collective-permute-start | bytes 24584 | tf_op jit(solution)/shard_map/ppermute | solution.py:25
  125.0 7.7 %collective-permute-start.40 = (f32[1,2048]{1,0:T(1,128)S(1)}, f32[1,2048]{1,0:T(1,128)S(1)}, u32[]{:S(2)}, u32[]{:S(2)}) collective-permute-start(f32[1,2048]{1,0:T(1,128)S(1)} %add.17), channel_id=1, source_target_pairs={{0,16},{4,20},{8,24},{12,28},{16,0},{20,4},{24,8},{28,12},{1,17},{... | collective-permute-start | bytes 24584 | tf_op jit(solution)/shard_map/ppermute | solution.py:25
  126.6 6.2 %collective-permute-start.41 = (f32[1,2048]{1,0:T(1,128)S(1)}, f32[1,2048]{1,0:T(1,128)S(1)}, u32[]{:S(2)}, u32[]{:S(2)}) collective-permute-start(f32[1,2048]{1,0:T(1,128)S(1)} %add.17), channel_id=1, source_target_pairs={{0,24},{4,28},{8,16},{12,20},{16,8},{20,12},{24,0},{28,4},{1,25},{... | collective-permute-start | bytes 24584 | tf_op jit(solution)/shard_map/ppermute | solution.py:25
  132.7 12.8 %collective-permute-start.42 = (f32[1,2048]{1,0:T(1,128)S(1)}, f32[1,2048]{1,0:T(1,128)S(1)}, u32[]{:S(2)}, u32[]{:S(2)}) collective-permute-start(f32[1,2048]{1,0:T(1,128)S(1)} %add_add_fusion.refs_0_), channel_id=1, source_target_pairs={{0,1},{1,0},{2,3},{3,2},{4,5},{5,4},{6,7},{7,6},{8,9},{9,8},{10,11... | collective-permute-start | bytes 24584 | tf_op jit(solution)/shard_map/ppermute | solution.py:29
  134.4 11.2 %collective-permute-start.43 = (f32[1,2048]{1,0:T(1,128)S(1)}, f32[1,2048]{1,0:T(1,128)S(1)}, u32[]{:S(2)}, u32[]{:S(2)}) collective-permute-start(f32[1,2048]{1,0:T(1,128)S(1)} %add_add_fusion.refs_0_), channel_id=1, source_target_pairs={{0,2},{1,3},{2,0},{3,1},{4,6},{5,7},{6,4},{7,5},{8,10},{9,11},{10,... | collective-permute-start | bytes 24584 | tf_op jit(solution)/shard_map/ppermute | solution.py:29
  137.0 8.6 %collective-permute-start.44 = (f32[1,2048]{1,0:T(1,128)S(1)}, f32[1,2048]{1,0:T(1,128)S(1)}, u32[]{:S(2)}, u32[]{:S(2)}) collective-permute-start(f32[1,2048]{1,0:T(1,128)S(1)} %add_add_fusion.refs_0_), channel_id=1, source_target_pairs={{0,3},{1,2},{2,1},{3,0},{4,7},{5,6},{6,5},{7,4},{8,11},{9,10},{10,... | collective-permute-start | bytes 24584 | tf_op jit(solution)/shard_map/ppermute | solution.py:29
  (21 other events, 110.8 us)

commit v5 on v4

--- a/solution.py
+++ b/solution.py
@@ -9,6 +9,7 @@
 
 EPSILON = 1e-06
 SEGMENTS = 8
+LARGE = 1e37
 F32 = jnp.float32
 BF16 = jnp.bfloat16
 
@@ -188,16 +189,25 @@
 
 
 def gates(x):
-    small = jnp.exp(-jnp.abs(x))
-    large = 1.0 / (1.0 + small)
-    small = small * large
-    up = x >= 0
-    return jnp.where(up, large, small), jnp.where(up, small, large)
+    under = 1.0 + jnp.minimum(jnp.exp(-x), LARGE)
+    rough = pl.reciprocal(under, approx=True)
+    update = rough * (2.0 - under * rough)
+    return update, 1.0 - update
 
 
 def slab_pair(ref, pair, span):
-    both = ref[pair * 2 * SEGMENTS : (pair + 1) * 2 * SEGMENTS, span].astype(F32)
+    return split(ref[pair * 2 * SEGMENTS : (pair + 1) * 2 * SEGMENTS, span])
+
+
+def split(both):
+    both = both.astype(F32)
     return both[:SEGMENTS], both[SEGMENTS:]
+
+
+def chosen_pair(where_ref, first_ref, second_ref, pair, span):
+    here = slice(pair * 2 * SEGMENTS, (pair + 1) * 2 * SEGMENTS)
+    gate, cand = choose(where_ref, first_ref[here, span], second_ref[here, span])
+    return split(gate), split(cand)
 
 
 def choose(where_ref, one, other):
@@ -227,9 +237,8 @@
             keep = jnp.ones((SEGMENTS, tile), F32)
             state = leaving = jnp.zeros((SEGMENTS, tile), F32)
             for pair in range(pairs):
-                slabs = [slab_pair(ref, pair, span) for ref in (first_ref, second_ref, back_ref)]
-                for a, b, g in zip(*slabs):
-                    gate, cand = choose(where_ref, a, b)
+                slabs = chosen_pair(where_ref, first_ref, second_ref, pair, span)
+                for gate, cand, g in zip(*slabs, slab_pair(back_ref, pair, span)):
                     update, retain = gates(gate + bias)
                     keep = keep * retain
                     state = retain * state + update * cand
@@ -303,8 +312,7 @@
 
             for pair in range(pairs):
                 states, retains, ups, slope = [], [], [], []
-                for a, b in zip(slab_pair(first_ref, pair, span), slab_pair(second_ref, pair, span)):
-                    gate, cand = choose(where_ref, a, b)
+                for gate, cand in zip(*chosen_pair(where_ref, first_ref, second_ref, pair, span)):
                     update, retain = gates(gate + bias)
                     retains.append(retain)
                     ups.append(update)
@@ -329,9 +337,9 @@
                 gate_grad = carried * slope
                 cand_grad = carried * update
                 total = total + gate_grad[:SEGMENTS] + gate_grad[SEGMENTS:]
-                one, other = choose(where_ref, gate_grad, cand_grad)
-                one_hold[here, :] = one.astype(BF16)
-                other_hold[here, :] = other.astype(BF16)
+                one, other = choose(where_ref, gate_grad.astype(BF16), cand_grad.astype(BF16))
+                one_hold[here, :] = one
+                other_hold[here, :] = other
             bias_grad_ref[:, span] = jnp.sum(total, axis=0, keepdims=True)
             state_ref[:, span] = dot(order, state_hold[...]).astype(BF16)
             one_ref[span, :] = dot(order, one_hold[...]).T.astype(BF16)
@@ -469,12 +477,14 @@
     f2b, f4b = send(f_b, 2), send(f_b, 4)
     t2a, t4a = send(t_a, 2), send(t_a, 4)
     sa = over(stack(f2a, f4a))
-    f2b, f4b, f3a, f5a, s1 = after((f2b, f4b, f2a, f4a, own_s))
-    f3a, f5a, s1 = core(f3a), core(f5a), core(s1)
-    f2b, f4b, sa, t2a, t4a, f3a, f5a, s1, t_b, f2a = after((f2b, f4b, sa, t2a, t4a, f3a, f5a, s1, t_b, f2a))
+    f2b, f4b, f3a, f5a = after((f2b, f4b, f2a, f4a))
+    f3a, f5a = core(f3a), core(f5a)
+    f2b, f4b, f_b2, sa, t2a, t4a, f3a, f5a, t_b, f2a = after(
+        (f2b, f4b, stack(f2b, f4b), sa, t2a, t4a, f3a, f5a, t_b, f2a)
+    )
     f6a, f6b = send(f2a, 4), send(f4b, 2)
     t2b, t4b = send(t_b, 2), send(t_b, 4)
-    sb = over(stack(f2b, f4b))
+    sb = over(f_b2)
     f6a, f6b, f3b, f5b, t3a, t5a = after((f6a, f6b, f2b, f4b, t2a, t4a))
     f3b, f5b, t3a, t5a = core(f3b), core(f5b), core(t3a), core(t5a)
     both, f6a, f6b, sb, t2b, t4b, f3b, f5b, t3a, t5a, sa, t2a = after(
@@ -482,10 +492,10 @@
     )
     t6a, t6b = send(t2a, 4), send(t4b, 2)
     s6a = over(f6a)
-    f7, cs = core(stack(f6a, f6b)), core(stack(sa, sb))
+    f7, cs = core(stack(f6a, f6b)), core(stack(sa, sb, own_s))
     first = Shards([own_f, [f1a, f1b], [f2a, f2b], [f3a, f3b], [f4a, f4b], [f5a, f5b], [f6a, f6b], [f7]])
     pairs = lambda one, two, row: cut(one, row) + cut(two, row)
-    most = [[own_s], [s1], pairs(sa, sb, 0), cut(cs, 0, 2), pairs(sa, sb, 1), cut(cs, 1, 3)]
+    most = [[own_s], cut(cs, 4, 5), pairs(sa, sb, 0), cut(cs, 0, 2), pairs(sa, sb, 1), cut(cs, 1, 3)]
     first_pre = project_call(normed, first, tile, BF16)
     partial = project_call(normed, Shards(most), tile, F32)
     t6a, t6b, s6a, sb_out, first_pre, partial, own_t, both = after(

time: 147 us -> 140 us (0.952)
  waiting for transfers between devices: 70.6 us -> 62.6 us
    ppermute x39 -> x38, waiting for transfers between devices: 68.2 us -> 60.5 us  [hop(): return lax.ppermute(value, 'seq', [(i, i ^ offset) for i in range(count)])]
    ppermute x39 -> x38, starting transfers between devices: 28.2 us -> 29.3 us  [hop(): return lax.ppermute(value, 'seq', [(i, i ^ offset) for i in range(count)])]
  transfers between devices with their start and end apart: 45 -> 44, of which waited for: 27 -> 26; matrix products, arithmetic and copies ran while one was open for 1% -> 1% of each run, Pallas kernels for 17% -> 18%
where the time goes in v5:
time: 140 us
  waiting for transfers between devices  62.6 us (45%)
  starting transfers between devices  38.6 us (28%)
  Pallas kernels  33.6 us (24%)
  other arithmetic  3.47 us (2%)
    ppermute x38, waiting for transfers between devices, hop(): return lax.ppermute(value, 'seq', [(i, i ^ offset) for i in range(count)])  60.5 us
    ppermute x38, starting transfers between devices, hop(): return lax.ppermute(value, 'seq', [(i, i ^ offset) for i in range(count)])  29.3 us
    ppermute x6, starting transfers between devices, swap_batch(): return lax.ppermute(value, 'batch', [(i, i ^ offset) for i in range(count)])  9.25 us
    pallas_call x1, Pallas kernels, input_grad_call(): pl.pallas_call(kernel, out_shape=jax.ShapeDtypeStruct((rows, width), BF16...  8.38 us
    pallas_call x2, Pallas kernels, project_call(): pl.pallas_call(kernel, out_shape=jax.ShapeDtypeStruct((rows, width), dtyp...  5.15 us
    pallas_call x1, Pallas kernels, layer_call(): pl.pallas_call(kernel, out_shape=jax.ShapeDtypeStruct((rows, width), BF16...  4.73 us
    pallas_call x1, Pallas kernels, scan_call(): pl.pallas_call(kernel, out_shape=[wide, tall, tall, flat, flat], in_specs...  4.62 us
    pallas_call x1, Pallas kernels, totals_call(): pl.pallas_call(kernel, out_shape=[jax.ShapeDtypeStruct((rows, width), BF1...  3.3 us
  transfers between devices with their start and end apart: 44, of which 26 were waited for; matrix products, arithmetic and copies ran while one was open for 1% of the time, Pallas kernels for 18%

profile of v5, /device:TPU:0, one launch (start us, length us, event | category | flops | bytes accessed | tf_op | source)
XLA Modules:
  0.0 139.6 jit_solution(11469749657665365938)
XLA Ops:
  2.2 3.0 %collective-permute-start = (bf16[128,2048]{1,0:T(8,128)(2,1)S(1)}, bf16[128,2048]{1,0:T(8,128)(2,1)S(1)}, u32[]{:S(2)}, u32[]{:S(2)}) collective-permute-start(bf16[128,2048]{1,0:T(8,128)(2,1)S(1)} %slice_select_fusion.1.refs_0_), channel_id=1, source_target_pairs={{0,8},{4,12},{8,0},{12,4},{16,24},{20,28},{24,16},{28,20},{1,9},{5... | collective-permute-start | bytes 1572872 | tf_op jit(solution)/shard_map/ppermute | solution.py:26
  5.2 1.5 %collective-permute-start.1 = (bf16[128,2048]{1,0:T(8,128)(2,1)S(1)}, bf16[128,2048]{1,0:T(8,128)(2,1)S(1)}, u32[]{:S(2)}, u32[]{:S(2)}) collective-permute-start(bf16[128,2048]{1,0:T(8,128)(2,1)S(1)} %slice_select_fusion.1.refs_0_), channel_id=1, source_target_pairs={{0,16},{4,20},{8,24},{12,28},{16,0},{20,4},{24,8},{28,12},{1,17},{... | collective-permute-start | bytes 1572872 | tf_op jit(solution)/shard_map/ppermute | solution.py:26
  10.7 3.3 %norm_rows.1 = (bf16[256,2048]{1,0:T(8,128)(2,1)S(1)}, bf16[2048,256]{1,0:T(8,128)(2,1)S(1)}) custom-call(s32[3]{0:T(128)S(1)} %pad_add_fusion.where_ref, bf16[256,2048]{1,0:T(8,128)(2,1)S(1)} %bitcast.11, bf16[256,2048]{1,0:T(8,128)(2,1)S(1)} %bitcast.14, f32[1,2048]{1,0:T(1,128)S(1)} %bitcast.16), custom_call_target="tpu_custom_call" | custom-call | flops 536870912 | bytes 4194304 | tf_op jit(solution)/shard_map/norm_rows/pallas_call | solution.py:132
  13.9 3.3 %collective-permute-done.5 = f32[2,512]{1,0:T(2,128)S(1)} collective-permute-done((f32[2,512]{1,0:T(2,128)S(1)}, f32[2,512]{1,0:T(2,128)S(1)}, u32[]{:S(2)}, u32[]{:S(2)}) %collective-permute-start.5) | collective-permute-done | bytes 4128 | tf_op jit(solution)/shard_map/ppermute | solution.py:26
  19.1 1.6 %collective-permute-start.7 = (bf16[128,2048]{1,0:T(8,128)(2,1)S(1)}, bf16[128,2048]{1,0:T(8,128)(2,1)S(1)}, u32[]{:S(2)}, u32[]{:S(2)}) collective-permute-start(bf16[128,2048]{1,0:T(8,128)(2,1)S(1)} %slice_select_fusion.refs_1_), channel_id=1, source_target_pairs={{0,16},{4,20},{8,24},{12,28},{16,0},{20,4},{24,8},{28,12},{1,17},{... | collective-permute-start | bytes 1572872 | tf_op jit(solution)/shard_map/ppermute | solution.py:26
  20.8 1.6 %collective-permute-start.8 = (bf16[256,2048]{1,0:T(8,128)(2,1)S(1)}, bf16[256,2048]{1,0:T(8,128)(2,1)S(1)}, u32[]{:S(2)}, u32[]{:S(2)}) collective-permute-start(bf16[256,2048]{1,0:T(8,128)(2,1)S(1)} %pad_maximum_fusion.2), channel_id=1, source_target_pairs={{0,1},{1,0},{2,3},{3,2},{4,5},{5,4},{6,7},{7,6},{8,9},{9,8},{10,11... | collective-permute-start | bytes 3145736 | tf_op jit(solution)/shard_map/ppermute | solution.py:30
  22.9 1.5 %collective-permute-start.9 = (bf16[128,2048]{1,0:T(8,128)(2,1)S(1)}, bf16[128,2048]{1,0:T(8,128)(2,1)S(1)}, u32[]{:S(2)}, u32[]{:S(2)}) collective-permute-start(bf16[128,2048]{1,0:T(8,128)(2,1)S(1)} %get-tuple-element.100), channel_id=1, source_target_pairs={{0,8},{4,12},{8,0},{12,4},{16,24},{20,28},{24,16},{28,20},{1,9},{5... | collective-permute-start | bytes 1572872 | tf_op jit(solution)/shard_map/ppermute | solution.py:26
  24.4 9.1 %collective-permute-done.6.refs_5_ = bf16[128,2048]{1,0:T(8,128)(2,1)S(1)} collective-permute-done((bf16[128,2048]{1,0:T(8,128)(2,1)S(1)}, bf16[128,2048]{1,0:T(8,128)(2,1)S(1)}, u32[]{:S(2)}, u32[]{:S(2)}) %collective-permute-start.6) | collective-permute-done | bytes 524320 | tf_op jit(solution)/shard_map/ppermute | solution.py:26
  34.5 8.3 %collective-permute-done.10.refs_5_ = bf16[128,2048]{1,0:T(8,128)(2,1)S(1)} collective-permute-done((bf16[128,2048]{1,0:T(8,128)(2,1)S(1)}, bf16[128,2048]{1,0:T(8,128)(2,1)S(1)}, u32[]{:S(2)}, u32[]{:S(2)}) %collective-permute-start.10) | collective-permute-done | bytes 524320 | tf_op jit(solution)/shard_map/ppermute | solution.py:26
  46.8 1.5 %collective-permute-start.17 = (bf16[128,2048]{1,0:T(8,128)(2,1)S(1)}, bf16[128,2048]{1,0:T(8,128)(2,1)S(1)}, u32[]{:S(2)}, u32[]{:S(2)}) collective-permute-start(bf16[128,2048]{1,0:T(8,128)(2,1)S(1)} %get-tuple-element.112), channel_id=1, source_target_pairs={{0,16},{4,20},{8,24},{12,28},{16,0},{20,4},{24,8},{28,12},{1,17},{... | collective-permute-start | bytes 1572872 | tf_op jit(solution)/shard_map/ppermute | solution.py:26
  48.3 1.6 %collective-permute-start.15 = (bf16[256,2048]{1,0:T(8,128)(2,1)S(1)}, bf16[256,2048]{1,0:T(8,128)(2,1)S(1)}, u32[]{:S(2)}, u32[]{:S(2)}) collective-permute-start(bf16[256,2048]{1,0:T(8,128)(2,1)S(1)} %pad_maximum_fusion.1), channel_id=1, source_target_pairs={{0,1},{1,0},{2,3},{3,2},{4,5},{5,4},{6,7},{7,6},{8,9},{9,8},{10,11... | collective-permute-start | bytes 3145736 | tf_op jit(solution)/shard_map/ppermute | solution.py:30
  49.9 9.2 %collective-permute-done.13.refs_12_ = bf16[128,2048]{1,0:T(8,128)(2,1)S(1)} collective-permute-done((bf16[128,2048]{1,0:T(8,128)(2,1)S(1)}, bf16[128,2048]{1,0:T(8,128)(2,1)S(1)}, u32[]{:S(2)}, u32[]{:S(2)}) %collective-permute-start.13) | collective-permute-done | bytes 524320 | tf_op jit(solution)/shard_map/ppermute | solution.py:26
  60.1 6.9 %collective-permute-done.16.refs_3_ = bf16[128,2048]{1,0:T(8,128)(2,1)S(1)} collective-permute-done((bf16[128,2048]{1,0:T(8,128)(2,1)S(1)}, bf16[128,2048]{1,0:T(8,128)(2,1)S(1)}, u32[]{:S(2)}, u32[]{:S(2)}) %collective-permute-start.16) | collective-permute-done | bytes 524320 | tf_op jit(solution)/shard_map/ppermute | solution.py:26
  70.7 1.5 %collective-permute-start.22 = (bf16[128,2048]{1,0:T(8,128)(2,1)S(1)}, bf16[128,2048]{1,0:T(8,128)(2,1)S(1)}, u32[]{:S(2)}, u32[]{:S(2)}) collective-permute-start(bf16[128,2048]{1,0:T(8,128)(2,1)S(1)} %collective-permute-done.9.refs_2_), channel_id=1, source_target_pairs={{0,16},{4,20},{8,24},{12,28},{16,0},{20,4},{24,8},{28,12},{1,17},{... | collective-permute-start | bytes 1572872 | tf_op jit(solution)/shard_map/ppermute | solution.py:26
  73.1 1.6 %collective-permute-start.24 = (bf16[128,2048]{1,0:T(8,128)(2,1)S(1)}, bf16[128,2048]{1,0:T(8,128)(2,1)S(1)}, u32[]{:S(2)}, u32[]{:S(2)}) collective-permute-start(bf16[128,2048]{1,0:T(8,128)(2,1)S(1)} %collective-permute-done.13.refs_12_), channel_id=1, source_target_pairs={{0,1},{1,0},{2,3},{3,2},{4,5},{5,4},{6,7},{7,6},{8,9},{9,8},{10,11... | collective-permute-start | bytes 1572872 | tf_op jit(solution)/shard_map/ppermute | solution.py:30
  74.7 2.5 %collective-permute-done.25.refs_14_ = bf16[256,2048]{1,0:T(8,128)(2,1)S(1)} collective-permute-done((bf16[256,2048]{1,0:T(8,128)(2,1)S(1)}, bf16[256,2048]{1,0:T(8,128)(2,1)S(1)}, u32[]{:S(2)}, u32[]{:S(2)}) %collective-permute-start.25) | collective-permute-done | bytes 1048608 | tf_op jit(solution)/shard_map/ppermute | solution.py:26
  77.2 2.9 %project.2.first_ref = bf16[256,2048]{1,0:T(8,128)(2,1)S(1)} custom-call(bf16[256,2048]{1,0:T(8,128)(2,1)S(1)} %get-tuple-element.122.x_ref, bf16[128,2048]{1,0:T(8,128)(2,1)S(1)} %slice_select_fusion.1.refs_0_, bf16[128,2048]{1,0:T(8,128)(2,1)S(1)} %slice_select_fusion.refs_1_, bf16[128,2048]{1,0:T(8,128)(2,1)S(1)} %collective-permute-done.2.refs_2_, ...), custom_call_target="tpu_custom_call" | custom-call | flops 2147483648 | bytes 8388608 | tf_op jit(solution)/shard_map/project/pallas_call | solution.py:156
  80.1 2.3 %project.3.refs_0_ = f32[256,2048]{1,0:T(8,128)S(1)} custom-call(bf16[256,2048]{1,0:T(8,128)(2,1)S(1)} %get-tuple-element.122.x_ref, bf16[256,2048]{1,0:T(8,128)(2,1)S(1)} %broadcast_select_fusion.refs_0_.refs_15_, bf16[768,2048]{1,0:T(8,128)(2,1)S(1)} %collective-permute-done.26.refs_1_.refs_16_, ...), custom_call_target="tpu_custom_call" | custom-call | flops 1610612736 | bytes 6291456 | tf_op jit(solution)/shard_map/project/pallas_call | solution.py:156
  82.4 2.3 %collective-permute-done.22.refs_8_ = bf16[128,2048]{1,0:T(8,128)(2,1)S(1)} collective-permute-done((bf16[128,2048]{1,0:T(8,128)(2,1)S(1)}, bf16[128,2048]{1,0:T(8,128)(2,1)S(1)}, u32[]{:S(2)}, u32[]{:S(2)}) %collective-permute-start.22) | collective-permute-done | bytes 524320 | tf_op jit(solution)/shard_map/ppermute | solution.py:26
  88.8 1.5 %collective-permute-start.28 = (bf16[64,2048]{1,0:T(8,128)(2,1)S(1)}, bf16[64,2048]{1,0:T(8,128)(2,1)S(1)}, u32[]{:S(2)}, u32[]{:S(2)}) collective-permute-start(bf16[64,2048]{1,0:T(8,128)(2,1)S(1)} %get-tuple-element.170), channel_id=1, source_target_pairs={{0,16},{4,20},{8,24},{12,28},{16,0},{20,4},{24,8},{28,12},{1,17},{... | collective-permute-start | bytes 786440 | tf_op jit(solution)/shard_map/ppermute | solution.py:26
  90.6 1.9 %collective-permute-done.30.refs_1_ = bf16[768,2048]{1,0:T(8,128)(2,1)S(1)} collective-permute-done((bf16[768,2048]{1,0:T(8,128)(2,1)S(1)}, bf16[768,2048]{1,0:T(8,128)(2,1)S(1)}, u32[]{:S(2)}, u32[]{:S(2)}) %collective-permute-start.30) | collective-permute-done | bytes 3145760 | tf_op jit(solution)/shard_map/ppermute | solution.py:26
  92.5 3.0 %back_rows.1.back_ref = bf16[256,2048]{1,0:T(8,128)(2,1)S(1)} custom-call(s32[3]{0:T(128)S(1)} %pad_add_fusion.where_ref, bf16[2048,256]{1,0:T(8,128)(2,1)S(1)} %get-tuple-element.137.g_ref, bf16[256,2048]{1,0:T(8,128)(2,1)S(1)} %copy-done, bf16[768,2048]{1,0:T(8,128)(2,1)S(1)} %collective-permute-done.30.refs_1_, ...), custom_call_target="tpu_custom_call" | custom-call | flops 2147483648 | bytes 8388608 | tf_op jit(solution)/shard_map/back_rows/pallas_call | solution.py:180
  97.3 1.9 %collective-permute-done.32.refs_5_.refs_23_ = bf16[128,2048]{1,0:T(8,128)(2,1)S(1)} collective-permute-done((bf16[128,2048]{1,0:T(8,128)(2,1)S(1)}, bf16[128,2048]{1,0:T(8,128)(2,1)S(1)}, u32[]{:S(2)}, u32[]{:S(2)}) %collective-permute-start.32) | collective-permute-done | bytes 524320 | tf_op jit(solution)/shard_map/ppermute | solution.py:26
  99.2 3.3 %project_totals.1 = (bf16[256,2048]{1,0:T(8,128)(2,1)S(1)}, f32[3,8,2048]{2,1,0:T(8,128)S(1)}, f32[3,2048]{1,0:T(4,128)S(1)}, f32[2,2048]{1,0:T(2,128)S(1)}) custom-call(s32[3]{0:T(128)S(1)} %pad_add_fusion.where_ref, bf16[256,2048]{1,0:T(8,128)(2,1)S(1)} %get-tuple-element.122.x_ref, bf16[256,2048]{1,0:T(8,128)(2,1)S(1)} %project.2.first_ref, ...), custom_call_target="tpu_custom_call" | custom-call | flops 536870912 | bytes 2097152 | tf_op jit(solution)/shard_map/project_totals/pallas_call | solution.py:258
  104.7 1.5 %collective-permute-start.35 = (f32[2,3,2048]{2,1,0:T(4,128)S(1)}, f32[2,3,2048]{2,1,0:T(4,128)S(1)}, u32[]{:S(2)}, u32[]{:S(2)}) collective-permute-start(f32[2,3,2048]{2,1,0:T(4,128)S(1)} %pad_maximum_fusion.5.refs_0_), channel_id=1, source_target_pairs={{0,16},{4,20},{8,24},{12,28},{16,0},{20,4},{24,8},{28,12},{1,17},{... | collective-permute-start | bytes 147464 | tf_op jit(solution)/shard_map/ppermute | solution.py:26
  109.0 2.4 %collective-permute-done.36.refs_3_ = f32[2,3,2048]{2,1,0:T(4,128)S(1)} collective-permute-done((f32[2,3,2048]{2,1,0:T(4,128)S(1)}, f32[2,3,2048]{2,1,0:T(4,128)S(1)}, u32[]{:S(2)}, u32[]{:S(2)}) %collective-permute-start.36) | collective-permute-done | bytes 49184 | tf_op jit(solution)/shard_map/ppermute | solution.py:26
  111.4 4.6 %scan_rows.1 = (bf16[256,2048]{1,0:T(8,128)(2,1)S(1)}, bf16[2048,256]{1,0:T(8,128)(2,1)S(1)}, bf16[2048,256]{1,0:T(8,128)(2,1)S(1)}, f32[1,2048]{1,0:T(1,128)S(1)}, f32[1,2048]{1,0:T(1,128)S(1)}) custom-call(s32[3]{0:T(128)S(1)} %pad_add_fusion.where_ref, bf16[256,2048]{1,0:T(8,128)(2,1)S(1)} %project.2.first_ref, ...), custom_call_target="tpu_custom_call" | custom-call | flops 805306368 | bytes 6291456 | tf_op jit(solution)/shard_map/scan_rows/pallas_call | solution.py:353
  119.0 1.8 %collective-permute-start.40 = (f32[1,2048]{1,0:T(1,128)S(1)}, f32[1,2048]{1,0:T(1,128)S(1)}, u32[]{:S(2)}, u32[]{:S(2)}) collective-permute-start(f32[1,2048]{1,0:T(1,128)S(1)} %add.17), channel_id=1, source_target_pairs={{0,24},{4,28},{8,16},{12,20},{16,8},{20,12},{24,0},{28,4},{1,25},{... | collective-permute-start | bytes 24584 | tf_op jit(solution)/shard_map/ppermute | solution.py:26
  120.8 4.7 %layer_rows.1 = bf16[256,2048]{1,0:T(8,128)(2,1)} custom-call(s32[3]{0:T(128)S(1)} %pad_add_fusion.where_ref, bf16[256,2048]{1,0:T(8,128)(2,1)S(1)} %get-tuple-element.155.x_ref, bf16[256,2048]{1,0:T(8,128)(2,1)S(1)} %bitcast.12, bf16[256,2048]{1,0:T(8,128)(2,1)S(1)} %copy-done, bf16[768,2048]{1,0:T(8,128)(2,1)S(1)} %collective-permute-done.30.refs_1_, ...), custom_call_target="tpu_custom_call" | custom-call | flops 2147483648 | bytes 8388608 | tf_op jit(solution)/shard_map/layer_rows/pallas_call | solution.py:383
  125.6 1.6 %collective-permute-start.41 = (f32[1,2048]{1,0:T(1,128)S(1)}, f32[1,2048]{1,0:T(1,128)S(1)}, u32[]{:S(2)}, u32[]{:S(2)}) collective-permute-start(f32[1,2048]{1,0:T(1,128)S(1)} %add_add_fusion.refs_0_), channel_id=1, source_target_pairs={{0,1},{1,0},{2,3},{3,2},{4,5},{5,4},{6,7},{7,6},{8,9},{9,8},{10,11... | collective-permute-start | bytes 24584 | tf_op jit(solution)/shard_map/ppermute | solution.py:30
  127.3 2.6 %collective-permute-start.42 = (f32[1,2048]{1,0:T(1,128)S(1)}, f32[1,2048]{1,0:T(1,128)S(1)}, u32[]{:S(2)}, u32[]{:S(2)}) collective-permute-start(f32[1,2048]{1,0:T(1,128)S(1)} %add_add_fusion.refs_0_), channel_id=1, source_target_pairs={{0,2},{1,3},{2,0},{3,1},{4,6},{5,7},{6,4},{7,5},{8,10},{9,11},{10,... | collective-permute-start | bytes 24584 | tf_op jit(solution)/shard_map/ppermute | solution.py:30
  130.1 8.4 %input_grad_rows.1 = bf16[256,2048]{1,0:T(8,128)(2,1)} custom-call(s32[3]{0:T(128)S(1)} %pad_add_fusion.where_ref, bf16[2048,256]{1,0:T(8,128)(2,1)S(1)} %get-tuple-element.164.one_ref, bf16[2048,256]{1,0:T(8,128)(2,1)S(1)} %get-tuple-element.165.other_ref, bf16[256,2048]{1,0:T(8,128)(2,1)S(1)} %bitcast.13, bf16[256,2048]{1,0:T(8,128)(2,1)S(1)} %bitcast.15, ...), custom_call_target="tpu_custom_call" | custom-call | flops 4294967296 | bytes 16777216 | tf_op jit(solution)/shard_map/input_grad_rows/pallas_call | solution.py:423
  (104 shorter events, 34.0 us)
Async XLA Ops:
  2.2 15.0 %collective-permute-start = (bf16[128,2048]{1,0:T(8,128)(2,1)S(1)}, bf16[128,2048]{1,0:T(8,128)(2,1)S(1)}, u32[]{:S(2)}, u32[]{:S(2)}) collective-permute-start(bf16[128,2048]{1,0:T(8,128)(2,1)S(1)} %slice_select_fusion.1.refs_0_), channel_id=1, source_target_pairs={{0,8},{4,12},{8,0},{12,4},{16,24},{20,28},{24,16},{28,20},{1,9},{5... | collective-permute-start | bytes 1572872 | tf_op jit(solution)/shard_map/ppermute | solution.py:26
  5.2 13.4 %collective-permute-start.1 = (bf16[128,2048]{1,0:T(8,128)(2,1)S(1)}, bf16[128,2048]{1,0:T(8,128)(2,1)S(1)}, u32[]{:S(2)}, u32[]{:S(2)}) collective-permute-start(bf16[128,2048]{1,0:T(8,128)(2,1)S(1)} %slice_select_fusion.1.refs_0_), channel_id=1, source_target_pairs={{0,16},{4,20},{8,24},{12,28},{16,0},{20,4},{24,8},{28,12},{1,17},{... | collective-permute-start | bytes 1572872 | tf_op jit(solution)/shard_map/ppermute | solution.py:26
  6.7 11.9 %collective-permute-start.2 = (bf16[128,2048]{1,0:T(8,128)(2,1)S(1)}, bf16[128,2048]{1,0:T(8,128)(2,1)S(1)}, u32[]{:S(2)}, u32[]{:S(2)}) collective-permute-start(bf16[128,2048]{1,0:T(8,128)(2,1)S(1)} %slice_select_fusion.1.refs_0_), channel_id=1, source_target_pairs={{0,4},{4,0},{8,12},{12,8},{16,20},{20,16},{24,28},{28,24},{1,5},{5... | collective-permute-start | bytes 1572872 | tf_op jit(solution)/shard_map/ppermute | solution.py:26
  8.0 9.2 %collective-permute-start.3 = (bf16[128,2048]{1,0:T(8,128)(2,1)S(1)}, bf16[128,2048]{1,0:T(8,128)(2,1)S(1)}, u32[]{:S(2)}, u32[]{:S(2)}) collective-permute-start(bf16[128,2048]{1,0:T(8,128)(2,1)S(1)} %slice_select_fusion.refs_1_), channel_id=1, source_target_pairs={{0,4},{4,0},{8,12},{12,8},{16,20},{20,16},{24,28},{28,24},{1,5},{5... | collective-permute-start | bytes 1572872 | tf_op jit(solution)/shard_map/ppermute | solution.py:26
  10.1 7.1 %collective-permute-start.5 = (f32[2,512]{1,0:T(2,128)S(1)}, f32[2,512]{1,0:T(2,128)S(1)}, u32[]{:S(2)}, u32[]{:S(2)}) collective-permute-start(f32[2,512]{1,0:T(2,128)S(1)} %pad_maximum_fusion.8), channel_id=1, source_target_pairs={{0,8},{4,12},{8,0},{12,4},{16,24},{20,28},{24,16},{28,20},{1,9},{5... | collective-permute-start | bytes 12296 | tf_op jit(solution)/shard_map/ppermute | solution.py:26
  18.6 14.9 %collective-permute-start.6 = (bf16[128,2048]{1,0:T(8,128)(2,1)S(1)}, bf16[128,2048]{1,0:T(8,128)(2,1)S(1)}, u32[]{:S(2)}, u32[]{:S(2)}) collective-permute-start(bf16[128,2048]{1,0:T(8,128)(2,1)S(1)} %slice_select_fusion.refs_1_), channel_id=1, source_target_pairs={{0,8},{4,12},{8,0},{12,4},{16,24},{20,28},{24,16},{28,20},{1,9},{5... | collective-permute-start | bytes 1572872 | tf_op jit(solution)/shard_map/ppermute | solution.py:26
  19.1 14.9 %collective-permute-start.7 = (bf16[128,2048]{1,0:T(8,128)(2,1)S(1)}, bf16[128,2048]{1,0:T(8,128)(2,1)S(1)}, u32[]{:S(2)}, u32[]{:S(2)}) collective-permute-start(bf16[128,2048]{1,0:T(8,128)(2,1)S(1)} %slice_select_fusion.refs_1_), channel_id=1, source_target_pairs={{0,16},{4,20},{8,24},{12,28},{16,0},{20,4},{24,8},{28,12},{1,17},{... | collective-permute-start | bytes 1572872 | tf_op jit(solution)/shard_map/ppermute | solution.py:26
  20.8 23.5 %collective-permute-start.8 = (bf16[256,2048]{1,0:T(8,128)(2,1)S(1)}, bf16[256,2048]{1,0:T(8,128)(2,1)S(1)}, u32[]{:S(2)}, u32[]{:S(2)}) collective-permute-start(bf16[256,2048]{1,0:T(8,128)(2,1)S(1)} %pad_maximum_fusion.2), channel_id=1, source_target_pairs={{0,1},{1,0},{2,3},{3,2},{4,5},{5,4},{6,7},{7,6},{8,9},{9,8},{10,11... | collective-permute-start | bytes 3145736 | tf_op jit(solution)/shard_map/ppermute | solution.py:30
  22.4 20.4 %collective-permute-start.10 = (bf16[128,2048]{1,0:T(8,128)(2,1)S(1)}, bf16[128,2048]{1,0:T(8,128)(2,1)S(1)}, u32[]{:S(2)}, u32[]{:S(2)}) collective-permute-start(bf16[128,2048]{1,0:T(8,128)(2,1)S(1)} %get-tuple-element.100), channel_id=1, source_target_pairs={{0,16},{4,20},{8,24},{12,28},{16,0},{20,4},{24,8},{28,12},{1,17},{... | collective-permute-start | bytes 1572872 | tf_op jit(solution)/shard_map/ppermute | solution.py:26
  22.9 19.9 %collective-permute-start.9 = (bf16[128,2048]{1,0:T(8,128)(2,1)S(1)}, bf16[128,2048]{1,0:T(8,128)(2,1)S(1)}, u32[]{:S(2)}, u32[]{:S(2)}) collective-permute-start(bf16[128,2048]{1,0:T(8,128)(2,1)S(1)} %get-tuple-element.100), channel_id=1, source_target_pairs={{0,8},{4,12},{8,0},{12,4},{16,24},{20,28},{24,16},{28,20},{1,9},{5... | collective-permute-start | bytes 1572872 | tf_op jit(solution)/shard_map/ppermute | solution.py:26
  34.0 10.3 %collective-permute-start.11 = (bf16[128,2048]{1,0:T(8,128)(2,1)S(1)}, bf16[128,2048]{1,0:T(8,128)(2,1)S(1)}, u32[]{:S(2)}, u32[]{:S(2)}) collective-permute-start(bf16[128,2048]{1,0:T(8,128)(2,1)S(1)} %collective-permute-done.refs_4_), channel_id=1, source_target_pairs={{0,4},{4,0},{8,12},{12,8},{16,20},{20,16},{24,28},{28,24},{1,5},{5... | collective-permute-start | bytes 1572872 | tf_op jit(solution)/shard_map/ppermute | solution.py:26
  34.0 10.3 %collective-permute-start.12 = (bf16[128,2048]{1,0:T(8,128)(2,1)S(1)}, bf16[128,2048]{1,0:T(8,128)(2,1)S(1)}, u32[]{:S(2)}, u32[]{:S(2)}) collective-permute-start(bf16[128,2048]{1,0:T(8,128)(2,1)S(1)} %collective-permute-done.1.refs_8_), channel_id=1, source_target_pairs={{0,4},{4,0},{8,12},{12,8},{16,20},{20,16},{24,28},{28,24},{1,5},{5... | collective-permute-start | bytes 1572872 | tf_op jit(solution)/shard_map/ppermute | solution.py:26
  44.3 14.9 %collective-permute-start.13 = (bf16[128,2048]{1,0:T(8,128)(2,1)S(1)}, bf16[128,2048]{1,0:T(8,128)(2,1)S(1)}, u32[]{:S(2)}, u32[]{:S(2)}) collective-permute-start(bf16[128,2048]{1,0:T(8,128)(2,1)S(1)} %collective-permute-done.refs_4_), channel_id=1, source_target_pairs={{0,16},{4,20},{8,24},{12,28},{16,0},{20,4},{24,8},{28,12},{1,17},{... | collective-permute-start | bytes 1572872 | tf_op jit(solution)/shard_map/ppermute | solution.py:26
  44.8 14.9 %collective-permute-start.14 = (bf16[128,2048]{1,0:T(8,128)(2,1)S(1)}, bf16[128,2048]{1,0:T(8,128)(2,1)S(1)}, u32[]{:S(2)}, u32[]{:S(2)}) collective-permute-start(bf16[128,2048]{1,0:T(8,128)(2,1)S(1)} %collective-permute-done.7.refs_9_), channel_id=1, source_target_pairs={{0,8},{4,12},{8,0},{12,4},{16,24},{20,28},{24,16},{28,20},{1,9},{5... | collective-permute-start | bytes 1572872 | tf_op jit(solution)/shard_map/ppermute | solution.py:26
  46.0 21.0 %collective-permute-start.16 = (bf16[128,2048]{1,0:T(8,128)(2,1)S(1)}, bf16[128,2048]{1,0:T(8,128)(2,1)S(1)}, u32[]{:S(2)}, u32[]{:S(2)}) collective-permute-start(bf16[128,2048]{1,0:T(8,128)(2,1)S(1)} %get-tuple-element.112), channel_id=1, source_target_pairs={{0,8},{4,12},{8,0},{12,4},{16,24},{20,28},{24,16},{28,20},{1,9},{5... | collective-permute-start | bytes 1572872 | tf_op jit(solution)/shard_map/ppermute | solution.py:26
  46.8 20.2 %collective-permute-start.17 = (bf16[128,2048]{1,0:T(8,128)(2,1)S(1)}, bf16[128,2048]{1,0:T(8,128)(2,1)S(1)}, u32[]{:S(2)}, u32[]{:S(2)}) collective-permute-start(bf16[128,2048]{1,0:T(8,128)(2,1)S(1)} %get-tuple-element.112), channel_id=1, source_target_pairs={{0,16},{4,20},{8,24},{12,28},{16,0},{20,4},{24,8},{28,12},{1,17},{... | collective-permute-start | bytes 1572872 | tf_op jit(solution)/shard_map/ppermute | solution.py:26
  48.3 21.4 %collective-permute-start.15 = (bf16[256,2048]{1,0:T(8,128)(2,1)S(1)}, bf16[256,2048]{1,0:T(8,128)(2,1)S(1)}, u32[]{:S(2)}, u32[]{:S(2)}) collective-permute-start(bf16[256,2048]{1,0:T(8,128)(2,1)S(1)} %pad_maximum_fusion.1), channel_id=1, source_target_pairs={{0,1},{1,0},{2,3},{3,2},{4,5},{5,4},{6,7},{7,6},{8,9},{9,8},{10,11... | collective-permute-start | bytes 3145736 | tf_op jit(solution)/shard_map/ppermute | solution.py:30
  59.6 7.9 %collective-permute-start.18 = (bf16[128,2048]{1,0:T(8,128)(2,1)S(1)}, bf16[128,2048]{1,0:T(8,128)(2,1)S(1)}, u32[]{:S(2)}, u32[]{:S(2)}) collective-permute-start(bf16[128,2048]{1,0:T(8,128)(2,1)S(1)} %collective-permute-done.6.refs_5_), channel_id=1, source_target_pairs={{0,4},{4,0},{8,12},{12,8},{16,20},{20,16},{24,28},{28,24},{1,5},{5... | collective-permute-start | bytes 1572872 | tf_op jit(solution)/shard_map/ppermute | solution.py:26
  59.6 7.9 %collective-permute-start.19 = (bf16[128,2048]{1,0:T(8,128)(2,1)S(1)}, bf16[128,2048]{1,0:T(8,128)(2,1)S(1)}, u32[]{:S(2)}, u32[]{:S(2)}) collective-permute-start(bf16[128,2048]{1,0:T(8,128)(2,1)S(1)} %collective-permute-done.7.refs_9_), channel_id=1, source_target_pairs={{0,4},{4,0},{8,12},{12,8},{16,20},{20,16},{24,28},{28,24},{1,5},{5... | collective-permute-start | bytes 1572872 | tf_op jit(solution)/shard_map/ppermute | solution.py:26
  70.0 10.1 %collective-permute-start.26 = (bf16[768,2048]{1,0:T(8,128)(2,1)S(1)}, bf16[768,2048]{1,0:T(8,128)(2,1)S(1)}, u32[]{:S(2)}, u32[]{:S(2)}) collective-permute-start(bf16[768,2048]{1,0:T(8,128)(2,1)S(1)} %pad_maximum_fusion), channel_id=1, source_target_pairs={{0,4},{4,0},{8,12},{12,8},{16,20},{20,16},{24,28},{28,24},{1,5},{5... | collective-permute-start | bytes 9437192 | tf_op jit(solution)/shard_map/ppermute | solution.py:26
  70.2 7.0 %collective-permute-start.25 = (bf16[256,2048]{1,0:T(8,128)(2,1)S(1)}, bf16[256,2048]{1,0:T(8,128)(2,1)S(1)}, u32[]{:S(2)}, u32[]{:S(2)}) collective-permute-start(bf16[256,2048]{1,0:T(8,128)(2,1)S(1)} %pad_maximum_fusion.3), channel_id=1, source_target_pairs={{0,4},{4,0},{8,12},{12,8},{16,20},{20,16},{24,28},{28,24},{1,5},{5... | collective-permute-start | bytes 3145736 | tf_op jit(solution)/shard_map/ppermute | solution.py:26
  70.7 14.0 %collective-permute-start.22 = (bf16[128,2048]{1,0:T(8,128)(2,1)S(1)}, bf16[128,2048]{1,0:T(8,128)(2,1)S(1)}, u32[]{:S(2)}, u32[]{:S(2)}) collective-permute-start(bf16[128,2048]{1,0:T(8,128)(2,1)S(1)} %collective-permute-done.9.refs_2_), channel_id=1, source_target_pairs={{0,16},{4,20},{8,24},{12,28},{16,0},{20,4},{24,8},{28,12},{1,17},{... | collective-permute-start | bytes 1572872 | tf_op jit(solution)/shard_map/ppermute | solution.py:26
  72.1 13.7 %collective-permute-start.23 = (bf16[128,2048]{1,0:T(8,128)(2,1)S(1)}, bf16[128,2048]{1,0:T(8,128)(2,1)S(1)}, u32[]{:S(2)}, u32[]{:S(2)}) collective-permute-start(bf16[128,2048]{1,0:T(8,128)(2,1)S(1)} %collective-permute-done.17.refs_6_), channel_id=1, source_target_pairs={{0,8},{4,12},{8,0},{12,4},{16,24},{20,28},{24,16},{28,20},{1,9},{5... | collective-permute-start | bytes 1572872 | tf_op jit(solution)/shard_map/ppermute | solution.py:26
  73.1 13.4 %collective-permute-start.24 = (bf16[128,2048]{1,0:T(8,128)(2,1)S(1)}, bf16[128,2048]{1,0:T(8,128)(2,1)S(1)}, u32[]{:S(2)}, u32[]{:S(2)}) collective-permute-start(bf16[128,2048]{1,0:T(8,128)(2,1)S(1)} %collective-permute-done.13.refs_12_), channel_id=1, source_target_pairs={{0,1},{1,0},{2,3},{3,2},{4,5},{5,4},{6,7},{7,6},{8,9},{9,8},{10,11... | collective-permute-start | bytes 1572872 | tf_op jit(solution)/shard_map/ppermute | solution.py:30
  87.5 9.7 %collective-permute-start.29 = (bf16[128,2048]{1,0:T(8,128)(2,1)S(1)}, bf16[128,2048]{1,0:T(8,128)(2,1)S(1)}, u32[]{:S(2)}, u32[]{:S(2)}) collective-permute-start(bf16[128,2048]{1,0:T(8,128)(2,1)S(1)} %collective-permute-done.24.refs_1_.refs_19_), channel_id=1, source_target_pairs={{0,4},{4,0},{8,12},{12,8},{16,20},{20,16},{24,28},{28,24},{1,5},{5... | collective-permute-start | bytes 1572872 | tf_op jit(solution)/shard_map/ppermute | solution.py:26
  87.7 8.6 %collective-permute-start.27 = (bf16[64,2048]{1,0:T(8,128)(2,1)S(1)}, bf16[64,2048]{1,0:T(8,128)(2,1)S(1)}, u32[]{:S(2)}, u32[]{:S(2)}) collective-permute-start(bf16[64,2048]{1,0:T(8,128)(2,1)S(1)} %get-tuple-element.171), channel_id=1, source_target_pairs={{0,8},{4,12},{8,0},{12,4},{16,24},{20,28},{24,16},{28,20},{1,9},{5... | collective-permute-start | bytes 786440 | tf_op jit(solution)/shard_map/ppermute | solution.py:26
  88.8 8.3 %collective-permute-start.28 = (bf16[64,2048]{1,0:T(8,128)(2,1)S(1)}, bf16[64,2048]{1,0:T(8,128)(2,1)S(1)}, u32[]{:S(2)}, u32[]{:S(2)}) collective-permute-start(bf16[64,2048]{1,0:T(8,128)(2,1)S(1)} %get-tuple-element.170), channel_id=1, source_target_pairs={{0,16},{4,20},{8,24},{12,28},{16,0},{20,4},{24,8},{28,12},{1,17},{... | collective-permute-start | bytes 786440 | tf_op jit(solution)/shard_map/ppermute | solution.py:26
  117.3 8.3 %collective-permute-start.38 = (f32[1,2048]{1,0:T(1,128)S(1)}, f32[1,2048]{1,0:T(1,128)S(1)}, u32[]{:S(2)}, u32[]{:S(2)}) collective-permute-start(f32[1,2048]{1,0:T(1,128)S(1)} %add.17), channel_id=1, source_target_pairs={{0,8},{4,12},{8,0},{12,4},{16,24},{20,28},{24,16},{28,20},{1,9},{5... | collective-permute-start | bytes 24584 | tf_op jit(solution)/shard_map/ppermute | solution.py:26
  118.4 7.1 %collective-permute-start.39 = (f32[1,2048]{1,0:T(1,128)S(1)}, f32[1,2048]{1,0:T(1,128)S(1)}, u32[]{:S(2)}, u32[]{:S(2)}) collective-permute-start(f32[1,2048]{1,0:T(1,128)S(1)} %add.17), channel_id=1, source_target_pairs={{0,16},{4,20},{8,24},{12,28},{16,0},{20,4},{24,8},{28,12},{1,17},{... | collective-permute-start | bytes 24584 | tf_op jit(solution)/shard_map/ppermute | solution.py:26
  125.6 12.8 %collective-permute-start.41 = (f32[1,2048]{1,0:T(1,128)S(1)}, f32[1,2048]{1,0:T(1,128)S(1)}, u32[]{:S(2)}, u32[]{:S(2)}) collective-permute-start(f32[1,2048]{1,0:T(1,128)S(1)} %add_add_fusion.refs_0_), channel_id=1, source_target_pairs={{0,1},{1,0},{2,3},{3,2},{4,5},{5,4},{6,7},{7,6},{8,9},{9,8},{10,11... | collective-permute-start | bytes 24584 | tf_op jit(solution)/shard_map/ppermute | solution.py:30
  127.3 11.2 %collective-permute-start.42 = (f32[1,2048]{1,0:T(1,128)S(1)}, f32[1,2048]{1,0:T(1,128)S(1)}, u32[]{:S(2)}, u32[]{:S(2)}) collective-permute-start(f32[1,2048]{1,0:T(1,128)S(1)} %add_add_fusion.refs_0_), channel_id=1, source_target_pairs={{0,2},{1,3},{2,0},{3,1},{4,6},{5,7},{6,4},{7,5},{8,10},{9,11},{10,... | collective-permute-start | bytes 24584 | tf_op jit(solution)/shard_map/ppermute | solution.py:30
  129.8 8.6 %collective-permute-start.43 = (f32[1,2048]{1,0:T(1,128)S(1)}, f32[1,2048]{1,0:T(1,128)S(1)}, u32[]{:S(2)}, u32[]{:S(2)}) collective-permute-start(f32[1,2048]{1,0:T(1,128)S(1)} %add_add_fusion.refs_0_), channel_id=1, source_target_pairs={{0,3},{1,2},{2,1},{3,0},{4,7},{5,6},{6,5},{7,4},{8,11},{9,10},{10,... | collective-permute-start | bytes 24584 | tf_op jit(solution)/shard_map/ppermute | solution.py:30
  (20 other events, 105.8 us)

commit v6 on v5

--- a/solution.py
+++ b/solution.py
@@ -235,23 +235,46 @@
             second_ref[:, span] = total.astype(BF16)
             bias = rows_ref[0:1, span]
             keep = jnp.ones((SEGMENTS, tile), F32)
-            state = leaving = jnp.zeros((SEGMENTS, tile), F32)
+            state = leaving = slope_run = slopes = updates = crossed = jnp.zeros((SEGMENTS, tile), F32)
             for pair in range(pairs):
                 slabs = chosen_pair(where_ref, first_ref, second_ref, pair, span)
                 for gate, cand, g in zip(*slabs, slab_pair(back_ref, pair, span)):
                     update, retain = gates(gate + bias)
+                    slope = (cand - state) * update * retain
                     keep = keep * retain
                     state = retain * state + update * cand
-                    leaving = leaving + keep * g
+                    kept_grad = keep * g
+                    leaving = leaving + kept_grad
+                    slope_run = retain * slope_run + slope
+                    slopes = slopes + g * slope_run
+                    updates = updates + update
+                    crossed = crossed + kept_grad * updates
             parts_ref[0, :, span], parts_ref[1, :, span], parts_ref[2, :, span] = keep, state, leaving
-            whole_keep, whole_state = keep[0:1], state[0:1]
-            for s in range(1, SEGMENTS):
-                whole_state = keep[s : s + 1] * whole_state + state[s : s + 1]
-                whole_keep = whole_keep * keep[s : s + 1]
-            whole_leaving = leaving[SEGMENTS - 1 :]
-            for s in range(SEGMENTS - 2, -1, -1):
-                whole_leaving = keep[s : s + 1] * whole_leaving + leaving[s : s + 1]
-            whole_ref[0:1, span], whole_ref[1:2, span], whole_ref[2:3, span] = whole_keep, whole_state, whole_leaving
+            both_sides = keep * updates
+            row = lambda value, s: value[s : s + 1]
+            zero, one = row(keep, 0) * 0.0, row(keep, 0) * 0.0 + 1.0
+            start, start_slope = [zero], [one]
+            for s in range(SEGMENTS):
+                start.append(row(keep, s) * start[-1] + row(state, s))
+                start_slope.append(row(keep, s) * start_slope[-1])
+            tail, tail_slope = [zero], [one]
+            for s in range(SEGMENTS - 1, -1, -1):
+                tail.append(row(keep, s) * tail[-1] + row(leaving, s))
+                tail_slope.append(row(keep, s) * tail_slope[-1])
+            whole = [start_slope[-1], start[-1], tail[-1]]
+            start, start_slope = jnp.concatenate(start[:-1], axis=0), jnp.concatenate(start_slope[:-1], axis=0)
+            tail = jnp.concatenate(tail[-2::-1], axis=0)
+            tail_slope = jnp.concatenate(tail_slope[-2::-1], axis=0)
+            by_tail = slope_run - both_sides * start
+            by_start = crossed + both_sides * tail
+            sums = [
+                slopes + slope_run * tail - by_start * start,
+                by_tail * tail_slope,
+                by_start * start_slope,
+                both_sides * tail_slope * start_slope,
+            ]
+            whole += [jnp.sum(value, axis=0, keepdims=True) for value in sums] + [zero]
+            whole_ref[:, span] = jnp.concatenate(whole, axis=0)
 
         tiles(width, tile, body)
 
@@ -260,7 +283,7 @@
         out_shape=[
             jax.ShapeDtypeStruct((rows, width), BF16),
             jax.ShapeDtypeStruct((3, SEGMENTS, width), F32),
-            jax.ShapeDtypeStruct((3, width), F32),
+            jax.ShapeDtypeStruct((8, width), F32),
             jax.ShapeDtypeStruct((2, width), F32),
         ],
         in_specs=[SMEM_SPEC] + [VMEM_SPEC] * (4 + len(extra)) + [VMEM_SPEC] * len(shards.pieces),
@@ -271,7 +294,7 @@
     )(where, *map(near, (x, first_pre, back, both, *extra)), *shards.operands())
 
 
-def scan_call(where, first_pre, second_pre, back, both, parts, wholes, ranks, tile):
+def scan_call(where, first_pre, second_pre, back, both, parts, wholes, offsets, ranks, tile):
     rows, width = first_pre.shape
     pairs = rows // (2 * SEGMENTS)
 
@@ -280,25 +303,29 @@
         (state_ref, one_ref, other_ref, bias_grad_ref, state_grad_ref) = refs[:5]
         hold, kept, updates, slopes, one_hold, other_hold, state_hold = refs[5:]
         me = where_ref[2]
-        order = place_back(rows)
+        order, order_back = place_back(rows), place(rows)
 
         def body(span):
-            entering = both_ref[1:2, span]
-            per = ranks // len(wholes)
-            for index, ref in enumerate(whole_refs):
-                for member in range(per):
-                    offset = index * per + member
-                    hold[me ^ offset if len(wholes) > 1 else offset, 0:3, :] = ref[member, :, span]
+            for ref, members in zip(whole_refs, offsets):
+                for member, offset in enumerate(members):
+                    hold[where_ref[0] ^ offset] = ref[member, :, span]
             blocks = [hold[rank] for rank in range(ranks)]
+            held = both_ref[1:2, span]
+            entering, held_by = held, []
             for rank in range(ranks):
                 block = blocks[rank]
-                entering = jnp.where(rank < me, block[0:1] * entering + block[1:2], entering)
-            arriving = state_grad = blocks[0][2:3] * 0.0
+                entering = jnp.where(rank == me, held, entering)
+                held_by.append(held)
+                held = block[0:1] * held + block[1:2]
+            arriving = state_grad = bias_sum = held * 0.0
             for rank in range(ranks - 1, -1, -1):
-                block = blocks[rank]
+                block, held = blocks[rank], held_by[rank]
                 arriving = jnp.where(rank == me, state_grad, arriving)
+                by_tail = block[4:5] - block[6:7] * held
+                bias_sum = bias_sum + block[3:4] - block[5:6] * held + by_tail * state_grad
                 state_grad = block[0:1] * state_grad + block[2:3]
             state_grad_ref[:, span] = state_grad
+            bias_grad_ref[:, span] = bias_sum
             keep, ends, leaves = parts_ref[0, :, span], parts_ref[1, :, span], parts_ref[2, :, span]
             starts = [entering]
             for s in range(SEGMENTS - 1):
@@ -325,7 +352,6 @@
                 updates[here, :] = jnp.concatenate(ups, axis=0)
                 slopes[here, :] = jnp.concatenate(slope, axis=0)
 
-            total = jnp.zeros((SEGMENTS, tile), F32)
             for pair in range(pairs - 1, -1, -1):
                 here = slice(pair * 2 * SEGMENTS, (pair + 1) * 2 * SEGMENTS)
                 grads = slab_pair(back_ref, pair, span)
@@ -336,14 +362,12 @@
                 carried = jnp.concatenate([early, late], axis=0)
                 gate_grad = carried * slope
                 cand_grad = carried * update
-                total = total + gate_grad[:SEGMENTS] + gate_grad[SEGMENTS:]
                 one, other = choose(where_ref, gate_grad.astype(BF16), cand_grad.astype(BF16))
                 one_hold[here, :] = one
                 other_hold[here, :] = other
-            bias_grad_ref[:, span] = jnp.sum(total, axis=0, keepdims=True)
             state_ref[:, span] = dot(order, state_hold[...]).astype(BF16)
-            one_ref[span, :] = dot(order, one_hold[...]).T.astype(BF16)
-            other_ref[span, :] = dot(order, other_hold[...]).T.astype(BF16)
+            one_ref[span, :] = dot(one_hold[...].T, order_back).astype(BF16)
+            other_ref[span, :] = dot(other_hold[...].T, order_back).astype(BF16)
 
         tiles(width, tile, body)
 
@@ -552,28 +576,28 @@
         found = front(where, tile, *given)
     where, first, second, third, first_pre, second_pre, back, both, parts, whole = found
     if cube:
-        chip = jnp.stack([whole, hop(whole, 1, ranks)])
-        wholes = [chip] + [hop(chip, offset, ranks) for offset in (2, 4, 6)]
+        found = jnp.stack([hop(whole, offset, ranks) for offset in (2, 4, 6)])
+        wholes = [jnp.stack([whole, hop(whole, 1, ranks)]), found, hop(found, 1, ranks)]
+        offsets = [(0, 1), (2, 4, 6), (3, 5, 7)]
     else:
-        wholes = [lax.all_gather(whole, "seq")]
+        wholes, offsets = [lax.all_gather(whole, "seq")], [range(ranks)]
     state_rows, one, other, bias_part, state_grad = scan_call(
-        where, first_pre, second_pre, back, both, parts, wholes, ranks, tile
+        where, first_pre, second_pre, back, both, parts, wholes, offsets, ranks, tile
     )
     width = hidden // ranks
     if cube:
-        pair = bias_part + hop(bias_part, 1, ranks)
+        came = swap_batch(bias_part, 1, batches)
         layer_out = layer_call(where, state_rows, rows_in, third, tile)
-        plane = [hop(pair, offset, ranks) for offset in (2, 4, 6)]
-        layer_out, pair, *plane = after((layer_out, pair) + tuple(plane))
-        plane = pair + plane[0] + plane[1] + plane[2]
-        far = [swap_batch(plane, offset, batches) for offset in range(1, batches)]
-        one, other, plane = after((one, other, plane), layer_out)
+        layer_out, bias_part, came, one, other = after((layer_out, bias_part, came, one, other))
+        for offset in range(1, batches.bit_length() - 1):
+            bias_part = bias_part + came
+            came = swap_batch(bias_part, 1 << offset, batches)
         input_grad = input_grad_call(where, one, other, first, second, rows_in, grad_rows, gain)
-        state_out, bias_grad = close_call(where, state_grad, [plane] + far, width)
+        state_out, bias_grad = close_call(where, state_grad, [bias_part, came], width)
         bias_grad = bias_grad[0]
     else:
-        over_seq = lax.psum_scatter(bias_part[0], "seq", scatter_dimension=0, tiled=True)
-        bias_grad = lax.psum(over_seq, "batch")
+        own_block = lax.dynamic_slice_in_dim(bias_part[0], me * width, width, 0)
+        bias_grad = lax.psum(own_block, "batch")
         layer_out = layer_call(where, state_rows, rows_in, third, tile)
         input_grad = input_grad_call(where, one, other, first, second, rows_in, grad_rows, gain)
         state_out = lax.dynamic_slice_in_dim(state_grad, me * width, width, 1)

time: 140 us -> 135 us (0.964)
  starting transfers between devices: 38.6 us -> 34.7 us
    ppermute x38 -> x35, starting transfers between devices: 29.3 us -> 25.6 us  [hop(): return lax.ppermute(value, 'seq', [(i, i ^ offset) for i in range(count)])]
    ppermute x38 -> x35, waiting for transfers between devices: 60.5 us -> 59.2 us  [hop(): return lax.ppermute(value, 'seq', [(i, i ^ offset) for i in range(count)])]
    ppermute x6 -> x5, starting transfers between devices: 9.25 us -> 9.09 us  [swap_batch(): return lax.ppermute(value, 'batch', [(i, i ^ offset) for i in range(count)])]
  transfers between devices with their start and end apart: 44 -> 40, of which waited for: 26 -> 25; matrix products, arithmetic and copies ran while one was open for 1% -> 1% of each run, Pallas kernels for 18% -> 18%
where the time goes in v6:
time: 135 us
  waiting for transfers between devices  61.3 us (45%)
  starting transfers between devices  34.7 us (26%)
  Pallas kernels  34.5 us (26%)
  other arithmetic  3.53 us (3%)
    ppermute x35, waiting for transfers between devices, hop(): return lax.ppermute(value, 'seq', [(i, i ^ offset) for i in range(count)])  59.2 us
    ppermute x35, starting transfers between devices, hop(): return lax.ppermute(value, 'seq', [(i, i ^ offset) for i in range(count)])  25.6 us
    ppermute x5, starting transfers between devices, swap_batch(): return lax.ppermute(value, 'batch', [(i, i ^ offset) for i in range(count)])  9.09 us
    pallas_call x1, Pallas kernels, input_grad_call(): pl.pallas_call(kernel, out_shape=jax.ShapeDtypeStruct((rows, width), BF16...  8.38 us
    pallas_call x2, Pallas kernels, project_call(): pl.pallas_call(kernel, out_shape=jax.ShapeDtypeStruct((rows, width), dtyp...  5.15 us
    pallas_call x1, Pallas kernels, layer_call(): pl.pallas_call(kernel, out_shape=jax.ShapeDtypeStruct((rows, width), BF16...  4.73 us
    pallas_call x1, Pallas kernels, totals_call(): pl.pallas_call(kernel, out_shape=[jax.ShapeDtypeStruct((rows, width), BF1...  4.42 us
    pallas_call x1, Pallas kernels, scan_call(): pl.pallas_call(kernel, out_shape=[wide, tall, tall, flat, flat], in_specs...  4.39 us
  transfers between devices with their start and end apart: 40, of which 25 were waited for; matrix products, arithmetic and copies ran while one was open for 1% of the time, Pallas kernels for 18%

profile of v6, /device:TPU:0, one launch (start us, length us, event | category | flops | bytes accessed | tf_op | source)
XLA Modules:
  0.0 135.3 jit_solution(2389723352253652478)
XLA Ops:
  2.2 3.0 %collective-permute-start = (bf16[128,2048]{1,0:T(8,128)(2,1)S(1)}, bf16[128,2048]{1,0:T(8,128)(2,1)S(1)}, u32[]{:S(2)}, u32[]{:S(2)}) collective-permute-start(bf16[128,2048]{1,0:T(8,128)(2,1)S(1)} %slice_select_fusion.1.refs_0_), channel_id=1, source_target_pairs={{0,8},{4,12},{8,0},{12,4},{16,24},{20,28},{24,16},{28,20},{1,9},{5... | collective-permute-start | bytes 1572872 | tf_op jit(solution)/shard_map/ppermute | solution.py:26
  5.2 1.5 %collective-permute-start.1 = (bf16[128,2048]{1,0:T(8,128)(2,1)S(1)}, bf16[128,2048]{1,0:T(8,128)(2,1)S(1)}, u32[]{:S(2)}, u32[]{:S(2)}) collective-permute-start(bf16[128,2048]{1,0:T(8,128)(2,1)S(1)} %slice_select_fusion.1.refs_0_), channel_id=1, source_target_pairs={{0,16},{4,20},{8,24},{12,28},{16,0},{20,4},{24,8},{28,12},{1,17},{... | collective-permute-start | bytes 1572872 | tf_op jit(solution)/shard_map/ppermute | solution.py:26
  10.7 3.3 %norm_rows.1 = (bf16[256,2048]{1,0:T(8,128)(2,1)S(1)}, bf16[2048,256]{1,0:T(8,128)(2,1)S(1)}) custom-call(s32[3]{0:T(128)S(1)} %pad_add_fusion.where_ref, bf16[256,2048]{1,0:T(8,128)(2,1)S(1)} %bitcast.14, bf16[256,2048]{1,0:T(8,128)(2,1)S(1)} %bitcast.17, f32[1,2048]{1,0:T(1,128)S(1)} %bitcast.20), custom_call_target="tpu_custom_call" | custom-call | flops 536870912 | bytes 4194304 | tf_op jit(solution)/shard_map/norm_rows/pallas_call | solution.py:132
  13.9 3.3 %collective-permute-done.5 = f32[2,512]{1,0:T(2,128)S(1)} collective-permute-done((f32[2,512]{1,0:T(2,128)S(1)}, f32[2,512]{1,0:T(2,128)S(1)}, u32[]{:S(2)}, u32[]{:S(2)}) %collective-permute-start.5) | collective-permute-done | bytes 4128 | tf_op jit(solution)/shard_map/ppermute | solution.py:26
  19.1 1.6 %collective-permute-start.7 = (bf16[128,2048]{1,0:T(8,128)(2,1)S(1)}, bf16[128,2048]{1,0:T(8,128)(2,1)S(1)}, u32[]{:S(2)}, u32[]{:S(2)}) collective-permute-start(bf16[128,2048]{1,0:T(8,128)(2,1)S(1)} %slice_select_fusion.refs_1_), channel_id=1, source_target_pairs={{0,16},{4,20},{8,24},{12,28},{16,0},{20,4},{24,8},{28,12},{1,17},{... | collective-permute-start | bytes 1572872 | tf_op jit(solution)/shard_map/ppermute | solution.py:26
  20.8 1.6 %collective-permute-start.8 = (bf16[256,2048]{1,0:T(8,128)(2,1)S(1)}, bf16[256,2048]{1,0:T(8,128)(2,1)S(1)}, u32[]{:S(2)}, u32[]{:S(2)}) collective-permute-start(bf16[256,2048]{1,0:T(8,128)(2,1)S(1)} %pad_maximum_fusion.2), channel_id=1, source_target_pairs={{0,1},{1,0},{2,3},{3,2},{4,5},{5,4},{6,7},{7,6},{8,9},{9,8},{10,11... | collective-permute-start | bytes 3145736 | tf_op jit(solution)/shard_map/ppermute | solution.py:30
  22.9 1.5 %collective-permute-start.9 = (bf16[128,2048]{1,0:T(8,128)(2,1)S(1)}, bf16[128,2048]{1,0:T(8,128)(2,1)S(1)}, u32[]{:S(2)}, u32[]{:S(2)}) collective-permute-start(bf16[128,2048]{1,0:T(8,128)(2,1)S(1)} %get-tuple-element.97), channel_id=1, source_target_pairs={{0,8},{4,12},{8,0},{12,4},{16,24},{20,28},{24,16},{28,20},{1,9},{5... | collective-permute-start | bytes 1572872 | tf_op jit(solution)/shard_map/ppermute | solution.py:26
  24.4 9.1 %collective-permute-done.6.refs_5_ = bf16[128,2048]{1,0:T(8,128)(2,1)S(1)} collective-permute-done((bf16[128,2048]{1,0:T(8,128)(2,1)S(1)}, bf16[128,2048]{1,0:T(8,128)(2,1)S(1)}, u32[]{:S(2)}, u32[]{:S(2)}) %collective-permute-start.6) | collective-permute-done | bytes 524320 | tf_op jit(solution)/shard_map/ppermute | solution.py:26
  34.6 8.3 %collective-permute-done.10.refs_5_ = bf16[128,2048]{1,0:T(8,128)(2,1)S(1)} collective-permute-done((bf16[128,2048]{1,0:T(8,128)(2,1)S(1)}, bf16[128,2048]{1,0:T(8,128)(2,1)S(1)}, u32[]{:S(2)}, u32[]{:S(2)}) %collective-permute-start.10) | collective-permute-done | bytes 524320 | tf_op jit(solution)/shard_map/ppermute | solution.py:26
  42.8 1.4 %collective-permute-done.8.refs_2_.refs_17_ = bf16[256,2048]{1,0:T(8,128)(2,1)S(1)} collective-permute-done((bf16[256,2048]{1,0:T(8,128)(2,1)S(1)}, bf16[256,2048]{1,0:T(8,128)(2,1)S(1)}, u32[]{:S(2)}, u32[]{:S(2)}) %collective-permute-start.8) | collective-permute-done | bytes 1048608 | tf_op jit(solution)/shard_map/ppermute | solution.py:30
  46.8 1.5 %collective-permute-start.17 = (bf16[128,2048]{1,0:T(8,128)(2,1)S(1)}, bf16[128,2048]{1,0:T(8,128)(2,1)S(1)}, u32[]{:S(2)}, u32[]{:S(2)}) collective-permute-start(bf16[128,2048]{1,0:T(8,128)(2,1)S(1)} %get-tuple-element.109), channel_id=1, source_target_pairs={{0,16},{4,20},{8,24},{12,28},{16,0},{20,4},{24,8},{28,12},{1,17},{... | collective-permute-start | bytes 1572872 | tf_op jit(solution)/shard_map/ppermute | solution.py:26
  48.3 1.6 %collective-permute-start.15 = (bf16[256,2048]{1,0:T(8,128)(2,1)S(1)}, bf16[256,2048]{1,0:T(8,128)(2,1)S(1)}, u32[]{:S(2)}, u32[]{:S(2)}) collective-permute-start(bf16[256,2048]{1,0:T(8,128)(2,1)S(1)} %pad_maximum_fusion.1), channel_id=1, source_target_pairs={{0,1},{1,0},{2,3},{3,2},{4,5},{5,4},{6,7},{7,6},{8,9},{9,8},{10,11... | collective-permute-start | bytes 3145736 | tf_op jit(solution)/shard_map/ppermute | solution.py:30
  49.9 9.2 %collective-permute-done.13.refs_12_ = bf16[128,2048]{1,0:T(8,128)(2,1)S(1)} collective-permute-done((bf16[128,2048]{1,0:T(8,128)(2,1)S(1)}, bf16[128,2048]{1,0:T(8,128)(2,1)S(1)}, u32[]{:S(2)}, u32[]{:S(2)}) %collective-permute-start.13) | collective-permute-done | bytes 524320 | tf_op jit(solution)/shard_map/ppermute | solution.py:26
  60.1 6.9 %collective-permute-done.16.refs_3_ = bf16[128,2048]{1,0:T(8,128)(2,1)S(1)} collective-permute-done((bf16[128,2048]{1,0:T(8,128)(2,1)S(1)}, bf16[128,2048]{1,0:T(8,128)(2,1)S(1)}, u32[]{:S(2)}, u32[]{:S(2)}) %collective-permute-start.16) | collective-permute-done | bytes 524320 | tf_op jit(solution)/shard_map/ppermute | solution.py:26
  70.7 1.5 %collective-permute-start.22 = (bf16[128,2048]{1,0:T(8,128)(2,1)S(1)}, bf16[128,2048]{1,0:T(8,128)(2,1)S(1)}, u32[]{:S(2)}, u32[]{:S(2)}) collective-permute-start(bf16[128,2048]{1,0:T(8,128)(2,1)S(1)} %collective-permute-done.9.refs_2_), channel_id=1, source_target_pairs={{0,16},{4,20},{8,24},{12,28},{16,0},{20,4},{24,8},{28,12},{1,17},{... | collective-permute-start | bytes 1572872 | tf_op jit(solution)/shard_map/ppermute | solution.py:26
  73.1 1.6 %collective-permute-start.24 = (bf16[128,2048]{1,0:T(8,128)(2,1)S(1)}, bf16[128,2048]{1,0:T(8,128)(2,1)S(1)}, u32[]{:S(2)}, u32[]{:S(2)}) collective-permute-start(bf16[128,2048]{1,0:T(8,128)(2,1)S(1)} %collective-permute-done.13.refs_12_), channel_id=1, source_target_pairs={{0,1},{1,0},{2,3},{3,2},{4,5},{5,4},{6,7},{7,6},{8,9},{9,8},{10,11... | collective-permute-start | bytes 1572872 | tf_op jit(solution)/shard_map/ppermute | solution.py:30
  74.7 2.5 %collective-permute-done.25.refs_14_ = bf16[256,2048]{1,0:T(8,128)(2,1)S(1)} collective-permute-done((bf16[256,2048]{1,0:T(8,128)(2,1)S(1)}, bf16[256,2048]{1,0:T(8,128)(2,1)S(1)}, u32[]{:S(2)}, u32[]{:S(2)}) %collective-permute-start.25) | collective-permute-done | bytes 1048608 | tf_op jit(solution)/shard_map/ppermute | solution.py:26
  77.2 2.9 %project.2.first_ref = bf16[256,2048]{1,0:T(8,128)(2,1)S(1)} custom-call(bf16[256,2048]{1,0:T(8,128)(2,1)S(1)} %get-tuple-element.119.x_ref, bf16[128,2048]{1,0:T(8,128)(2,1)S(1)} %slice_select_fusion.1.refs_0_, bf16[128,2048]{1,0:T(8,128)(2,1)S(1)} %slice_select_fusion.refs_1_, bf16[128,2048]{1,0:T(8,128)(2,1)S(1)} %collective-permute-done.2.refs_2_, ...), custom_call_target="tpu_custom_call" | custom-call | flops 2147483648 | bytes 8388608 | tf_op jit(solution)/shard_map/project/pallas_call | solution.py:156
  80.1 2.3 %project.3.refs_0_ = f32[256,2048]{1,0:T(8,128)S(1)} custom-call(bf16[256,2048]{1,0:T(8,128)(2,1)S(1)} %get-tuple-element.119.x_ref, bf16[256,2048]{1,0:T(8,128)(2,1)S(1)} %broadcast_select_fusion.refs_0_.refs_15_, bf16[768,2048]{1,0:T(8,128)(2,1)S(1)} %collective-permute-done.26.refs_1_.refs_16_, ...), custom_call_target="tpu_custom_call" | custom-call | flops 1610612736 | bytes 6291456 | tf_op jit(solution)/shard_map/project/pallas_call | solution.py:156
  82.4 2.3 %collective-permute-done.22.refs_8_ = bf16[128,2048]{1,0:T(8,128)(2,1)S(1)} collective-permute-done((bf16[128,2048]{1,0:T(8,128)(2,1)S(1)}, bf16[128,2048]{1,0:T(8,128)(2,1)S(1)}, u32[]{:S(2)}, u32[]{:S(2)}) %collective-permute-start.22) | collective-permute-done | bytes 524320 | tf_op jit(solution)/shard_map/ppermute | solution.py:26
  88.9 1.5 %collective-permute-start.28 = (bf16[64,2048]{1,0:T(8,128)(2,1)S(1)}, bf16[64,2048]{1,0:T(8,128)(2,1)S(1)}, u32[]{:S(2)}, u32[]{:S(2)}) collective-permute-start(bf16[64,2048]{1,0:T(8,128)(2,1)S(1)} %get-tuple-element.164), channel_id=1, source_target_pairs={{0,16},{4,20},{8,24},{12,28},{16,0},{20,4},{24,8},{28,12},{1,17},{... | collective-permute-start | bytes 786440 | tf_op jit(solution)/shard_map/ppermute | solution.py:26
  90.6 1.9 %collective-permute-done.30.refs_1_ = bf16[768,2048]{1,0:T(8,128)(2,1)S(1)} collective-permute-done((bf16[768,2048]{1,0:T(8,128)(2,1)S(1)}, bf16[768,2048]{1,0:T(8,128)(2,1)S(1)}, u32[]{:S(2)}, u32[]{:S(2)}) %collective-permute-start.30) | collective-permute-done | bytes 3145760 | tf_op jit(solution)/shard_map/ppermute | solution.py:26
  92.5 3.0 %back_rows.1.back_ref = bf16[256,2048]{1,0:T(8,128)(2,1)S(1)} custom-call(s32[3]{0:T(128)S(1)} %pad_add_fusion.where_ref, bf16[2048,256]{1,0:T(8,128)(2,1)S(1)} %get-tuple-element.134.g_ref, bf16[256,2048]{1,0:T(8,128)(2,1)S(1)} %copy-done, bf16[768,2048]{1,0:T(8,128)(2,1)S(1)} %collective-permute-done.30.refs_1_, ...), custom_call_target="tpu_custom_call" | custom-call | flops 2147483648 | bytes 8388608 | tf_op jit(solution)/shard_map/back_rows/pallas_call | solution.py:180
  97.3 1.9 %collective-permute-done.32.refs_5_.refs_23_ = bf16[128,2048]{1,0:T(8,128)(2,1)S(1)} collective-permute-done((bf16[128,2048]{1,0:T(8,128)(2,1)S(1)}, bf16[128,2048]{1,0:T(8,128)(2,1)S(1)}, u32[]{:S(2)}, u32[]{:S(2)}) %collective-permute-start.32) | collective-permute-done | bytes 524320 | tf_op jit(solution)/shard_map/ppermute | solution.py:26
  99.2 4.4 %project_totals.1 = (bf16[256,2048]{1,0:T(8,128)(2,1)S(1)}, f32[3,8,2048]{2,1,0:T(8,128)S(1)}, f32[8,2048]{1,0:T(8,128)S(1)}, f32[2,2048]{1,0:T(2,128)S(1)}) custom-call(s32[3]{0:T(128)S(1)} %pad_add_fusion.where_ref, bf16[256,2048]{1,0:T(8,128)(2,1)S(1)} %get-tuple-element.119.x_ref, bf16[256,2048]{1,0:T(8,128)(2,1)S(1)} %project.2.first_ref, ...), custom_call_target="tpu_custom_call" | custom-call | flops 536870912 | bytes 2097152 | tf_op jit(solution)/shard_map/project_totals/pallas_call | solution.py:281
  103.6 1.9 %collective-permute-start.36 = (f32[8,2048]{1,0:T(8,128)S(1)}, f32[8,2048]{1,0:T(8,128)S(1)}, u32[]{:S(2)}, u32[]{:S(2)}) collective-permute-start(f32[8,2048]{1,0:T(8,128)S(1)} %get-tuple-element.151), channel_id=1, source_target_pairs={{0,24},{4,28},{8,16},{12,20},{16,8},{20,12},{24,0},{28,4},{1,25},{... | collective-permute-start | bytes 196616 | tf_op jit(solution)/shard_map/ppermute | solution.py:26
  107.2 2.3 %collective-permute-done.36 = f32[8,2048]{1,0:T(8,128)S(1)} collective-permute-done((f32[8,2048]{1,0:T(8,128)S(1)}, f32[8,2048]{1,0:T(8,128)S(1)}, u32[]{:S(2)}, u32[]{:S(2)}) %collective-permute-start.36) | collective-permute-done | bytes 65568 | tf_op jit(solution)/shard_map/ppermute | solution.py:26
  112.4 4.4 %scan_rows.1 = (bf16[256,2048]{1,0:T(8,128)(2,1)S(1)}, bf16[2048,256]{1,0:T(8,128)(2,1)S(1)}, bf16[2048,256]{1,0:T(8,128)(2,1)S(1)}, f32[1,2048]{1,0:T(1,128)S(1)}, f32[1,2048]{1,0:T(1,128)S(1)}) custom-call(s32[3]{0:T(128)S(1)} %pad_add_fusion.where_ref, bf16[256,2048]{1,0:T(8,128)(2,1)S(1)} %project.2.first_ref, ...), custom_call_target="tpu_custom_call" | custom-call | flops 805306368 | bytes 6291456 | tf_op jit(solution)/shard_map/scan_rows/pallas_call | solution.py:377
  116.8 1.6 %collective-permute-start.38 = (f32[1,2048]{1,0:T(1,128)S(1)}, f32[1,2048]{1,0:T(1,128)S(1)}, u32[]{:S(2)}, u32[]{:S(2)}) collective-permute-start(f32[1,2048]{1,0:T(1,128)S(1)} %get-tuple-element.160), channel_id=1, source_target_pairs={{0,1},{1,0},{2,3},{3,2},{4,5},{5,4},{6,7},{7,6},{8,9},{9,8},{10,11... | collective-permute-start | bytes 24584 | tf_op jit(solution)/shard_map/ppermute | solution.py:30
  118.4 4.7 %layer_rows.1 = bf16[256,2048]{1,0:T(8,128)(2,1)} custom-call(s32[3]{0:T(128)S(1)} %pad_add_fusion.where_ref, bf16[256,2048]{1,0:T(8,128)(2,1)S(1)} %get-tuple-element.152.x_ref, bf16[256,2048]{1,0:T(8,128)(2,1)S(1)} %bitcast.15, bf16[256,2048]{1,0:T(8,128)(2,1)S(1)} %copy-done, bf16[768,2048]{1,0:T(8,128)(2,1)S(1)} %collective-permute-done.30.refs_1_, ...), custom_call_target="tpu_custom_call" | custom-call | flops 2147483648 | bytes 8388608 | tf_op jit(solution)/shard_map/layer_rows/pallas_call | solution.py:407
  123.2 2.7 %collective-permute-start.39 = (f32[1,2048]{1,0:T(1,128)S(1)}, f32[1,2048]{1,0:T(1,128)S(1)}, u32[]{:S(2)}, u32[]{:S(2)}) collective-permute-start(f32[1,2048]{1,0:T(1,128)S(1)} %add.8.refs_0_), channel_id=1, source_target_pairs={{0,2},{1,3},{2,0},{3,1},{4,6},{5,7},{6,4},{7,5},{8,10},{9,11},{10,... | collective-permute-start | bytes 24584 | tf_op jit(solution)/shard_map/ppermute | solution.py:30
  125.8 8.4 %input_grad_rows.1 = bf16[256,2048]{1,0:T(8,128)(2,1)} custom-call(s32[3]{0:T(128)S(1)} %pad_add_fusion.where_ref, bf16[2048,256]{1,0:T(8,128)(2,1)S(1)} %get-tuple-element.157.one_ref, bf16[2048,256]{1,0:T(8,128)(2,1)S(1)} %get-tuple-element.158.other_ref, bf16[256,2048]{1,0:T(8,128)(2,1)S(1)} %bitcast.16, bf16[256,2048]{1,0:T(8,128)(2,1)S(1)} %bitcast.18, ...), custom_call_target="tpu_custom_call" | custom-call | flops 4294967296 | bytes 16777216 | tf_op jit(solution)/shard_map/input_grad_rows/pallas_call | solution.py:447
  (96 shorter events, 28.9 us)
Async XLA Ops:
  2.2 15.0 %collective-permute-start = (bf16[128,2048]{1,0:T(8,128)(2,1)S(1)}, bf16[128,2048]{1,0:T(8,128)(2,1)S(1)}, u32[]{:S(2)}, u32[]{:S(2)}) collective-permute-start(bf16[128,2048]{1,0:T(8,128)(2,1)S(1)} %slice_select_fusion.1.refs_0_), channel_id=1, source_target_pairs={{0,8},{4,12},{8,0},{12,4},{16,24},{20,28},{24,16},{28,20},{1,9},{5... | collective-permute-start | bytes 1572872 | tf_op jit(solution)/shard_map/ppermute | solution.py:26
  5.2 13.4 %collective-permute-start.1 = (bf16[128,2048]{1,0:T(8,128)(2,1)S(1)}, bf16[128,2048]{1,0:T(8,128)(2,1)S(1)}, u32[]{:S(2)}, u32[]{:S(2)}) collective-permute-start(bf16[128,2048]{1,0:T(8,128)(2,1)S(1)} %slice_select_fusion.1.refs_0_), channel_id=1, source_target_pairs={{0,16},{4,20},{8,24},{12,28},{16,0},{20,4},{24,8},{28,12},{1,17},{... | collective-permute-start | bytes 1572872 | tf_op jit(solution)/shard_map/ppermute | solution.py:26
  6.7 11.9 %collective-permute-start.2 = (bf16[128,2048]{1,0:T(8,128)(2,1)S(1)}, bf16[128,2048]{1,0:T(8,128)(2,1)S(1)}, u32[]{:S(2)}, u32[]{:S(2)}) collective-permute-start(bf16[128,2048]{1,0:T(8,128)(2,1)S(1)} %slice_select_fusion.1.refs_0_), channel_id=1, source_target_pairs={{0,4},{4,0},{8,12},{12,8},{16,20},{20,16},{24,28},{28,24},{1,5},{5... | collective-permute-start | bytes 1572872 | tf_op jit(solution)/shard_map/ppermute | solution.py:26
  8.0 9.2 %collective-permute-start.3 = (bf16[128,2048]{1,0:T(8,128)(2,1)S(1)}, bf16[128,2048]{1,0:T(8,128)(2,1)S(1)}, u32[]{:S(2)}, u32[]{:S(2)}) collective-permute-start(bf16[128,2048]{1,0:T(8,128)(2,1)S(1)} %slice_select_fusion.refs_1_), channel_id=1, source_target_pairs={{0,4},{4,0},{8,12},{12,8},{16,20},{20,16},{24,28},{28,24},{1,5},{5... | collective-permute-start | bytes 1572872 | tf_op jit(solution)/shard_map/ppermute | solution.py:26
  10.1 7.1 %collective-permute-start.5 = (f32[2,512]{1,0:T(2,128)S(1)}, f32[2,512]{1,0:T(2,128)S(1)}, u32[]{:S(2)}, u32[]{:S(2)}) collective-permute-start(f32[2,512]{1,0:T(2,128)S(1)} %pad_maximum_fusion.9), channel_id=1, source_target_pairs={{0,8},{4,12},{8,0},{12,4},{16,24},{20,28},{24,16},{28,20},{1,9},{5... | collective-permute-start | bytes 12296 | tf_op jit(solution)/shard_map/ppermute | solution.py:26
  18.6 14.9 %collective-permute-start.6 = (bf16[128,2048]{1,0:T(8,128)(2,1)S(1)}, bf16[128,2048]{1,0:T(8,128)(2,1)S(1)}, u32[]{:S(2)}, u32[]{:S(2)}) collective-permute-start(bf16[128,2048]{1,0:T(8,128)(2,1)S(1)} %slice_select_fusion.refs_1_), channel_id=1, source_target_pairs={{0,8},{4,12},{8,0},{12,4},{16,24},{20,28},{24,16},{28,20},{1,9},{5... | collective-permute-start | bytes 1572872 | tf_op jit(solution)/shard_map/ppermute | solution.py:26
  19.1 14.9 %collective-permute-start.7 = (bf16[128,2048]{1,0:T(8,128)(2,1)S(1)}, bf16[128,2048]{1,0:T(8,128)(2,1)S(1)}, u32[]{:S(2)}, u32[]{:S(2)}) collective-permute-start(bf16[128,2048]{1,0:T(8,128)(2,1)S(1)} %slice_select_fusion.refs_1_), channel_id=1, source_target_pairs={{0,16},{4,20},{8,24},{12,28},{16,0},{20,4},{24,8},{28,12},{1,17},{... | collective-permute-start | bytes 1572872 | tf_op jit(solution)/shard_map/ppermute | solution.py:26
  20.8 23.5 %collective-permute-start.8 = (bf16[256,2048]{1,0:T(8,128)(2,1)S(1)}, bf16[256,2048]{1,0:T(8,128)(2,1)S(1)}, u32[]{:S(2)}, u32[]{:S(2)}) collective-permute-start(bf16[256,2048]{1,0:T(8,128)(2,1)S(1)} %pad_maximum_fusion.2), channel_id=1, source_target_pairs={{0,1},{1,0},{2,3},{3,2},{4,5},{5,4},{6,7},{7,6},{8,9},{9,8},{10,11... | collective-permute-start | bytes 3145736 | tf_op jit(solution)/shard_map/ppermute | solution.py:30
  22.4 20.4 %collective-permute-start.10 = (bf16[128,2048]{1,0:T(8,128)(2,1)S(1)}, bf16[128,2048]{1,0:T(8,128)(2,1)S(1)}, u32[]{:S(2)}, u32[]{:S(2)}) collective-permute-start(bf16[128,2048]{1,0:T(8,128)(2,1)S(1)} %get-tuple-element.97), channel_id=1, source_target_pairs={{0,16},{4,20},{8,24},{12,28},{16,0},{20,4},{24,8},{28,12},{1,17},{... | collective-permute-start | bytes 1572872 | tf_op jit(solution)/shard_map/ppermute | solution.py:26
  22.9 19.9 %collective-permute-start.9 = (bf16[128,2048]{1,0:T(8,128)(2,1)S(1)}, bf16[128,2048]{1,0:T(8,128)(2,1)S(1)}, u32[]{:S(2)}, u32[]{:S(2)}) collective-permute-start(bf16[128,2048]{1,0:T(8,128)(2,1)S(1)} %get-tuple-element.97), channel_id=1, source_target_pairs={{0,8},{4,12},{8,0},{12,4},{16,24},{20,28},{24,16},{28,20},{1,9},{5... | collective-permute-start | bytes 1572872 | tf_op jit(solution)/shard_map/ppermute | solution.py:26
  34.0 10.3 %collective-permute-start.11 = (bf16[128,2048]{1,0:T(8,128)(2,1)S(1)}, bf16[128,2048]{1,0:T(8,128)(2,1)S(1)}, u32[]{:S(2)}, u32[]{:S(2)}) collective-permute-start(bf16[128,2048]{1,0:T(8,128)(2,1)S(1)} %collective-permute-done.refs_4_), channel_id=1, source_target_pairs={{0,4},{4,0},{8,12},{12,8},{16,20},{20,16},{24,28},{28,24},{1,5},{5... | collective-permute-start | bytes 1572872 | tf_op jit(solution)/shard_map/ppermute | solution.py:26
  34.0 10.3 %collective-permute-start.12 = (bf16[128,2048]{1,0:T(8,128)(2,1)S(1)}, bf16[128,2048]{1,0:T(8,128)(2,1)S(1)}, u32[]{:S(2)}, u32[]{:S(2)}) collective-permute-start(bf16[128,2048]{1,0:T(8,128)(2,1)S(1)} %collective-permute-done.1.refs_8_), channel_id=1, source_target_pairs={{0,4},{4,0},{8,12},{12,8},{16,20},{20,16},{24,28},{28,24},{1,5},{5... | collective-permute-start | bytes 1572872 | tf_op jit(solution)/shard_map/ppermute | solution.py:26
  44.3 14.9 %collective-permute-start.13 = (bf16[128,2048]{1,0:T(8,128)(2,1)S(1)}, bf16[128,2048]{1,0:T(8,128)(2,1)S(1)}, u32[]{:S(2)}, u32[]{:S(2)}) collective-permute-start(bf16[128,2048]{1,0:T(8,128)(2,1)S(1)} %collective-permute-done.refs_4_), channel_id=1, source_target_pairs={{0,16},{4,20},{8,24},{12,28},{16,0},{20,4},{24,8},{28,12},{1,17},{... | collective-permute-start | bytes 1572872 | tf_op jit(solution)/shard_map/ppermute | solution.py:26
  44.8 14.9 %collective-permute-start.14 = (bf16[128,2048]{1,0:T(8,128)(2,1)S(1)}, bf16[128,2048]{1,0:T(8,128)(2,1)S(1)}, u32[]{:S(2)}, u32[]{:S(2)}) collective-permute-start(bf16[128,2048]{1,0:T(8,128)(2,1)S(1)} %collective-permute-done.7.refs_9_), channel_id=1, source_target_pairs={{0,8},{4,12},{8,0},{12,4},{16,24},{20,28},{24,16},{28,20},{1,9},{5... | collective-permute-start | bytes 1572872 | tf_op jit(solution)/shard_map/ppermute | solution.py:26
  46.0 21.0 %collective-permute-start.16 = (bf16[128,2048]{1,0:T(8,128)(2,1)S(1)}, bf16[128,2048]{1,0:T(8,128)(2,1)S(1)}, u32[]{:S(2)}, u32[]{:S(2)}) collective-permute-start(bf16[128,2048]{1,0:T(8,128)(2,1)S(1)} %get-tuple-element.109), channel_id=1, source_target_pairs={{0,8},{4,12},{8,0},{12,4},{16,24},{20,28},{24,16},{28,20},{1,9},{5... | collective-permute-start | bytes 1572872 | tf_op jit(solution)/shard_map/ppermute | solution.py:26
  46.8 20.2 %collective-permute-start.17 = (bf16[128,2048]{1,0:T(8,128)(2,1)S(1)}, bf16[128,2048]{1,0:T(8,128)(2,1)S(1)}, u32[]{:S(2)}, u32[]{:S(2)}) collective-permute-start(bf16[128,2048]{1,0:T(8,128)(2,1)S(1)} %get-tuple-element.109), channel_id=1, source_target_pairs={{0,16},{4,20},{8,24},{12,28},{16,0},{20,4},{24,8},{28,12},{1,17},{... | collective-permute-start | bytes 1572872 | tf_op jit(solution)/shard_map/ppermute | solution.py:26
  48.3 21.4 %collective-permute-start.15 = (bf16[256,2048]{1,0:T(8,128)(2,1)S(1)}, bf16[256,2048]{1,0:T(8,128)(2,1)S(1)}, u32[]{:S(2)}, u32[]{:S(2)}) collective-permute-start(bf16[256,2048]{1,0:T(8,128)(2,1)S(1)} %pad_maximum_fusion.1), channel_id=1, source_target_pairs={{0,1},{1,0},{2,3},{3,2},{4,5},{5,4},{6,7},{7,6},{8,9},{9,8},{10,11... | collective-permute-start | bytes 3145736 | tf_op jit(solution)/shard_map/ppermute | solution.py:30
  59.6 7.9 %collective-permute-start.18 = (bf16[128,2048]{1,0:T(8,128)(2,1)S(1)}, bf16[128,2048]{1,0:T(8,128)(2,1)S(1)}, u32[]{:S(2)}, u32[]{:S(2)}) collective-permute-start(bf16[128,2048]{1,0:T(8,128)(2,1)S(1)} %collective-permute-done.6.refs_5_), channel_id=1, source_target_pairs={{0,4},{4,0},{8,12},{12,8},{16,20},{20,16},{24,28},{28,24},{1,5},{5... | collective-permute-start | bytes 1572872 | tf_op jit(solution)/shard_map/ppermute | solution.py:26
  59.6 7.9 %collective-permute-start.19 = (bf16[128,2048]{1,0:T(8,128)(2,1)S(1)}, bf16[128,2048]{1,0:T(8,128)(2,1)S(1)}, u32[]{:S(2)}, u32[]{:S(2)}) collective-permute-start(bf16[128,2048]{1,0:T(8,128)(2,1)S(1)} %collective-permute-done.7.refs_9_), channel_id=1, source_target_pairs={{0,4},{4,0},{8,12},{12,8},{16,20},{20,16},{24,28},{28,24},{1,5},{5... | collective-permute-start | bytes 1572872 | tf_op jit(solution)/shard_map/ppermute | solution.py:26
  70.0 10.1 %collective-permute-start.26 = (bf16[768,2048]{1,0:T(8,128)(2,1)S(1)}, bf16[768,2048]{1,0:T(8,128)(2,1)S(1)}, u32[]{:S(2)}, u32[]{:S(2)}) collective-permute-start(bf16[768,2048]{1,0:T(8,128)(2,1)S(1)} %pad_maximum_fusion), channel_id=1, source_target_pairs={{0,4},{4,0},{8,12},{12,8},{16,20},{20,16},{24,28},{28,24},{1,5},{5... | collective-permute-start | bytes 9437192 | tf_op jit(solution)/shard_map/ppermute | solution.py:26
  70.3 6.9 %collective-permute-start.25 = (bf16[256,2048]{1,0:T(8,128)(2,1)S(1)}, bf16[256,2048]{1,0:T(8,128)(2,1)S(1)}, u32[]{:S(2)}, u32[]{:S(2)}) collective-permute-start(bf16[256,2048]{1,0:T(8,128)(2,1)S(1)} %pad_maximum_fusion.3), channel_id=1, source_target_pairs={{0,4},{4,0},{8,12},{12,8},{16,20},{20,16},{24,28},{28,24},{1,5},{5... | collective-permute-start | bytes 3145736 | tf_op jit(solution)/shard_map/ppermute | solution.py:26
  70.7 14.0 %collective-permute-start.22 = (bf16[128,2048]{1,0:T(8,128)(2,1)S(1)}, bf16[128,2048]{1,0:T(8,128)(2,1)S(1)}, u32[]{:S(2)}, u32[]{:S(2)}) collective-permute-start(bf16[128,2048]{1,0:T(8,128)(2,1)S(1)} %collective-permute-done.9.refs_2_), channel_id=1, source_target_pairs={{0,16},{4,20},{8,24},{12,28},{16,0},{20,4},{24,8},{28,12},{1,17},{... | collective-permute-start | bytes 1572872 | tf_op jit(solution)/shard_map/ppermute | solution.py:26
  72.2 13.7 %collective-permute-start.23 = (bf16[128,2048]{1,0:T(8,128)(2,1)S(1)}, bf16[128,2048]{1,0:T(8,128)(2,1)S(1)}, u32[]{:S(2)}, u32[]{:S(2)}) collective-permute-start(bf16[128,2048]{1,0:T(8,128)(2,1)S(1)} %collective-permute-done.17.refs_6_), channel_id=1, source_target_pairs={{0,8},{4,12},{8,0},{12,4},{16,24},{20,28},{24,16},{28,20},{1,9},{5... | collective-permute-start | bytes 1572872 | tf_op jit(solution)/shard_map/ppermute | solution.py:26
  73.1 13.4 %collective-permute-start.24 = (bf16[128,2048]{1,0:T(8,128)(2,1)S(1)}, bf16[128,2048]{1,0:T(8,128)(2,1)S(1)}, u32[]{:S(2)}, u32[]{:S(2)}) collective-permute-start(bf16[128,2048]{1,0:T(8,128)(2,1)S(1)} %collective-permute-done.13.refs_12_), channel_id=1, source_target_pairs={{0,1},{1,0},{2,3},{3,2},{4,5},{5,4},{6,7},{7,6},{8,9},{9,8},{10,11... | collective-permute-start | bytes 1572872 | tf_op jit(solution)/shard_map/ppermute | solution.py:30
  86.8 5.7 %collective-permute-start.30 = (bf16[768,2048]{1,0:T(8,128)(2,1)S(1)}, bf16[768,2048]{1,0:T(8,128)(2,1)S(1)}, u32[]{:S(2)}, u32[]{:S(2)}) collective-permute-start(bf16[768,2048]{1,0:T(8,128)(2,1)S(1)} %constant_dynamic-update-slice_fusion), channel_id=1, source_target_pairs={{0,4},{4,0},{8,12},{12,8},{16,20},{20,16},{24,28},{28,24},{1,5},{5... | collective-permute-start | bytes 9437192 | tf_op jit(solution)/shard_map/ppermute | solution.py:26
  87.5 9.7 %collective-permute-start.29 = (bf16[128,2048]{1,0:T(8,128)(2,1)S(1)}, bf16[128,2048]{1,0:T(8,128)(2,1)S(1)}, u32[]{:S(2)}, u32[]{:S(2)}) collective-permute-start(bf16[128,2048]{1,0:T(8,128)(2,1)S(1)} %collective-permute-done.24.refs_1_.refs_19_), channel_id=1, source_target_pairs={{0,4},{4,0},{8,12},{12,8},{16,20},{20,16},{24,28},{28,24},{1,5},{5... | collective-permute-start | bytes 1572872 | tf_op jit(solution)/shard_map/ppermute | solution.py:26
  87.7 8.6 %collective-permute-start.27 = (bf16[64,2048]{1,0:T(8,128)(2,1)S(1)}, bf16[64,2048]{1,0:T(8,128)(2,1)S(1)}, u32[]{:S(2)}, u32[]{:S(2)}) collective-permute-start(bf16[64,2048]{1,0:T(8,128)(2,1)S(1)} %get-tuple-element.165), channel_id=1, source_target_pairs={{0,8},{4,12},{8,0},{12,4},{16,24},{20,28},{24,16},{28,20},{1,9},{5... | collective-permute-start | bytes 786440 | tf_op jit(solution)/shard_map/ppermute | solution.py:26
  88.9 8.3 %collective-permute-start.28 = (bf16[64,2048]{1,0:T(8,128)(2,1)S(1)}, bf16[64,2048]{1,0:T(8,128)(2,1)S(1)}, u32[]{:S(2)}, u32[]{:S(2)}) collective-permute-start(bf16[64,2048]{1,0:T(8,128)(2,1)S(1)} %get-tuple-element.164), channel_id=1, source_target_pairs={{0,16},{4,20},{8,24},{12,28},{16,0},{20,4},{24,8},{28,12},{1,17},{... | collective-permute-start | bytes 786440 | tf_op jit(solution)/shard_map/ppermute | solution.py:26
  103.6 5.9 %collective-permute-start.36 = (f32[8,2048]{1,0:T(8,128)S(1)}, f32[8,2048]{1,0:T(8,128)S(1)}, u32[]{:S(2)}, u32[]{:S(2)}) collective-permute-start(f32[8,2048]{1,0:T(8,128)S(1)} %get-tuple-element.151), channel_id=1, source_target_pairs={{0,24},{4,28},{8,16},{12,20},{16,8},{20,12},{24,0},{28,4},{1,25},{... | collective-permute-start | bytes 196616 | tf_op jit(solution)/shard_map/ppermute | solution.py:26
  105.5 4.6 %collective-permute-start.34 = (f32[8,2048]{1,0:T(8,128)S(1)}, f32[8,2048]{1,0:T(8,128)S(1)}, u32[]{:S(2)}, u32[]{:S(2)}) collective-permute-start(f32[8,2048]{1,0:T(8,128)S(1)} %get-tuple-element.151), channel_id=1, source_target_pairs={{0,8},{4,12},{8,0},{12,4},{16,24},{20,28},{24,16},{28,20},{1,9},{5... | collective-permute-start | bytes 196616 | tf_op jit(solution)/shard_map/ppermute | solution.py:26
  116.8 6.4 %collective-permute-start.38 = (f32[1,2048]{1,0:T(1,128)S(1)}, f32[1,2048]{1,0:T(1,128)S(1)}, u32[]{:S(2)}, u32[]{:S(2)}) collective-permute-start(f32[1,2048]{1,0:T(1,128)S(1)} %get-tuple-element.160), channel_id=1, source_target_pairs={{0,1},{1,0},{2,3},{3,2},{4,5},{5,4},{6,7},{7,6},{8,9},{9,8},{10,11... | collective-permute-start | bytes 24584 | tf_op jit(solution)/shard_map/ppermute | solution.py:30
  123.2 11.0 %collective-permute-start.39 = (f32[1,2048]{1,0:T(1,128)S(1)}, f32[1,2048]{1,0:T(1,128)S(1)}, u32[]{:S(2)}, u32[]{:S(2)}) collective-permute-start(f32[1,2048]{1,0:T(1,128)S(1)} %add.8.refs_0_), channel_id=1, source_target_pairs={{0,2},{1,3},{2,0},{3,1},{4,6},{5,7},{6,4},{7,5},{8,10},{9,11},{10,... | collective-permute-start | bytes 24584 | tf_op jit(solution)/shard_map/ppermute | solution.py:30
  (16 other events, 86.8 us)

commit v7 on v6

--- a/solution.py
+++ b/solution.py
@@ -294,7 +294,7 @@
     )(where, *map(near, (x, first_pre, back, both, *extra)), *shards.operands())
 
 
-def scan_call(where, first_pre, second_pre, back, both, parts, wholes, offsets, ranks, tile):
+def scan_call(where, first_pre, second_pre, back, both, parts, wholes, offsets, ranks, shard, tile):
     rows, width = first_pre.shape
     pairs = rows // (2 * SEGMENTS)
 
@@ -365,7 +365,13 @@
                 one, other = choose(where_ref, gate_grad.astype(BF16), cand_grad.astype(BF16))
                 one_hold[here, :] = one
                 other_hold[here, :] = other
-            state_ref[:, span] = dot(order, state_hold[...]).astype(BF16)
+            found = dot(order, state_hold[...]).astype(BF16)
+            size = min(shard, tile)
+            for part in range(0, tile, size):
+                target = span.start + part
+                if shard <= tile:
+                    target = (where_ref[0] ^ lax.div(target, shard)) * shard
+                state_ref[:, pl.ds(pl.multiple_of(target, size), size)] = found[:, part : part + size]
             one_ref[span, :] = dot(one_hold[...].T, order_back).astype(BF16)
             other_ref[span, :] = dot(other_hold[...].T, order_back).astype(BF16)
 
@@ -393,13 +399,9 @@
     count, depth = len(shards.groups), shards.depth
 
     def kernel(where_ref, x_ref, residual_ref, *refs):
-        refs, (out_ref, ordered) = refs[:-2], refs[-2:]
-        for index in range(count):
-            source = pl.ds(pl.multiple_of((where_ref[0] ^ index) * depth, depth), depth)
-            ordered[:, index * depth : (index + 1) * depth] = x_ref[:, source]
-
+        refs, out_ref = refs[:-1], refs[-1]
         def body(span):
-            total = shards.product(ordered, 0, refs, span)
+            total = shards.product(x_ref, 0, refs, span)
             out_ref[:, span] = (residual_ref[:, span].astype(F32) + total).astype(BF16)
 
         tiles(width, tile, body)
@@ -409,7 +411,6 @@
         out_shape=jax.ShapeDtypeStruct((rows, width), BF16),
         in_specs=[SMEM_SPEC] + [VMEM_SPEC] * 2 + [VMEM_SPEC] * len(shards.pieces),
         out_specs=VMEM_SPEC,
-        scratch_shapes=[pltpu.VMEM((rows, count * depth), BF16)],
         compiler_params=params(14),
         cost_estimate=cost(2 * rows * count * depth * width, 2 * count * depth * width),
         name="layer_rows",
@@ -509,11 +510,9 @@
     f6a, f6b = send(f2a, 4), send(f4b, 2)
     t2b, t4b = send(t_b, 2), send(t_b, 4)
     sb = over(f_b2)
-    f6a, f6b, f3b, f5b, t3a, t5a = after((f6a, f6b, f2b, f4b, t2a, t4a))
-    f3b, f5b, t3a, t5a = core(f3b), core(f5b), core(t3a), core(t5a)
-    both, f6a, f6b, sb, t2b, t4b, f3b, f5b, t3a, t5a, sa, t2a = after(
-        (both, f6a, f6b, sb, t2b, t4b, f3b, f5b, t3a, t5a, sa, t2a)
-    )
+    f6a, f6b, f3b, f5b = after((f6a, f6b, f2b, f4b))
+    f3b, f5b = core(f3b), core(f5b)
+    both, f6a, f6b, sb, t2b, t4b, f3b, f5b, sa, t2a = after((both, f6a, f6b, sb, t2b, t4b, f3b, f5b, sa, t2a))
     t6a, t6b = send(t2a, 4), send(t4b, 2)
     s6a = over(f6a)
     f7, cs = core(stack(f6a, f6b)), core(stack(sa, sb, own_s))
@@ -522,18 +521,18 @@
     most = [[own_s], cut(cs, 4, 5), pairs(sa, sb, 0), cut(cs, 0, 2), pairs(sa, sb, 1), cut(cs, 1, 3)]
     first_pre = project_call(normed, first, tile, BF16)
     partial = project_call(normed, Shards(most), tile, F32)
+    both = jnp.concatenate([both, send(after((both,), partial)[0], 4)], axis=1)
     t6a, t6b, s6a, sb_out, first_pre, partial, own_t, both = after(
         (t6a, t6b, s6a, sb, first_pre, partial, own_t, both)
     )
     quarter = half // 2
     s6b = [send(sb_out[half : half + quarter], 2), send(sb_out[quarter:half], 4)]
     s7a = core(s6a)
-    c4 = core(stack(t6a, t6b, t2b, t4b, own_t))
+    c4 = core(stack(t6a, t6b, t2b, t4b, own_t, t2a, t4a))
     third = Shards(
-        [[own_t], cut(c4, 4, 5), [t2a, t2b], [t3a, (c4, 2 * half, half)], [t4a, t4b], [t5a, (c4, 3 * half, half)]]
+        [[own_t], cut(c4, 4, 5), [t2a, t2b], cut(c4, 6, 2), [t4a, t4b], cut(c4, 7, 3)]
         + [[t6a, t6b], cut(c4, 0, 1)]
     )
-    both = jnp.concatenate([both, send(both, 4)], axis=1)
     back = back_call(where, grads, third)
     s6b_low, s6b_high, s7a, back, both = after((*s6b, s7a, back, both))
     last = [[s6a, s6b_low, s6b_high], [s7a, core(stack(s6b_low, s6b_high))]]
@@ -582,7 +581,7 @@
     else:
         wholes, offsets = [lax.all_gather(whole, "seq")], [range(ranks)]
     state_rows, one, other, bias_part, state_grad = scan_call(
-        where, first_pre, second_pre, back, both, parts, wholes, offsets, ranks, tile
+        where, first_pre, second_pre, back, both, parts, wholes, offsets, ranks, third.depth, tile
     )
     width = hidden // ranks
     if cube:

time: 135 us -> 132 us (0.978)
  waiting for transfers between devices: 61.3 us -> 57 us
  other arithmetic: 3.53 us -> 5.61 us
    ppermute x35 -> x33, waiting for transfers between devices: 59.2 us -> 54.9 us  [hop(): return lax.ppermute(value, 'seq', [(i, i ^ offset) for i in range(count)])]
    ppermute x35 -> x33, starting transfers between devices: 25.6 us -> 25.6 us  [hop(): return lax.ppermute(value, 'seq', [(i, i ^ offset) for i in range(count)])]
  transfers between devices with their start and end apart: 40 -> 38, of which waited for: 25 -> 18; matrix products, arithmetic and copies ran while one was open for 1% -> 3% of each run, Pallas kernels for 18% -> 18%
where the time goes in v7:
time: 132 us
  waiting for transfers between devices  57 us (43%)
  Pallas kernels  34.4 us (26%)
  starting transfers between devices  33.6 us (25%)
  other arithmetic  5.61 us (4%)
    ppermute x33, waiting for transfers between devices, hop(): return lax.ppermute(value, 'seq', [(i, i ^ offset) for i in range(count)])  54.9 us
    ppermute x33, starting transfers between devices, hop(): return lax.ppermute(value, 'seq', [(i, i ^ offset) for i in range(count)])  25.6 us
    pallas_call x1, Pallas kernels, input_grad_call(): pl.pallas_call(kernel, out_shape=jax.ShapeDtypeStruct((rows, width), BF16...  8.38 us
    ppermute x5, starting transfers between devices, swap_batch(): return lax.ppermute(value, 'batch', [(i, i ^ offset) for i in range(count)])  7.95 us
    pallas_call x2, Pallas kernels, project_call(): pl.pallas_call(kernel, out_shape=jax.ShapeDtypeStruct((rows, width), dtyp...  5.15 us
    pallas_call x1, Pallas kernels, layer_call(): pl.pallas_call(kernel, out_shape=jax.ShapeDtypeStruct((rows, width), BF16...  4.56 us
    pallas_call x1, Pallas kernels, scan_call(): pl.pallas_call(kernel, out_shape=[wide, tall, tall, flat, flat], in_specs...  4.43 us
    pallas_call x1, Pallas kernels, totals_call(): pl.pallas_call(kernel, out_shape=[jax.ShapeDtypeStruct((rows, width), BF1...  4.41 us
  transfers between devices with their start and end apart: 38, of which 18 were waited for; matrix products, arithmetic and copies ran while one was open for 3% of the time, Pallas kernels for 18%

profile of v7, /device:TPU:0, one launch (start us, length us, event | category | flops | bytes accessed | tf_op | source)
XLA Modules:
  0.0 132.1 jit_solution(6827294250772665043)
XLA Ops:
  0.8 1.4 %slice_select_fusion.1.refs_0_ = bf16[128,2048]{1,0:T(8,128)(2,1)S(1)} fusion(bf16[256,2048]{1,0:T(8,128)(2,1)} %param.14, bf16[256,2048]{1,0:T(8,128)(2,1)} %param.13, pred[]{:T(512)S(6)} %eq.5), kind=kLoop, calls=%fused_computation.7 | loop fusion | flops 262144 | bytes 1572865 | tf_op jit(solution)/shard_map/jit(_where)/select_n | solution.py:486
  2.2 3.0 %collective-permute-start = (bf16[128,2048]{1,0:T(8,128)(2,1)S(1)}, bf16[128,2048]{1,0:T(8,128)(2,1)S(1)}, u32[]{:S(2)}, u32[]{:S(2)}) collective-permute-start(bf16[128,2048]{1,0:T(8,128)(2,1)S(1)} %slice_select_fusion.1.refs_0_), channel_id=1, source_target_pairs={{0,8},{4,12},{8,0},{12,4},{16,24},{20,28},{24,16},{28,20},{1,9},{5... | collective-permute-start | bytes 1572872 | tf_op jit(solution)/shard_map/ppermute | solution.py:26
  5.2 1.5 %collective-permute-start.1 = (bf16[128,2048]{1,0:T(8,128)(2,1)S(1)}, bf16[128,2048]{1,0:T(8,128)(2,1)S(1)}, u32[]{:S(2)}, u32[]{:S(2)}) collective-permute-start(bf16[128,2048]{1,0:T(8,128)(2,1)S(1)} %slice_select_fusion.1.refs_0_), channel_id=1, source_target_pairs={{0,16},{4,20},{8,24},{12,28},{16,0},{20,4},{24,8},{28,12},{1,17},{... | collective-permute-start | bytes 1572872 | tf_op jit(solution)/shard_map/ppermute | solution.py:26
  11.4 3.3 %norm_rows.1 = (bf16[256,2048]{1,0:T(8,128)(2,1)S(1)}, bf16[2048,256]{1,0:T(8,128)(2,1)S(1)}) custom-call(s32[3]{0:T(128)S(1)} %pad_add_fusion.where_ref, bf16[256,2048]{1,0:T(8,128)(2,1)S(1)} %bitcast.14, bf16[256,2048]{1,0:T(8,128)(2,1)S(1)} %bitcast.17, f32[1,2048]{1,0:T(1,128)S(1)} %bitcast.20), custom_call_target="tpu_custom_call" | custom-call | flops 536870912 | bytes 4194304 | tf_op jit(solution)/shard_map/norm_rows/pallas_call | solution.py:132
  14.7 2.5 %collective-permute-done.5 = f32[2,512]{1,0:T(2,128)S(1)} collective-permute-done((f32[2,512]{1,0:T(2,128)S(1)}, f32[2,512]{1,0:T(2,128)S(1)}, u32[]{:S(2)}, u32[]{:S(2)}) %collective-permute-start.5) | collective-permute-done | bytes 4128 | tf_op jit(solution)/shard_map/ppermute | solution.py:26
  19.0 1.6 %collective-permute-start.7 = (bf16[128,2048]{1,0:T(8,128)(2,1)S(1)}, bf16[128,2048]{1,0:T(8,128)(2,1)S(1)}, u32[]{:S(2)}, u32[]{:S(2)}) collective-permute-start(bf16[128,2048]{1,0:T(8,128)(2,1)S(1)} %slice_select_fusion.refs_1_), channel_id=1, source_target_pairs={{0,16},{4,20},{8,24},{12,28},{16,0},{20,4},{24,8},{28,12},{1,17},{... | collective-permute-start | bytes 1572872 | tf_op jit(solution)/shard_map/ppermute | solution.py:26
  20.7 1.6 %collective-permute-start.8 = (bf16[256,2048]{1,0:T(8,128)(2,1)S(1)}, bf16[256,2048]{1,0:T(8,128)(2,1)S(1)}, u32[]{:S(2)}, u32[]{:S(2)}) collective-permute-start(bf16[256,2048]{1,0:T(8,128)(2,1)S(1)} %pad_maximum_fusion.2), channel_id=1, source_target_pairs={{0,1},{1,0},{2,3},{3,2},{4,5},{5,4},{6,7},{7,6},{8,9},{9,8},{10,11... | collective-permute-start | bytes 3145736 | tf_op jit(solution)/shard_map/ppermute | solution.py:30
  22.9 1.5 %collective-permute-start.9 = (bf16[128,2048]{1,0:T(8,128)(2,1)S(1)}, bf16[128,2048]{1,0:T(8,128)(2,1)S(1)}, u32[]{:S(2)}, u32[]{:S(2)}) collective-permute-start(bf16[128,2048]{1,0:T(8,128)(2,1)S(1)} %get-tuple-element.94), channel_id=1, source_target_pairs={{0,8},{4,12},{8,0},{12,4},{16,24},{20,28},{24,16},{28,20},{1,9},{5... | collective-permute-start | bytes 1572872 | tf_op jit(solution)/shard_map/ppermute | solution.py:26
  24.4 9.1 %collective-permute-done.6.refs_5_ = bf16[128,2048]{1,0:T(8,128)(2,1)S(1)} collective-permute-done((bf16[128,2048]{1,0:T(8,128)(2,1)S(1)}, bf16[128,2048]{1,0:T(8,128)(2,1)S(1)}, u32[]{:S(2)}, u32[]{:S(2)}) %collective-permute-start.6) | collective-permute-done | bytes 524320 | tf_op jit(solution)/shard_map/ppermute | solution.py:26
  34.5 8.3 %collective-permute-done.10.refs_4_ = bf16[128,2048]{1,0:T(8,128)(2,1)S(1)} collective-permute-done((bf16[128,2048]{1,0:T(8,128)(2,1)S(1)}, bf16[128,2048]{1,0:T(8,128)(2,1)S(1)}, u32[]{:S(2)}, u32[]{:S(2)}) %collective-permute-start.10) | collective-permute-done | bytes 524320 | tf_op jit(solution)/shard_map/ppermute | solution.py:26
  42.8 1.4 %collective-permute-done.8.refs_2_.refs_17_ = bf16[256,2048]{1,0:T(8,128)(2,1)S(1)} collective-permute-done((bf16[256,2048]{1,0:T(8,128)(2,1)S(1)}, bf16[256,2048]{1,0:T(8,128)(2,1)S(1)}, u32[]{:S(2)}, u32[]{:S(2)}) %collective-permute-start.8) | collective-permute-done | bytes 1048608 | tf_op jit(solution)/shard_map/ppermute | solution.py:30
  45.9 1.6 %collective-permute-start.15 = (bf16[256,2048]{1,0:T(8,128)(2,1)S(1)}, bf16[256,2048]{1,0:T(8,128)(2,1)S(1)}, u32[]{:S(2)}, u32[]{:S(2)}) collective-permute-start(bf16[256,2048]{1,0:T(8,128)(2,1)S(1)} %pad_maximum_fusion.1), channel_id=1, source_target_pairs={{0,1},{1,0},{2,3},{3,2},{4,5},{5,4},{6,7},{7,6},{8,9},{9,8},{10,11... | collective-permute-start | bytes 3145736 | tf_op jit(solution)/shard_map/ppermute | solution.py:30
  48.3 1.5 %collective-permute-start.17 = (bf16[128,2048]{1,0:T(8,128)(2,1)S(1)}, bf16[128,2048]{1,0:T(8,128)(2,1)S(1)}, u32[]{:S(2)}, u32[]{:S(2)}) collective-permute-start(bf16[128,2048]{1,0:T(8,128)(2,1)S(1)} %get-tuple-element.104), channel_id=1, source_target_pairs={{0,16},{4,20},{8,24},{12,28},{16,0},{20,4},{24,8},{28,12},{1,17},{... | collective-permute-start | bytes 1572872 | tf_op jit(solution)/shard_map/ppermute | solution.py:26
  49.8 9.2 %collective-permute-done.13.refs_12_ = bf16[128,2048]{1,0:T(8,128)(2,1)S(1)} collective-permute-done((bf16[128,2048]{1,0:T(8,128)(2,1)S(1)}, bf16[128,2048]{1,0:T(8,128)(2,1)S(1)}, u32[]{:S(2)}, u32[]{:S(2)}) %collective-permute-start.13) | collective-permute-done | bytes 524320 | tf_op jit(solution)/shard_map/ppermute | solution.py:26
  60.1 6.9 %collective-permute-done.16.refs_3_ = bf16[128,2048]{1,0:T(8,128)(2,1)S(1)} collective-permute-done((bf16[128,2048]{1,0:T(8,128)(2,1)S(1)}, bf16[128,2048]{1,0:T(8,128)(2,1)S(1)}, u32[]{:S(2)}, u32[]{:S(2)}) %collective-permute-start.16) | collective-permute-done | bytes 524320 | tf_op jit(solution)/shard_map/ppermute | solution.py:26
  68.8 1.6 %collective-permute-start.22 = (bf16[128,2048]{1,0:T(8,128)(2,1)S(1)}, bf16[128,2048]{1,0:T(8,128)(2,1)S(1)}, u32[]{:S(2)}, u32[]{:S(2)}) collective-permute-start(bf16[128,2048]{1,0:T(8,128)(2,1)S(1)} %collective-permute-done.13.refs_12_), channel_id=1, source_target_pairs={{0,1},{1,0},{2,3},{3,2},{4,5},{5,4},{6,7},{7,6},{8,9},{9,8},{10,11... | collective-permute-start | bytes 1572872 | tf_op jit(solution)/shard_map/ppermute | solution.py:30
  70.4 1.5 %collective-permute-start.20 = (bf16[128,2048]{1,0:T(8,128)(2,1)S(1)}, bf16[128,2048]{1,0:T(8,128)(2,1)S(1)}, u32[]{:S(2)}, u32[]{:S(2)}) collective-permute-start(bf16[128,2048]{1,0:T(8,128)(2,1)S(1)} %collective-permute-done.9.refs_2_), channel_id=1, source_target_pairs={{0,16},{4,20},{8,24},{12,28},{16,0},{20,4},{24,8},{28,12},{1,17},{... | collective-permute-start | bytes 1572872 | tf_op jit(solution)/shard_map/ppermute | solution.py:26
  73.8 2.3 %project.3.refs_0_ = f32[256,2048]{1,0:T(8,128)S(1)} custom-call(bf16[256,2048]{1,0:T(8,128)(2,1)S(1)} %get-tuple-element.113.x_ref, bf16[256,2048]{1,0:T(8,128)(2,1)S(1)} %broadcast_select_fusion.refs_0_.refs_15_, bf16[768,2048]{1,0:T(8,128)(2,1)S(1)} %collective-permute-done.24.refs_1_.refs_16_, ...), custom_call_target="tpu_custom_call" | custom-call | flops 1610612736 | bytes 6291456 | tf_op jit(solution)/shard_map/project/pallas_call | solution.py:156
  76.1 1.6 %collective-permute-start.25 = (f32[2,1024]{1,0:T(2,128)S(1)}, f32[2,1024]{1,0:T(2,128)S(1)}, u32[]{:S(2)}, u32[]{:S(2)}) collective-permute-start(f32[2,1024]{1,0:T(2,128)S(1)} %pad_maximum_fusion.8), channel_id=1, source_target_pairs={{0,16},{4,20},{8,24},{12,28},{16,0},{20,4},{24,8},{28,12},{1,17},{... | collective-permute-start | bytes 24584 | tf_op jit(solution)/shard_map/ppermute | solution.py:26
  77.7 2.9 %project.2.first_ref = bf16[256,2048]{1,0:T(8,128)(2,1)S(1)} custom-call(bf16[256,2048]{1,0:T(8,128)(2,1)S(1)} %get-tuple-element.113.x_ref, bf16[128,2048]{1,0:T(8,128)(2,1)S(1)} %slice_select_fusion.1.refs_0_, bf16[128,2048]{1,0:T(8,128)(2,1)S(1)} %slice_select_fusion.refs_1_, bf16[128,2048]{1,0:T(8,128)(2,1)S(1)} %collective-permute-done.2.refs_2_, ...), custom_call_target="tpu_custom_call" | custom-call | flops 2147483648 | bytes 8388608 | tf_op jit(solution)/shard_map/project/pallas_call | solution.py:156
  80.6 3.6 %collective-permute-done.25 = f32[2,1024]{1,0:T(2,128)S(1)} collective-permute-done((f32[2,1024]{1,0:T(2,128)S(1)}, f32[2,1024]{1,0:T(2,128)S(1)}, u32[]{:S(2)}, u32[]{:S(2)}) %collective-permute-start.25) | collective-permute-done | bytes 8224 | tf_op jit(solution)/shard_map/ppermute | solution.py:26
  87.9 5.0 %collective-permute-done.29.refs_1_ = bf16[1024,2048]{1,0:T(8,128)(2,1)S(1)} collective-permute-done((bf16[1024,2048]{1,0:T(8,128)(2,1)S(1)}, bf16[1024,2048]{1,0:T(8,128)(2,1)S(1)}, u32[]{:S(2)}, u32[]{:S(2)}) %collective-permute-start.29) | collective-permute-done | bytes 4194336 | tf_op jit(solution)/shard_map/ppermute | solution.py:26
  92.9 3.0 %back_rows.1.back_ref = bf16[256,2048]{1,0:T(8,128)(2,1)S(1)} custom-call(s32[3]{0:T(128)S(1)} %pad_add_fusion.where_ref, bf16[2048,256]{1,0:T(8,128)(2,1)S(1)} %get-tuple-element.129.g_ref, bf16[256,2048]{1,0:T(8,128)(2,1)S(1)} %copy-done, bf16[1024,2048]{1,0:T(8,128)(2,1)S(1)} %collective-permute-done.29.refs_1_, ...), custom_call_target="tpu_custom_call" | custom-call | flops 2147483648 | bytes 8388608 | tf_op jit(solution)/shard_map/back_rows/pallas_call | solution.py:180
  96.2 1.8 %collective-permute-done.30.refs_5_.refs_23_ = bf16[128,2048]{1,0:T(8,128)(2,1)S(1)} collective-permute-done((bf16[128,2048]{1,0:T(8,128)(2,1)S(1)}, bf16[128,2048]{1,0:T(8,128)(2,1)S(1)}, u32[]{:S(2)}, u32[]{:S(2)}) %collective-permute-start.30) | collective-permute-done | bytes 524320 | tf_op jit(solution)/shard_map/ppermute | solution.py:26
  98.0 4.4 %project_totals.1 = (bf16[256,2048]{1,0:T(8,128)(2,1)S(1)}, f32[3,8,2048]{2,1,0:T(8,128)S(1)}, f32[8,2048]{1,0:T(8,128)S(1)}, f32[2,2048]{1,0:T(2,128)S(1)}) custom-call(s32[3]{0:T(128)S(1)} %pad_add_fusion.where_ref, bf16[256,2048]{1,0:T(8,128)(2,1)S(1)} %get-tuple-element.113.x_ref, bf16[256,2048]{1,0:T(8,128)(2,1)S(1)} %project.2.first_ref, ...), custom_call_target="tpu_custom_call" | custom-call | flops 536870912 | bytes 2097152 | tf_op jit(solution)/shard_map/project_totals/pallas_call | solution.py:281
  104.4 1.5 %collective-permute-start.33 = (f32[8,2048]{1,0:T(8,128)S(1)}, f32[8,2048]{1,0:T(8,128)S(1)}, u32[]{:S(2)}, u32[]{:S(2)}) collective-permute-start(f32[8,2048]{1,0:T(8,128)S(1)} %get-tuple-element.145), channel_id=1, source_target_pairs={{0,16},{4,20},{8,24},{12,28},{16,0},{20,4},{24,8},{28,12},{1,17},{... | collective-permute-start | bytes 196616 | tf_op jit(solution)/shard_map/ppermute | solution.py:26
  106.0 2.3 %collective-permute-done.34 = f32[8,2048]{1,0:T(8,128)S(1)} collective-permute-done((f32[8,2048]{1,0:T(8,128)S(1)}, f32[8,2048]{1,0:T(8,128)S(1)}, u32[]{:S(2)}, u32[]{:S(2)}) %collective-permute-start.34) | collective-permute-done | bytes 65568 | tf_op jit(solution)/shard_map/ppermute | solution.py:26
  109.0 1.4 %collective-permute-done.35.refs_2_ = f32[3,8,2048]{2,1,0:T(8,128)S(1)} collective-permute-done((f32[3,8,2048]{2,1,0:T(8,128)S(1)}, f32[3,8,2048]{2,1,0:T(8,128)S(1)}, u32[]{:S(2)}, u32[]{:S(2)}) %collective-permute-start.35) | collective-permute-done | bytes 196640 | tf_op jit(solution)/shard_map/ppermute | solution.py:26
  110.4 4.4 %scan_rows.1 = (bf16[256,2048]{1,0:T(8,128)(2,1)S(1)}, bf16[2048,256]{1,0:T(8,128)(2,1)S(1)}, bf16[2048,256]{1,0:T(8,128)(2,1)S(1)}, f32[1,2048]{1,0:T(1,128)S(1)}, f32[1,2048]{1,0:T(1,128)S(1)}) custom-call(s32[3]{0:T(128)S(1)} %pad_add_fusion.where_ref, bf16[256,2048]{1,0:T(8,128)(2,1)S(1)} %project.2.first_ref, ...), custom_call_target="tpu_custom_call" | custom-call | flops 805306368 | bytes 6291456 | tf_op jit(solution)/shard_map/scan_rows/pallas_call | solution.py:383
  115.4 4.6 %layer_rows.1 = bf16[256,2048]{1,0:T(8,128)(2,1)} custom-call(s32[3]{0:T(128)S(1)} %pad_add_fusion.where_ref, bf16[256,2048]{1,0:T(8,128)(2,1)S(1)} %get-tuple-element.146.x_ref, bf16[256,2048]{1,0:T(8,128)(2,1)S(1)} %bitcast.15, bf16[256,2048]{1,0:T(8,128)(2,1)S(1)} %copy-done, bf16[1024,2048]{1,0:T(8,128)(2,1)S(1)} %collective-permute-done.29.refs_1_, ...), custom_call_target="tpu_custom_call" | custom-call | flops 2147483648 | bytes 8388608 | tf_op jit(solution)/shard_map/layer_rows/pallas_call | solution.py:409
  119.9 2.6 %collective-permute-start.37 = (f32[1,2048]{1,0:T(1,128)S(1)}, f32[1,2048]{1,0:T(1,128)S(1)}, u32[]{:S(2)}, u32[]{:S(2)}) collective-permute-start(f32[1,2048]{1,0:T(1,128)S(1)} %add.8.refs_0_), channel_id=1, source_target_pairs={{0,2},{1,3},{2,0},{3,1},{4,6},{5,7},{6,4},{7,5},{8,10},{9,11},{10,... | collective-permute-start | bytes 24584 | tf_op jit(solution)/shard_map/ppermute | solution.py:30
  122.6 8.4 %input_grad_rows.1 = bf16[256,2048]{1,0:T(8,128)(2,1)} custom-call(s32[3]{0:T(128)S(1)} %pad_add_fusion.where_ref, bf16[2048,256]{1,0:T(8,128)(2,1)S(1)} %get-tuple-element.151.one_ref, bf16[2048,256]{1,0:T(8,128)(2,1)S(1)} %get-tuple-element.152.other_ref, bf16[256,2048]{1,0:T(8,128)(2,1)S(1)} %bitcast.16, bf16[256,2048]{1,0:T(8,128)(2,1)S(1)} %bitcast.18, ...), custom_call_target="tpu_custom_call" | custom-call | flops 4294967296 | bytes 16777216 | tf_op jit(solution)/shard_map/input_grad_rows/pallas_call | solution.py:448
  (90 shorter events, 23.7 us)
Async XLA Ops:
  2.2 15.0 %collective-permute-start = (bf16[128,2048]{1,0:T(8,128)(2,1)S(1)}, bf16[128,2048]{1,0:T(8,128)(2,1)S(1)}, u32[]{:S(2)}, u32[]{:S(2)}) collective-permute-start(bf16[128,2048]{1,0:T(8,128)(2,1)S(1)} %slice_select_fusion.1.refs_0_), channel_id=1, source_target_pairs={{0,8},{4,12},{8,0},{12,4},{16,24},{20,28},{24,16},{28,20},{1,9},{5... | collective-permute-start | bytes 1572872 | tf_op jit(solution)/shard_map/ppermute | solution.py:26
  5.2 13.4 %collective-permute-start.1 = (bf16[128,2048]{1,0:T(8,128)(2,1)S(1)}, bf16[128,2048]{1,0:T(8,128)(2,1)S(1)}, u32[]{:S(2)}, u32[]{:S(2)}) collective-permute-start(bf16[128,2048]{1,0:T(8,128)(2,1)S(1)} %slice_select_fusion.1.refs_0_), channel_id=1, source_target_pairs={{0,16},{4,20},{8,24},{12,28},{16,0},{20,4},{24,8},{28,12},{1,17},{... | collective-permute-start | bytes 1572872 | tf_op jit(solution)/shard_map/ppermute | solution.py:26
  6.7 11.9 %collective-permute-start.2 = (bf16[128,2048]{1,0:T(8,128)(2,1)S(1)}, bf16[128,2048]{1,0:T(8,128)(2,1)S(1)}, u32[]{:S(2)}, u32[]{:S(2)}) collective-permute-start(bf16[128,2048]{1,0:T(8,128)(2,1)S(1)} %slice_select_fusion.1.refs_0_), channel_id=1, source_target_pairs={{0,4},{4,0},{8,12},{12,8},{16,20},{20,16},{24,28},{28,24},{1,5},{5... | collective-permute-start | bytes 1572872 | tf_op jit(solution)/shard_map/ppermute | solution.py:26
  8.0 9.2 %collective-permute-start.3 = (bf16[128,2048]{1,0:T(8,128)(2,1)S(1)}, bf16[128,2048]{1,0:T(8,128)(2,1)S(1)}, u32[]{:S(2)}, u32[]{:S(2)}) collective-permute-start(bf16[128,2048]{1,0:T(8,128)(2,1)S(1)} %slice_select_fusion.refs_1_), channel_id=1, source_target_pairs={{0,4},{4,0},{8,12},{12,8},{16,20},{20,16},{24,28},{28,24},{1,5},{5... | collective-permute-start | bytes 1572872 | tf_op jit(solution)/shard_map/ppermute | solution.py:26
  10.8 6.4 %collective-permute-start.5 = (f32[2,512]{1,0:T(2,128)S(1)}, f32[2,512]{1,0:T(2,128)S(1)}, u32[]{:S(2)}, u32[]{:S(2)}) collective-permute-start(f32[2,512]{1,0:T(2,128)S(1)} %pad_maximum_fusion.9), channel_id=1, source_target_pairs={{0,8},{4,12},{8,0},{12,4},{16,24},{20,28},{24,16},{28,20},{1,9},{5... | collective-permute-start | bytes 12296 | tf_op jit(solution)/shard_map/ppermute | solution.py:26
  18.6 14.9 %collective-permute-start.6 = (bf16[128,2048]{1,0:T(8,128)(2,1)S(1)}, bf16[128,2048]{1,0:T(8,128)(2,1)S(1)}, u32[]{:S(2)}, u32[]{:S(2)}) collective-permute-start(bf16[128,2048]{1,0:T(8,128)(2,1)S(1)} %slice_select_fusion.refs_1_), channel_id=1, source_target_pairs={{0,8},{4,12},{8,0},{12,4},{16,24},{20,28},{24,16},{28,20},{1,9},{5... | collective-permute-start | bytes 1572872 | tf_op jit(solution)/shard_map/ppermute | solution.py:26
  19.0 14.9 %collective-permute-start.7 = (bf16[128,2048]{1,0:T(8,128)(2,1)S(1)}, bf16[128,2048]{1,0:T(8,128)(2,1)S(1)}, u32[]{:S(2)}, u32[]{:S(2)}) collective-permute-start(bf16[128,2048]{1,0:T(8,128)(2,1)S(1)} %slice_select_fusion.refs_1_), channel_id=1, source_target_pairs={{0,16},{4,20},{8,24},{12,28},{16,0},{20,4},{24,8},{28,12},{1,17},{... | collective-permute-start | bytes 1572872 | tf_op jit(solution)/shard_map/ppermute | solution.py:26
  20.7 23.5 %collective-permute-start.8 = (bf16[256,2048]{1,0:T(8,128)(2,1)S(1)}, bf16[256,2048]{1,0:T(8,128)(2,1)S(1)}, u32[]{:S(2)}, u32[]{:S(2)}) collective-permute-start(bf16[256,2048]{1,0:T(8,128)(2,1)S(1)} %pad_maximum_fusion.2), channel_id=1, source_target_pairs={{0,1},{1,0},{2,3},{3,2},{4,5},{5,4},{6,7},{7,6},{8,9},{9,8},{10,11... | collective-permute-start | bytes 3145736 | tf_op jit(solution)/shard_map/ppermute | solution.py:30
  22.4 20.4 %collective-permute-start.10 = (bf16[128,2048]{1,0:T(8,128)(2,1)S(1)}, bf16[128,2048]{1,0:T(8,128)(2,1)S(1)}, u32[]{:S(2)}, u32[]{:S(2)}) collective-permute-start(bf16[128,2048]{1,0:T(8,128)(2,1)S(1)} %get-tuple-element.94), channel_id=1, source_target_pairs={{0,16},{4,20},{8,24},{12,28},{16,0},{20,4},{24,8},{28,12},{1,17},{... | collective-permute-start | bytes 1572872 | tf_op jit(solution)/shard_map/ppermute | solution.py:26
  22.9 19.9 %collective-permute-start.9 = (bf16[128,2048]{1,0:T(8,128)(2,1)S(1)}, bf16[128,2048]{1,0:T(8,128)(2,1)S(1)}, u32[]{:S(2)}, u32[]{:S(2)}) collective-permute-start(bf16[128,2048]{1,0:T(8,128)(2,1)S(1)} %get-tuple-element.94), channel_id=1, source_target_pairs={{0,8},{4,12},{8,0},{12,4},{16,24},{20,28},{24,16},{28,20},{1,9},{5... | collective-permute-start | bytes 1572872 | tf_op jit(solution)/shard_map/ppermute | solution.py:26
  33.9 10.3 %collective-permute-start.11 = (bf16[128,2048]{1,0:T(8,128)(2,1)S(1)}, bf16[128,2048]{1,0:T(8,128)(2,1)S(1)}, u32[]{:S(2)}, u32[]{:S(2)}) collective-permute-start(bf16[128,2048]{1,0:T(8,128)(2,1)S(1)} %collective-permute-done.refs_4_), channel_id=1, source_target_pairs={{0,4},{4,0},{8,12},{12,8},{16,20},{20,16},{24,28},{28,24},{1,5},{5... | collective-permute-start | bytes 1572872 | tf_op jit(solution)/shard_map/ppermute | solution.py:26
  33.9 10.3 %collective-permute-start.12 = (bf16[128,2048]{1,0:T(8,128)(2,1)S(1)}, bf16[128,2048]{1,0:T(8,128)(2,1)S(1)}, u32[]{:S(2)}, u32[]{:S(2)}) collective-permute-start(bf16[128,2048]{1,0:T(8,128)(2,1)S(1)} %collective-permute-done.1.refs_8_), channel_id=1, source_target_pairs={{0,4},{4,0},{8,12},{12,8},{16,20},{20,16},{24,28},{28,24},{1,5},{5... | collective-permute-start | bytes 1572872 | tf_op jit(solution)/shard_map/ppermute | solution.py:26
  44.2 14.9 %collective-permute-start.13 = (bf16[128,2048]{1,0:T(8,128)(2,1)S(1)}, bf16[128,2048]{1,0:T(8,128)(2,1)S(1)}, u32[]{:S(2)}, u32[]{:S(2)}) collective-permute-start(bf16[128,2048]{1,0:T(8,128)(2,1)S(1)} %collective-permute-done.refs_4_), channel_id=1, source_target_pairs={{0,16},{4,20},{8,24},{12,28},{16,0},{20,4},{24,8},{28,12},{1,17},{... | collective-permute-start | bytes 1572872 | tf_op jit(solution)/shard_map/ppermute | solution.py:26
  44.7 14.9 %collective-permute-start.14 = (bf16[128,2048]{1,0:T(8,128)(2,1)S(1)}, bf16[128,2048]{1,0:T(8,128)(2,1)S(1)}, u32[]{:S(2)}, u32[]{:S(2)}) collective-permute-start(bf16[128,2048]{1,0:T(8,128)(2,1)S(1)} %collective-permute-done.7.refs_9_), channel_id=1, source_target_pairs={{0,8},{4,12},{8,0},{12,4},{16,24},{20,28},{24,16},{28,20},{1,9},{5... | collective-permute-start | bytes 1572872 | tf_op jit(solution)/shard_map/ppermute | solution.py:26
  45.9 21.7 %collective-permute-start.15 = (bf16[256,2048]{1,0:T(8,128)(2,1)S(1)}, bf16[256,2048]{1,0:T(8,128)(2,1)S(1)}, u32[]{:S(2)}, u32[]{:S(2)}) collective-permute-start(bf16[256,2048]{1,0:T(8,128)(2,1)S(1)} %pad_maximum_fusion.1), channel_id=1, source_target_pairs={{0,1},{1,0},{2,3},{3,2},{4,5},{5,4},{6,7},{7,6},{8,9},{9,8},{10,11... | collective-permute-start | bytes 3145736 | tf_op jit(solution)/shard_map/ppermute | solution.py:30
  47.5 19.5 %collective-permute-start.16 = (bf16[128,2048]{1,0:T(8,128)(2,1)S(1)}, bf16[128,2048]{1,0:T(8,128)(2,1)S(1)}, u32[]{:S(2)}, u32[]{:S(2)}) collective-permute-start(bf16[128,2048]{1,0:T(8,128)(2,1)S(1)} %get-tuple-element.104), channel_id=1, source_target_pairs={{0,8},{4,12},{8,0},{12,4},{16,24},{20,28},{24,16},{28,20},{1,9},{5... | collective-permute-start | bytes 1572872 | tf_op jit(solution)/shard_map/ppermute | solution.py:26
  48.3 18.7 %collective-permute-start.17 = (bf16[128,2048]{1,0:T(8,128)(2,1)S(1)}, bf16[128,2048]{1,0:T(8,128)(2,1)S(1)}, u32[]{:S(2)}, u32[]{:S(2)}) collective-permute-start(bf16[128,2048]{1,0:T(8,128)(2,1)S(1)} %get-tuple-element.104), channel_id=1, source_target_pairs={{0,16},{4,20},{8,24},{12,28},{16,0},{20,4},{24,8},{28,12},{1,17},{... | collective-permute-start | bytes 1572872 | tf_op jit(solution)/shard_map/ppermute | solution.py:26
  59.6 7.4 %collective-permute-start.18 = (bf16[128,2048]{1,0:T(8,128)(2,1)S(1)}, bf16[128,2048]{1,0:T(8,128)(2,1)S(1)}, u32[]{:S(2)}, u32[]{:S(2)}) collective-permute-start(bf16[128,2048]{1,0:T(8,128)(2,1)S(1)} %collective-permute-done.6.refs_5_), channel_id=1, source_target_pairs={{0,4},{4,0},{8,12},{12,8},{16,20},{20,16},{24,28},{28,24},{1,5},{5... | collective-permute-start | bytes 1572872 | tf_op jit(solution)/shard_map/ppermute | solution.py:26
  59.6 7.4 %collective-permute-start.19 = (bf16[128,2048]{1,0:T(8,128)(2,1)S(1)}, bf16[128,2048]{1,0:T(8,128)(2,1)S(1)}, u32[]{:S(2)}, u32[]{:S(2)}) collective-permute-start(bf16[128,2048]{1,0:T(8,128)(2,1)S(1)} %collective-permute-done.7.refs_9_), channel_id=1, source_target_pairs={{0,4},{4,0},{8,12},{12,8},{16,20},{20,16},{24,28},{28,24},{1,5},{5... | collective-permute-start | bytes 1572872 | tf_op jit(solution)/shard_map/ppermute | solution.py:26
  68.1 5.7 %collective-permute-start.24 = (bf16[768,2048]{1,0:T(8,128)(2,1)S(1)}, bf16[768,2048]{1,0:T(8,128)(2,1)S(1)}, u32[]{:S(2)}, u32[]{:S(2)}) collective-permute-start(bf16[768,2048]{1,0:T(8,128)(2,1)S(1)} %pad_maximum_fusion), channel_id=1, source_target_pairs={{0,4},{4,0},{8,12},{12,8},{16,20},{20,16},{24,28},{28,24},{1,5},{5... | collective-permute-start | bytes 9437192 | tf_op jit(solution)/shard_map/ppermute | solution.py:26
  68.2 9.5 %collective-permute-start.23 = (bf16[256,2048]{1,0:T(8,128)(2,1)S(1)}, bf16[256,2048]{1,0:T(8,128)(2,1)S(1)}, u32[]{:S(2)}, u32[]{:S(2)}) collective-permute-start(bf16[256,2048]{1,0:T(8,128)(2,1)S(1)} %pad_maximum_fusion.3), channel_id=1, source_target_pairs={{0,4},{4,0},{8,12},{12,8},{16,20},{20,16},{24,28},{28,24},{1,5},{5... | collective-permute-start | bytes 3145736 | tf_op jit(solution)/shard_map/ppermute | solution.py:26
  68.8 16.4 %collective-permute-start.22 = (bf16[128,2048]{1,0:T(8,128)(2,1)S(1)}, bf16[128,2048]{1,0:T(8,128)(2,1)S(1)}, u32[]{:S(2)}, u32[]{:S(2)}) collective-permute-start(bf16[128,2048]{1,0:T(8,128)(2,1)S(1)} %collective-permute-done.13.refs_12_), channel_id=1, source_target_pairs={{0,1},{1,0},{2,3},{3,2},{4,5},{5,4},{6,7},{7,6},{8,9},{9,8},{10,11... | collective-permute-start | bytes 1572872 | tf_op jit(solution)/shard_map/ppermute | solution.py:30
  70.4 13.8 %collective-permute-start.20 = (bf16[128,2048]{1,0:T(8,128)(2,1)S(1)}, bf16[128,2048]{1,0:T(8,128)(2,1)S(1)}, u32[]{:S(2)}, u32[]{:S(2)}) collective-permute-start(bf16[128,2048]{1,0:T(8,128)(2,1)S(1)} %collective-permute-done.9.refs_2_), channel_id=1, source_target_pairs={{0,16},{4,20},{8,24},{12,28},{16,0},{20,4},{24,8},{28,12},{1,17},{... | collective-permute-start | bytes 1572872 | tf_op jit(solution)/shard_map/ppermute | solution.py:26
  71.9 13.3 %collective-permute-start.21 = (bf16[128,2048]{1,0:T(8,128)(2,1)S(1)}, bf16[128,2048]{1,0:T(8,128)(2,1)S(1)}, u32[]{:S(2)}, u32[]{:S(2)}) collective-permute-start(bf16[128,2048]{1,0:T(8,128)(2,1)S(1)} %collective-permute-done.17.refs_5_), channel_id=1, source_target_pairs={{0,8},{4,12},{8,0},{12,4},{16,24},{20,28},{24,16},{28,20},{1,9},{5... | collective-permute-start | bytes 1572872 | tf_op jit(solution)/shard_map/ppermute | solution.py:26
  76.1 8.1 %collective-permute-start.25 = (f32[2,1024]{1,0:T(2,128)S(1)}, f32[2,1024]{1,0:T(2,128)S(1)}, u32[]{:S(2)}, u32[]{:S(2)}) collective-permute-start(f32[2,1024]{1,0:T(2,128)S(1)} %pad_maximum_fusion.8), channel_id=1, source_target_pairs={{0,16},{4,20},{8,24},{12,28},{16,0},{20,4},{24,8},{28,12},{1,17},{... | collective-permute-start | bytes 24584 | tf_op jit(solution)/shard_map/ppermute | solution.py:26
  85.6 7.2 %collective-permute-start.29 = (bf16[1024,2048]{1,0:T(8,128)(2,1)S(1)}, bf16[1024,2048]{1,0:T(8,128)(2,1)S(1)}, u32[]{:S(2)}, u32[]{:S(2)}) collective-permute-start(bf16[1024,2048]{1,0:T(8,128)(2,1)S(1)} %constant_dynamic-update-slice_fusion), channel_id=1, source_target_pairs={{0,4},{4,0},{8,12},{12,8},{16,20},{20,16},{24,28},{28,24},{1,5},{5... | collective-permute-start | bytes 12582920 | tf_op jit(solution)/shard_map/ppermute | solution.py:26
  85.7 10.2 %collective-permute-start.28 = (bf16[128,2048]{1,0:T(8,128)(2,1)S(1)}, bf16[128,2048]{1,0:T(8,128)(2,1)S(1)}, u32[]{:S(2)}, u32[]{:S(2)}) collective-permute-start(bf16[128,2048]{1,0:T(8,128)(2,1)S(1)} %collective-permute-done.22.refs_1_.refs_19_), channel_id=1, source_target_pairs={{0,4},{4,0},{8,12},{12,8},{16,20},{20,16},{24,28},{28,24},{1,5},{5... | collective-permute-start | bytes 1572872 | tf_op jit(solution)/shard_map/ppermute | solution.py:26
  86.3 9.7 %collective-permute-start.26 = (bf16[64,2048]{1,0:T(8,128)(2,1)S(1)}, bf16[64,2048]{1,0:T(8,128)(2,1)S(1)}, u32[]{:S(2)}, u32[]{:S(2)}) collective-permute-start(bf16[64,2048]{1,0:T(8,128)(2,1)S(1)} %get-tuple-element.159), channel_id=1, source_target_pairs={{0,8},{4,12},{8,0},{12,4},{16,24},{20,28},{24,16},{28,20},{1,9},{5... | collective-permute-start | bytes 786440 | tf_op jit(solution)/shard_map/ppermute | solution.py:26
  87.4 8.5 %collective-permute-start.27 = (bf16[64,2048]{1,0:T(8,128)(2,1)S(1)}, bf16[64,2048]{1,0:T(8,128)(2,1)S(1)}, u32[]{:S(2)}, u32[]{:S(2)}) collective-permute-start(bf16[64,2048]{1,0:T(8,128)(2,1)S(1)} %get-tuple-element.158), channel_id=1, source_target_pairs={{0,16},{4,20},{8,24},{12,28},{16,0},{20,4},{24,8},{28,12},{1,17},{... | collective-permute-start | bytes 786440 | tf_op jit(solution)/shard_map/ppermute | solution.py:26
  102.4 5.9 %collective-permute-start.34 = (f32[8,2048]{1,0:T(8,128)S(1)}, f32[8,2048]{1,0:T(8,128)S(1)}, u32[]{:S(2)}, u32[]{:S(2)}) collective-permute-start(f32[8,2048]{1,0:T(8,128)S(1)} %get-tuple-element.145), channel_id=1, source_target_pairs={{0,24},{4,28},{8,16},{12,20},{16,8},{20,12},{24,0},{28,4},{1,25},{... | collective-permute-start | bytes 196616 | tf_op jit(solution)/shard_map/ppermute | solution.py:26
  114.9 5.1 %collective-permute-start.36 = (f32[1,2048]{1,0:T(1,128)S(1)}, f32[1,2048]{1,0:T(1,128)S(1)}, u32[]{:S(2)}, u32[]{:S(2)}) collective-permute-start(f32[1,2048]{1,0:T(1,128)S(1)} %get-tuple-element.154), channel_id=1, source_target_pairs={{0,1},{1,0},{2,3},{3,2},{4,5},{5,4},{6,7},{7,6},{8,9},{9,8},{10,11... | collective-permute-start | bytes 24584 | tf_op jit(solution)/shard_map/ppermute | solution.py:30
  119.9 11.0 %collective-permute-start.37 = (f32[1,2048]{1,0:T(1,128)S(1)}, f32[1,2048]{1,0:T(1,128)S(1)}, u32[]{:S(2)}, u32[]{:S(2)}) collective-permute-start(f32[1,2048]{1,0:T(1,128)S(1)} %add.8.refs_0_), channel_id=1, source_target_pairs={{0,2},{1,3},{2,0},{3,1},{4,6},{5,7},{6,4},{7,5},{8,10},{9,11},{10,... | collective-permute-start | bytes 24584 | tf_op jit(solution)/shard_map/ppermute | solution.py:30
  (12 other events, 79.1 us)

commit v8 on v7

--- a/solution.py
+++ b/solution.py
@@ -58,6 +58,11 @@
     @pl.loop(0, count // tile)
     def _(index):
         body(pl.ds(pl.multiple_of(index * tile, tile), tile))
+
+
+def unrolled(count, tile, body):
+    for index in range(count // tile):
+        body(pl.ds(index * tile, tile))
 
 
 class Shards:
@@ -112,10 +117,11 @@
 def norm_call(where, x, g, gain, depth):
     rows, width = x.shape
 
-    def kernel(where_ref, x_ref, g_ref, gain_ref, normed_ref, grads_ref, hold):
+    def kernel(where_ref, x_ref, g_ref, gain_ref, normed_ref, grads_ref, scale_ref, hold):
         def rows_body(span):
             x = x_ref[span, :].astype(F32)
             scale = lax.rsqrt(jnp.mean(x * x, axis=-1, keepdims=True) + EPSILON)
+            scale_ref[span, :] = scale
             hold[span, :] = (x * scale * gain_ref[...]).astype(BF16)
 
         tiles(rows, min(32, rows), rows_body)
@@ -131,9 +137,13 @@
 
     return pl.pallas_call(
         kernel,
-        out_shape=[jax.ShapeDtypeStruct((rows, width), BF16), jax.ShapeDtypeStruct((width, rows), BF16)],
+        out_shape=[
+            jax.ShapeDtypeStruct((rows, width), BF16),
+            jax.ShapeDtypeStruct((width, rows), BF16),
+            jax.ShapeDtypeStruct((rows, 1), F32),
+        ],
         in_specs=[SMEM_SPEC] + [VMEM_SPEC] * 3,
-        out_specs=[VMEM_SPEC] * 2,
+        out_specs=[VMEM_SPEC] * 3,
         scratch_shapes=[pltpu.VMEM(x.shape, BF16)],
         compiler_params=params(14),
         cost_estimate=cost(4 * rows * x.size, 8 * x.size),
@@ -276,7 +286,7 @@
             whole += [jnp.sum(value, axis=0, keepdims=True) for value in sums] + [zero]
             whole_ref[:, span] = jnp.concatenate(whole, axis=0)
 
-        tiles(width, tile, body)
+        unrolled(width, tile, body)
 
     return pl.pallas_call(
         kernel,
@@ -375,7 +385,7 @@
             one_ref[span, :] = dot(one_hold[...].T, order_back).astype(BF16)
             other_ref[span, :] = dot(other_hold[...].T, order_back).astype(BF16)
 
-        tiles(width, tile, body)
+        unrolled(width, tile, body)
 
     wide = jax.ShapeDtypeStruct((rows, width), BF16)
     tall = jax.ShapeDtypeStruct((width, rows), BF16)
@@ -404,7 +414,7 @@
             total = shards.product(x_ref, 0, refs, span)
             out_ref[:, span] = (residual_ref[:, span].astype(F32) + total).astype(BF16)
 
-        tiles(width, tile, body)
+        unrolled(width, tile, body)
 
     return pl.pallas_call(
         kernel,
@@ -417,12 +427,12 @@
     )(where, near(state_rows), near(residual), *shards.operands())
 
 
-def input_grad_call(where, one, other, first, second, x, grads, gain):
+def input_grad_call(where, one, other, first, second, x, scale, grads, gain):
     rows, width = x.shape
     hidden = one.shape[0]
     count, depth = len(first.groups), first.depth
 
-    def kernel(where_ref, one_ref, other_ref, x_ref, grads_ref, gain_ref, *refs):
+    def kernel(where_ref, one_ref, other_ref, x_ref, scale_ref, grads_ref, gain_ref, *refs):
         first_refs = refs[: len(first.pieces)]
         second_refs = refs[len(first.pieces) : len(first.pieces) + len(second.pieces)]
         out_ref, total = refs[-2:]
@@ -436,25 +446,25 @@
 
         def body(span):
             x = x_ref[span, :].astype(F32)
-            scale = lax.rsqrt(jnp.mean(x * x, axis=-1, keepdims=True) + EPSILON)
+            scale = scale_ref[span, :]
             unit = x * scale
             unit_grad = total[span, :] * gain_ref[...]
             along = jnp.mean(unit_grad * unit, axis=-1, keepdims=True)
             out = grads_ref[span, :].astype(F32) + scale * (unit_grad - unit * along)
             out_ref[span, :] = out.astype(BF16)
 
-        tiles(rows, min(32, rows), body)
+        unrolled(rows, min(32, rows), body)
 
     return pl.pallas_call(
         kernel,
         out_shape=jax.ShapeDtypeStruct((rows, width), BF16),
-        in_specs=[SMEM_SPEC] + [VMEM_SPEC] * 5 + [VMEM_SPEC] * (len(first.pieces) + len(second.pieces)),
+        in_specs=[SMEM_SPEC] + [VMEM_SPEC] * 6 + [VMEM_SPEC] * (len(first.pieces) + len(second.pieces)),
         out_specs=VMEM_SPEC,
         scratch_shapes=[pltpu.VMEM((rows, width), F32)],
         compiler_params=params(14),
         cost_estimate=cost(4 * one.size * width, 4 * hidden * width),
         name="input_grad_rows",
-    )(where, *map(near, (one, other, x, grads, gain)), *first.operands(), *second.operands())
+    )(where, *map(near, (one, other, x, scale, grads, gain)), *first.operands(), *second.operands())
 
 
 def close_call(where, state_grad, rows, block):
@@ -493,7 +503,7 @@
     both = jnp.stack([gate_bias, state_in[0]])
     both = jnp.concatenate([both, core(both)], axis=1)
     both = jnp.concatenate([both, send(both, 2)], axis=1)
-    normed, grads = norm_call(where, rows_in, grad_rows, gain, depth)
+    normed, grads, scale = norm_call(where, rows_in, grad_rows, gain, depth)
     own_s = jnp.where(straight, w_cand, w_gate)
     t_a, t_b = halves(own_t)
     f2a, f4a, f1a, f1b, both, normed, grads, f_b, own_s, own_t, t_a, t_b = after(
@@ -540,7 +550,7 @@
     second_pre, parts, whole, both = totals_call(
         where, normed, partial, Shards(last), len(most) * depth, first_pre, back, both, depth, tile
     )
-    return where, first, second, third, first_pre, second_pre, back, both, parts, whole
+    return where, scale, first, second, third, first_pre, second_pre, back, both, parts, whole
 
 
 def front(where, tile, rows_in, grad_rows, gain, gate_bias, state_in, w_gate, w_cand, w_out):
@@ -548,13 +558,13 @@
         Shards([[lax.all_gather(w, "seq", tiled=True)]]) for w in (w_gate, w_cand, w_out)
     )
     both = lax.all_gather(jnp.stack([gate_bias, state_in[0]]), "seq", axis=1, tiled=True)
-    normed, grads = norm_call(where, rows_in, grad_rows, gain, first.depth)
+    normed, grads, scale = norm_call(where, rows_in, grad_rows, gain, first.depth)
     first_pre = project_call(normed, first, tile, BF16)
     back = back_call(where, grads, third)
     second_pre, parts, whole, both = totals_call(
         where, normed, None, second, 0, first_pre, back, both, first.depth, tile
     )
-    return where, first, second, third, first_pre, second_pre, back, both, parts, whole
+    return where, scale, first, second, third, first_pre, second_pre, back, both, parts, whole
 
 
 def on_device(ranks, batches, inputs, output_grad, norm_gain, gate_bias, state_in, w_gate, w_cand, w_out):
@@ -573,7 +583,7 @@
         nought = jnp.zeros_like(me)
         where = jnp.stack([nought, nought, me]).astype(jnp.int32)
         found = front(where, tile, *given)
-    where, first, second, third, first_pre, second_pre, back, both, parts, whole = found
+    where, scale, first, second, third, first_pre, second_pre, back, both, parts, whole = found
     if cube:
         found = jnp.stack([hop(whole, offset, ranks) for offset in (2, 4, 6)])
         wholes = [jnp.stack([whole, hop(whole, 1, ranks)]), found, hop(found, 1, ranks)]
@@ -591,14 +601,14 @@
         for offset in range(1, batches.bit_length() - 1):
             bias_part = bias_part + came
             came = swap_batch(bias_part, 1 << offset, batches)
-        input_grad = input_grad_call(where, one, other, first, second, rows_in, grad_rows, gain)
+        input_grad = input_grad_call(where, one, other, first, second, rows_in, scale, grad_rows, gain)
         state_out, bias_grad = close_call(where, state_grad, [bias_part, came], width)
         bias_grad = bias_grad[0]
     else:
         own_block = lax.dynamic_slice_in_dim(bias_part[0], me * width, width, 0)
         bias_grad = lax.psum(own_block, "batch")
         layer_out = layer_call(where, state_rows, rows_in, third, tile)
-        input_grad = input_grad_call(where, one, other, first, second, rows_in, grad_rows, gain)
+        input_grad = input_grad_call(where, one, other, first, second, rows_in, scale, grad_rows, gain)
         state_out = lax.dynamic_slice_in_dim(state_grad, me * width, width, 1)
     return (layer_out[None], input_grad[None], state_out, bias_grad)
 

time: 132 us -> 129 us (0.977)
  Pallas kernels: 34.4 us -> 31.7 us
where the time goes in v8:
time: 129 us
  waiting for transfers between devices  56.8 us (44%)
  starting transfers between devices  33.6 us (26%)
  Pallas kernels  31.7 us (25%)
  other arithmetic  5.61 us (4%)
    ppermute x33, waiting for transfers between devices, hop(): return lax.ppermute(value, 'seq', [(i, i ^ offset) for i in range(count)])  54.8 us
    ppermute x33, starting transfers between devices, hop(): return lax.ppermute(value, 'seq', [(i, i ^ offset) for i in range(count)])  25.6 us
    ppermute x5, starting transfers between devices, swap_batch(): return lax.ppermute(value, 'batch', [(i, i ^ offset) for i in range(count)])  7.95 us
    pallas_call x1, Pallas kernels, input_grad_call(): pl.pallas_call(kernel, out_shape=jax.ShapeDtypeStruct((rows, width), BF16...  7.32 us
    pallas_call x2, Pallas kernels, project_call(): pl.pallas_call(kernel, out_shape=jax.ShapeDtypeStruct((rows, width), dtyp...  5.33 us
    pallas_call x1, Pallas kernels, scan_call(): pl.pallas_call(kernel, out_shape=[wide, tall, tall, flat, flat], in_specs...  3.92 us
    pallas_call x1, Pallas kernels, layer_call(): pl.pallas_call(kernel, out_shape=jax.ShapeDtypeStruct((rows, width), BF16...  3.89 us
    pallas_call x1, Pallas kernels, totals_call(): pl.pallas_call(kernel, out_shape=[jax.ShapeDtypeStruct((rows, width), BF1...  3.82 us
  transfers between devices with their start and end apart: 38, of which 18 were waited for; matrix products, arithmetic and copies ran while one was open for 3% of the time, Pallas kernels for 18%

profile of v8, /device:TPU:0, one launch (start us, length us, event | category | flops | bytes accessed | tf_op | source)
XLA Modules:
  0.0 129.3 jit_solution(2018240880151296996)
XLA Ops:
  0.8 1.4 %slice_select_fusion.1.refs_0_ = bf16[128,2048]{1,0:T(8,128)(2,1)S(1)} fusion(bf16[256,2048]{1,0:T(8,128)(2,1)} %param.14, bf16[256,2048]{1,0:T(8,128)(2,1)} %param.13, pred[]{:T(512)S(6)} %eq.5), kind=kLoop, calls=%fused_computation.7 | loop fusion | flops 262144 | bytes 1572865 | tf_op jit(solution)/shard_map/jit(_where)/select_n | solution.py:496
  2.2 3.0 %collective-permute-start = (bf16[128,2048]{1,0:T(8,128)(2,1)S(1)}, bf16[128,2048]{1,0:T(8,128)(2,1)S(1)}, u32[]{:S(2)}, u32[]{:S(2)}) collective-permute-start(bf16[128,2048]{1,0:T(8,128)(2,1)S(1)} %slice_select_fusion.1.refs_0_), channel_id=1, source_target_pairs={{0,8},{4,12},{8,0},{12,4},{16,24},{20,28},{24,16},{28,20},{1,9},{5... | collective-permute-start | bytes 1572872 | tf_op jit(solution)/shard_map/ppermute | solution.py:26
  5.2 1.5 %collective-permute-start.1 = (bf16[128,2048]{1,0:T(8,128)(2,1)S(1)}, bf16[128,2048]{1,0:T(8,128)(2,1)S(1)}, u32[]{:S(2)}, u32[]{:S(2)}) collective-permute-start(bf16[128,2048]{1,0:T(8,128)(2,1)S(1)} %slice_select_fusion.1.refs_0_), channel_id=1, source_target_pairs={{0,16},{4,20},{8,24},{12,28},{16,0},{20,4},{24,8},{28,12},{1,17},{... | collective-permute-start | bytes 1572872 | tf_op jit(solution)/shard_map/ppermute | solution.py:26
  11.4 3.3 %norm_rows.1 = (bf16[256,2048]{1,0:T(8,128)(2,1)S(1)}, bf16[2048,256]{1,0:T(8,128)(2,1)S(1)}, f32[256,1]{1,0:T(8,128)S(1)}) custom-call(s32[3]{0:T(128)S(1)} %pad_add_fusion.where_ref, bf16[256,2048]{1,0:T(8,128)(2,1)S(1)} %bitcast.14, bf16[256,2048]{1,0:T(8,128)(2,1)S(1)} %bitcast.17, f32[1,2048]{1,0:T(1,128)S(1)} %bitcast.20), custom_call_target="tpu_custom_call" | custom-call | flops 536870912 | bytes 4194304 | tf_op jit(solution)/shard_map/norm_rows/pallas_call | solution.py:138
  14.6 2.6 %collective-permute-done.5 = f32[2,512]{1,0:T(2,128)S(1)} collective-permute-done((f32[2,512]{1,0:T(2,128)S(1)}, f32[2,512]{1,0:T(2,128)S(1)}, u32[]{:S(2)}, u32[]{:S(2)}) %collective-permute-start.5) | collective-permute-done | bytes 4128 | tf_op jit(solution)/shard_map/ppermute | solution.py:26
  19.0 1.6 %collective-permute-start.7 = (bf16[128,2048]{1,0:T(8,128)(2,1)S(1)}, bf16[128,2048]{1,0:T(8,128)(2,1)S(1)}, u32[]{:S(2)}, u32[]{:S(2)}) collective-permute-start(bf16[128,2048]{1,0:T(8,128)(2,1)S(1)} %slice_select_fusion.refs_1_), channel_id=1, source_target_pairs={{0,16},{4,20},{8,24},{12,28},{16,0},{20,4},{24,8},{28,12},{1,17},{... | collective-permute-start | bytes 1572872 | tf_op jit(solution)/shard_map/ppermute | solution.py:26
  20.7 1.6 %collective-permute-start.8 = (bf16[256,2048]{1,0:T(8,128)(2,1)S(1)}, bf16[256,2048]{1,0:T(8,128)(2,1)S(1)}, u32[]{:S(2)}, u32[]{:S(2)}) collective-permute-start(bf16[256,2048]{1,0:T(8,128)(2,1)S(1)} %pad_maximum_fusion.2), channel_id=1, source_target_pairs={{0,1},{1,0},{2,3},{3,2},{4,5},{5,4},{6,7},{7,6},{8,9},{9,8},{10,11... | collective-permute-start | bytes 3145736 | tf_op jit(solution)/shard_map/ppermute | solution.py:30
  22.9 1.5 %collective-permute-start.9 = (bf16[128,2048]{1,0:T(8,128)(2,1)S(1)}, bf16[128,2048]{1,0:T(8,128)(2,1)S(1)}, u32[]{:S(2)}, u32[]{:S(2)}) collective-permute-start(bf16[128,2048]{1,0:T(8,128)(2,1)S(1)} %get-tuple-element.95), channel_id=1, source_target_pairs={{0,8},{4,12},{8,0},{12,4},{16,24},{20,28},{24,16},{28,20},{1,9},{5... | collective-permute-start | bytes 1572872 | tf_op jit(solution)/shard_map/ppermute | solution.py:26
  24.4 9.1 %collective-permute-done.6.refs_5_ = bf16[128,2048]{1,0:T(8,128)(2,1)S(1)} collective-permute-done((bf16[128,2048]{1,0:T(8,128)(2,1)S(1)}, bf16[128,2048]{1,0:T(8,128)(2,1)S(1)}, u32[]{:S(2)}, u32[]{:S(2)}) %collective-permute-start.6) | collective-permute-done | bytes 524320 | tf_op jit(solution)/shard_map/ppermute | solution.py:26
  34.5 8.3 %collective-permute-done.10.refs_4_ = bf16[128,2048]{1,0:T(8,128)(2,1)S(1)} collective-permute-done((bf16[128,2048]{1,0:T(8,128)(2,1)S(1)}, bf16[128,2048]{1,0:T(8,128)(2,1)S(1)}, u32[]{:S(2)}, u32[]{:S(2)}) %collective-permute-start.10) | collective-permute-done | bytes 524320 | tf_op jit(solution)/shard_map/ppermute | solution.py:26
  42.8 1.4 %collective-permute-done.8.refs_2_.refs_17_ = bf16[256,2048]{1,0:T(8,128)(2,1)S(1)} collective-permute-done((bf16[256,2048]{1,0:T(8,128)(2,1)S(1)}, bf16[256,2048]{1,0:T(8,128)(2,1)S(1)}, u32[]{:S(2)}, u32[]{:S(2)}) %collective-permute-start.8) | collective-permute-done | bytes 1048608 | tf_op jit(solution)/shard_map/ppermute | solution.py:30
  45.9 1.6 %collective-permute-start.15 = (bf16[256,2048]{1,0:T(8,128)(2,1)S(1)}, bf16[256,2048]{1,0:T(8,128)(2,1)S(1)}, u32[]{:S(2)}, u32[]{:S(2)}) collective-permute-start(bf16[256,2048]{1,0:T(8,128)(2,1)S(1)} %pad_maximum_fusion.1), channel_id=1, source_target_pairs={{0,1},{1,0},{2,3},{3,2},{4,5},{5,4},{6,7},{7,6},{8,9},{9,8},{10,11... | collective-permute-start | bytes 3145736 | tf_op jit(solution)/shard_map/ppermute | solution.py:30
  48.3 1.5 %collective-permute-start.17 = (bf16[128,2048]{1,0:T(8,128)(2,1)S(1)}, bf16[128,2048]{1,0:T(8,128)(2,1)S(1)}, u32[]{:S(2)}, u32[]{:S(2)}) collective-permute-start(bf16[128,2048]{1,0:T(8,128)(2,1)S(1)} %get-tuple-element.105), channel_id=1, source_target_pairs={{0,16},{4,20},{8,24},{12,28},{16,0},{20,4},{24,8},{28,12},{1,17},{... | collective-permute-start | bytes 1572872 | tf_op jit(solution)/shard_map/ppermute | solution.py:26
  49.8 9.2 %collective-permute-done.13.refs_12_ = bf16[128,2048]{1,0:T(8,128)(2,1)S(1)} collective-permute-done((bf16[128,2048]{1,0:T(8,128)(2,1)S(1)}, bf16[128,2048]{1,0:T(8,128)(2,1)S(1)}, u32[]{:S(2)}, u32[]{:S(2)}) %collective-permute-start.13) | collective-permute-done | bytes 524320 | tf_op jit(solution)/shard_map/ppermute | solution.py:26
  60.1 6.9 %collective-permute-done.16.refs_3_ = bf16[128,2048]{1,0:T(8,128)(2,1)S(1)} collective-permute-done((bf16[128,2048]{1,0:T(8,128)(2,1)S(1)}, bf16[128,2048]{1,0:T(8,128)(2,1)S(1)}, u32[]{:S(2)}, u32[]{:S(2)}) %collective-permute-start.16) | collective-permute-done | bytes 524320 | tf_op jit(solution)/shard_map/ppermute | solution.py:26
  68.8 1.6 %collective-permute-start.22 = (bf16[128,2048]{1,0:T(8,128)(2,1)S(1)}, bf16[128,2048]{1,0:T(8,128)(2,1)S(1)}, u32[]{:S(2)}, u32[]{:S(2)}) collective-permute-start(bf16[128,2048]{1,0:T(8,128)(2,1)S(1)} %collective-permute-done.13.refs_12_), channel_id=1, source_target_pairs={{0,1},{1,0},{2,3},{3,2},{4,5},{5,4},{6,7},{7,6},{8,9},{9,8},{10,11... | collective-permute-start | bytes 1572872 | tf_op jit(solution)/shard_map/ppermute | solution.py:30
  70.4 1.5 %collective-permute-start.20 = (bf16[128,2048]{1,0:T(8,128)(2,1)S(1)}, bf16[128,2048]{1,0:T(8,128)(2,1)S(1)}, u32[]{:S(2)}, u32[]{:S(2)}) collective-permute-start(bf16[128,2048]{1,0:T(8,128)(2,1)S(1)} %collective-permute-done.9.refs_2_), channel_id=1, source_target_pairs={{0,16},{4,20},{8,24},{12,28},{16,0},{20,4},{24,8},{28,12},{1,17},{... | collective-permute-start | bytes 1572872 | tf_op jit(solution)/shard_map/ppermute | solution.py:26
  73.8 2.3 %project.3.refs_0_ = f32[256,2048]{1,0:T(8,128)S(1)} custom-call(bf16[256,2048]{1,0:T(8,128)(2,1)S(1)} %get-tuple-element.114.x_ref, bf16[256,2048]{1,0:T(8,128)(2,1)S(1)} %broadcast_select_fusion.refs_0_.refs_15_, bf16[768,2048]{1,0:T(8,128)(2,1)S(1)} %collective-permute-done.24.refs_1_.refs_16_, ...), custom_call_target="tpu_custom_call" | custom-call | flops 1610612736 | bytes 6291456 | tf_op jit(solution)/shard_map/project/pallas_call | solution.py:166
  76.1 1.6 %collective-permute-start.25 = (f32[2,1024]{1,0:T(2,128)S(1)}, f32[2,1024]{1,0:T(2,128)S(1)}, u32[]{:S(2)}, u32[]{:S(2)}) collective-permute-start(f32[2,1024]{1,0:T(2,128)S(1)} %pad_maximum_fusion.8), channel_id=1, source_target_pairs={{0,16},{4,20},{8,24},{12,28},{16,0},{20,4},{24,8},{28,12},{1,17},{... | collective-permute-start | bytes 24584 | tf_op jit(solution)/shard_map/ppermute | solution.py:26
  77.7 3.0 %project.2.first_ref = bf16[256,2048]{1,0:T(8,128)(2,1)S(1)} custom-call(bf16[256,2048]{1,0:T(8,128)(2,1)S(1)} %get-tuple-element.114.x_ref, bf16[128,2048]{1,0:T(8,128)(2,1)S(1)} %slice_select_fusion.1.refs_0_, bf16[128,2048]{1,0:T(8,128)(2,1)S(1)} %slice_select_fusion.refs_1_, bf16[128,2048]{1,0:T(8,128)(2,1)S(1)} %collective-permute-done.2.refs_2_, ...), custom_call_target="tpu_custom_call" | custom-call | flops 2147483648 | bytes 8388608 | tf_op jit(solution)/shard_map/project/pallas_call | solution.py:166
  80.7 3.4 %collective-permute-done.25 = f32[2,1024]{1,0:T(2,128)S(1)} collective-permute-done((f32[2,1024]{1,0:T(2,128)S(1)}, f32[2,1024]{1,0:T(2,128)S(1)}, u32[]{:S(2)}, u32[]{:S(2)}) %collective-permute-start.25) | collective-permute-done | bytes 8224 | tf_op jit(solution)/shard_map/ppermute | solution.py:26
  87.9 5.0 %collective-permute-done.29.refs_1_ = bf16[1024,2048]{1,0:T(8,128)(2,1)S(1)} collective-permute-done((bf16[1024,2048]{1,0:T(8,128)(2,1)S(1)}, bf16[1024,2048]{1,0:T(8,128)(2,1)S(1)}, u32[]{:S(2)}, u32[]{:S(2)}) %collective-permute-start.29) | collective-permute-done | bytes 4194336 | tf_op jit(solution)/shard_map/ppermute | solution.py:26
  92.9 3.0 %back_rows.1.back_ref = bf16[256,2048]{1,0:T(8,128)(2,1)S(1)} custom-call(s32[3]{0:T(128)S(1)} %pad_add_fusion.where_ref, bf16[2048,256]{1,0:T(8,128)(2,1)S(1)} %get-tuple-element.130.g_ref, bf16[256,2048]{1,0:T(8,128)(2,1)S(1)} %copy-done, bf16[1024,2048]{1,0:T(8,128)(2,1)S(1)} %collective-permute-done.29.refs_1_, ...), custom_call_target="tpu_custom_call" | custom-call | flops 2147483648 | bytes 8388608 | tf_op jit(solution)/shard_map/back_rows/pallas_call | solution.py:190
  96.2 1.8 %collective-permute-done.30.refs_5_.refs_23_ = bf16[128,2048]{1,0:T(8,128)(2,1)S(1)} collective-permute-done((bf16[128,2048]{1,0:T(8,128)(2,1)S(1)}, bf16[128,2048]{1,0:T(8,128)(2,1)S(1)}, u32[]{:S(2)}, u32[]{:S(2)}) %collective-permute-start.30) | collective-permute-done | bytes 524320 | tf_op jit(solution)/shard_map/ppermute | solution.py:26
  98.0 3.8 %project_totals.1 = (bf16[256,2048]{1,0:T(8,128)(2,1)S(1)}, f32[3,8,2048]{2,1,0:T(8,128)S(1)}, f32[8,2048]{1,0:T(8,128)S(1)}, f32[2,2048]{1,0:T(2,128)S(1)}) custom-call(s32[3]{0:T(128)S(1)} %pad_add_fusion.where_ref, bf16[256,2048]{1,0:T(8,128)(2,1)S(1)} %get-tuple-element.114.x_ref, bf16[256,2048]{1,0:T(8,128)(2,1)S(1)} %project.2.first_ref, ...), custom_call_target="tpu_custom_call" | custom-call | flops 536870912 | bytes 2097152 | tf_op jit(solution)/shard_map/project_totals/pallas_call | solution.py:291
  103.8 1.5 %collective-permute-start.33 = (f32[8,2048]{1,0:T(8,128)S(1)}, f32[8,2048]{1,0:T(8,128)S(1)}, u32[]{:S(2)}, u32[]{:S(2)}) collective-permute-start(f32[8,2048]{1,0:T(8,128)S(1)} %get-tuple-element.146), channel_id=1, source_target_pairs={{0,16},{4,20},{8,24},{12,28},{16,0},{20,4},{24,8},{28,12},{1,17},{... | collective-permute-start | bytes 196616 | tf_op jit(solution)/shard_map/ppermute | solution.py:26
  105.4 2.3 %collective-permute-done.34 = f32[8,2048]{1,0:T(8,128)S(1)} collective-permute-done((f32[8,2048]{1,0:T(8,128)S(1)}, f32[8,2048]{1,0:T(8,128)S(1)}, u32[]{:S(2)}, u32[]{:S(2)}) %collective-permute-start.34) | collective-permute-done | bytes 65568 | tf_op jit(solution)/shard_map/ppermute | solution.py:26
  108.4 1.4 %collective-permute-done.35.refs_2_ = f32[3,8,2048]{2,1,0:T(8,128)S(1)} collective-permute-done((f32[3,8,2048]{2,1,0:T(8,128)S(1)}, f32[3,8,2048]{2,1,0:T(8,128)S(1)}, u32[]{:S(2)}, u32[]{:S(2)}) %collective-permute-start.35) | collective-permute-done | bytes 196640 | tf_op jit(solution)/shard_map/ppermute | solution.py:26
  109.8 3.9 %scan_rows.1 = (bf16[256,2048]{1,0:T(8,128)(2,1)S(1)}, bf16[2048,256]{1,0:T(8,128)(2,1)S(1)}, bf16[2048,256]{1,0:T(8,128)(2,1)S(1)}, f32[1,2048]{1,0:T(1,128)S(1)}, f32[1,2048]{1,0:T(1,128)S(1)}) custom-call(s32[3]{0:T(128)S(1)} %pad_add_fusion.where_ref, bf16[256,2048]{1,0:T(8,128)(2,1)S(1)} %project.2.first_ref, ...), custom_call_target="tpu_custom_call" | custom-call | flops 805306368 | bytes 6291456 | tf_op jit(solution)/shard_map/scan_rows/pallas_call | solution.py:393
  114.3 3.9 %layer_rows.1 = bf16[256,2048]{1,0:T(8,128)(2,1)} custom-call(s32[3]{0:T(128)S(1)} %pad_add_fusion.where_ref, bf16[256,2048]{1,0:T(8,128)(2,1)S(1)} %get-tuple-element.147.x_ref, bf16[256,2048]{1,0:T(8,128)(2,1)S(1)} %bitcast.15, bf16[256,2048]{1,0:T(8,128)(2,1)S(1)} %copy-done, bf16[1024,2048]{1,0:T(8,128)(2,1)S(1)} %collective-permute-done.29.refs_1_, ...), custom_call_target="tpu_custom_call" | custom-call | flops 2147483648 | bytes 8388608 | tf_op jit(solution)/shard_map/layer_rows/pallas_call | solution.py:419
  118.2 2.6 %collective-permute-start.37 = (f32[1,2048]{1,0:T(1,128)S(1)}, f32[1,2048]{1,0:T(1,128)S(1)}, u32[]{:S(2)}, u32[]{:S(2)}) collective-permute-start(f32[1,2048]{1,0:T(1,128)S(1)} %add.8.refs_0_), channel_id=1, source_target_pairs={{0,2},{1,3},{2,0},{3,1},{4,6},{5,7},{6,4},{7,5},{8,10},{9,11},{10,... | collective-permute-start | bytes 24584 | tf_op jit(solution)/shard_map/ppermute | solution.py:30
  120.8 7.3 %input_grad_rows.1 = bf16[256,2048]{1,0:T(8,128)(2,1)} custom-call(s32[3]{0:T(128)S(1)} %pad_add_fusion.where_ref, bf16[2048,256]{1,0:T(8,128)(2,1)S(1)} %get-tuple-element.152.one_ref, bf16[2048,256]{1,0:T(8,128)(2,1)S(1)} %get-tuple-element.153.other_ref, bf16[256,2048]{1,0:T(8,128)(2,1)S(1)} %bitcast.16, f32[256,1]{1,0:T(8,128)S(1)} %get-tuple-element.154.scale_ref, ...), custom_call_target="tpu_custom_call" | custom-call | flops 4294967296 | bytes 16777216 | tf_op jit(solution)/shard_map/input_grad_rows/pallas_call | solution.py:458
  (90 shorter events, 23.8 us)
Async XLA Ops:
  2.2 15.0 %collective-permute-start = (bf16[128,2048]{1,0:T(8,128)(2,1)S(1)}, bf16[128,2048]{1,0:T(8,128)(2,1)S(1)}, u32[]{:S(2)}, u32[]{:S(2)}) collective-permute-start(bf16[128,2048]{1,0:T(8,128)(2,1)S(1)} %slice_select_fusion.1.refs_0_), channel_id=1, source_target_pairs={{0,8},{4,12},{8,0},{12,4},{16,24},{20,28},{24,16},{28,20},{1,9},{5... | collective-permute-start | bytes 1572872 | tf_op jit(solution)/shard_map/ppermute | solution.py:26
  5.2 13.4 %collective-permute-start.1 = (bf16[128,2048]{1,0:T(8,128)(2,1)S(1)}, bf16[128,2048]{1,0:T(8,128)(2,1)S(1)}, u32[]{:S(2)}, u32[]{:S(2)}) collective-permute-start(bf16[128,2048]{1,0:T(8,128)(2,1)S(1)} %slice_select_fusion.1.refs_0_), channel_id=1, source_target_pairs={{0,16},{4,20},{8,24},{12,28},{16,0},{20,4},{24,8},{28,12},{1,17},{... | collective-permute-start | bytes 1572872 | tf_op jit(solution)/shard_map/ppermute | solution.py:26
  6.7 11.9 %collective-permute-start.2 = (bf16[128,2048]{1,0:T(8,128)(2,1)S(1)}, bf16[128,2048]{1,0:T(8,128)(2,1)S(1)}, u32[]{:S(2)}, u32[]{:S(2)}) collective-permute-start(bf16[128,2048]{1,0:T(8,128)(2,1)S(1)} %slice_select_fusion.1.refs_0_), channel_id=1, source_target_pairs={{0,4},{4,0},{8,12},{12,8},{16,20},{20,16},{24,28},{28,24},{1,5},{5... | collective-permute-start | bytes 1572872 | tf_op jit(solution)/shard_map/ppermute | solution.py:26
  8.0 9.2 %collective-permute-start.3 = (bf16[128,2048]{1,0:T(8,128)(2,1)S(1)}, bf16[128,2048]{1,0:T(8,128)(2,1)S(1)}, u32[]{:S(2)}, u32[]{:S(2)}) collective-permute-start(bf16[128,2048]{1,0:T(8,128)(2,1)S(1)} %slice_select_fusion.refs_1_), channel_id=1, source_target_pairs={{0,4},{4,0},{8,12},{12,8},{16,20},{20,16},{24,28},{28,24},{1,5},{5... | collective-permute-start | bytes 1572872 | tf_op jit(solution)/shard_map/ppermute | solution.py:26
  10.8 6.4 %collective-permute-start.5 = (f32[2,512]{1,0:T(2,128)S(1)}, f32[2,512]{1,0:T(2,128)S(1)}, u32[]{:S(2)}, u32[]{:S(2)}) collective-permute-start(f32[2,512]{1,0:T(2,128)S(1)} %pad_maximum_fusion.9), channel_id=1, source_target_pairs={{0,8},{4,12},{8,0},{12,4},{16,24},{20,28},{24,16},{28,20},{1,9},{5... | collective-permute-start | bytes 12296 | tf_op jit(solution)/shard_map/ppermute | solution.py:26
  18.6 14.9 %collective-permute-start.6 = (bf16[128,2048]{1,0:T(8,128)(2,1)S(1)}, bf16[128,2048]{1,0:T(8,128)(2,1)S(1)}, u32[]{:S(2)}, u32[]{:S(2)}) collective-permute-start(bf16[128,2048]{1,0:T(8,128)(2,1)S(1)} %slice_select_fusion.refs_1_), channel_id=1, source_target_pairs={{0,8},{4,12},{8,0},{12,4},{16,24},{20,28},{24,16},{28,20},{1,9},{5... | collective-permute-start | bytes 1572872 | tf_op jit(solution)/shard_map/ppermute | solution.py:26
  19.0 14.9 %collective-permute-start.7 = (bf16[128,2048]{1,0:T(8,128)(2,1)S(1)}, bf16[128,2048]{1,0:T(8,128)(2,1)S(1)}, u32[]{:S(2)}, u32[]{:S(2)}) collective-permute-start(bf16[128,2048]{1,0:T(8,128)(2,1)S(1)} %slice_select_fusion.refs_1_), channel_id=1, source_target_pairs={{0,16},{4,20},{8,24},{12,28},{16,0},{20,4},{24,8},{28,12},{1,17},{... | collective-permute-start | bytes 1572872 | tf_op jit(solution)/shard_map/ppermute | solution.py:26
  20.7 23.5 %collective-permute-start.8 = (bf16[256,2048]{1,0:T(8,128)(2,1)S(1)}, bf16[256,2048]{1,0:T(8,128)(2,1)S(1)}, u32[]{:S(2)}, u32[]{:S(2)}) collective-permute-start(bf16[256,2048]{1,0:T(8,128)(2,1)S(1)} %pad_maximum_fusion.2), channel_id=1, source_target_pairs={{0,1},{1,0},{2,3},{3,2},{4,5},{5,4},{6,7},{7,6},{8,9},{9,8},{10,11... | collective-permute-start | bytes 3145736 | tf_op jit(solution)/shard_map/ppermute | solution.py:30
  22.4 20.4 %collective-permute-start.10 = (bf16[128,2048]{1,0:T(8,128)(2,1)S(1)}, bf16[128,2048]{1,0:T(8,128)(2,1)S(1)}, u32[]{:S(2)}, u32[]{:S(2)}) collective-permute-start(bf16[128,2048]{1,0:T(8,128)(2,1)S(1)} %get-tuple-element.95), channel_id=1, source_target_pairs={{0,16},{4,20},{8,24},{12,28},{16,0},{20,4},{24,8},{28,12},{1,17},{... | collective-permute-start | bytes 1572872 | tf_op jit(solution)/shard_map/ppermute | solution.py:26
  22.9 19.9 %collective-permute-start.9 = (bf16[128,2048]{1,0:T(8,128)(2,1)S(1)}, bf16[128,2048]{1,0:T(8,128)(2,1)S(1)}, u32[]{:S(2)}, u32[]{:S(2)}) collective-permute-start(bf16[128,2048]{1,0:T(8,128)(2,1)S(1)} %get-tuple-element.95), channel_id=1, source_target_pairs={{0,8},{4,12},{8,0},{12,4},{16,24},{20,28},{24,16},{28,20},{1,9},{5... | collective-permute-start | bytes 1572872 | tf_op jit(solution)/shard_map/ppermute | solution.py:26
  33.9 10.3 %collective-permute-start.11 = (bf16[128,2048]{1,0:T(8,128)(2,1)S(1)}, bf16[128,2048]{1,0:T(8,128)(2,1)S(1)}, u32[]{:S(2)}, u32[]{:S(2)}) collective-permute-start(bf16[128,2048]{1,0:T(8,128)(2,1)S(1)} %collective-permute-done.refs_4_), channel_id=1, source_target_pairs={{0,4},{4,0},{8,12},{12,8},{16,20},{20,16},{24,28},{28,24},{1,5},{5... | collective-permute-start | bytes 1572872 | tf_op jit(solution)/shard_map/ppermute | solution.py:26
  33.9 10.3 %collective-permute-start.12 = (bf16[128,2048]{1,0:T(8,128)(2,1)S(1)}, bf16[128,2048]{1,0:T(8,128)(2,1)S(1)}, u32[]{:S(2)}, u32[]{:S(2)}) collective-permute-start(bf16[128,2048]{1,0:T(8,128)(2,1)S(1)} %collective-permute-done.1.refs_8_), channel_id=1, source_target_pairs={{0,4},{4,0},{8,12},{12,8},{16,20},{20,16},{24,28},{28,24},{1,5},{5... | collective-permute-start | bytes 1572872 | tf_op jit(solution)/shard_map/ppermute | solution.py:26
  44.2 14.9 %collective-permute-start.13 = (bf16[128,2048]{1,0:T(8,128)(2,1)S(1)}, bf16[128,2048]{1,0:T(8,128)(2,1)S(1)}, u32[]{:S(2)}, u32[]{:S(2)}) collective-permute-start(bf16[128,2048]{1,0:T(8,128)(2,1)S(1)} %collective-permute-done.refs_4_), channel_id=1, source_target_pairs={{0,16},{4,20},{8,24},{12,28},{16,0},{20,4},{24,8},{28,12},{1,17},{... | collective-permute-start | bytes 1572872 | tf_op jit(solution)/shard_map/ppermute | solution.py:26
  44.7 14.9 %collective-permute-start.14 = (bf16[128,2048]{1,0:T(8,128)(2,1)S(1)}, bf16[128,2048]{1,0:T(8,128)(2,1)S(1)}, u32[]{:S(2)}, u32[]{:S(2)}) collective-permute-start(bf16[128,2048]{1,0:T(8,128)(2,1)S(1)} %collective-permute-done.7.refs_9_), channel_id=1, source_target_pairs={{0,8},{4,12},{8,0},{12,4},{16,24},{20,28},{24,16},{28,20},{1,9},{5... | collective-permute-start | bytes 1572872 | tf_op jit(solution)/shard_map/ppermute | solution.py:26
  45.9 21.7 %collective-permute-start.15 = (bf16[256,2048]{1,0:T(8,128)(2,1)S(1)}, bf16[256,2048]{1,0:T(8,128)(2,1)S(1)}, u32[]{:S(2)}, u32[]{:S(2)}) collective-permute-start(bf16[256,2048]{1,0:T(8,128)(2,1)S(1)} %pad_maximum_fusion.1), channel_id=1, source_target_pairs={{0,1},{1,0},{2,3},{3,2},{4,5},{5,4},{6,7},{7,6},{8,9},{9,8},{10,11... | collective-permute-start | bytes 3145736 | tf_op jit(solution)/shard_map/ppermute | solution.py:30
  47.5 19.5 %collective-permute-start.16 = (bf16[128,2048]{1,0:T(8,128)(2,1)S(1)}, bf16[128,2048]{1,0:T(8,128)(2,1)S(1)}, u32[]{:S(2)}, u32[]{:S(2)}) collective-permute-start(bf16[128,2048]{1,0:T(8,128)(2,1)S(1)} %get-tuple-element.105), channel_id=1, source_target_pairs={{0,8},{4,12},{8,0},{12,4},{16,24},{20,28},{24,16},{28,20},{1,9},{5... | collective-permute-start | bytes 1572872 | tf_op jit(solution)/shard_map/ppermute | solution.py:26
  48.3 18.7 %collective-permute-start.17 = (bf16[128,2048]{1,0:T(8,128)(2,1)S(1)}, bf16[128,2048]{1,0:T(8,128)(2,1)S(1)}, u32[]{:S(2)}, u32[]{:S(2)}) collective-permute-start(bf16[128,2048]{1,0:T(8,128)(2,1)S(1)} %get-tuple-element.105), channel_id=1, source_target_pairs={{0,16},{4,20},{8,24},{12,28},{16,0},{20,4},{24,8},{28,12},{1,17},{... | collective-permute-start | bytes 1572872 | tf_op jit(solution)/shard_map/ppermute | solution.py:26
  59.6 7.4 %collective-permute-start.18 = (bf16[128,2048]{1,0:T(8,128)(2,1)S(1)}, bf16[128,2048]{1,0:T(8,128)(2,1)S(1)}, u32[]{:S(2)}, u32[]{:S(2)}) collective-permute-start(bf16[128,2048]{1,0:T(8,128)(2,1)S(1)} %collective-permute-done.6.refs_5_), channel_id=1, source_target_pairs={{0,4},{4,0},{8,12},{12,8},{16,20},{20,16},{24,28},{28,24},{1,5},{5... | collective-permute-start | bytes 1572872 | tf_op jit(solution)/shard_map/ppermute | solution.py:26
  59.6 7.4 %collective-permute-start.19 = (bf16[128,2048]{1,0:T(8,128)(2,1)S(1)}, bf16[128,2048]{1,0:T(8,128)(2,1)S(1)}, u32[]{:S(2)}, u32[]{:S(2)}) collective-permute-start(bf16[128,2048]{1,0:T(8,128)(2,1)S(1)} %collective-permute-done.7.refs_9_), channel_id=1, source_target_pairs={{0,4},{4,0},{8,12},{12,8},{16,20},{20,16},{24,28},{28,24},{1,5},{5... | collective-permute-start | bytes 1572872 | tf_op jit(solution)/shard_map/ppermute | solution.py:26
  68.1 5.7 %collective-permute-start.24 = (bf16[768,2048]{1,0:T(8,128)(2,1)S(1)}, bf16[768,2048]{1,0:T(8,128)(2,1)S(1)}, u32[]{:S(2)}, u32[]{:S(2)}) collective-permute-start(bf16[768,2048]{1,0:T(8,128)(2,1)S(1)} %pad_maximum_fusion), channel_id=1, source_target_pairs={{0,4},{4,0},{8,12},{12,8},{16,20},{20,16},{24,28},{28,24},{1,5},{5... | collective-permute-start | bytes 9437192 | tf_op jit(solution)/shard_map/ppermute | solution.py:26
  68.2 9.5 %collective-permute-start.23 = (bf16[256,2048]{1,0:T(8,128)(2,1)S(1)}, bf16[256,2048]{1,0:T(8,128)(2,1)S(1)}, u32[]{:S(2)}, u32[]{:S(2)}) collective-permute-start(bf16[256,2048]{1,0:T(8,128)(2,1)S(1)} %pad_maximum_fusion.3), channel_id=1, source_target_pairs={{0,4},{4,0},{8,12},{12,8},{16,20},{20,16},{24,28},{28,24},{1,5},{5... | collective-permute-start | bytes 3145736 | tf_op jit(solution)/shard_map/ppermute | solution.py:26
  68.8 16.4 %collective-permute-start.22 = (bf16[128,2048]{1,0:T(8,128)(2,1)S(1)}, bf16[128,2048]{1,0:T(8,128)(2,1)S(1)}, u32[]{:S(2)}, u32[]{:S(2)}) collective-permute-start(bf16[128,2048]{1,0:T(8,128)(2,1)S(1)} %collective-permute-done.13.refs_12_), channel_id=1, source_target_pairs={{0,1},{1,0},{2,3},{3,2},{4,5},{5,4},{6,7},{7,6},{8,9},{9,8},{10,11... | collective-permute-start | bytes 1572872 | tf_op jit(solution)/shard_map/ppermute | solution.py:30
  70.4 13.8 %collective-permute-start.20 = (bf16[128,2048]{1,0:T(8,128)(2,1)S(1)}, bf16[128,2048]{1,0:T(8,128)(2,1)S(1)}, u32[]{:S(2)}, u32[]{:S(2)}) collective-permute-start(bf16[128,2048]{1,0:T(8,128)(2,1)S(1)} %collective-permute-done.9.refs_2_), channel_id=1, source_target_pairs={{0,16},{4,20},{8,24},{12,28},{16,0},{20,4},{24,8},{28,12},{1,17},{... | collective-permute-start | bytes 1572872 | tf_op jit(solution)/shard_map/ppermute | solution.py:26
  71.9 13.3 %collective-permute-start.21 = (bf16[128,2048]{1,0:T(8,128)(2,1)S(1)}, bf16[128,2048]{1,0:T(8,128)(2,1)S(1)}, u32[]{:S(2)}, u32[]{:S(2)}) collective-permute-start(bf16[128,2048]{1,0:T(8,128)(2,1)S(1)} %collective-permute-done.17.refs_5_), channel_id=1, source_target_pairs={{0,8},{4,12},{8,0},{12,4},{16,24},{20,28},{24,16},{28,20},{1,9},{5... | collective-permute-start | bytes 1572872 | tf_op jit(solution)/shard_map/ppermute | solution.py:26
  76.1 8.1 %collective-permute-start.25 = (f32[2,1024]{1,0:T(2,128)S(1)}, f32[2,1024]{1,0:T(2,128)S(1)}, u32[]{:S(2)}, u32[]{:S(2)}) collective-permute-start(f32[2,1024]{1,0:T(2,128)S(1)} %pad_maximum_fusion.8), channel_id=1, source_target_pairs={{0,16},{4,20},{8,24},{12,28},{16,0},{20,4},{24,8},{28,12},{1,17},{... | collective-permute-start | bytes 24584 | tf_op jit(solution)/shard_map/ppermute | solution.py:26
  85.6 7.2 %collective-permute-start.29 = (bf16[1024,2048]{1,0:T(8,128)(2,1)S(1)}, bf16[1024,2048]{1,0:T(8,128)(2,1)S(1)}, u32[]{:S(2)}, u32[]{:S(2)}) collective-permute-start(bf16[1024,2048]{1,0:T(8,128)(2,1)S(1)} %constant_dynamic-update-slice_fusion), channel_id=1, source_target_pairs={{0,4},{4,0},{8,12},{12,8},{16,20},{20,16},{24,28},{28,24},{1,5},{5... | collective-permute-start | bytes 12582920 | tf_op jit(solution)/shard_map/ppermute | solution.py:26
  85.7 10.2 %collective-permute-start.28 = (bf16[128,2048]{1,0:T(8,128)(2,1)S(1)}, bf16[128,2048]{1,0:T(8,128)(2,1)S(1)}, u32[]{:S(2)}, u32[]{:S(2)}) collective-permute-start(bf16[128,2048]{1,0:T(8,128)(2,1)S(1)} %collective-permute-done.22.refs_1_.refs_19_), channel_id=1, source_target_pairs={{0,4},{4,0},{8,12},{12,8},{16,20},{20,16},{24,28},{28,24},{1,5},{5... | collective-permute-start | bytes 1572872 | tf_op jit(solution)/shard_map/ppermute | solution.py:26
  86.3 9.7 %collective-permute-start.26 = (bf16[64,2048]{1,0:T(8,128)(2,1)S(1)}, bf16[64,2048]{1,0:T(8,128)(2,1)S(1)}, u32[]{:S(2)}, u32[]{:S(2)}) collective-permute-start(bf16[64,2048]{1,0:T(8,128)(2,1)S(1)} %get-tuple-element.161), channel_id=1, source_target_pairs={{0,8},{4,12},{8,0},{12,4},{16,24},{20,28},{24,16},{28,20},{1,9},{5... | collective-permute-start | bytes 786440 | tf_op jit(solution)/shard_map/ppermute | solution.py:26
  87.4 8.5 %collective-permute-start.27 = (bf16[64,2048]{1,0:T(8,128)(2,1)S(1)}, bf16[64,2048]{1,0:T(8,128)(2,1)S(1)}, u32[]{:S(2)}, u32[]{:S(2)}) collective-permute-start(bf16[64,2048]{1,0:T(8,128)(2,1)S(1)} %get-tuple-element.160), channel_id=1, source_target_pairs={{0,16},{4,20},{8,24},{12,28},{16,0},{20,4},{24,8},{28,12},{1,17},{... | collective-permute-start | bytes 786440 | tf_op jit(solution)/shard_map/ppermute | solution.py:26
  101.8 5.9 %collective-permute-start.34 = (f32[8,2048]{1,0:T(8,128)S(1)}, f32[8,2048]{1,0:T(8,128)S(1)}, u32[]{:S(2)}, u32[]{:S(2)}) collective-permute-start(f32[8,2048]{1,0:T(8,128)S(1)} %get-tuple-element.146), channel_id=1, source_target_pairs={{0,24},{4,28},{8,16},{12,20},{16,8},{20,12},{24,0},{28,4},{1,25},{... | collective-permute-start | bytes 196616 | tf_op jit(solution)/shard_map/ppermute | solution.py:26
  102.9 4.8 %collective-permute-start.32 = (f32[8,2048]{1,0:T(8,128)S(1)}, f32[8,2048]{1,0:T(8,128)S(1)}, u32[]{:S(2)}, u32[]{:S(2)}) collective-permute-start(f32[8,2048]{1,0:T(8,128)S(1)} %get-tuple-element.146), channel_id=1, source_target_pairs={{0,8},{4,12},{8,0},{12,4},{16,24},{20,28},{24,16},{28,20},{1,9},{5... | collective-permute-start | bytes 196616 | tf_op jit(solution)/shard_map/ppermute | solution.py:26
  118.2 10.0 %collective-permute-start.37 = (f32[1,2048]{1,0:T(1,128)S(1)}, f32[1,2048]{1,0:T(1,128)S(1)}, u32[]{:S(2)}, u32[]{:S(2)}) collective-permute-start(f32[1,2048]{1,0:T(1,128)S(1)} %add.8.refs_0_), channel_id=1, source_target_pairs={{0,2},{1,3},{2,0},{3,1},{4,6},{5,7},{6,4},{7,5},{8,10},{9,11},{10,... | collective-permute-start | bytes 24584 | tf_op jit(solution)/shard_map/ppermute | solution.py:30
  (12 other events, 78.7 us)

commit v9 on v8

--- a/solution.py
+++ b/solution.py
@@ -525,7 +525,7 @@
     both, f6a, f6b, sb, t2b, t4b, f3b, f5b, sa, t2a = after((both, f6a, f6b, sb, t2b, t4b, f3b, f5b, sa, t2a))
     t6a, t6b = send(t2a, 4), send(t4b, 2)
     s6a = over(f6a)
-    f7, cs = core(stack(f6a, f6b)), core(stack(sa, sb, own_s))
+    f7, cs = core(stack(f6a, f6b)), core(stack(sa, sb, own_s, own_t))
     first = Shards([own_f, [f1a, f1b], [f2a, f2b], [f3a, f3b], [f4a, f4b], [f5a, f5b], [f6a, f6b], [f7]])
     pairs = lambda one, two, row: cut(one, row) + cut(two, row)
     most = [[own_s], cut(cs, 4, 5), pairs(sa, sb, 0), cut(cs, 0, 2), pairs(sa, sb, 1), cut(cs, 1, 3)]
@@ -538,9 +538,9 @@
     quarter = half // 2
     s6b = [send(sb_out[half : half + quarter], 2), send(sb_out[quarter:half], 4)]
     s7a = core(s6a)
-    c4 = core(stack(t6a, t6b, t2b, t4b, own_t, t2a, t4a))
+    c4 = core(stack(t6a, t6b, t2b, t4b, t2a, t4a))
     third = Shards(
-        [[own_t], cut(c4, 4, 5), [t2a, t2b], cut(c4, 6, 2), [t4a, t4b], cut(c4, 7, 3)]
+        [[own_t], cut(cs, 6, 7), [t2a, t2b], cut(c4, 4, 2), [t4a, t4b], cut(c4, 5, 3)]
         + [[t6a, t6b], cut(c4, 0, 1)]
     )
     back = back_call(where, grads, third)

time: 129 us -> 129 us (level)
  other arithmetic: 5.61 us -> 3.81 us
  waiting for transfers between devices: 56.8 us -> 58.4 us
    ppermute x33, waiting for transfers between devices: 54.8 us -> 56.4 us  [hop(): return lax.ppermute(value, 'seq', [(i, i ^ offset) for i in range(count)])]
  transfers between devices with their start and end apart: 38 -> 38, of which waited for: 18 -> 21; matrix products, arithmetic and copies ran while one was open for 3% -> 1% of each run, Pallas kernels for 18% -> 18%
where the time goes in v9:
time: 129 us
  waiting for transfers between devices  58.4 us (45%)
  starting transfers between devices  33.5 us (26%)
  Pallas kernels  31.7 us (25%)
  other arithmetic  3.81 us (3%)
    ppermute x33, waiting for transfers between devices, hop(): return lax.ppermute(value, 'seq', [(i, i ^ offset) for i in range(count)])  56.4 us
    ppermute x33, starting transfers between devices, hop(): return lax.ppermute(value, 'seq', [(i, i ^ offset) for i in range(count)])  25.5 us
    ppermute x5, starting transfers between devices, swap_batch(): return lax.ppermute(value, 'batch', [(i, i ^ offset) for i in range(count)])  7.97 us
    pallas_call x1, Pallas kernels, input_grad_call(): pl.pallas_call(kernel, out_shape=jax.ShapeDtypeStruct((rows, width), BF16...  7.29 us
    pallas_call x2, Pallas kernels, project_call(): pl.pallas_call(kernel, out_shape=jax.ShapeDtypeStruct((rows, width), dtyp...  5.38 us
    pallas_call x1, Pallas kernels, scan_call(): pl.pallas_call(kernel, out_shape=[wide, tall, tall, flat, flat], in_specs...  3.92 us
    pallas_call x1, Pallas kernels, layer_call(): pl.pallas_call(kernel, out_shape=jax.ShapeDtypeStruct((rows, width), BF16...  3.92 us
    pallas_call x1, Pallas kernels, totals_call(): pl.pallas_call(kernel, out_shape=[jax.ShapeDtypeStruct((rows, width), BF1...  3.79 us
  transfers between devices with their start and end apart: 38, of which 21 were waited for; matrix products, arithmetic and copies ran while one was open for 1% of the time, Pallas kernels for 18%

profile of v9, /device:TPU:0, one launch (start us, length us, event | category | flops | bytes accessed | tf_op | source)
XLA Modules:
  0.0 128.8 jit_solution(9713606117707604278)
XLA Ops:
  0.8 1.4 %slice_select_fusion.1.refs_0_ = bf16[128,2048]{1,0:T(8,128)(2,1)S(1)} fusion(bf16[256,2048]{1,0:T(8,128)(2,1)} %param.14, bf16[256,2048]{1,0:T(8,128)(2,1)} %param.13, pred[]{:T(512)S(6)} %eq.5), kind=kLoop, calls=%fused_computation.7 | loop fusion | flops 262144 | bytes 1572865 | tf_op jit(solution)/shard_map/jit(_where)/select_n | solution.py:496
  2.2 3.0 %collective-permute-start = (bf16[128,2048]{1,0:T(8,128)(2,1)S(1)}, bf16[128,2048]{1,0:T(8,128)(2,1)S(1)}, u32[]{:S(2)}, u32[]{:S(2)}) collective-permute-start(bf16[128,2048]{1,0:T(8,128)(2,1)S(1)} %slice_select_fusion.1.refs_0_), channel_id=1, source_target_pairs={{0,8},{4,12},{8,0},{12,4},{16,24},{20,28},{24,16},{28,20},{1,9},{5... | collective-permute-start | bytes 1572872 | tf_op jit(solution)/shard_map/ppermute | solution.py:26
  5.2 1.5 %collective-permute-start.1 = (bf16[128,2048]{1,0:T(8,128)(2,1)S(1)}, bf16[128,2048]{1,0:T(8,128)(2,1)S(1)}, u32[]{:S(2)}, u32[]{:S(2)}) collective-permute-start(bf16[128,2048]{1,0:T(8,128)(2,1)S(1)} %slice_select_fusion.1.refs_0_), channel_id=1, source_target_pairs={{0,16},{4,20},{8,24},{12,28},{16,0},{20,4},{24,8},{28,12},{1,17},{... | collective-permute-start | bytes 1572872 | tf_op jit(solution)/shard_map/ppermute | solution.py:26
  10.7 3.3 %norm_rows.1 = (bf16[256,2048]{1,0:T(8,128)(2,1)S(1)}, bf16[2048,256]{1,0:T(8,128)(2,1)S(1)}, f32[256,1]{1,0:T(8,128)S(1)}) custom-call(s32[3]{0:T(128)S(1)} %pad_add_fusion.where_ref, bf16[256,2048]{1,0:T(8,128)(2,1)S(1)} %bitcast.14, bf16[256,2048]{1,0:T(8,128)(2,1)S(1)} %bitcast.17, f32[1,2048]{1,0:T(1,128)S(1)} %bitcast.20), custom_call_target="tpu_custom_call" | custom-call | flops 536870912 | bytes 4194304 | tf_op jit(solution)/shard_map/norm_rows/pallas_call | solution.py:138
  13.9 3.3 %collective-permute-done.5 = f32[2,512]{1,0:T(2,128)S(1)} collective-permute-done((f32[2,512]{1,0:T(2,128)S(1)}, f32[2,512]{1,0:T(2,128)S(1)}, u32[]{:S(2)}, u32[]{:S(2)}) %collective-permute-start.5) | collective-permute-done | bytes 4128 | tf_op jit(solution)/shard_map/ppermute | solution.py:26
  19.1 1.6 %collective-permute-start.7 = (bf16[128,2048]{1,0:T(8,128)(2,1)S(1)}, bf16[128,2048]{1,0:T(8,128)(2,1)S(1)}, u32[]{:S(2)}, u32[]{:S(2)}) collective-permute-start(bf16[128,2048]{1,0:T(8,128)(2,1)S(1)} %slice_select_fusion.refs_1_), channel_id=1, source_target_pairs={{0,16},{4,20},{8,24},{12,28},{16,0},{20,4},{24,8},{28,12},{1,17},{... | collective-permute-start | bytes 1572872 | tf_op jit(solution)/shard_map/ppermute | solution.py:26
  20.7 1.6 %collective-permute-start.8 = (bf16[256,2048]{1,0:T(8,128)(2,1)S(1)}, bf16[256,2048]{1,0:T(8,128)(2,1)S(1)}, u32[]{:S(2)}, u32[]{:S(2)}) collective-permute-start(bf16[256,2048]{1,0:T(8,128)(2,1)S(1)} %pad_maximum_fusion.2), channel_id=1, source_target_pairs={{0,1},{1,0},{2,3},{3,2},{4,5},{5,4},{6,7},{7,6},{8,9},{9,8},{10,11... | collective-permute-start | bytes 3145736 | tf_op jit(solution)/shard_map/ppermute | solution.py:30
  22.9 1.5 %collective-permute-start.9 = (bf16[128,2048]{1,0:T(8,128)(2,1)S(1)}, bf16[128,2048]{1,0:T(8,128)(2,1)S(1)}, u32[]{:S(2)}, u32[]{:S(2)}) collective-permute-start(bf16[128,2048]{1,0:T(8,128)(2,1)S(1)} %get-tuple-element.95), channel_id=1, source_target_pairs={{0,8},{4,12},{8,0},{12,4},{16,24},{20,28},{24,16},{28,20},{1,9},{5... | collective-permute-start | bytes 1572872 | tf_op jit(solution)/shard_map/ppermute | solution.py:26
  24.4 9.1 %collective-permute-done.6.refs_5_ = bf16[128,2048]{1,0:T(8,128)(2,1)S(1)} collective-permute-done((bf16[128,2048]{1,0:T(8,128)(2,1)S(1)}, bf16[128,2048]{1,0:T(8,128)(2,1)S(1)}, u32[]{:S(2)}, u32[]{:S(2)}) %collective-permute-start.6) | collective-permute-done | bytes 524320 | tf_op jit(solution)/shard_map/ppermute | solution.py:26
  34.5 8.3 %collective-permute-done.10.refs_5_ = bf16[128,2048]{1,0:T(8,128)(2,1)S(1)} collective-permute-done((bf16[128,2048]{1,0:T(8,128)(2,1)S(1)}, bf16[128,2048]{1,0:T(8,128)(2,1)S(1)}, u32[]{:S(2)}, u32[]{:S(2)}) %collective-permute-start.10) | collective-permute-done | bytes 524320 | tf_op jit(solution)/shard_map/ppermute | solution.py:26
  46.0 1.6 %collective-permute-start.15 = (bf16[256,2048]{1,0:T(8,128)(2,1)S(1)}, bf16[256,2048]{1,0:T(8,128)(2,1)S(1)}, u32[]{:S(2)}, u32[]{:S(2)}) collective-permute-start(bf16[256,2048]{1,0:T(8,128)(2,1)S(1)} %pad_maximum_fusion.1), channel_id=1, source_target_pairs={{0,1},{1,0},{2,3},{3,2},{4,5},{5,4},{6,7},{7,6},{8,9},{9,8},{10,11... | collective-permute-start | bytes 3145736 | tf_op jit(solution)/shard_map/ppermute | solution.py:30
  48.3 1.5 %collective-permute-start.17 = (bf16[128,2048]{1,0:T(8,128)(2,1)S(1)}, bf16[128,2048]{1,0:T(8,128)(2,1)S(1)}, u32[]{:S(2)}, u32[]{:S(2)}) collective-permute-start(bf16[128,2048]{1,0:T(8,128)(2,1)S(1)} %get-tuple-element.105), channel_id=1, source_target_pairs={{0,16},{4,20},{8,24},{12,28},{16,0},{20,4},{24,8},{28,12},{1,17},{... | collective-permute-start | bytes 1572872 | tf_op jit(solution)/shard_map/ppermute | solution.py:26
  49.9 9.2 %collective-permute-done.13.refs_12_ = bf16[128,2048]{1,0:T(8,128)(2,1)S(1)} collective-permute-done((bf16[128,2048]{1,0:T(8,128)(2,1)S(1)}, bf16[128,2048]{1,0:T(8,128)(2,1)S(1)}, u32[]{:S(2)}, u32[]{:S(2)}) %collective-permute-start.13) | collective-permute-done | bytes 524320 | tf_op jit(solution)/shard_map/ppermute | solution.py:26
  60.1 6.9 %collective-permute-done.16.refs_3_ = bf16[128,2048]{1,0:T(8,128)(2,1)S(1)} collective-permute-done((bf16[128,2048]{1,0:T(8,128)(2,1)S(1)}, bf16[128,2048]{1,0:T(8,128)(2,1)S(1)}, u32[]{:S(2)}, u32[]{:S(2)}) %collective-permute-start.16) | collective-permute-done | bytes 524320 | tf_op jit(solution)/shard_map/ppermute | solution.py:26
  69.0 1.6 %collective-permute-start.22 = (bf16[128,2048]{1,0:T(8,128)(2,1)S(1)}, bf16[128,2048]{1,0:T(8,128)(2,1)S(1)}, u32[]{:S(2)}, u32[]{:S(2)}) collective-permute-start(bf16[128,2048]{1,0:T(8,128)(2,1)S(1)} %collective-permute-done.13.refs_12_), channel_id=1, source_target_pairs={{0,1},{1,0},{2,3},{3,2},{4,5},{5,4},{6,7},{7,6},{8,9},{9,8},{10,11... | collective-permute-start | bytes 1572872 | tf_op jit(solution)/shard_map/ppermute | solution.py:30
  70.6 1.5 %collective-permute-start.20 = (bf16[128,2048]{1,0:T(8,128)(2,1)S(1)}, bf16[128,2048]{1,0:T(8,128)(2,1)S(1)}, u32[]{:S(2)}, u32[]{:S(2)}) collective-permute-start(bf16[128,2048]{1,0:T(8,128)(2,1)S(1)} %collective-permute-done.9.refs_2_), channel_id=1, source_target_pairs={{0,16},{4,20},{8,24},{12,28},{16,0},{20,4},{24,8},{28,12},{1,17},{... | collective-permute-start | bytes 1572872 | tf_op jit(solution)/shard_map/ppermute | solution.py:26
  73.2 2.4 %collective-permute-done.24.refs_1_.refs_16_ = bf16[1024,2048]{1,0:T(8,128)(2,1)S(1)} collective-permute-done((bf16[1024,2048]{1,0:T(8,128)(2,1)S(1)}, bf16[1024,2048]{1,0:T(8,128)(2,1)S(1)}, u32[]{:S(2)}, u32[]{:S(2)}) %collective-permute-start.24) | collective-permute-done | bytes 4194336 | tf_op jit(solution)/shard_map/ppermute | solution.py:26
  75.5 2.3 %project.3.refs_0_ = f32[256,2048]{1,0:T(8,128)S(1)} custom-call(bf16[256,2048]{1,0:T(8,128)(2,1)S(1)} %get-tuple-element.114.x_ref, bf16[256,2048]{1,0:T(8,128)(2,1)S(1)} %broadcast_select_fusion.refs_0_.refs_15_, bf16[1024,2048]{1,0:T(8,128)(2,1)S(1)} %collective-permute-done.24.refs_1_.refs_16_, ...), custom_call_target="tpu_custom_call" | custom-call | flops 1610612736 | bytes 6291456 | tf_op jit(solution)/shard_map/project/pallas_call | solution.py:166
  77.9 1.5 %collective-permute-start.25 = (f32[2,1024]{1,0:T(2,128)S(1)}, f32[2,1024]{1,0:T(2,128)S(1)}, u32[]{:S(2)}, u32[]{:S(2)}) collective-permute-start(f32[2,1024]{1,0:T(2,128)S(1)} %pad_maximum_fusion.8), channel_id=1, source_target_pairs={{0,16},{4,20},{8,24},{12,28},{16,0},{20,4},{24,8},{28,12},{1,17},{... | collective-permute-start | bytes 24584 | tf_op jit(solution)/shard_map/ppermute | solution.py:26
  79.4 3.1 %project.2.first_ref = bf16[256,2048]{1,0:T(8,128)(2,1)S(1)} custom-call(bf16[256,2048]{1,0:T(8,128)(2,1)S(1)} %get-tuple-element.114.x_ref, bf16[128,2048]{1,0:T(8,128)(2,1)S(1)} %slice_select_fusion.1.refs_0_, bf16[128,2048]{1,0:T(8,128)(2,1)S(1)} %slice_select_fusion.refs_1_, bf16[128,2048]{1,0:T(8,128)(2,1)S(1)} %collective-permute-done.2.refs_2_, ...), custom_call_target="tpu_custom_call" | custom-call | flops 2147483648 | bytes 8388608 | tf_op jit(solution)/shard_map/project/pallas_call | solution.py:166
  82.5 1.9 %collective-permute-done.25 = f32[2,1024]{1,0:T(2,128)S(1)} collective-permute-done((f32[2,1024]{1,0:T(2,128)S(1)}, f32[2,1024]{1,0:T(2,128)S(1)}, u32[]{:S(2)}, u32[]{:S(2)}) %collective-permute-start.25) | collective-permute-done | bytes 8224 | tf_op jit(solution)/shard_map/ppermute | solution.py:26
  88.0 3.4 %collective-permute-done.29.refs_4_ = bf16[768,2048]{1,0:T(8,128)(2,1)S(1)} collective-permute-done((bf16[768,2048]{1,0:T(8,128)(2,1)S(1)}, bf16[768,2048]{1,0:T(8,128)(2,1)S(1)}, u32[]{:S(2)}, u32[]{:S(2)}) %collective-permute-start.29) | collective-permute-done | bytes 3145760 | tf_op jit(solution)/shard_map/ppermute | solution.py:26
  91.4 3.0 %back_rows.1.back_ref = bf16[256,2048]{1,0:T(8,128)(2,1)S(1)} custom-call(s32[3]{0:T(128)S(1)} %pad_add_fusion.where_ref, bf16[2048,256]{1,0:T(8,128)(2,1)S(1)} %get-tuple-element.130.g_ref, bf16[256,2048]{1,0:T(8,128)(2,1)S(1)} %copy-done, bf16[1024,2048]{1,0:T(8,128)(2,1)S(1)} %collective-permute-done.24.refs_1_.refs_16_, ...), custom_call_target="tpu_custom_call" | custom-call | flops 2147483648 | bytes 8388608 | tf_op jit(solution)/shard_map/back_rows/pallas_call | solution.py:190
  95.6 1.9 %collective-permute-done.30.refs_5_.refs_23_ = bf16[128,2048]{1,0:T(8,128)(2,1)S(1)} collective-permute-done((bf16[128,2048]{1,0:T(8,128)(2,1)S(1)}, bf16[128,2048]{1,0:T(8,128)(2,1)S(1)}, u32[]{:S(2)}, u32[]{:S(2)}) %collective-permute-start.30) | collective-permute-done | bytes 524320 | tf_op jit(solution)/shard_map/ppermute | solution.py:26
  97.5 3.8 %project_totals.1 = (bf16[256,2048]{1,0:T(8,128)(2,1)S(1)}, f32[3,8,2048]{2,1,0:T(8,128)S(1)}, f32[8,2048]{1,0:T(8,128)S(1)}, f32[2,2048]{1,0:T(2,128)S(1)}) custom-call(s32[3]{0:T(128)S(1)} %pad_add_fusion.where_ref, bf16[256,2048]{1,0:T(8,128)(2,1)S(1)} %get-tuple-element.114.x_ref, bf16[256,2048]{1,0:T(8,128)(2,1)S(1)} %project.2.first_ref, ...), custom_call_target="tpu_custom_call" | custom-call | flops 536870912 | bytes 2097152 | tf_op jit(solution)/shard_map/project_totals/pallas_call | solution.py:291
  103.4 1.5 %collective-permute-start.33 = (f32[8,2048]{1,0:T(8,128)S(1)}, f32[8,2048]{1,0:T(8,128)S(1)}, u32[]{:S(2)}, u32[]{:S(2)}) collective-permute-start(f32[8,2048]{1,0:T(8,128)S(1)} %get-tuple-element.146), channel_id=1, source_target_pairs={{0,16},{4,20},{8,24},{12,28},{16,0},{20,4},{24,8},{28,12},{1,17},{... | collective-permute-start | bytes 196616 | tf_op jit(solution)/shard_map/ppermute | solution.py:26
  104.9 2.3 %collective-permute-done.34 = f32[8,2048]{1,0:T(8,128)S(1)} collective-permute-done((f32[8,2048]{1,0:T(8,128)S(1)}, f32[8,2048]{1,0:T(8,128)S(1)}, u32[]{:S(2)}, u32[]{:S(2)}) %collective-permute-start.34) | collective-permute-done | bytes 65568 | tf_op jit(solution)/shard_map/ppermute | solution.py:26
  107.9 1.4 %collective-permute-done.35.refs_2_ = f32[3,8,2048]{2,1,0:T(8,128)S(1)} collective-permute-done((f32[3,8,2048]{2,1,0:T(8,128)S(1)}, f32[3,8,2048]{2,1,0:T(8,128)S(1)}, u32[]{:S(2)}, u32[]{:S(2)}) %collective-permute-start.35) | collective-permute-done | bytes 196640 | tf_op jit(solution)/shard_map/ppermute | solution.py:26
  109.3 3.9 %scan_rows.1 = (bf16[256,2048]{1,0:T(8,128)(2,1)S(1)}, bf16[2048,256]{1,0:T(8,128)(2,1)S(1)}, bf16[2048,256]{1,0:T(8,128)(2,1)S(1)}, f32[1,2048]{1,0:T(1,128)S(1)}, f32[1,2048]{1,0:T(1,128)S(1)}) custom-call(s32[3]{0:T(128)S(1)} %pad_add_fusion.where_ref, bf16[256,2048]{1,0:T(8,128)(2,1)S(1)} %project.2.first_ref, ...), custom_call_target="tpu_custom_call" | custom-call | flops 805306368 | bytes 6291456 | tf_op jit(solution)/shard_map/scan_rows/pallas_call | solution.py:393
  113.8 3.9 %layer_rows.1 = bf16[256,2048]{1,0:T(8,128)(2,1)} custom-call(s32[3]{0:T(128)S(1)} %pad_add_fusion.where_ref, bf16[256,2048]{1,0:T(8,128)(2,1)S(1)} %get-tuple-element.147.x_ref, bf16[256,2048]{1,0:T(8,128)(2,1)S(1)} %bitcast.15, bf16[256,2048]{1,0:T(8,128)(2,1)S(1)} %copy-done, bf16[1024,2048]{1,0:T(8,128)(2,1)S(1)} %collective-permute-done.24.refs_1_.refs_16_, ...), custom_call_target="tpu_custom_call" | custom-call | flops 2147483648 | bytes 8388608 | tf_op jit(solution)/shard_map/layer_rows/pallas_call | solution.py:419
  117.7 2.7 %collective-permute-start.37 = (f32[1,2048]{1,0:T(1,128)S(1)}, f32[1,2048]{1,0:T(1,128)S(1)}, u32[]{:S(2)}, u32[]{:S(2)}) collective-permute-start(f32[1,2048]{1,0:T(1,128)S(1)} %add.8.refs_0_), channel_id=1, source_target_pairs={{0,2},{1,3},{2,0},{3,1},{4,6},{5,7},{6,4},{7,5},{8,10},{9,11},{10,... | collective-permute-start | bytes 24584 | tf_op jit(solution)/shard_map/ppermute | solution.py:30
  120.4 7.3 %input_grad_rows.1 = bf16[256,2048]{1,0:T(8,128)(2,1)} custom-call(s32[3]{0:T(128)S(1)} %pad_add_fusion.where_ref, bf16[2048,256]{1,0:T(8,128)(2,1)S(1)} %get-tuple-element.152.one_ref, bf16[2048,256]{1,0:T(8,128)(2,1)S(1)} %get-tuple-element.153.other_ref, bf16[256,2048]{1,0:T(8,128)(2,1)S(1)} %bitcast.16, f32[256,1]{1,0:T(8,128)S(1)} %get-tuple-element.154.scale_ref, ...), custom_call_target="tpu_custom_call" | custom-call | flops 4294967296 | bytes 16777216 | tf_op jit(solution)/shard_map/input_grad_rows/pallas_call | solution.py:458
  (93 shorter events, 24.6 us)
Async XLA Ops:
  2.2 15.0 %collective-permute-start = (bf16[128,2048]{1,0:T(8,128)(2,1)S(1)}, bf16[128,2048]{1,0:T(8,128)(2,1)S(1)}, u32[]{:S(2)}, u32[]{:S(2)}) collective-permute-start(bf16[128,2048]{1,0:T(8,128)(2,1)S(1)} %slice_select_fusion.1.refs_0_), channel_id=1, source_target_pairs={{0,8},{4,12},{8,0},{12,4},{16,24},{20,28},{24,16},{28,20},{1,9},{5... | collective-permute-start | bytes 1572872 | tf_op jit(solution)/shard_map/ppermute | solution.py:26
  5.2 13.4 %collective-permute-start.1 = (bf16[128,2048]{1,0:T(8,128)(2,1)S(1)}, bf16[128,2048]{1,0:T(8,128)(2,1)S(1)}, u32[]{:S(2)}, u32[]{:S(2)}) collective-permute-start(bf16[128,2048]{1,0:T(8,128)(2,1)S(1)} %slice_select_fusion.1.refs_0_), channel_id=1, source_target_pairs={{0,16},{4,20},{8,24},{12,28},{16,0},{20,4},{24,8},{28,12},{1,17},{... | collective-permute-start | bytes 1572872 | tf_op jit(solution)/shard_map/ppermute | solution.py:26
  6.7 11.9 %collective-permute-start.2 = (bf16[128,2048]{1,0:T(8,128)(2,1)S(1)}, bf16[128,2048]{1,0:T(8,128)(2,1)S(1)}, u32[]{:S(2)}, u32[]{:S(2)}) collective-permute-start(bf16[128,2048]{1,0:T(8,128)(2,1)S(1)} %slice_select_fusion.1.refs_0_), channel_id=1, source_target_pairs={{0,4},{4,0},{8,12},{12,8},{16,20},{20,16},{24,28},{28,24},{1,5},{5... | collective-permute-start | bytes 1572872 | tf_op jit(solution)/shard_map/ppermute | solution.py:26
  8.0 9.2 %collective-permute-start.3 = (bf16[128,2048]{1,0:T(8,128)(2,1)S(1)}, bf16[128,2048]{1,0:T(8,128)(2,1)S(1)}, u32[]{:S(2)}, u32[]{:S(2)}) collective-permute-start(bf16[128,2048]{1,0:T(8,128)(2,1)S(1)} %slice_select_fusion.refs_1_), channel_id=1, source_target_pairs={{0,4},{4,0},{8,12},{12,8},{16,20},{20,16},{24,28},{28,24},{1,5},{5... | collective-permute-start | bytes 1572872 | tf_op jit(solution)/shard_map/ppermute | solution.py:26
  10.1 7.1 %collective-permute-start.5 = (f32[2,512]{1,0:T(2,128)S(1)}, f32[2,512]{1,0:T(2,128)S(1)}, u32[]{:S(2)}, u32[]{:S(2)}) collective-permute-start(f32[2,512]{1,0:T(2,128)S(1)} %pad_maximum_fusion.9), channel_id=1, source_target_pairs={{0,8},{4,12},{8,0},{12,4},{16,24},{20,28},{24,16},{28,20},{1,9},{5... | collective-permute-start | bytes 12296 | tf_op jit(solution)/shard_map/ppermute | solution.py:26
  18.6 14.9 %collective-permute-start.6 = (bf16[128,2048]{1,0:T(8,128)(2,1)S(1)}, bf16[128,2048]{1,0:T(8,128)(2,1)S(1)}, u32[]{:S(2)}, u32[]{:S(2)}) collective-permute-start(bf16[128,2048]{1,0:T(8,128)(2,1)S(1)} %slice_select_fusion.refs_1_), channel_id=1, source_target_pairs={{0,8},{4,12},{8,0},{12,4},{16,24},{20,28},{24,16},{28,20},{1,9},{5... | collective-permute-start | bytes 1572872 | tf_op jit(solution)/shard_map/ppermute | solution.py:26
  19.1 14.9 %collective-permute-start.7 = (bf16[128,2048]{1,0:T(8,128)(2,1)S(1)}, bf16[128,2048]{1,0:T(8,128)(2,1)S(1)}, u32[]{:S(2)}, u32[]{:S(2)}) collective-permute-start(bf16[128,2048]{1,0:T(8,128)(2,1)S(1)} %slice_select_fusion.refs_1_), channel_id=1, source_target_pairs={{0,16},{4,20},{8,24},{12,28},{16,0},{20,4},{24,8},{28,12},{1,17},{... | collective-permute-start | bytes 1572872 | tf_op jit(solution)/shard_map/ppermute | solution.py:26
  20.7 23.5 %collective-permute-start.8 = (bf16[256,2048]{1,0:T(8,128)(2,1)S(1)}, bf16[256,2048]{1,0:T(8,128)(2,1)S(1)}, u32[]{:S(2)}, u32[]{:S(2)}) collective-permute-start(bf16[256,2048]{1,0:T(8,128)(2,1)S(1)} %pad_maximum_fusion.2), channel_id=1, source_target_pairs={{0,1},{1,0},{2,3},{3,2},{4,5},{5,4},{6,7},{7,6},{8,9},{9,8},{10,11... | collective-permute-start | bytes 3145736 | tf_op jit(solution)/shard_map/ppermute | solution.py:30
  22.4 20.5 %collective-permute-start.10 = (bf16[128,2048]{1,0:T(8,128)(2,1)S(1)}, bf16[128,2048]{1,0:T(8,128)(2,1)S(1)}, u32[]{:S(2)}, u32[]{:S(2)}) collective-permute-start(bf16[128,2048]{1,0:T(8,128)(2,1)S(1)} %get-tuple-element.95), channel_id=1, source_target_pairs={{0,16},{4,20},{8,24},{12,28},{16,0},{20,4},{24,8},{28,12},{1,17},{... | collective-permute-start | bytes 1572872 | tf_op jit(solution)/shard_map/ppermute | solution.py:26
  22.9 20.0 %collective-permute-start.9 = (bf16[128,2048]{1,0:T(8,128)(2,1)S(1)}, bf16[128,2048]{1,0:T(8,128)(2,1)S(1)}, u32[]{:S(2)}, u32[]{:S(2)}) collective-permute-start(bf16[128,2048]{1,0:T(8,128)(2,1)S(1)} %get-tuple-element.95), channel_id=1, source_target_pairs={{0,8},{4,12},{8,0},{12,4},{16,24},{20,28},{24,16},{28,20},{1,9},{5... | collective-permute-start | bytes 1572872 | tf_op jit(solution)/shard_map/ppermute | solution.py:26
  34.0 10.3 %collective-permute-start.11 = (bf16[128,2048]{1,0:T(8,128)(2,1)S(1)}, bf16[128,2048]{1,0:T(8,128)(2,1)S(1)}, u32[]{:S(2)}, u32[]{:S(2)}) collective-permute-start(bf16[128,2048]{1,0:T(8,128)(2,1)S(1)} %collective-permute-done.refs_4_), channel_id=1, source_target_pairs={{0,4},{4,0},{8,12},{12,8},{16,20},{20,16},{24,28},{28,24},{1,5},{5... | collective-permute-start | bytes 1572872 | tf_op jit(solution)/shard_map/ppermute | solution.py:26
  34.0 10.3 %collective-permute-start.12 = (bf16[128,2048]{1,0:T(8,128)(2,1)S(1)}, bf16[128,2048]{1,0:T(8,128)(2,1)S(1)}, u32[]{:S(2)}, u32[]{:S(2)}) collective-permute-start(bf16[128,2048]{1,0:T(8,128)(2,1)S(1)} %collective-permute-done.1.refs_8_), channel_id=1, source_target_pairs={{0,4},{4,0},{8,12},{12,8},{16,20},{20,16},{24,28},{28,24},{1,5},{5... | collective-permute-start | bytes 1572872 | tf_op jit(solution)/shard_map/ppermute | solution.py:26
  44.2 14.9 %collective-permute-start.13 = (bf16[128,2048]{1,0:T(8,128)(2,1)S(1)}, bf16[128,2048]{1,0:T(8,128)(2,1)S(1)}, u32[]{:S(2)}, u32[]{:S(2)}) collective-permute-start(bf16[128,2048]{1,0:T(8,128)(2,1)S(1)} %collective-permute-done.refs_4_), channel_id=1, source_target_pairs={{0,16},{4,20},{8,24},{12,28},{16,0},{20,4},{24,8},{28,12},{1,17},{... | collective-permute-start | bytes 1572872 | tf_op jit(solution)/shard_map/ppermute | solution.py:26
  44.7 14.9 %collective-permute-start.14 = (bf16[128,2048]{1,0:T(8,128)(2,1)S(1)}, bf16[128,2048]{1,0:T(8,128)(2,1)S(1)}, u32[]{:S(2)}, u32[]{:S(2)}) collective-permute-start(bf16[128,2048]{1,0:T(8,128)(2,1)S(1)} %collective-permute-done.7.refs_9_), channel_id=1, source_target_pairs={{0,8},{4,12},{8,0},{12,4},{16,24},{20,28},{24,16},{28,20},{1,9},{5... | collective-permute-start | bytes 1572872 | tf_op jit(solution)/shard_map/ppermute | solution.py:26
  46.0 21.7 %collective-permute-start.15 = (bf16[256,2048]{1,0:T(8,128)(2,1)S(1)}, bf16[256,2048]{1,0:T(8,128)(2,1)S(1)}, u32[]{:S(2)}, u32[]{:S(2)}) collective-permute-start(bf16[256,2048]{1,0:T(8,128)(2,1)S(1)} %pad_maximum_fusion.1), channel_id=1, source_target_pairs={{0,1},{1,0},{2,3},{3,2},{4,5},{5,4},{6,7},{7,6},{8,9},{9,8},{10,11... | collective-permute-start | bytes 3145736 | tf_op jit(solution)/shard_map/ppermute | solution.py:30
  47.5 19.5 %collective-permute-start.16 = (bf16[128,2048]{1,0:T(8,128)(2,1)S(1)}, bf16[128,2048]{1,0:T(8,128)(2,1)S(1)}, u32[]{:S(2)}, u32[]{:S(2)}) collective-permute-start(bf16[128,2048]{1,0:T(8,128)(2,1)S(1)} %get-tuple-element.105), channel_id=1, source_target_pairs={{0,8},{4,12},{8,0},{12,4},{16,24},{20,28},{24,16},{28,20},{1,9},{5... | collective-permute-start | bytes 1572872 | tf_op jit(solution)/shard_map/ppermute | solution.py:26
  48.3 18.7 %collective-permute-start.17 = (bf16[128,2048]{1,0:T(8,128)(2,1)S(1)}, bf16[128,2048]{1,0:T(8,128)(2,1)S(1)}, u32[]{:S(2)}, u32[]{:S(2)}) collective-permute-start(bf16[128,2048]{1,0:T(8,128)(2,1)S(1)} %get-tuple-element.105), channel_id=1, source_target_pairs={{0,16},{4,20},{8,24},{12,28},{16,0},{20,4},{24,8},{28,12},{1,17},{... | collective-permute-start | bytes 1572872 | tf_op jit(solution)/shard_map/ppermute | solution.py:26
  59.6 7.4 %collective-permute-start.18 = (bf16[128,2048]{1,0:T(8,128)(2,1)S(1)}, bf16[128,2048]{1,0:T(8,128)(2,1)S(1)}, u32[]{:S(2)}, u32[]{:S(2)}) collective-permute-start(bf16[128,2048]{1,0:T(8,128)(2,1)S(1)} %collective-permute-done.6.refs_5_), channel_id=1, source_target_pairs={{0,4},{4,0},{8,12},{12,8},{16,20},{20,16},{24,28},{28,24},{1,5},{5... | collective-permute-start | bytes 1572872 | tf_op jit(solution)/shard_map/ppermute | solution.py:26
  59.6 7.4 %collective-permute-start.19 = (bf16[128,2048]{1,0:T(8,128)(2,1)S(1)}, bf16[128,2048]{1,0:T(8,128)(2,1)S(1)}, u32[]{:S(2)}, u32[]{:S(2)}) collective-permute-start(bf16[128,2048]{1,0:T(8,128)(2,1)S(1)} %collective-permute-done.7.refs_9_), channel_id=1, source_target_pairs={{0,4},{4,0},{8,12},{12,8},{16,20},{20,16},{24,28},{28,24},{1,5},{5... | collective-permute-start | bytes 1572872 | tf_op jit(solution)/shard_map/ppermute | solution.py:26
  68.3 7.2 %collective-permute-start.24 = (bf16[1024,2048]{1,0:T(8,128)(2,1)S(1)}, bf16[1024,2048]{1,0:T(8,128)(2,1)S(1)}, u32[]{:S(2)}, u32[]{:S(2)}) collective-permute-start(bf16[1024,2048]{1,0:T(8,128)(2,1)S(1)} %pad_maximum_fusion), channel_id=1, source_target_pairs={{0,4},{4,0},{8,12},{12,8},{16,20},{20,16},{24,28},{28,24},{1,5},{5... | collective-permute-start | bytes 12582920 | tf_op jit(solution)/shard_map/ppermute | solution.py:26
  68.5 11.0 %collective-permute-start.23 = (bf16[256,2048]{1,0:T(8,128)(2,1)S(1)}, bf16[256,2048]{1,0:T(8,128)(2,1)S(1)}, u32[]{:S(2)}, u32[]{:S(2)}) collective-permute-start(bf16[256,2048]{1,0:T(8,128)(2,1)S(1)} %pad_maximum_fusion.3), channel_id=1, source_target_pairs={{0,4},{4,0},{8,12},{12,8},{16,20},{20,16},{24,28},{28,24},{1,5},{5... | collective-permute-start | bytes 3145736 | tf_op jit(solution)/shard_map/ppermute | solution.py:26
  69.0 16.4 %collective-permute-start.22 = (bf16[128,2048]{1,0:T(8,128)(2,1)S(1)}, bf16[128,2048]{1,0:T(8,128)(2,1)S(1)}, u32[]{:S(2)}, u32[]{:S(2)}) collective-permute-start(bf16[128,2048]{1,0:T(8,128)(2,1)S(1)} %collective-permute-done.13.refs_12_), channel_id=1, source_target_pairs={{0,1},{1,0},{2,3},{3,2},{4,5},{5,4},{6,7},{7,6},{8,9},{9,8},{10,11... | collective-permute-start | bytes 1572872 | tf_op jit(solution)/shard_map/ppermute | solution.py:30
  70.6 13.8 %collective-permute-start.20 = (bf16[128,2048]{1,0:T(8,128)(2,1)S(1)}, bf16[128,2048]{1,0:T(8,128)(2,1)S(1)}, u32[]{:S(2)}, u32[]{:S(2)}) collective-permute-start(bf16[128,2048]{1,0:T(8,128)(2,1)S(1)} %collective-permute-done.9.refs_2_), channel_id=1, source_target_pairs={{0,16},{4,20},{8,24},{12,28},{16,0},{20,4},{24,8},{28,12},{1,17},{... | collective-permute-start | bytes 1572872 | tf_op jit(solution)/shard_map/ppermute | solution.py:26
  72.1 13.3 %collective-permute-start.21 = (bf16[128,2048]{1,0:T(8,128)(2,1)S(1)}, bf16[128,2048]{1,0:T(8,128)(2,1)S(1)}, u32[]{:S(2)}, u32[]{:S(2)}) collective-permute-start(bf16[128,2048]{1,0:T(8,128)(2,1)S(1)} %collective-permute-done.17.refs_6_), channel_id=1, source_target_pairs={{0,8},{4,12},{8,0},{12,4},{16,24},{20,28},{24,16},{28,20},{1,9},{5... | collective-permute-start | bytes 1572872 | tf_op jit(solution)/shard_map/ppermute | solution.py:26
  77.9 6.5 %collective-permute-start.25 = (f32[2,1024]{1,0:T(2,128)S(1)}, f32[2,1024]{1,0:T(2,128)S(1)}, u32[]{:S(2)}, u32[]{:S(2)}) collective-permute-start(f32[2,1024]{1,0:T(2,128)S(1)} %pad_maximum_fusion.8), channel_id=1, source_target_pairs={{0,16},{4,20},{8,24},{12,28},{16,0},{20,4},{24,8},{28,12},{1,17},{... | collective-permute-start | bytes 24584 | tf_op jit(solution)/shard_map/ppermute | solution.py:26
  85.7 5.7 %collective-permute-start.29 = (bf16[768,2048]{1,0:T(8,128)(2,1)S(1)}, bf16[768,2048]{1,0:T(8,128)(2,1)S(1)}, u32[]{:S(2)}, u32[]{:S(2)}) collective-permute-start(bf16[768,2048]{1,0:T(8,128)(2,1)S(1)} %constant_dynamic-update-slice_fusion), channel_id=1, source_target_pairs={{0,4},{4,0},{8,12},{12,8},{16,20},{20,16},{24,28},{28,24},{1,5},{5... | collective-permute-start | bytes 9437192 | tf_op jit(solution)/shard_map/ppermute | solution.py:26
  85.8 9.7 %collective-permute-start.28 = (bf16[128,2048]{1,0:T(8,128)(2,1)S(1)}, bf16[128,2048]{1,0:T(8,128)(2,1)S(1)}, u32[]{:S(2)}, u32[]{:S(2)}) collective-permute-start(bf16[128,2048]{1,0:T(8,128)(2,1)S(1)} %collective-permute-done.22.refs_1_.refs_19_), channel_id=1, source_target_pairs={{0,4},{4,0},{8,12},{12,8},{16,20},{20,16},{24,28},{28,24},{1,5},{5... | collective-permute-start | bytes 1572872 | tf_op jit(solution)/shard_map/ppermute | solution.py:26
  86.3 8.4 %collective-permute-start.26 = (bf16[64,2048]{1,0:T(8,128)(2,1)S(1)}, bf16[64,2048]{1,0:T(8,128)(2,1)S(1)}, u32[]{:S(2)}, u32[]{:S(2)}) collective-permute-start(bf16[64,2048]{1,0:T(8,128)(2,1)S(1)} %get-tuple-element.161), channel_id=1, source_target_pairs={{0,8},{4,12},{8,0},{12,4},{16,24},{20,28},{24,16},{28,20},{1,9},{5... | collective-permute-start | bytes 786440 | tf_op jit(solution)/shard_map/ppermute | solution.py:26
  87.5 8.0 %collective-permute-start.27 = (bf16[64,2048]{1,0:T(8,128)(2,1)S(1)}, bf16[64,2048]{1,0:T(8,128)(2,1)S(1)}, u32[]{:S(2)}, u32[]{:S(2)}) collective-permute-start(bf16[64,2048]{1,0:T(8,128)(2,1)S(1)} %get-tuple-element.160), channel_id=1, source_target_pairs={{0,16},{4,20},{8,24},{12,28},{16,0},{20,4},{24,8},{28,12},{1,17},{... | collective-permute-start | bytes 786440 | tf_op jit(solution)/shard_map/ppermute | solution.py:26
  101.3 5.8 %collective-permute-start.34 = (f32[8,2048]{1,0:T(8,128)S(1)}, f32[8,2048]{1,0:T(8,128)S(1)}, u32[]{:S(2)}, u32[]{:S(2)}) collective-permute-start(f32[8,2048]{1,0:T(8,128)S(1)} %get-tuple-element.146), channel_id=1, source_target_pairs={{0,24},{4,28},{8,16},{12,20},{16,8},{20,12},{24,0},{28,4},{1,25},{... | collective-permute-start | bytes 196616 | tf_op jit(solution)/shard_map/ppermute | solution.py:26
  102.3 4.8 %collective-permute-start.32 = (f32[8,2048]{1,0:T(8,128)S(1)}, f32[8,2048]{1,0:T(8,128)S(1)}, u32[]{:S(2)}, u32[]{:S(2)}) collective-permute-start(f32[8,2048]{1,0:T(8,128)S(1)} %get-tuple-element.146), channel_id=1, source_target_pairs={{0,8},{4,12},{8,0},{12,4},{16,24},{20,28},{24,16},{28,20},{1,9},{5... | collective-permute-start | bytes 196616 | tf_op jit(solution)/shard_map/ppermute | solution.py:26
  117.7 9.9 %collective-permute-start.37 = (f32[1,2048]{1,0:T(1,128)S(1)}, f32[1,2048]{1,0:T(1,128)S(1)}, u32[]{:S(2)}, u32[]{:S(2)}) collective-permute-start(f32[1,2048]{1,0:T(1,128)S(1)} %add.8.refs_0_), channel_id=1, source_target_pairs={{0,2},{1,3},{2,0},{3,1},{4,6},{5,7},{6,4},{7,5},{8,10},{9,11},{10,... | collective-permute-start | bytes 24584 | tf_op jit(solution)/shard_map/ppermute | solution.py:30
  (14 other events, 82.3 us)

commit v10 on v9

--- a/solution.py
+++ b/solution.py
@@ -532,11 +532,11 @@
     first_pre = project_call(normed, first, tile, BF16)
     partial = project_call(normed, Shards(most), tile, F32)
     both = jnp.concatenate([both, send(after((both,), partial)[0], 4)], axis=1)
-    t6a, t6b, s6a, sb_out, first_pre, partial, own_t, both = after(
-        (t6a, t6b, s6a, sb, first_pre, partial, own_t, both)
-    )
-    quarter = half // 2
-    s6b = [send(sb_out[half : half + quarter], 2), send(sb_out[quarter:half], 4)]
+    t6a, t6b, s6a, sb_out, f6b_out, first_pre, partial, own_t, both = after(
+        (t6a, t6b, s6a, sb, f6b, first_pre, partial, own_t, both)
+    )
+    share = half * 3 // 8
+    s6b = [send(sb_out[half : half + share], 2), send(sb_out[share : 2 * share], 4), over(f6b_out[2 * share :])]
     s7a = core(s6a)
     c4 = core(stack(t6a, t6b, t2b, t4b, t2a, t4a))
     third = Shards(
@@ -544,8 +544,8 @@
         + [[t6a, t6b], cut(c4, 0, 1)]
     )
     back = back_call(where, grads, third)
-    s6b_low, s6b_high, s7a, back, both = after((*s6b, s7a, back, both))
-    last = [[s6a, s6b_low, s6b_high], [s7a, core(stack(s6b_low, s6b_high))]]
+    *s6b, s7a, back, both = after((*s6b, s7a, back, both))
+    last = [[s6a, *s6b], [s7a, core(stack(*s6b))]]
     second = Shards(most + last)
     second_pre, parts, whole, both = totals_call(
         where, normed, partial, Shards(last), len(most) * depth, first_pre, back, both, depth, tile

time: 129 us -> 128 us (level)
  waiting for transfers between devices: 58.4 us -> 56.7 us
    ppermute x33, waiting for transfers between devices: 56.4 us -> 54.7 us  [hop(): return lax.ppermute(value, 'seq', [(i, i ^ offset) for i in range(count)])]
    ppermute x5 -> x6, starting transfers between devices: 7.97 us -> 8.51 us  [swap_batch(): return lax.ppermute(value, 'batch', [(i, i ^ offset) for i in range(count)])]
  transfers between devices with their start and end apart: 38 -> 39, of which waited for: 21 -> 19; matrix products, arithmetic and copies ran while one was open for 1% -> 1% of each run, Pallas kernels for 18% -> 18%
where the time goes in v10:
time: 128 us
  waiting for transfers between devices  56.7 us (44%)
  starting transfers between devices  34.2 us (27%)
  Pallas kernels  31.7 us (25%)
  other arithmetic  3.81 us (3%)
    ppermute x33, waiting for transfers between devices, hop(): return lax.ppermute(value, 'seq', [(i, i ^ offset) for i in range(count)])  54.7 us
    ppermute x33, starting transfers between devices, hop(): return lax.ppermute(value, 'seq', [(i, i ^ offset) for i in range(count)])  25.6 us
    ppermute x6, starting transfers between devices, swap_batch(): return lax.ppermute(value, 'batch', [(i, i ^ offset) for i in range(count)])  8.51 us
    pallas_call x1, Pallas kernels, input_grad_call(): pl.pallas_call(kernel, out_shape=jax.ShapeDtypeStruct((rows, width), BF16...  7.29 us
    pallas_call x2, Pallas kernels, project_call(): pl.pallas_call(kernel, out_shape=jax.ShapeDtypeStruct((rows, width), dtyp...  5.38 us
    pallas_call x1, Pallas kernels, layer_call(): pl.pallas_call(kernel, out_shape=jax.ShapeDtypeStruct((rows, width), BF16...  3.91 us
    pallas_call x1, Pallas kernels, scan_call(): pl.pallas_call(kernel, out_shape=[wide, tall, tall, flat, flat], in_specs...  3.91 us
    pallas_call x1, Pallas kernels, totals_call(): pl.pallas_call(kernel, out_shape=[jax.ShapeDtypeStruct((rows, width), BF1...  3.81 us
  transfers between devices with their start and end apart: 39, of which 19 were waited for; matrix products, arithmetic and copies ran while one was open for 1% of the time, Pallas kernels for 18%

profile of v10, /device:TPU:0, one launch (start us, length us, event | category | flops | bytes accessed | tf_op | source)
XLA Modules:
  0.0 127.8 jit_solution(127387858911675533)
XLA Ops:
  0.8 1.4 %slice_select_fusion.1.refs_0_ = bf16[128,2048]{1,0:T(8,128)(2,1)S(1)} fusion(bf16[256,2048]{1,0:T(8,128)(2,1)} %param.14, bf16[256,2048]{1,0:T(8,128)(2,1)} %param.13, pred[]{:T(512)S(6)} %eq.5), kind=kLoop, calls=%fused_computation.7 | loop fusion | flops 262144 | bytes 1572865 | tf_op jit(solution)/shard_map/jit(_where)/select_n | solution.py:496
  2.2 3.0 %collective-permute-start = (bf16[128,2048]{1,0:T(8,128)(2,1)S(1)}, bf16[128,2048]{1,0:T(8,128)(2,1)S(1)}, u32[]{:S(2)}, u32[]{:S(2)}) collective-permute-start(bf16[128,2048]{1,0:T(8,128)(2,1)S(1)} %slice_select_fusion.1.refs_0_), channel_id=1, source_target_pairs={{0,8},{4,12},{8,0},{12,4},{16,24},{20,28},{24,16},{28,20},{1,9},{5... | collective-permute-start | bytes 1572872 | tf_op jit(solution)/shard_map/ppermute | solution.py:26
  5.2 1.5 %collective-permute-start.1 = (bf16[128,2048]{1,0:T(8,128)(2,1)S(1)}, bf16[128,2048]{1,0:T(8,128)(2,1)S(1)}, u32[]{:S(2)}, u32[]{:S(2)}) collective-permute-start(bf16[128,2048]{1,0:T(8,128)(2,1)S(1)} %slice_select_fusion.1.refs_0_), channel_id=1, source_target_pairs={{0,16},{4,20},{8,24},{12,28},{16,0},{20,4},{24,8},{28,12},{1,17},{... | collective-permute-start | bytes 1572872 | tf_op jit(solution)/shard_map/ppermute | solution.py:26
  10.7 3.3 %norm_rows.1 = (bf16[256,2048]{1,0:T(8,128)(2,1)S(1)}, bf16[2048,256]{1,0:T(8,128)(2,1)S(1)}, f32[256,1]{1,0:T(8,128)S(1)}) custom-call(s32[3]{0:T(128)S(1)} %pad_add_fusion.where_ref, bf16[256,2048]{1,0:T(8,128)(2,1)S(1)} %bitcast.14, bf16[256,2048]{1,0:T(8,128)(2,1)S(1)} %bitcast.17, f32[1,2048]{1,0:T(1,128)S(1)} %bitcast.20), custom_call_target="tpu_custom_call" | custom-call | flops 536870912 | bytes 4194304 | tf_op jit(solution)/shard_map/norm_rows/pallas_call | solution.py:138
  13.9 3.3 %collective-permute-done.5 = f32[2,512]{1,0:T(2,128)S(1)} collective-permute-done((f32[2,512]{1,0:T(2,128)S(1)}, f32[2,512]{1,0:T(2,128)S(1)}, u32[]{:S(2)}, u32[]{:S(2)}) %collective-permute-start.5) | collective-permute-done | bytes 4128 | tf_op jit(solution)/shard_map/ppermute | solution.py:26
  19.1 1.6 %collective-permute-start.7 = (bf16[128,2048]{1,0:T(8,128)(2,1)S(1)}, bf16[128,2048]{1,0:T(8,128)(2,1)S(1)}, u32[]{:S(2)}, u32[]{:S(2)}) collective-permute-start(bf16[128,2048]{1,0:T(8,128)(2,1)S(1)} %slice_select_fusion.refs_1_), channel_id=1, source_target_pairs={{0,16},{4,20},{8,24},{12,28},{16,0},{20,4},{24,8},{28,12},{1,17},{... | collective-permute-start | bytes 1572872 | tf_op jit(solution)/shard_map/ppermute | solution.py:26
  20.7 1.6 %collective-permute-start.8 = (bf16[256,2048]{1,0:T(8,128)(2,1)S(1)}, bf16[256,2048]{1,0:T(8,128)(2,1)S(1)}, u32[]{:S(2)}, u32[]{:S(2)}) collective-permute-start(bf16[256,2048]{1,0:T(8,128)(2,1)S(1)} %pad_maximum_fusion.2), channel_id=1, source_target_pairs={{0,1},{1,0},{2,3},{3,2},{4,5},{5,4},{6,7},{7,6},{8,9},{9,8},{10,11... | collective-permute-start | bytes 3145736 | tf_op jit(solution)/shard_map/ppermute | solution.py:30
  22.9 1.5 %collective-permute-start.9 = (bf16[128,2048]{1,0:T(8,128)(2,1)S(1)}, bf16[128,2048]{1,0:T(8,128)(2,1)S(1)}, u32[]{:S(2)}, u32[]{:S(2)}) collective-permute-start(bf16[128,2048]{1,0:T(8,128)(2,1)S(1)} %get-tuple-element.97), channel_id=1, source_target_pairs={{0,8},{4,12},{8,0},{12,4},{16,24},{20,28},{24,16},{28,20},{1,9},{5... | collective-permute-start | bytes 1572872 | tf_op jit(solution)/shard_map/ppermute | solution.py:26
  24.4 9.1 %collective-permute-done.6.refs_5_ = bf16[128,2048]{1,0:T(8,128)(2,1)S(1)} collective-permute-done((bf16[128,2048]{1,0:T(8,128)(2,1)S(1)}, bf16[128,2048]{1,0:T(8,128)(2,1)S(1)}, u32[]{:S(2)}, u32[]{:S(2)}) %collective-permute-start.6) | collective-permute-done | bytes 524320 | tf_op jit(solution)/shard_map/ppermute | solution.py:26
  34.5 8.3 %collective-permute-done.10.refs_5_ = bf16[128,2048]{1,0:T(8,128)(2,1)S(1)} collective-permute-done((bf16[128,2048]{1,0:T(8,128)(2,1)S(1)}, bf16[128,2048]{1,0:T(8,128)(2,1)S(1)}, u32[]{:S(2)}, u32[]{:S(2)}) %collective-permute-start.10) | collective-permute-done | bytes 524320 | tf_op jit(solution)/shard_map/ppermute | solution.py:26
  46.0 1.6 %collective-permute-start.15 = (bf16[256,2048]{1,0:T(8,128)(2,1)S(1)}, bf16[256,2048]{1,0:T(8,128)(2,1)S(1)}, u32[]{:S(2)}, u32[]{:S(2)}) collective-permute-start(bf16[256,2048]{1,0:T(8,128)(2,1)S(1)} %pad_maximum_fusion.1), channel_id=1, source_target_pairs={{0,1},{1,0},{2,3},{3,2},{4,5},{5,4},{6,7},{7,6},{8,9},{9,8},{10,11... | collective-permute-start | bytes 3145736 | tf_op jit(solution)/shard_map/ppermute | solution.py:30
  48.3 1.5 %collective-permute-start.17 = (bf16[128,2048]{1,0:T(8,128)(2,1)S(1)}, bf16[128,2048]{1,0:T(8,128)(2,1)S(1)}, u32[]{:S(2)}, u32[]{:S(2)}) collective-permute-start(bf16[128,2048]{1,0:T(8,128)(2,1)S(1)} %get-tuple-element.107), channel_id=1, source_target_pairs={{0,16},{4,20},{8,24},{12,28},{16,0},{20,4},{24,8},{28,12},{1,17},{... | collective-permute-start | bytes 1572872 | tf_op jit(solution)/shard_map/ppermute | solution.py:26
  49.9 9.2 %collective-permute-done.13.refs_12_ = bf16[128,2048]{1,0:T(8,128)(2,1)S(1)} collective-permute-done((bf16[128,2048]{1,0:T(8,128)(2,1)S(1)}, bf16[128,2048]{1,0:T(8,128)(2,1)S(1)}, u32[]{:S(2)}, u32[]{:S(2)}) %collective-permute-start.13) | collective-permute-done | bytes 524320 | tf_op jit(solution)/shard_map/ppermute | solution.py:26
  60.1 6.9 %collective-permute-done.16.refs_3_ = bf16[128,2048]{1,0:T(8,128)(2,1)S(1)} collective-permute-done((bf16[128,2048]{1,0:T(8,128)(2,1)S(1)}, bf16[128,2048]{1,0:T(8,128)(2,1)S(1)}, u32[]{:S(2)}, u32[]{:S(2)}) %collective-permute-start.16) | collective-permute-done | bytes 524320 | tf_op jit(solution)/shard_map/ppermute | solution.py:26
  69.0 1.6 %collective-permute-start.22 = (bf16[128,2048]{1,0:T(8,128)(2,1)S(1)}, bf16[128,2048]{1,0:T(8,128)(2,1)S(1)}, u32[]{:S(2)}, u32[]{:S(2)}) collective-permute-start(bf16[128,2048]{1,0:T(8,128)(2,1)S(1)} %collective-permute-done.13.refs_12_), channel_id=1, source_target_pairs={{0,1},{1,0},{2,3},{3,2},{4,5},{5,4},{6,7},{7,6},{8,9},{9,8},{10,11... | collective-permute-start | bytes 1572872 | tf_op jit(solution)/shard_map/ppermute | solution.py:30
  70.6 1.5 %collective-permute-start.20 = (bf16[128,2048]{1,0:T(8,128)(2,1)S(1)}, bf16[128,2048]{1,0:T(8,128)(2,1)S(1)}, u32[]{:S(2)}, u32[]{:S(2)}) collective-permute-start(bf16[128,2048]{1,0:T(8,128)(2,1)S(1)} %collective-permute-done.9.refs_2_), channel_id=1, source_target_pairs={{0,16},{4,20},{8,24},{12,28},{16,0},{20,4},{24,8},{28,12},{1,17},{... | collective-permute-start | bytes 1572872 | tf_op jit(solution)/shard_map/ppermute | solution.py:26
  73.2 2.4 %collective-permute-done.24.refs_1_.refs_16_ = bf16[1024,2048]{1,0:T(8,128)(2,1)S(1)} collective-permute-done((bf16[1024,2048]{1,0:T(8,128)(2,1)S(1)}, bf16[1024,2048]{1,0:T(8,128)(2,1)S(1)}, u32[]{:S(2)}, u32[]{:S(2)}) %collective-permute-start.24) | collective-permute-done | bytes 4194336 | tf_op jit(solution)/shard_map/ppermute | solution.py:26
  75.5 2.3 %project.3.refs_0_ = f32[256,2048]{1,0:T(8,128)S(1)} custom-call(bf16[256,2048]{1,0:T(8,128)(2,1)S(1)} %get-tuple-element.117.x_ref, bf16[256,2048]{1,0:T(8,128)(2,1)S(1)} %broadcast_select_fusion.refs_0_.refs_15_, bf16[1024,2048]{1,0:T(8,128)(2,1)S(1)} %collective-permute-done.24.refs_1_.refs_16_, ...), custom_call_target="tpu_custom_call" | custom-call | flops 1610612736 | bytes 6291456 | tf_op jit(solution)/shard_map/project/pallas_call | solution.py:166
  77.9 1.5 %collective-permute-start.25 = (f32[2,1024]{1,0:T(2,128)S(1)}, f32[2,1024]{1,0:T(2,128)S(1)}, u32[]{:S(2)}, u32[]{:S(2)}) collective-permute-start(f32[2,1024]{1,0:T(2,128)S(1)} %pad_maximum_fusion.8), channel_id=1, source_target_pairs={{0,16},{4,20},{8,24},{12,28},{16,0},{20,4},{24,8},{28,12},{1,17},{... | collective-permute-start | bytes 24584 | tf_op jit(solution)/shard_map/ppermute | solution.py:26
  79.4 3.1 %project.2.first_ref = bf16[256,2048]{1,0:T(8,128)(2,1)S(1)} custom-call(bf16[256,2048]{1,0:T(8,128)(2,1)S(1)} %get-tuple-element.117.x_ref, bf16[128,2048]{1,0:T(8,128)(2,1)S(1)} %slice_select_fusion.1.refs_0_, bf16[128,2048]{1,0:T(8,128)(2,1)S(1)} %slice_select_fusion.refs_1_, bf16[128,2048]{1,0:T(8,128)(2,1)S(1)} %collective-permute-done.2.refs_2_, ...), custom_call_target="tpu_custom_call" | custom-call | flops 2147483648 | bytes 8388608 | tf_op jit(solution)/shard_map/project/pallas_call | solution.py:166
  82.5 1.9 %collective-permute-done.25 = f32[2,1024]{1,0:T(2,128)S(1)} collective-permute-done((f32[2,1024]{1,0:T(2,128)S(1)}, f32[2,1024]{1,0:T(2,128)S(1)}, u32[]{:S(2)}, u32[]{:S(2)}) %collective-permute-start.25) | collective-permute-done | bytes 8224 | tf_op jit(solution)/shard_map/ppermute | solution.py:26
  88.5 2.9 %collective-permute-done.30.refs_4_ = bf16[768,2048]{1,0:T(8,128)(2,1)S(1)} collective-permute-done((bf16[768,2048]{1,0:T(8,128)(2,1)S(1)}, bf16[768,2048]{1,0:T(8,128)(2,1)S(1)}, u32[]{:S(2)}, u32[]{:S(2)}) %collective-permute-start.30) | collective-permute-done | bytes 3145760 | tf_op jit(solution)/shard_map/ppermute | solution.py:26
  91.4 3.0 %back_rows.1.back_ref = bf16[256,2048]{1,0:T(8,128)(2,1)S(1)} custom-call(s32[3]{0:T(128)S(1)} %pad_add_fusion.where_ref, bf16[2048,256]{1,0:T(8,128)(2,1)S(1)} %get-tuple-element.133.g_ref, bf16[256,2048]{1,0:T(8,128)(2,1)S(1)} %copy-done, bf16[1024,2048]{1,0:T(8,128)(2,1)S(1)} %collective-permute-done.24.refs_1_.refs_16_, ...), custom_call_target="tpu_custom_call" | custom-call | flops 2147483648 | bytes 8388608 | tf_op jit(solution)/shard_map/back_rows/pallas_call | solution.py:190
  94.7 1.8 %collective-permute-done.31.refs_6_.refs_24_ = bf16[128,2048]{1,0:T(8,128)(2,1)S(1)} collective-permute-done((bf16[128,2048]{1,0:T(8,128)(2,1)S(1)}, bf16[128,2048]{1,0:T(8,128)(2,1)S(1)}, u32[]{:S(2)}, u32[]{:S(2)}) %collective-permute-start.31) | collective-permute-done | bytes 524320 | tf_op jit(solution)/shard_map/ppermute | solution.py:26
  96.5 3.8 %project_totals.1 = (bf16[256,2048]{1,0:T(8,128)(2,1)S(1)}, f32[3,8,2048]{2,1,0:T(8,128)S(1)}, f32[8,2048]{1,0:T(8,128)S(1)}, f32[2,2048]{1,0:T(2,128)S(1)}) custom-call(s32[3]{0:T(128)S(1)} %pad_add_fusion.where_ref, bf16[256,2048]{1,0:T(8,128)(2,1)S(1)} %get-tuple-element.117.x_ref, bf16[256,2048]{1,0:T(8,128)(2,1)S(1)} %project.2.first_ref, ...), custom_call_target="tpu_custom_call" | custom-call | flops 536870912 | bytes 2097152 | tf_op jit(solution)/shard_map/project_totals/pallas_call | solution.py:291
  102.4 1.5 %collective-permute-start.34 = (f32[8,2048]{1,0:T(8,128)S(1)}, f32[8,2048]{1,0:T(8,128)S(1)}, u32[]{:S(2)}, u32[]{:S(2)}) collective-permute-start(f32[8,2048]{1,0:T(8,128)S(1)} %get-tuple-element.150), channel_id=1, source_target_pairs={{0,16},{4,20},{8,24},{12,28},{16,0},{20,4},{24,8},{28,12},{1,17},{... | collective-permute-start | bytes 196616 | tf_op jit(solution)/shard_map/ppermute | solution.py:26
  103.9 2.3 %collective-permute-done.35 = f32[8,2048]{1,0:T(8,128)S(1)} collective-permute-done((f32[8,2048]{1,0:T(8,128)S(1)}, f32[8,2048]{1,0:T(8,128)S(1)}, u32[]{:S(2)}, u32[]{:S(2)}) %collective-permute-start.35) | collective-permute-done | bytes 65568 | tf_op jit(solution)/shard_map/ppermute | solution.py:26
  106.9 1.4 %collective-permute-done.36.refs_2_ = f32[3,8,2048]{2,1,0:T(8,128)S(1)} collective-permute-done((f32[3,8,2048]{2,1,0:T(8,128)S(1)}, f32[3,8,2048]{2,1,0:T(8,128)S(1)}, u32[]{:S(2)}, u32[]{:S(2)}) %collective-permute-start.36) | collective-permute-done | bytes 196640 | tf_op jit(solution)/shard_map/ppermute | solution.py:26
  108.3 3.9 %scan_rows.1 = (bf16[256,2048]{1,0:T(8,128)(2,1)S(1)}, bf16[2048,256]{1,0:T(8,128)(2,1)S(1)}, bf16[2048,256]{1,0:T(8,128)(2,1)S(1)}, f32[1,2048]{1,0:T(1,128)S(1)}, f32[1,2048]{1,0:T(1,128)S(1)}) custom-call(s32[3]{0:T(128)S(1)} %pad_add_fusion.where_ref, bf16[256,2048]{1,0:T(8,128)(2,1)S(1)} %project.2.first_ref, ...), custom_call_target="tpu_custom_call" | custom-call | flops 805306368 | bytes 6291456 | tf_op jit(solution)/shard_map/scan_rows/pallas_call | solution.py:393
  112.8 3.9 %layer_rows.1 = bf16[256,2048]{1,0:T(8,128)(2,1)} custom-call(s32[3]{0:T(128)S(1)} %pad_add_fusion.where_ref, bf16[256,2048]{1,0:T(8,128)(2,1)S(1)} %get-tuple-element.151.x_ref, bf16[256,2048]{1,0:T(8,128)(2,1)S(1)} %bitcast.15, bf16[256,2048]{1,0:T(8,128)(2,1)S(1)} %copy-done, bf16[1024,2048]{1,0:T(8,128)(2,1)S(1)} %collective-permute-done.24.refs_1_.refs_16_, ...), custom_call_target="tpu_custom_call" | custom-call | flops 2147483648 | bytes 8388608 | tf_op jit(solution)/shard_map/layer_rows/pallas_call | solution.py:419
  116.7 2.6 %collective-permute-start.38 = (f32[1,2048]{1,0:T(1,128)S(1)}, f32[1,2048]{1,0:T(1,128)S(1)}, u32[]{:S(2)}, u32[]{:S(2)}) collective-permute-start(f32[1,2048]{1,0:T(1,128)S(1)} %add.8.refs_0_), channel_id=1, source_target_pairs={{0,2},{1,3},{2,0},{3,1},{4,6},{5,7},{6,4},{7,5},{8,10},{9,11},{10,... | collective-permute-start | bytes 24584 | tf_op jit(solution)/shard_map/ppermute | solution.py:30
  119.4 7.3 %input_grad_rows.1 = bf16[256,2048]{1,0:T(8,128)(2,1)} custom-call(s32[3]{0:T(128)S(1)} %pad_add_fusion.where_ref, bf16[2048,256]{1,0:T(8,128)(2,1)S(1)} %get-tuple-element.156.one_ref, bf16[2048,256]{1,0:T(8,128)(2,1)S(1)} %get-tuple-element.157.other_ref, bf16[256,2048]{1,0:T(8,128)(2,1)S(1)} %bitcast.16, f32[256,1]{1,0:T(8,128)S(1)} %get-tuple-element.158.scale_ref, ...), custom_call_target="tpu_custom_call" | custom-call | flops 4294967296 | bytes 16777216 | tf_op jit(solution)/shard_map/input_grad_rows/pallas_call | solution.py:458
  (96 shorter events, 24.2 us)
Async XLA Ops:
  2.2 15.0 %collective-permute-start = (bf16[128,2048]{1,0:T(8,128)(2,1)S(1)}, bf16[128,2048]{1,0:T(8,128)(2,1)S(1)}, u32[]{:S(2)}, u32[]{:S(2)}) collective-permute-start(bf16[128,2048]{1,0:T(8,128)(2,1)S(1)} %slice_select_fusion.1.refs_0_), channel_id=1, source_target_pairs={{0,8},{4,12},{8,0},{12,4},{16,24},{20,28},{24,16},{28,20},{1,9},{5... | collective-permute-start | bytes 1572872 | tf_op jit(solution)/shard_map/ppermute | solution.py:26
  5.2 13.4 %collective-permute-start.1 = (bf16[128,2048]{1,0:T(8,128)(2,1)S(1)}, bf16[128,2048]{1,0:T(8,128)(2,1)S(1)}, u32[]{:S(2)}, u32[]{:S(2)}) collective-permute-start(bf16[128,2048]{1,0:T(8,128)(2,1)S(1)} %slice_select_fusion.1.refs_0_), channel_id=1, source_target_pairs={{0,16},{4,20},{8,24},{12,28},{16,0},{20,4},{24,8},{28,12},{1,17},{... | collective-permute-start | bytes 1572872 | tf_op jit(solution)/shard_map/ppermute | solution.py:26
  6.7 11.9 %collective-permute-start.2 = (bf16[128,2048]{1,0:T(8,128)(2,1)S(1)}, bf16[128,2048]{1,0:T(8,128)(2,1)S(1)}, u32[]{:S(2)}, u32[]{:S(2)}) collective-permute-start(bf16[128,2048]{1,0:T(8,128)(2,1)S(1)} %slice_select_fusion.1.refs_0_), channel_id=1, source_target_pairs={{0,4},{4,0},{8,12},{12,8},{16,20},{20,16},{24,28},{28,24},{1,5},{5... | collective-permute-start | bytes 1572872 | tf_op jit(solution)/shard_map/ppermute | solution.py:26
  8.0 9.2 %collective-permute-start.3 = (bf16[128,2048]{1,0:T(8,128)(2,1)S(1)}, bf16[128,2048]{1,0:T(8,128)(2,1)S(1)}, u32[]{:S(2)}, u32[]{:S(2)}) collective-permute-start(bf16[128,2048]{1,0:T(8,128)(2,1)S(1)} %slice_select_fusion.refs_1_), channel_id=1, source_target_pairs={{0,4},{4,0},{8,12},{12,8},{16,20},{20,16},{24,28},{28,24},{1,5},{5... | collective-permute-start | bytes 1572872 | tf_op jit(solution)/shard_map/ppermute | solution.py:26
  10.1 7.1 %collective-permute-start.5 = (f32[2,512]{1,0:T(2,128)S(1)}, f32[2,512]{1,0:T(2,128)S(1)}, u32[]{:S(2)}, u32[]{:S(2)}) collective-permute-start(f32[2,512]{1,0:T(2,128)S(1)} %pad_maximum_fusion.9), channel_id=1, source_target_pairs={{0,8},{4,12},{8,0},{12,4},{16,24},{20,28},{24,16},{28,20},{1,9},{5... | collective-permute-start | bytes 12296 | tf_op jit(solution)/shard_map/ppermute | solution.py:26
  18.6 14.9 %collective-permute-start.6 = (bf16[128,2048]{1,0:T(8,128)(2,1)S(1)}, bf16[128,2048]{1,0:T(8,128)(2,1)S(1)}, u32[]{:S(2)}, u32[]{:S(2)}) collective-permute-start(bf16[128,2048]{1,0:T(8,128)(2,1)S(1)} %slice_select_fusion.refs_1_), channel_id=1, source_target_pairs={{0,8},{4,12},{8,0},{12,4},{16,24},{20,28},{24,16},{28,20},{1,9},{5... | collective-permute-start | bytes 1572872 | tf_op jit(solution)/shard_map/ppermute | solution.py:26
  19.1 14.9 %collective-permute-start.7 = (bf16[128,2048]{1,0:T(8,128)(2,1)S(1)}, bf16[128,2048]{1,0:T(8,128)(2,1)S(1)}, u32[]{:S(2)}, u32[]{:S(2)}) collective-permute-start(bf16[128,2048]{1,0:T(8,128)(2,1)S(1)} %slice_select_fusion.refs_1_), channel_id=1, source_target_pairs={{0,16},{4,20},{8,24},{12,28},{16,0},{20,4},{24,8},{28,12},{1,17},{... | collective-permute-start | bytes 1572872 | tf_op jit(solution)/shard_map/ppermute | solution.py:26
  20.7 23.5 %collective-permute-start.8 = (bf16[256,2048]{1,0:T(8,128)(2,1)S(1)}, bf16[256,2048]{1,0:T(8,128)(2,1)S(1)}, u32[]{:S(2)}, u32[]{:S(2)}) collective-permute-start(bf16[256,2048]{1,0:T(8,128)(2,1)S(1)} %pad_maximum_fusion.2), channel_id=1, source_target_pairs={{0,1},{1,0},{2,3},{3,2},{4,5},{5,4},{6,7},{7,6},{8,9},{9,8},{10,11... | collective-permute-start | bytes 3145736 | tf_op jit(solution)/shard_map/ppermute | solution.py:30
  22.4 20.5 %collective-permute-start.10 = (bf16[128,2048]{1,0:T(8,128)(2,1)S(1)}, bf16[128,2048]{1,0:T(8,128)(2,1)S(1)}, u32[]{:S(2)}, u32[]{:S(2)}) collective-permute-start(bf16[128,2048]{1,0:T(8,128)(2,1)S(1)} %get-tuple-element.97), channel_id=1, source_target_pairs={{0,16},{4,20},{8,24},{12,28},{16,0},{20,4},{24,8},{28,12},{1,17},{... | collective-permute-start | bytes 1572872 | tf_op jit(solution)/shard_map/ppermute | solution.py:26
  22.9 20.0 %collective-permute-start.9 = (bf16[128,2048]{1,0:T(8,128)(2,1)S(1)}, bf16[128,2048]{1,0:T(8,128)(2,1)S(1)}, u32[]{:S(2)}, u32[]{:S(2)}) collective-permute-start(bf16[128,2048]{1,0:T(8,128)(2,1)S(1)} %get-tuple-element.97), channel_id=1, source_target_pairs={{0,8},{4,12},{8,0},{12,4},{16,24},{20,28},{24,16},{28,20},{1,9},{5... | collective-permute-start | bytes 1572872 | tf_op jit(solution)/shard_map/ppermute | solution.py:26
  34.0 10.3 %collective-permute-start.11 = (bf16[128,2048]{1,0:T(8,128)(2,1)S(1)}, bf16[128,2048]{1,0:T(8,128)(2,1)S(1)}, u32[]{:S(2)}, u32[]{:S(2)}) collective-permute-start(bf16[128,2048]{1,0:T(8,128)(2,1)S(1)} %collective-permute-done.refs_4_), channel_id=1, source_target_pairs={{0,4},{4,0},{8,12},{12,8},{16,20},{20,16},{24,28},{28,24},{1,5},{5... | collective-permute-start | bytes 1572872 | tf_op jit(solution)/shard_map/ppermute | solution.py:26
  34.0 10.3 %collective-permute-start.12 = (bf16[128,2048]{1,0:T(8,128)(2,1)S(1)}, bf16[128,2048]{1,0:T(8,128)(2,1)S(1)}, u32[]{:S(2)}, u32[]{:S(2)}) collective-permute-start(bf16[128,2048]{1,0:T(8,128)(2,1)S(1)} %collective-permute-done.1.refs_8_), channel_id=1, source_target_pairs={{0,4},{4,0},{8,12},{12,8},{16,20},{20,16},{24,28},{28,24},{1,5},{5... | collective-permute-start | bytes 1572872 | tf_op jit(solution)/shard_map/ppermute | solution.py:26
  44.2 14.9 %collective-permute-start.13 = (bf16[128,2048]{1,0:T(8,128)(2,1)S(1)}, bf16[128,2048]{1,0:T(8,128)(2,1)S(1)}, u32[]{:S(2)}, u32[]{:S(2)}) collective-permute-start(bf16[128,2048]{1,0:T(8,128)(2,1)S(1)} %collective-permute-done.refs_4_), channel_id=1, source_target_pairs={{0,16},{4,20},{8,24},{12,28},{16,0},{20,4},{24,8},{28,12},{1,17},{... | collective-permute-start | bytes 1572872 | tf_op jit(solution)/shard_map/ppermute | solution.py:26
  44.7 14.9 %collective-permute-start.14 = (bf16[128,2048]{1,0:T(8,128)(2,1)S(1)}, bf16[128,2048]{1,0:T(8,128)(2,1)S(1)}, u32[]{:S(2)}, u32[]{:S(2)}) collective-permute-start(bf16[128,2048]{1,0:T(8,128)(2,1)S(1)} %collective-permute-done.7.refs_9_), channel_id=1, source_target_pairs={{0,8},{4,12},{8,0},{12,4},{16,24},{20,28},{24,16},{28,20},{1,9},{5... | collective-permute-start | bytes 1572872 | tf_op jit(solution)/shard_map/ppermute | solution.py:26
  46.0 21.7 %collective-permute-start.15 = (bf16[256,2048]{1,0:T(8,128)(2,1)S(1)}, bf16[256,2048]{1,0:T(8,128)(2,1)S(1)}, u32[]{:S(2)}, u32[]{:S(2)}) collective-permute-start(bf16[256,2048]{1,0:T(8,128)(2,1)S(1)} %pad_maximum_fusion.1), channel_id=1, source_target_pairs={{0,1},{1,0},{2,3},{3,2},{4,5},{5,4},{6,7},{7,6},{8,9},{9,8},{10,11... | collective-permute-start | bytes 3145736 | tf_op jit(solution)/shard_map/ppermute | solution.py:30
  47.5 19.5 %collective-permute-start.16 = (bf16[128,2048]{1,0:T(8,128)(2,1)S(1)}, bf16[128,2048]{1,0:T(8,128)(2,1)S(1)}, u32[]{:S(2)}, u32[]{:S(2)}) collective-permute-start(bf16[128,2048]{1,0:T(8,128)(2,1)S(1)} %get-tuple-element.107), channel_id=1, source_target_pairs={{0,8},{4,12},{8,0},{12,4},{16,24},{20,28},{24,16},{28,20},{1,9},{5... | collective-permute-start | bytes 1572872 | tf_op jit(solution)/shard_map/ppermute | solution.py:26
  48.3 18.7 %collective-permute-start.17 = (bf16[128,2048]{1,0:T(8,128)(2,1)S(1)}, bf16[128,2048]{1,0:T(8,128)(2,1)S(1)}, u32[]{:S(2)}, u32[]{:S(2)}) collective-permute-start(bf16[128,2048]{1,0:T(8,128)(2,1)S(1)} %get-tuple-element.107), channel_id=1, source_target_pairs={{0,16},{4,20},{8,24},{12,28},{16,0},{20,4},{24,8},{28,12},{1,17},{... | collective-permute-start | bytes 1572872 | tf_op jit(solution)/shard_map/ppermute | solution.py:26
  59.6 7.4 %collective-permute-start.18 = (bf16[128,2048]{1,0:T(8,128)(2,1)S(1)}, bf16[128,2048]{1,0:T(8,128)(2,1)S(1)}, u32[]{:S(2)}, u32[]{:S(2)}) collective-permute-start(bf16[128,2048]{1,0:T(8,128)(2,1)S(1)} %collective-permute-done.6.refs_5_), channel_id=1, source_target_pairs={{0,4},{4,0},{8,12},{12,8},{16,20},{20,16},{24,28},{28,24},{1,5},{5... | collective-permute-start | bytes 1572872 | tf_op jit(solution)/shard_map/ppermute | solution.py:26
  59.6 7.4 %collective-permute-start.19 = (bf16[128,2048]{1,0:T(8,128)(2,1)S(1)}, bf16[128,2048]{1,0:T(8,128)(2,1)S(1)}, u32[]{:S(2)}, u32[]{:S(2)}) collective-permute-start(bf16[128,2048]{1,0:T(8,128)(2,1)S(1)} %collective-permute-done.7.refs_9_), channel_id=1, source_target_pairs={{0,4},{4,0},{8,12},{12,8},{16,20},{20,16},{24,28},{28,24},{1,5},{5... | collective-permute-start | bytes 1572872 | tf_op jit(solution)/shard_map/ppermute | solution.py:26
  68.3 7.2 %collective-permute-start.24 = (bf16[1024,2048]{1,0:T(8,128)(2,1)S(1)}, bf16[1024,2048]{1,0:T(8,128)(2,1)S(1)}, u32[]{:S(2)}, u32[]{:S(2)}) collective-permute-start(bf16[1024,2048]{1,0:T(8,128)(2,1)S(1)} %pad_maximum_fusion), channel_id=1, source_target_pairs={{0,4},{4,0},{8,12},{12,8},{16,20},{20,16},{24,28},{28,24},{1,5},{5... | collective-permute-start | bytes 12582920 | tf_op jit(solution)/shard_map/ppermute | solution.py:26
  68.5 11.0 %collective-permute-start.23 = (bf16[256,2048]{1,0:T(8,128)(2,1)S(1)}, bf16[256,2048]{1,0:T(8,128)(2,1)S(1)}, u32[]{:S(2)}, u32[]{:S(2)}) collective-permute-start(bf16[256,2048]{1,0:T(8,128)(2,1)S(1)} %pad_maximum_fusion.3), channel_id=1, source_target_pairs={{0,4},{4,0},{8,12},{12,8},{16,20},{20,16},{24,28},{28,24},{1,5},{5... | collective-permute-start | bytes 3145736 | tf_op jit(solution)/shard_map/ppermute | solution.py:26
  69.0 16.4 %collective-permute-start.22 = (bf16[128,2048]{1,0:T(8,128)(2,1)S(1)}, bf16[128,2048]{1,0:T(8,128)(2,1)S(1)}, u32[]{:S(2)}, u32[]{:S(2)}) collective-permute-start(bf16[128,2048]{1,0:T(8,128)(2,1)S(1)} %collective-permute-done.13.refs_12_), channel_id=1, source_target_pairs={{0,1},{1,0},{2,3},{3,2},{4,5},{5,4},{6,7},{7,6},{8,9},{9,8},{10,11... | collective-permute-start | bytes 1572872 | tf_op jit(solution)/shard_map/ppermute | solution.py:30
  70.6 13.8 %collective-permute-start.20 = (bf16[128,2048]{1,0:T(8,128)(2,1)S(1)}, bf16[128,2048]{1,0:T(8,128)(2,1)S(1)}, u32[]{:S(2)}, u32[]{:S(2)}) collective-permute-start(bf16[128,2048]{1,0:T(8,128)(2,1)S(1)} %collective-permute-done.9.refs_2_), channel_id=1, source_target_pairs={{0,16},{4,20},{8,24},{12,28},{16,0},{20,4},{24,8},{28,12},{1,17},{... | collective-permute-start | bytes 1572872 | tf_op jit(solution)/shard_map/ppermute | solution.py:26
  72.1 13.3 %collective-permute-start.21 = (bf16[128,2048]{1,0:T(8,128)(2,1)S(1)}, bf16[128,2048]{1,0:T(8,128)(2,1)S(1)}, u32[]{:S(2)}, u32[]{:S(2)}) collective-permute-start(bf16[128,2048]{1,0:T(8,128)(2,1)S(1)} %collective-permute-done.17.refs_6_), channel_id=1, source_target_pairs={{0,8},{4,12},{8,0},{12,4},{16,24},{20,28},{24,16},{28,20},{1,9},{5... | collective-permute-start | bytes 1572872 | tf_op jit(solution)/shard_map/ppermute | solution.py:26
  77.9 6.5 %collective-permute-start.25 = (f32[2,1024]{1,0:T(2,128)S(1)}, f32[2,1024]{1,0:T(2,128)S(1)}, u32[]{:S(2)}, u32[]{:S(2)}) collective-permute-start(f32[2,1024]{1,0:T(2,128)S(1)} %pad_maximum_fusion.8), channel_id=1, source_target_pairs={{0,16},{4,20},{8,24},{12,28},{16,0},{20,4},{24,8},{28,12},{1,17},{... | collective-permute-start | bytes 24584 | tf_op jit(solution)/shard_map/ppermute | solution.py:26
  85.7 5.7 %collective-permute-start.30 = (bf16[768,2048]{1,0:T(8,128)(2,1)S(1)}, bf16[768,2048]{1,0:T(8,128)(2,1)S(1)}, u32[]{:S(2)}, u32[]{:S(2)}) collective-permute-start(bf16[768,2048]{1,0:T(8,128)(2,1)S(1)} %constant_dynamic-update-slice_fusion), channel_id=1, source_target_pairs={{0,4},{4,0},{8,12},{12,8},{16,20},{20,16},{24,28},{28,24},{1,5},{5... | collective-permute-start | bytes 9437192 | tf_op jit(solution)/shard_map/ppermute | solution.py:26
  85.8 8.7 %collective-permute-start.29 = (bf16[128,2048]{1,0:T(8,128)(2,1)S(1)}, bf16[128,2048]{1,0:T(8,128)(2,1)S(1)}, u32[]{:S(2)}, u32[]{:S(2)}) collective-permute-start(bf16[128,2048]{1,0:T(8,128)(2,1)S(1)} %collective-permute-done.22.refs_1_.refs_19_), channel_id=1, source_target_pairs={{0,4},{4,0},{8,12},{12,8},{16,20},{20,16},{24,28},{28,24},{1,5},{5... | collective-permute-start | bytes 1572872 | tf_op jit(solution)/shard_map/ppermute | solution.py:26
  86.3 8.1 %collective-permute-start.26 = (bf16[48,2048]{1,0:T(8,128)(2,1)S(1)}, bf16[48,2048]{1,0:T(8,128)(2,1)S(1)}, u32[]{:S(2)}, u32[]{:S(2)}) collective-permute-start(bf16[48,2048]{1,0:T(8,128)(2,1)S(1)} %get-tuple-element.165), channel_id=1, source_target_pairs={{0,8},{4,12},{8,0},{12,4},{16,24},{20,28},{24,16},{28,20},{1,9},{5... | collective-permute-start | bytes 589832 | tf_op jit(solution)/shard_map/ppermute | solution.py:26
  87.5 7.0 %collective-permute-start.27 = (bf16[48,2048]{1,0:T(8,128)(2,1)S(1)}, bf16[48,2048]{1,0:T(8,128)(2,1)S(1)}, u32[]{:S(2)}, u32[]{:S(2)}) collective-permute-start(bf16[48,2048]{1,0:T(8,128)(2,1)S(1)} %get-tuple-element.164), channel_id=1, source_target_pairs={{0,16},{4,20},{8,24},{12,28},{16,0},{20,4},{24,8},{28,12},{1,17},{... | collective-permute-start | bytes 589832 | tf_op jit(solution)/shard_map/ppermute | solution.py:26
  88.0 6.5 %collective-permute-start.28 = (bf16[32,2048]{1,0:T(8,128)(2,1)S(1)}, bf16[32,2048]{1,0:T(8,128)(2,1)S(1)}, u32[]{:S(2)}, u32[]{:S(2)}) collective-permute-start(bf16[32,2048]{1,0:T(8,128)(2,1)S(1)} %slice.35), channel_id=1, source_target_pairs={{0,1},{1,0},{2,3},{3,2},{4,5},{5,4},{6,7},{7,6},{8,9},{9,8},{10,11... | collective-permute-start | bytes 393224 | tf_op jit(solution)/shard_map/ppermute | solution.py:30
  100.3 5.9 %collective-permute-start.35 = (f32[8,2048]{1,0:T(8,128)S(1)}, f32[8,2048]{1,0:T(8,128)S(1)}, u32[]{:S(2)}, u32[]{:S(2)}) collective-permute-start(f32[8,2048]{1,0:T(8,128)S(1)} %get-tuple-element.150), channel_id=1, source_target_pairs={{0,24},{4,28},{8,16},{12,20},{16,8},{20,12},{24,0},{28,4},{1,25},{... | collective-permute-start | bytes 196616 | tf_op jit(solution)/shard_map/ppermute | solution.py:26
  116.7 9.9 %collective-permute-start.38 = (f32[1,2048]{1,0:T(1,128)S(1)}, f32[1,2048]{1,0:T(1,128)S(1)}, u32[]{:S(2)}, u32[]{:S(2)}) collective-permute-start(f32[1,2048]{1,0:T(1,128)S(1)} %add.8.refs_0_), channel_id=1, source_target_pairs={{0,2},{1,3},{2,0},{3,1},{4,6},{5,7},{6,4},{7,5},{8,10},{9,11},{10,... | collective-permute-start | bytes 24584 | tf_op jit(solution)/shard_map/ppermute | solution.py:30
  (15 other events, 87.1 us)
